TPU v7x, 256 devices: a whole 4x4x8 slice. The times are simulated.
256 devices in a mesh: gx: 8 (over y, x_lo), gy: 16 (over z, core), col: 2 (over x_hi).
Axes of the slice: x: 4 (x_hi: 2, x_lo: 2; x = x_hi * 2 + x_lo), y: 4, z: 8, core: 2. Of those that a mesh axis runs over, the one named last changes fastest.
Arguments:
- start_block: bfloat16 [2, 8, 64, 128, 256], P(None, 'gx', 'gy', None, 'col'), may hold values from -6 to 6
- hamiltonian: bfloat16 [2, 8, 64, 9, 128, 128], P(None, 'gx', 'gy'), as said below
- neighbour_index: int32 [8, 64, 9], P('gx', 'gy'), may hold values from 0 to 8, as said below
- block_count: int32 [8, 64], P('gx', 'gy'), may hold values from 1 to 9, as said below
Outputs:
- ritz_block: bfloat16 [2, 8, 64, 128, 256], P(None, 'gx', 'gy', None, 'col')
- projected: float32 [2, 256, 256], P(None, None, 'col')
Inputs may be any that keep to these rules, and one draw needn't show every extreme that they name: `neighbour_index`: slot 0 of every tile holds code 4 (the tile itself); a tile's 9 codes are distinct; the live codes of a tile stand in its first block_count slots; a bond is live on both of its sides or on neither. `block_count`: some tile has all 9 slots live. `hamiltonian`: the block of a tile toward code c equals the transpose of the block of that neighbour tile toward code 8 - c; the block toward code 4 is symmetric.
All inputs are finite; a program needn't handle non-finite values.
Results may differ from a plain program's by a relative error of at most 0.0067.
Values may be sent and summed in bfloat16 or wider, within the bound.
No kernel may reach another device: no remote copies, remote signals or barrier semaphores. Data moves between devices by JAX's collectives and lax.ppermute only.
A program may use at most 64 MiB of HBM per device.

v0:
```python
import jax
import jax.numpy as jnp
from jax import lax
from jax.sharding import PartitionSpec as P

NB = 9


def extended_2(block, sides, width):
    for axis, dim in sides:
        count = lax.axis_size(axis)
        forward = [(i, i + 1) for i in range(count - 1)]
        forward.append((count - 1, 0))
        backward = [(target, source) for source, target in forward]
        low = lax.ppermute(
            lax.slice_in_dim(block, block.shape[dim] - width, None, axis=dim), axis, forward
        )
        high = lax.ppermute(lax.slice_in_dim(block, 0, width, axis=dim), axis, backward)
        block = jnp.concatenate([low, block, high], axis=dim)
    return block


def offset_blocks(hamiltonian, neighbour_index, block_count):
    codes = jnp.arange(9, dtype=jnp.int32)
    slots = jnp.arange(NB, dtype=jnp.int32)
    selector = (neighbour_index[:, :, :, None] == codes) & (
        slots[None, None, :, None] < block_count[:, :, None, None]
    )
    return jnp.einsum(
        "xyjc,sxyjab->sxycab",
        selector.astype(jnp.bfloat16),
        hamiltonian,
        preferred_element_type=jnp.float32,
    ).astype(jnp.bfloat16)


def apply_ham(ordered, vectors):
    extended = extended_2(vectors, (("gx", 1), ("gy", 2)), 1)
    tiles_x = vectors.shape[1]
    tiles_y = vectors.shape[2]
    total = jnp.zeros(vectors.shape, jnp.float32)
    for code in range(9):
        beside = extended[:, code // 3 : code // 3 + tiles_x, code % 3 : code % 3 + tiles_y]
        total = total + jnp.einsum(
            "sxyij,sxyjk->sxyik", ordered[:, :, :, code], beside, preferred_element_type=jnp.float32
        )
    return total


def factor_parts(correlation, coupling):
    lower = jnp.linalg.cholesky(correlation)
    eye = jnp.broadcast_to(jnp.eye(correlation.shape[1], dtype=jnp.float32), lower.shape)
    inverse = lax.linalg.triangular_solve(lower, eye, left_side=True, lower=True)
    rotation = jnp.swapaxes(inverse, 1, 2).astype(jnp.bfloat16)
    half = jnp.einsum("sij,sjk->sik", inverse, coupling, precision=lax.Precision.HIGHEST)
    projected_full = jnp.einsum("sij,skj->sik", half, inverse, precision=lax.Precision.HIGHEST)
    return (rotation, projected_full)


def per_device(start_block, hamiltonian, neighbour_index, block_count):
    ordered = offset_blocks(hamiltonian, neighbour_index, block_count)
    first = (0.5 * apply_ham(ordered, start_block)).astype(jnp.bfloat16)
    second = (apply_ham(ordered, first) - start_block.astype(jnp.float32)).astype(jnp.bfloat16)
    image = apply_ham(ordered, second).astype(jnp.bfloat16)
    width_local = second.shape[4]
    owners = lax.axis_size("col")
    width_all = width_local * owners
    total_rows = (
        second.shape[1]
        * second.shape[2]
        * second.shape[3]
        * lax.axis_size("gx")
        * lax.axis_size("gy")
    )
    column_owner = lax.axis_index("col")
    every_column = lax.all_gather(second, "col", axis=4, tiled=True)
    paired = jnp.concatenate([second, image], axis=4)
    partial_gram = jnp.einsum(
        "sxytp,sxytq->spq", every_column, paired, preferred_element_type=jnp.float32
    )
    summed = lax.psum(partial_gram, ("gx", "gy")) / total_rows
    gathered = lax.all_gather(summed, "col", axis=2, tiled=True)
    gathered = gathered.reshape(2, width_all, owners, 2, width_local)
    correlation = gathered[:, :, :, 0, :].reshape(2, width_all, width_all)
    coupling = gathered[:, :, :, 1, :].reshape(2, width_all, width_all)
    rotation, projected_full = factor_parts(correlation, coupling)
    rotation_mine = lax.dynamic_slice_in_dim(rotation, column_owner * width_local, width_local, 2)
    ritz_block = jnp.einsum(
        "sxytp,spq->sxytq", every_column, rotation_mine, preferred_element_type=jnp.float32
    ).astype(jnp.bfloat16)
    projected = lax.dynamic_slice_in_dim(projected_full, column_owner * width_local, width_local, 2)
    return (ritz_block, projected)


def solution(mesh):
    return jax.shard_map(
        per_device,
        mesh=mesh,
        in_specs=(
            P(None, "gx", "gy", None, "col"),
            P(None, "gx", "gy", None, None, None),
            P("gx", "gy", None),
            P("gx", "gy"),
        ),
        out_specs=(P(None, "gx", "gy", None, "col"), P(None, None, "col")),
        check_vma=False,
    )
```

profile of v0, /device:TPU:1, one launch (start us, length us, event | category | flops | bytes accessed | tf_op | source)
XLA Modules:
  0.0 1247.7 jit_solution(17682293802342614680)
XLA Ops:
  7.2 2.1 collective-permute-start
  9.3 2.5 collective-permute-start.1
  12.6 2.5 convert_bitcast_fusion
  15.1 5.3 fusion.250
  22.2 3.1 collective-permute-start.2
  25.7 2.2 collective-permute-done.2
  28.3 2.3 collective-permute-done.3
  33.0 2.4 collective-permute-start.5
  36.2 1.5 fusion.167
  37.7 2.7 collective-permute-done.4
  40.4 4.5 collective-permute-done.5
  44.9 2.3 collective-permute-start.7
  48.7 1.4 fusion.146
  53.8 2.4 collective-permute-start.9
  56.1 12.3 all_gather.6
  68.8 6.3 collective-permute-start.11
  77.1 2.0 collective-permute-done.10
  82.3 998.5 %all-reduce.3.cloned.1.call-done = f32[2,256,256]{2,1,0:T(8,128)} async-done(((f32[2,256,256]{2,1,0:T(8,128)}), f32[2,256,256]{2,1,0:T(8,128)}) %all-reduce.3.cloned.1.call-update) | async-done | bytes 524304 | tf_op jit(solution)/shard_map/psum | solution.py:81
  1080.8 1.9 broadcast_multiply_fusion
  1085.2 21.9 %all-gather.2.cloned.1.call-done = f32[2,256,512]{2,1,0:T(8,128)} async-done(((f32[2,256,256]{2,1,0:T(8,128)}), f32[2,256,512]{2,1,0:T(8,128)}) %all-gather.2.cloned.1.call-update) | async-done | bytes 1048592 | tf_op jit(solution)/shard_map/all_gather | solution.py:82
  1107.1 1.9 reshape.323
  1109.0 2.8 slice_reduce_fusion
  1114.2 23.5 %custom-call.16 = f32[2,128,128]{2,1,0:T(8,128)S(1)} custom-call(f32[2,128,128]{2,1,0:T(8,128)S(1)} %cholesky.122), custom_call_target="Cholesky" | custom-call | tf_op jit(solution)/shard_map/jit(cholesky)/cholesky | solution.py:51
  1138.4 19.7 %custom-call.17 = f32[2,1,128,128]{2,3,1,0:T(8,128)S(1)} custom-call(f32[2,1,128,128]{3,2,1,0:T(8,128)S(1)} %select_bitcast_fusion), custom_call_target="InvertDiagBlocksLowerTriangular" | custom-call | tf_op jit(solution)/shard_map/jit(cholesky)/cholesky | solution.py:51
  1160.6 23.5 %custom-call.18 = f32[2,128,128]{2,1,0:T(8,128)S(1)} custom-call(f32[2,128,128]{2,1,0:T(8,128)S(1)} %convolution_subtract_fusion.1), custom_call_target="Cholesky" | custom-call | tf_op jit(solution)/shard_map/jit(cholesky)/cholesky | solution.py:51
  1185.9 5.2 while.1
  1186.6 2.0 bitcast_dynamic-update-slice_fusion.2
  1189.2 2.0 bitcast_dynamic-update-slice_fusion.2
  1191.2 40.1 %custom-call.19 = f32[2,2,128,128]{2,3,1,0:T(8,128)S(1)} custom-call(f32[2,2,128,128]{3,2,1,0:T(8,128)} %bitcast.247), custom_call_target="InvertDiagBlocksLowerTriangular" | custom-call | tf_op jit(solution)/shard_map/triangular_solve | solution.py:53
  1233.4 2.3 reshape_squeeze.7
  1235.7 1.7 fusion.34
  1238.1 2.1 fusion.28
  (122 shorter events, 31.7 us)
Async XLA Ops:
  7.2 5.5 copy-start
  7.2 1073.7 %all-reduce.3.cloned.1.call-start = ((), (), s32[]{:S(2)}) async-start(), calls=%async_computation | async-start | bytes 1048576 | tf_op jit(solution)/shard_map/psum | solution.py:81
  7.2 13.6 %collective-permute-start = (bf16[2,1,4,128,128]{4,3,2,0,1:T(8,128)(2,1)}, bf16[2,1,4,128,128]{4,3,2,0,1:T(8,128)(2,1)S(1)}, u32[]{:S(2)}, u32[]{:S(2)}) collective-permute-start(bf16[2,1,4,128,128]{4,3,2,0,1:T(8,128)(2,1)} %bitcast.226), channel_id=1, source_target_pairs={{0,32},{32,64},{64,96},{96,128},{128,160},{160,192},{192,224},{224... | collective-permute-start | bytes 786440 | tf_op jit(solution)/shard_map/ppermute | solution.py:15
  9.3 12.8 %collective-permute-start.1 = (bf16[2,1,4,128,128]{4,3,2,0,1:T(8,128)(2,1)}, bf16[2,1,4,128,128]{4,3,2,0,1:T(8,128)(2,1)S(1)}, u32[]{:S(2)}, u32[]{:S(2)}) collective-permute-start(bf16[2,1,4,128,128]{4,3,2,0,1:T(8,128)(2,1)} %bitcast.227), channel_id=1, source_target_pairs={{32,0},{64,32},{96,64},{128,96},{160,128},{192,160},{224,192},{0,2... | collective-permute-start | bytes 786440 | tf_op jit(solution)/shard_map/ppermute | solution.py:18
  20.5 10.4 copy-start.4
  20.5 10.4 copy-start.6
  20.5 10.4 copy-start.8
  20.5 10.4 copy-start.10
  20.5 10.4 copy-start.12
  20.5 10.4 copy-start.14
  20.5 10.4 copy-start.2
  20.5 10.7 copy-start.18
  20.5 10.9 copy-start.16
  22.2 5.7 collective-permute-start.2
  25.3 5.4 collective-permute-start.3
  31.7 8.7 collective-permute-start.4
  33.0 11.9 collective-permute-start.5
  36.2 14.1 %copy-start.9 = (bf16[2,1,4,1,128,128]{5,3,4,0,2,1:T(2,128)(2,1)S(1)}, bf16[2,1,4,1,128,128]{5,3,4,0,2,1:T(2,128)(2,1)}, u32[]{:S(2)}) copy-start(bf16[2,1,4,1,128,128]{5,3,4,0,2,1:T(2,128)(2,1)} %copy-done.8) | copy-start | bytes 786436
  36.2 14.4 %copy-start.7 = (bf16[2,1,4,1,128,128]{5,3,4,0,2,1:T(2,128)(2,1)S(1)}, bf16[2,1,4,1,128,128]{5,3,4,0,2,1:T(2,128)(2,1)}, u32[]{:S(2)}) copy-start(bf16[2,1,4,1,128,128]{5,3,4,0,2,1:T(2,128)(2,1)} %copy-done.6) | copy-start | bytes 786436
  36.2 14.8 %copy-start.5 = (bf16[2,1,4,1,128,128]{5,3,4,0,2,1:T(2,128)(2,1)S(1)}, bf16[2,1,4,1,128,128]{5,3,4,0,2,1:T(2,128)(2,1)}, u32[]{:S(2)}) copy-start(bf16[2,1,4,1,128,128]{5,3,4,0,2,1:T(2,128)(2,1)} %copy-done.4) | copy-start | bytes 786436
  37.7 13.6 %copy-start.3 = (bf16[2,1,4,1,128,128]{5,3,4,0,2,1:T(2,128)(2,1)S(1)}, bf16[2,1,4,1,128,128]{5,3,4,0,2,1:T(2,128)(2,1)}, u32[]{:S(2)}) copy-start(bf16[2,1,4,1,128,128]{5,3,4,0,2,1:T(2,128)(2,1)} %copy-done.2) | copy-start | bytes 786436
  44.9 6.1 collective-permute-start.7
  47.2 3.1 collective-permute-start.6
  51.7 16.7 %copy-start.15 = (bf16[2,1,4,1,128,128]{5,3,4,0,2,1:T(2,128)(2,1)S(1)}, bf16[2,1,4,1,128,128]{5,3,4,0,2,1:T(2,128)(2,1)}, u32[]{:S(2)}) copy-start(bf16[2,1,4,1,128,128]{5,3,4,0,2,1:T(2,128)(2,1)} %copy-done.14) | copy-start | bytes 786436
  52.1 24.4 %copy-start.13 = (bf16[2,1,4,1,128,128]{5,3,4,0,2,1:T(2,128)(2,1)S(1)}, bf16[2,1,4,1,128,128]{5,3,4,0,2,1:T(2,128)(2,1)}, u32[]{:S(2)}) copy-start(bf16[2,1,4,1,128,128]{5,3,4,0,2,1:T(2,128)(2,1)} %copy-done.12) | copy-start | bytes 786436
  52.1 24.7 %copy-start.11 = (bf16[2,1,4,1,128,128]{5,3,4,0,2,1:T(2,128)(2,1)S(1)}, bf16[2,1,4,1,128,128]{5,3,4,0,2,1:T(2,128)(2,1)}, u32[]{:S(2)}) copy-start(bf16[2,1,4,1,128,128]{5,3,4,0,2,1:T(2,128)(2,1)} %copy-done.10) | copy-start | bytes 786436
  52.5 16.2 %collective-permute-start.8 = (bf16[2,1,4,128,128]{3,4,2,0,1:T(8,128)(2,1)S(1)}, bf16[2,1,4,128,128]{3,4,2,0,1:T(8,128)(2,1)S(1)}, u32[]{:S(2)}, u32[]{:S(2)}) collective-permute-start(bf16[2,1,4,128,128]{3,4,2,0,1:T(8,128)(2,1)S(1)} %fusion.26), channel_id=1, source_target_pairs={{0,32},{32,64},{64,96},{96,128},{128,160},{160,192},{192,224},{224... | collective-permute-start | bytes 786440 | tf_op jit(solution)/shard_map/ppermute | solution.py:15
  53.8 15.0 %collective-permute-start.9 = (bf16[2,1,4,128,128]{3,4,2,0,1:T(8,128)(2,1)S(1)}, bf16[2,1,4,128,128]{3,4,2,0,1:T(8,128)(2,1)S(1)}, u32[]{:S(2)}, u32[]{:S(2)}) collective-permute-start(bf16[2,1,4,128,128]{3,4,2,0,1:T(8,128)(2,1)S(1)} %fusion.26), channel_id=1, source_target_pairs={{32,0},{64,32},{96,64},{128,96},{160,128},{192,160},{224,192},{0,2... | collective-permute-start | bytes 786440 | tf_op jit(solution)/shard_map/ppermute | solution.py:18
  68.4 12.7 %copy-start.20 = (bf16[2,1,4,128,256]{3,4,2,0,1:T(8,128)(2,1)}, bf16[2,1,4,128,256]{3,4,2,0,1:T(8,128)(2,1)S(1)}, u32[]{:S(2)}) copy-start(bf16[2,1,4,128,256]{3,4,2,0,1:T(8,128)(2,1)S(1)} %all_gather.6) | copy-start | bytes 1572868
  68.8 11.1 collective-permute-start.11
  75.1 4.0 collective-permute-start.10
  82.2 1024.9 %all-gather.2.cloned.1.call-start = ((), (), s32[]{:S(2)}) async-start(), calls=%async_computation.1 | async-start | bytes 1572864 | tf_op jit(solution)/shard_map/all_gather | solution.py:82
  (5 other events, 12.0 us)
Sparse Core Ops, SparseCore 0:
  82.4 998.4 all-reduce.2
  1082.8 24.2 all-gather.1
where the time goes:
time: 1250 us
  waiting for transfers between devices  1040 us (83%)
  other arithmetic  113 us (9%)
  starting transfers between devices  25.2 us (2%)
  matrix products  23.7 us (2%)
  local copies, waits for them, and re-layouts  22.8 us (2%)
  between operations  14.6 us (1%)
    psum x1, waiting for transfers between devices, per_device(): summed = lax.psum(partial_gram, ('gx', 'gy')) / total_rows  999 us
    another operation x9, other arithmetic, factor_parts(): lower = jnp.linalg.cholesky(correlation)  68.2 us
    another operation x4, other arithmetic, factor_parts(): lax.linalg.triangular_solve(lower, eye, left_side=True, lower=True)  42.3 us
  transfers between devices with their start and end apart: 14, of which 10 were waited for; matrix products, arithmetic and copies ran while one was open for 2% of the time, Pallas kernels for 0%

commit v1 on v0

v1 whole, which is shorter than its diff:
```python
import functools

import jax
import jax.numpy as jnp
from jax import lax
from jax.experimental import pallas as pl
from jax.experimental.pallas import tpu as pltpu
from jax.sharding import PartitionSpec as P

NB = 9
T = 128
AXES = ("gx", "gy", "col")
BF = jnp.bfloat16
F32 = jnp.float32
SPIN, COL, PAR_Y, PAR_X = 36, 37, 38, 39


def col_of(gx, spin):
    return spin ^ ((gx >> 1) & 1)


def device(sizes, gx, gy, col):
    return ((gx % sizes[0]) * sizes[1] + gy % sizes[1]) * sizes[2] + col


def pairs(sizes, target):
    out = []
    for gx in range(sizes[0]):
        for gy in range(sizes[1]):
            for spin in range(2):
                there = target(gx, gy)
                there_gx = there[0] % sizes[0]
                out.append(
                    (
                        device(sizes, gx, gy, col_of(gx, spin)),
                        device(sizes, there_gx, there[1], col_of(there_gx, spin)),
                    )
                )
    return out


def partner(index, kind):
    if kind == 0:
        return index
    return index + 1 if (index % 2 == 0) == (kind == 1) else index - 1


def swap(sizes, block, kind_x, kind_y):
    perm = pairs(sizes, lambda gx, gy: (partner(gx, kind_x), partner(gy, kind_y)))
    return lax.ppermute(block, AXES, perm)


def shift(sizes, block, dx, dy):
    return lax.ppermute(block, AXES, pairs(sizes, lambda gx, gy: (gx + dx, gy + dy)))


def swap_col(sizes, block):
    perm = [(d, d ^ 1) for d in range(sizes[0] * sizes[1] * 2)]
    return lax.ppermute(block, AXES, perm)


def exchange(sizes, pieces):
    groups = [
        [device(sizes, gx, gy, col_of(gx, spin)) for gx in range(sizes[0]) for gy in range(sizes[1])]
        for spin in range(2)
    ]
    return lax.all_to_all(pieces, AXES, 0, 0, axis_index_groups=groups, tiled=True)


def dot(a, b, dims=((1,), (0,))):
    return lax.dot_general(a, b, (dims, ((), ())), preferred_element_type=F32)


def split(a):
    high = a.astype(BF)
    return high, (a - high.astype(F32)).astype(BF)


def dot3(a, b, dims=((1,), (0,))):
    (ah, al), (bh, bl) = split(a), split(b)
    return dot(ah, bh, dims) + (dot(ah, bl, dims) + dot(al, bh, dims))


def h_block(m, h, tile, side, dy):
    slot = m[(tile * 3 + side) * 3 + dy]
    block = h[0, 0, tile, jnp.maximum(slot, 0)]
    return jnp.where(slot >= 0, block, jnp.zeros_like(block))


def h_row(m, h, tile, side, dys):
    return jnp.concatenate([h_block(m, h, tile, side, dy) for dy in dys], axis=1)


def fill(m, ext, middle, p, q):
    par = m[PAR_Y]
    ext[1:5] = middle
    ext[pl.ds(jnp.where(par == 0, 5, 0), 1)] = p
    ext[pl.ds(jnp.where(par == 0, 0, 5), 1)] = q


def store_sides(m, ref, p_ref, q_ref):
    par = m[PAR_Y]
    p_ref[...] = ref[pl.ds(jnp.where(par == 0, 3, 0), 1)]
    q_ref[...] = ref[pl.ds(jnp.where(par == 0, 0, 3), 1)]


def join_kernel(m, start, other, v, p, q):
    own = start[pl.ds(m[SPIN], 1)][0, 0]
    first_col = m[COL] == 0
    v[:, :, :T] = jnp.where(first_col, own, other[...])
    v[:, :, T:] = jnp.where(first_col, other[...], own)
    store_sides(m, v, p, q)


def own_kernel(m, h, v, p, q, acc, ext):
    fill(m, ext, v[...], p[...], q[...])
    for tile in range(4):
        row = h_row(m, h, tile, 0, range(3))
        acc[tile] = dot(row, ext[tile : tile + 3].reshape(3 * T, 2 * T))


def side_kernel(m, h, a, b, ca, cb, acc, *rest, last):
    if last:
        v, out, low, high, ext_a, ext_b = rest
    else:
        out, p, q, ext_a, ext_b = rest
    fill(m, ext_a, a[...], ca[0:1], ca[1:2])
    fill(m, ext_b, b[...], cb[0:1], cb[1:2])
    for tile in range(4):
        total = acc[tile]
        for side, ext in ((1, ext_a), (2, ext_b)):
            row = h_row(m, h, tile, side, range(3))
            total += dot(row, ext[tile : tile + 3].reshape(3 * T, 2 * T))
        if last:
            out[tile] = (total - v[tile].astype(F32)).astype(BF)
        else:
            out[tile] = (0.5 * total).astype(BF)
    if last:
        low[...] = out[0:1]
        high[...] = out[3:4]
    else:
        store_sides(m, out, p, q)


def inner_kernel(m, h, s, corr, acc):
    flat = s[...].reshape(4 * T, 2 * T)
    corr[...] = dot(flat, flat, ((0,), (0,)))
    for tile in range(4):
        total = 0.5 * dot(h_block(m, h, tile, 0, 1), s[tile])
        if tile < 3:
            total += dot(h_block(m, h, tile, 0, 2), s[tile + 1])
        acc[tile] = total


def places():
    shape = (2 * T, 2 * T)
    return lax.broadcasted_iota(jnp.int32, shape, 0), lax.broadcasted_iota(jnp.int32, shape, 1)


def gram_kernel(m, h, s, above, right, right_low, right_high, acc, corr, out, ext):
    ext[0:1] = right_low[...]
    ext[1:5] = right[...]
    ext[5:6] = right_high[...]
    side = 1 + m[PAR_X]
    half = jnp.zeros((2 * T, 2 * T), F32)
    for tile in range(4):
        total = acc[tile]
        if tile == 3:
            total += dot(h_block(m, h, tile, 0, 2), above[0])
        row = h_row(m, h, tile, side, range(3))
        total += dot(row, ext[tile : tile + 3].reshape(3 * T, 2 * T))
        high, low = split(total)
        half += dot(s[tile], high, ((0,), (0,))) + dot(s[tile], low, ((0,), (0,)))
    coupling = half + half.T
    rows, cols = places()
    both = jnp.where(rows >= cols, corr[...], coupling)
    diagonal = jnp.sum(jnp.where(rows == cols, coupling, 0.0), axis=1, keepdims=True)
    lane = lax.broadcasted_iota(jnp.int32, (T, T), 1)
    extra = jnp.where(lane == 0, diagonal[:T], jnp.where(lane == 1, diagonal[T:], 0.0))
    out[:, 0, :] = jnp.concatenate([both[:T], both[T:], extra], axis=1)


def lower_part(e, rows, cols):
    return jnp.where(rows > cols, e, jnp.where(rows == cols, 0.5 * e, 0.0))


def final_kernel(m, packed, s, keep, send, p_keep, p_send, x_ref, a_ref):
    rows, cols = places()
    table = packed[:, 0, :]
    both = jnp.concatenate([table[:, : 2 * T], table[:, 2 * T : 4 * T]], axis=0)
    diagonal = jnp.concatenate([table[:, 4 * T : 4 * T + 1], table[:, 4 * T + 1 : 4 * T + 2]], axis=0)
    turned = both.T
    corr = jnp.where(rows >= cols, both, turned)
    coupling = jnp.where(rows < cols, both, jnp.where(rows == cols, diagonal, turned))
    on_diagonal = jnp.where(rows == cols, corr, 0.0)
    scale_row = 1.0 / jnp.sqrt(jnp.sum(on_diagonal, axis=0, keepdims=True))
    scale_col = 1.0 / jnp.sqrt(jnp.sum(on_diagonal, axis=1, keepdims=True))
    scaled = corr * scale_row * scale_col
    unit = (rows == cols).astype(F32)

    a_ref[...] = scaled
    x_ref[...] = unit - lower_part(scaled - unit, rows, cols)

    def step(state):
        count, _ = state
        x = x_ref[...]
        e = dot3(dot3(x, a_ref[...]), x, ((1,), (1,))) - unit
        x_ref[...] = x - dot3(lower_part(e, rows, cols), x)
        return count + 1, jnp.sum(e * e)

    def more(state):
        count, size = state
        return (count < 12) & (size >= 4e-6) & (size < 1e4)

    _, size = lax.while_loop(more, step, (0, F32(1.0)))

    @pl.when(jnp.logical_not(size < 4e-6))
    def _():
        a_ref[...] = scaled
        x_ref[...] = unit

        def eliminate(j, carry):
            row = a_ref[pl.ds(j, 1), :]
            pivot = jnp.sum(jnp.where(cols[:1] == j, row, 0.0), axis=1, keepdims=True)
            a = a_ref[...]
            column = jnp.sum(jnp.where(cols == j, a, 0.0), axis=1, keepdims=True)
            factor = jnp.where(rows[:, :1] > j, column / pivot, 0.0)
            x = x_ref[...]
            x_row = x_ref[pl.ds(j, 1), :]
            a_ref[...] = a - factor * row
            x_ref[...] = x - factor * x_row
            return carry

        lax.fori_loop(0, 2 * T, eliminate, 0)
        pivots = jnp.sum(jnp.where(rows == cols, a_ref[...], 0.0), axis=1, keepdims=True)
        x_ref[...] = x_ref[...] / jnp.sqrt(pivots)

    x = x_ref[...] * scale_row
    rotation = x.astype(BF)
    ritz = dot(s[...].reshape(4 * T, 2 * T), rotation, ((1,), (1,))).astype(BF)
    ritz = ritz.reshape(4, T, 2 * T)
    projected = dot3(dot3(x, coupling), x, ((1,), (1,)))
    first_col = m[COL] == 0
    keep[...] = jnp.where(first_col, ritz[:, :, :T], ritz[:, :, T:])
    send[...] = jnp.where(first_col, ritz[:, :, T:], ritz[:, :, :T])
    p_keep[...] = jnp.where(first_col, projected[:, :T], projected[:, T:])
    p_send[...] = jnp.where(first_col, projected[:, T:], projected[:, :T])


def whole(shape):
    return pl.BlockSpec(shape, lambda i, m, n=len(shape): (0,) * n)


def call(kernel, m, arrays, outs, scratch=(), with_h=None, flops=0, name=None):
    specs = [whole(a.shape) for a in arrays]
    if with_h is not None:
        shape = (1,) + with_h.shape[1:]
        specs.insert(0, pl.BlockSpec(shape, lambda i, m: (m[SPIN], 0, 0, 0, 0, 0)))
        arrays = [with_h, *arrays]
    moved = sum(a.size * a.dtype.itemsize for a in arrays) + sum(o.size * o.dtype.itemsize for o in outs)
    return pl.pallas_call(
        kernel,
        out_shape=outs,
        grid_spec=pltpu.PrefetchScalarGridSpec(
            num_scalar_prefetch=1,
            grid=(1,),
            in_specs=specs,
            out_specs=[whole(o.shape) for o in outs],
            scratch_shapes=list(scratch),
        ),
        compiler_params=pltpu.CompilerParams(vmem_limit_bytes=32 * 1024 * 1024),
        cost_estimate=pl.CostEstimate(flops=flops, bytes_accessed=moved, transcendentals=0),
        name=name,
    )(m, *arrays)


def table(neighbour_index, block_count):
    gx, gy, col = (lax.axis_index(a) for a in AXES)
    spin = col ^ ((gx >> 1) & 1)
    toward = jnp.where(gx % 2 == 0, 1, -1)
    dx = jnp.stack([jnp.zeros_like(toward), toward, -toward])
    codes = (dx[:, None] + 1) * 3 + jnp.arange(3, dtype=jnp.int32)[None, :]
    slots = jnp.arange(NB, dtype=jnp.int32)
    index, count = neighbour_index[0], block_count[0]
    match = (index[:, None, None, :] == codes[None, :, :, None]) & (
        slots < count[:, None, None, None]
    )
    found = jnp.sum(jnp.where(match, slots + 1, 0), axis=-1) - 1
    scalars = jnp.stack([spin, col, gy % 2, gx % 2])
    return spin, col, jnp.concatenate([found.reshape(-1), scalars]).astype(jnp.int32)


def shaped(shape, dtype):
    return jax.ShapeDtypeStruct(shape, dtype)


def per_device(start_block, hamiltonian, neighbour_index, block_count):
    sizes = tuple(lax.axis_size(a) for a in AXES)
    members = sizes[0] * sizes[1]
    block, tile, full = (4, T, 2 * T), (1, T, 2 * T), (2 * T, 2 * T)
    ext = pltpu.VMEM((6, T, 2 * T), BF)
    spin, col, m = table(neighbour_index, block_count)

    other = swap_col(sizes, lax.dynamic_index_in_dim(start_block, 1 - spin, 0, keepdims=False)[0])
    v, p, q = call(
        join_kernel, m, [start_block, other],
        [shaped(block, BF), shaped(tile, BF), shaped(tile, BF)], name="join",
    )

    def apply_ham(x, p, q, before):
        p, q = swap(sizes, p, 0, 1), swap(sizes, q, 0, 2)
        a, b = swap(sizes, x, 1, 0), swap(sizes, x, 2, 0)
        ends = jnp.concatenate([p, q], axis=0)
        ca, cb = swap(sizes, ends, 1, 0), swap(sizes, ends, 2, 0)
        (acc,) = call(
            own_kernel, m, [x, p, q], [shaped(block, F32)], [ext], hamiltonian,
            2 * 12 * T * T * 2 * T, "own",
        )
        last = before is not None
        arrays = [a, b, ca, cb, acc] + ([before] if last else [])
        return call(
            functools.partial(side_kernel, last=last), m, arrays,
            [shaped(block, BF), shaped(tile, BF), shaped(tile, BF)], [ext, ext], hamiltonian,
            2 * 24 * T * T * 2 * T, "sides",
        )

    first, p, q = apply_ham(v, p, q, None)
    second, low, high = apply_ham(first, p, q, v)

    above = shift(sizes, low, 0, -1)
    right_high = shift(sizes, low, -1, -1)
    right_low = shift(sizes, high, -1, 1)
    right = shift(sizes, second, -1, 0)
    corr, acc = call(
        inner_kernel, m, [second], [shaped(full, F32), shaped(block, F32)], (), hamiltonian,
        2 * 15 * T * T * 2 * T, "inner",
    )
    (packed,) = call(
        gram_kernel, m, [second, above, right, right_low, right_high, acc, corr],
        [shaped((members, 1, 5 * T), F32)], [ext], hamiltonian, 2 * 21 * T * T * 2 * T, "gram",
    )

    rows = members * second.shape[0] * second.shape[1]
    mine = exchange(sizes, packed).sum(axis=0, keepdims=True) / rows
    spread = jnp.broadcast_to(mine, packed.shape)
    gathered = exchange(sizes, spread)

    half = (4, T, T)
    keep, send, p_keep, p_send = call(
        final_kernel, m, [gathered, second],
        [shaped(half, BF), shaped(half, BF), shaped((2 * T, T), F32), shaped((2 * T, T), F32)],
        [pltpu.VMEM(full, F32), pltpu.VMEM(full, F32)], None, 0, "final",
    )
    got, p_got = swap_col(sizes, send), swap_col(sizes, p_send)
    ritz = jnp.where(spin == 0, jnp.stack([keep, got]), jnp.stack([got, keep]))
    projected = jnp.where(spin == 0, jnp.stack([p_keep, p_got]), jnp.stack([p_got, p_keep]))
    return ritz[:, None], projected


def solution(mesh):
    return jax.shard_map(
        per_device,
        mesh=mesh,
        in_specs=(
            P(None, "gx", "gy", None, "col"),
            P(None, "gx", "gy", None, None, None),
            P("gx", "gy", None),
            P("gx", "gy"),
        ),
        out_specs=(P(None, "gx", "gy", None, "col"), P(None, None, "col")),
        check_vma=False,
    )
```

time: 1250 us -> 163 us (0.13)
  waiting for transfers between devices: 1040 us -> 18.2 us
  other arithmetic: 113 us -> 3.59 us
  Pallas kernels: 0 us -> 46.7 us
  blocking collectives: 12.3 us -> 52.5 us
  matrix products: 23.7 us -> 0 us
  local copies, waits for them, and re-layouts: 22.8 us -> 4.02 us
  between operations: 14.6 us -> 0.79 us
    psum x1 -> x0, waiting for transfers between devices: 999 us -> none  [per_device(): summed = lax.psum(partial_gram, ('gx', 'gy')) / total_rows]
    another operation x13 -> x0, other arithmetic: 110 us -> none  [the longest x9 68.2 us: factor_parts(): lower = jnp.linalg.cholesky(correlation)]
    all_to_all x0 -> x2, blocking collectives: none -> 52.5 us  [exchange(): lax.all_to_all(pieces, AXES, 0, 0, axis_index_groups=groups, tiled=True)]
    pallas_call x0 -> x8, Pallas kernels: none -> 46.7 us  [call(): pl.pallas_call(kernel, out_shape=outs, grid_spec=pltpu.PrefetchScalarGrid...]
    all_gather x1 -> x0, waiting for transfers between devices: 21.9 us -> none  [per_device(): gathered = lax.all_gather(summed, 'col', axis=2, tiled=True)]
    dot_general x32 -> x0, matrix products: 19.1 us -> none  [the longest x27 11 us: apply_ham(): jnp.einsum('sxyij,sxyjk->sxyik', ordered[:, :, :, code], beside, preferre...]
    ppermute x12 -> x19, starting transfers between devices: 25.2 us -> 36.9 us  [the longest x12 20.9 us: swap(): return lax.ppermute(block, AXES, perm)]
  transfers between devices with their start and end apart: 14 -> 19, of which waited for: 10 -> 8; matrix products, arithmetic and copies ran while one was open for 2% -> 2% of each run, Pallas kernels for 0% -> 2%
where the time goes in v1:
time: 163 us
  blocking collectives  52.5 us (32%)
  Pallas kernels  46.7 us (29%)
  starting transfers between devices  36.9 us (23%)
  waiting for transfers between devices  18.2 us (11%)
  local copies, waits for them, and re-layouts  4.02 us (2%)
  other arithmetic  3.59 us (2%)
    all_to_all x2, blocking collectives, exchange(): lax.all_to_all(pieces, AXES, 0, 0, axis_index_groups=groups, tiled=True)  52.5 us
    pallas_call x8, Pallas kernels, call(): pl.pallas_call(kernel, out_shape=outs, grid_spec=pltpu.PrefetchScalarGrid...  46.7 us
    ppermute x12, starting transfers between devices, swap(): return lax.ppermute(block, AXES, perm)  20.9 us
    ppermute x12, waiting for transfers between devices, swap(): return lax.ppermute(block, AXES, perm)  12.2 us
    ppermute x4, starting transfers between devices, shift(): lax.ppermute(block, AXES, pairs(sizes, lambda gx, gy: (gx + dx, gy + dy)))  9.28 us
    ppermute x3, starting transfers between devices, swap_col(): return lax.ppermute(block, AXES, perm)  6.71 us
    ppermute x3, waiting for transfers between devices, swap_col(): return lax.ppermute(block, AXES, perm)  5.57 us
  transfers between devices with their start and end apart: 19, of which 8 were waited for; matrix products, arithmetic and copies ran while one was open for 2% of the time, Pallas kernels for 2%

profile of v1, /device:TPU:1, one launch (start us, length us, event | category | flops | bytes accessed | tf_op | source)
XLA Modules:
  0.0 162.7 jit_solution(11002561457814928206)
XLA Ops:
  0.6 0.9 dynamic-slice_bitcast_fusion
  1.6 3.7 %collective-permute-start = (bf16[4,128,128]{2,1,0:T(8,128)(2,1)S(1)}, bf16[4,128,128]{2,1,0:T(8,128)(2,1)S(1)}, u32[]{:S(2)}, u32[]{:S(2)}) collective-permute-start(bf16[4,128,128]{2,1,0:T(8,128)(2,1)S(1)} %dynamic-slice_bitcast_fusion), channel_id=1, source_target_pairs={{0,1},{1,0},{2,3},{3,2},{4,5},{5,4},{6,7},{7,6},{8,9},{9,8},{10,11... | collective-permute-start | bytes 393224 | tf_op jit(solution)/shard_map/ppermute | solution.py:59
  6.1 1.0 select_reduce_fusion
  7.6 0.9 copy-done.2
  9.2 3.9 %collective-permute-start.3 = (bf16[1,128,256]{2,1,0:T(8,128)(2,1)S(1)}, bf16[1,128,256]{2,1,0:T(8,128)(2,1)S(1)}, u32[]{:S(2)}, u32[]{:S(2)}) collective-permute-start(bf16[1,128,256]{2,1,0:T(8,128)(2,1)S(1)} %get-tuple-element.18), channel_id=1, source_target_pairs={{0,2},{1,3},{2,0},{3,1},{4,6},{5,7},{6,4},{7,5},{8,10},{9,11},{10,... | collective-permute-start | bytes 196616 | tf_op jit(solution)/shard_map/ppermute | solution.py:50
  13.0 3.5 %collective-permute-start.2 = (bf16[4,128,256]{2,1,0:T(8,128)(2,1)S(1)}, bf16[4,128,256]{2,1,0:T(8,128)(2,1)S(1)}, u32[]{:S(2)}, u32[]{:S(2)}) collective-permute-start(bf16[4,128,256]{2,1,0:T(8,128)(2,1)S(1)} %get-tuple-element.17.v.rest_0_), channel_id=1, source_target_pairs={{0,225},{1,224},{2,227},{3,226},{4,229},{5,228},{6,231},{7,230},{8... | collective-permute-start | bytes 786440 | tf_op jit(solution)/shard_map/ppermute | solution.py:50
  16.5 1.9 %collective-permute-start.4 = (bf16[1,128,256]{2,1,0:T(8,128)(2,1)S(1)}, bf16[1,128,256]{2,1,0:T(8,128)(2,1)S(1)}, u32[]{:S(2)}, u32[]{:S(2)}) collective-permute-start(bf16[1,128,256]{2,1,0:T(8,128)(2,1)S(1)} %get-tuple-element.19), channel_id=1, source_target_pairs={{0,30},{1,31},{2,4},{3,5},{4,2},{5,3},{6,8},{7,9},{8,6},{9,7},{10,... | collective-permute-start | bytes 196616 | tf_op jit(solution)/shard_map/ppermute | solution.py:50
  18.4 2.2 %collective-permute-done.4.q = bf16[1,128,256]{2,1,0:T(8,128)(2,1)S(1)} collective-permute-done((bf16[1,128,256]{2,1,0:T(8,128)(2,1)S(1)}, bf16[1,128,256]{2,1,0:T(8,128)(2,1)S(1)}, u32[]{:S(2)}, u32[]{:S(2)}) %collective-permute-start.4) | collective-permute-done | bytes 65568 | tf_op jit(solution)/shard_map/ppermute | solution.py:50
  20.6 1.3 collective-permute-start.6
  22.5 1.7 %copy-done = bf16[2,1,4,9,128,128]{5,4,3,2,1,0:T(8,128)(2,1)S(1)} copy-done((bf16[2,1,4,9,128,128]{5,4,3,2,1,0:T(8,128)(2,1)S(1)}, bf16[2,1,4,9,128,128]{5,4,3,2,1,0:T(8,128)(2,1)}, u32[]{:S(2)}) %copy-start) | copy-done | bytes 2359320
  24.1 0.8 own.2.acc
  25.0 2.8 %collective-permute-done.6.cb = bf16[2,128,256]{2,1,0:T(8,128)(2,1)S(1)} collective-permute-done((bf16[2,128,256]{2,1,0:T(8,128)(2,1)S(1)}, bf16[2,128,256]{2,1,0:T(8,128)(2,1)S(1)}, u32[]{:S(2)}, u32[]{:S(2)}) %collective-permute-start.6) | collective-permute-done | bytes 131104 | tf_op jit(solution)/shard_map/ppermute | solution.py:50
  27.8 1.0 sides.2
  28.8 5.0 %collective-permute-start.9 = (bf16[1,128,256]{2,1,0:T(8,128)(2,1)S(1)}, bf16[1,128,256]{2,1,0:T(8,128)(2,1)S(1)}, u32[]{:S(2)}, u32[]{:S(2)}) collective-permute-start(bf16[1,128,256]{2,1,0:T(8,128)(2,1)S(1)} %get-tuple-element.21), channel_id=1, source_target_pairs={{0,2},{1,3},{2,0},{3,1},{4,6},{5,7},{6,4},{7,5},{8,10},{9,11},{10,... | collective-permute-start | bytes 196616 | tf_op jit(solution)/shard_map/ppermute | solution.py:50
  33.9 1.8 %collective-permute-start.8 = (bf16[4,128,256]{2,1,0:T(8,128)(2,1)S(1)}, bf16[4,128,256]{2,1,0:T(8,128)(2,1)S(1)}, u32[]{:S(2)}, u32[]{:S(2)}) collective-permute-start(bf16[4,128,256]{2,1,0:T(8,128)(2,1)S(1)} %get-tuple-element.20.v), channel_id=1, source_target_pairs={{0,225},{1,224},{2,227},{3,226},{4,229},{5,228},{6,231},{7,230},{8... | collective-permute-start | bytes 786440 | tf_op jit(solution)/shard_map/ppermute | solution.py:50
  35.6 4.0 %collective-permute-done.10.q = bf16[1,128,256]{2,1,0:T(8,128)(2,1)S(1)} collective-permute-done((bf16[1,128,256]{2,1,0:T(8,128)(2,1)S(1)}, bf16[1,128,256]{2,1,0:T(8,128)(2,1)S(1)}, u32[]{:S(2)}, u32[]{:S(2)}) %collective-permute-start.10) | collective-permute-done | bytes 65568 | tf_op jit(solution)/shard_map/ppermute | solution.py:50
  39.6 3.0 %collective-permute-start.12 = (bf16[2,128,256]{2,1,0:T(8,128)(2,1)S(1)}, bf16[2,128,256]{2,1,0:T(8,128)(2,1)S(1)}, u32[]{:S(2)}, u32[]{:S(2)}) collective-permute-start(bf16[2,128,256]{2,1,0:T(8,128)(2,1)S(1)} %constant_dynamic-update-slice_fusion.2), channel_id=1, source_target_pairs={{0,225},{1,224},{2,227},{3,226},{4,229},{5,228},{6,231},{7,230},{8... | collective-permute-start | bytes 393224 | tf_op jit(solution)/shard_map/ppermute | solution.py:50
  42.7 0.8 own.3.acc
  43.5 3.2 %collective-permute-done.12.cb = bf16[2,128,256]{2,1,0:T(8,128)(2,1)S(1)} collective-permute-done((bf16[2,128,256]{2,1,0:T(8,128)(2,1)S(1)}, bf16[2,128,256]{2,1,0:T(8,128)(2,1)S(1)}, u32[]{:S(2)}, u32[]{:S(2)}) %collective-permute-start.12) | collective-permute-done | bytes 131104 | tf_op jit(solution)/shard_map/ppermute | solution.py:50
  46.8 1.0 sides.3
  47.8 3.1 %collective-permute-start.14 = (bf16[4,128,256]{2,1,0:T(8,128)(2,1)S(1)}, bf16[4,128,256]{2,1,0:T(8,128)(2,1)S(1)}, u32[]{:S(2)}, u32[]{:S(2)}) collective-permute-start(bf16[4,128,256]{2,1,0:T(8,128)(2,1)S(1)} %get-tuple-element.23.s), channel_id=1, source_target_pairs={{0,225},{1,224},{2,227},{3,226},{4,229},{5,228},{6,231},{7,230},{8... | collective-permute-start | bytes 786440 | tf_op jit(solution)/shard_map/ppermute | solution.py:54
  51.6 2.0 %collective-permute-start.16 = (bf16[1,128,256]{2,1,0:T(8,128)(2,1)S(1)}, bf16[1,128,256]{2,1,0:T(8,128)(2,1)S(1)}, u32[]{:S(2)}, u32[]{:S(2)}) collective-permute-start(bf16[1,128,256]{2,1,0:T(8,128)(2,1)S(1)} %get-tuple-element.24), channel_id=1, source_target_pairs={{0,255},{1,254},{2,225},{3,224},{4,227},{5,226},{6,229},{7,228},{8... | collective-permute-start | bytes 196616 | tf_op jit(solution)/shard_map/ppermute | solution.py:54
  53.6 3.5 %collective-permute-start.13 = (bf16[1,128,256]{2,1,0:T(8,128)(2,1)S(1)}, bf16[1,128,256]{2,1,0:T(8,128)(2,1)S(1)}, u32[]{:S(2)}, u32[]{:S(2)}) collective-permute-start(bf16[1,128,256]{2,1,0:T(8,128)(2,1)S(1)} %get-tuple-element.24), channel_id=1, source_target_pairs={{0,30},{1,31},{2,0},{3,1},{4,2},{5,3},{6,4},{7,5},{8,6},{9,7},{10,... | collective-permute-start | bytes 196616 | tf_op jit(solution)/shard_map/ppermute | solution.py:54
  57.0 0.9 inner.1
  58.4 1.8 %gram.1 = f32[128,1,640]{2,1,0:T(1,128)S(1)} custom-call(s32[40]{0:T(128)S(1)} %concatenate.27.m, bf16[2,1,4,9,128,128]{5,4,3,2,1,0:T(8,128)(2,1)S(1)} %copy-done.1, bf16[4,128,256]{2,1,0:T(8,128)(2,1)S(1)} %get-tuple-element.23.s, bf16[1,128,256]{2,1,0:T(8,128)(2,1)S(1)} %collective-permute-done.13.above, ...), custom_call_target="tpu_custom_call" | custom-call | flops 176160768 | bytes 4194304 | tf_op jit(solution)/shard_map/gram/pallas_call | solution.py:261
  60.2 30.0 %all_to_all.10 = f32[128,1,640]{2,1,0:T(1,128)S(1)} all-to-all(f32[128,1,640]{2,1,0:T(1,128)S(1)} %gram.1), channel_id=1, replica_groups={{0,2,4,6,8,10,12,14,16,18,20,22,24,26,28,30,32,34,36,38,40,42,44,46,48,..., dimensions={0} | all-to-all | bytes 655360 | tf_op jit(solution)/shard_map/all_to_all | solution.py:67
  90.6 22.6 %all_to_all.11.packed = f32[128,1,640]{2,1,0:T(1,128)S(1)} all-to-all(f32[128,1,640]{2,1,0:T(1,128)S(1)} %broadcast_in_dim.12), channel_id=1, replica_groups={{0,2,4,6,8,10,12,14,16,18,20,22,24,26,28,30,32,34,36,38,40,42,44,46,48,..., dimensions={0} | all-to-all | bytes 655360 | tf_op jit(solution)/shard_map/all_to_all | solution.py:67
  113.1 39.7 %final.1 = (bf16[4,128,128]{2,1,0:T(8,128)(2,1)S(1)}, bf16[4,128,128]{2,1,0:T(8,128)(2,1)S(1)}, f32[256,128]{1,0:T(8,128)S(1)}, f32[256,128]{1,0:T(8,128)S(1)}) custom-call(s32[40]{0:T(128)S(1)} %concatenate.27.m, f32[128,1,640]{2,1,0:T(1,128)S(1)} %all_to_all.11.packed, bf16[4,128,256]{2,1,0:T(8,128)(2,1)S(1)} %get-tuple-element.23.s), custom_call_target="tpu_custom_call" | custom-call | bytes 1114112 | tf_op jit(solution)/shard_map/final/pallas_call | solution.py:261
  152.9 3.0 %collective-permute-start.18 = (f32[256,128]{1,0:T(8,128)S(1)}, f32[256,128]{1,0:T(8,128)S(1)}, u32[]{:S(2)}, u32[]{:S(2)}) collective-permute-start(f32[256,128]{1,0:T(8,128)S(1)} %get-tuple-element.31), channel_id=1, source_target_pairs={{0,1},{1,0},{2,3},{3,2},{4,5},{5,4},{6,7},{7,6},{8,9},{9,8},{10,11... | collective-permute-start | bytes 393224 | tf_op jit(solution)/shard_map/ppermute | solution.py:59
  155.9 3.3 %collective-permute-done.17 = bf16[4,128,128]{2,1,0:T(8,128)(2,1)S(1)} collective-permute-done((bf16[4,128,128]{2,1,0:T(8,128)(2,1)S(1)}, bf16[4,128,128]{2,1,0:T(8,128)(2,1)S(1)}, u32[]{:S(2)}, u32[]{:S(2)}) %collective-permute-start.17) | collective-permute-done | bytes 131104 | tf_op jit(solution)/shard_map/ppermute | solution.py:59
  159.2 0.7 maximum_select_fusion
  159.9 2.1 %collective-permute-done.18 = f32[256,128]{1,0:T(8,128)S(1)} collective-permute-done((f32[256,128]{1,0:T(8,128)S(1)}, f32[256,128]{1,0:T(8,128)S(1)}, u32[]{:S(2)}, u32[]{:S(2)}) %collective-permute-start.18) | collective-permute-done | bytes 131104 | tf_op jit(solution)/shard_map/ppermute | solution.py:59
  (41 shorter events, 5.0 us)
Async XLA Ops:
  1.6 6.0 %collective-permute-start = (bf16[4,128,128]{2,1,0:T(8,128)(2,1)S(1)}, bf16[4,128,128]{2,1,0:T(8,128)(2,1)S(1)}, u32[]{:S(2)}, u32[]{:S(2)}) collective-permute-start(bf16[4,128,128]{2,1,0:T(8,128)(2,1)S(1)} %dynamic-slice_bitcast_fusion), channel_id=1, source_target_pairs={{0,1},{1,0},{2,3},{3,2},{4,5},{5,4},{6,7},{7,6},{8,9},{9,8},{10,11... | collective-permute-start | bytes 393224 | tf_op jit(solution)/shard_map/ppermute | solution.py:59
  7.6 1.0 copy-start.2
  9.2 9.2 %collective-permute-start.3 = (bf16[1,128,256]{2,1,0:T(8,128)(2,1)S(1)}, bf16[1,128,256]{2,1,0:T(8,128)(2,1)S(1)}, u32[]{:S(2)}, u32[]{:S(2)}) collective-permute-start(bf16[1,128,256]{2,1,0:T(8,128)(2,1)S(1)} %get-tuple-element.18), channel_id=1, source_target_pairs={{0,2},{1,3},{2,0},{3,1},{4,6},{5,7},{6,4},{7,5},{8,10},{9,11},{10,... | collective-permute-start | bytes 196616 | tf_op jit(solution)/shard_map/ppermute | solution.py:50
  13.0 14.8 %collective-permute-start.2 = (bf16[4,128,256]{2,1,0:T(8,128)(2,1)S(1)}, bf16[4,128,256]{2,1,0:T(8,128)(2,1)S(1)}, u32[]{:S(2)}, u32[]{:S(2)}) collective-permute-start(bf16[4,128,256]{2,1,0:T(8,128)(2,1)S(1)} %get-tuple-element.17.v.rest_0_), channel_id=1, source_target_pairs={{0,225},{1,224},{2,227},{3,226},{4,229},{5,228},{6,231},{7,230},{8... | collective-permute-start | bytes 786440 | tf_op jit(solution)/shard_map/ppermute | solution.py:50
  16.5 11.3 %collective-permute-start.1 = (bf16[4,128,256]{2,1,0:T(8,128)(2,1)S(1)}, bf16[4,128,256]{2,1,0:T(8,128)(2,1)S(1)}, u32[]{:S(2)}, u32[]{:S(2)}) collective-permute-start(bf16[4,128,256]{2,1,0:T(8,128)(2,1)S(1)} %get-tuple-element.17.v.rest_0_), channel_id=1, source_target_pairs={{0,32},{1,33},{2,34},{3,35},{4,36},{5,37},{6,38},{7,39},{8,40},{9,... | collective-permute-start | bytes 786440 | tf_op jit(solution)/shard_map/ppermute | solution.py:50
  16.5 4.1 %collective-permute-start.4 = (bf16[1,128,256]{2,1,0:T(8,128)(2,1)S(1)}, bf16[1,128,256]{2,1,0:T(8,128)(2,1)S(1)}, u32[]{:S(2)}, u32[]{:S(2)}) collective-permute-start(bf16[1,128,256]{2,1,0:T(8,128)(2,1)S(1)} %get-tuple-element.19), channel_id=1, source_target_pairs={{0,30},{1,31},{2,4},{3,5},{4,2},{5,3},{6,8},{7,9},{8,6},{9,7},{10,... | collective-permute-start | bytes 196616 | tf_op jit(solution)/shard_map/ppermute | solution.py:50
  20.6 7.1 %collective-permute-start.6 = (bf16[2,128,256]{2,1,0:T(8,128)(2,1)S(1)}, bf16[2,128,256]{2,1,0:T(8,128)(2,1)S(1)}, u32[]{:S(2)}, u32[]{:S(2)}) collective-permute-start(bf16[2,128,256]{2,1,0:T(8,128)(2,1)S(1)} %constant_dynamic-update-slice_fusion), channel_id=1, source_target_pairs={{0,225},{1,224},{2,227},{3,226},{4,229},{5,228},{6,231},{7,230},{8... | collective-permute-start | bytes 393224 | tf_op jit(solution)/shard_map/ppermute | solution.py:50
  21.9 5.9 %collective-permute-start.5 = (bf16[2,128,256]{2,1,0:T(8,128)(2,1)S(1)}, bf16[2,128,256]{2,1,0:T(8,128)(2,1)S(1)}, u32[]{:S(2)}, u32[]{:S(2)}) collective-permute-start(bf16[2,128,256]{2,1,0:T(8,128)(2,1)S(1)} %constant_dynamic-update-slice_fusion), channel_id=1, source_target_pairs={{0,32},{1,33},{2,34},{3,35},{4,36},{5,37},{6,38},{7,39},{8,40},{9,... | collective-permute-start | bytes 393224 | tf_op jit(solution)/shard_map/ppermute | solution.py:50
  22.5 1.7 %copy-start = (bf16[2,1,4,9,128,128]{5,4,3,2,1,0:T(8,128)(2,1)S(1)}, bf16[2,1,4,9,128,128]{5,4,3,2,1,0:T(8,128)(2,1)}, u32[]{:S(2)}) copy-start(bf16[2,1,4,9,128,128]{5,4,3,2,1,0:T(8,128)(2,1)} %h.11) | copy-start | bytes 7077892
  24.1 3.6 %copy-start.1 = (bf16[2,1,4,9,128,128]{5,4,3,2,1,0:T(8,128)(2,1)S(1)}, bf16[2,1,4,9,128,128]{5,4,3,2,1,0:T(8,128)(2,1)}, u32[]{:S(2)}) copy-start(bf16[2,1,4,9,128,128]{5,4,3,2,1,0:T(8,128)(2,1)} %h.11) | copy-start | bytes 7077892
  28.8 6.8 %collective-permute-start.9 = (bf16[1,128,256]{2,1,0:T(8,128)(2,1)S(1)}, bf16[1,128,256]{2,1,0:T(8,128)(2,1)S(1)}, u32[]{:S(2)}, u32[]{:S(2)}) collective-permute-start(bf16[1,128,256]{2,1,0:T(8,128)(2,1)S(1)} %get-tuple-element.21), channel_id=1, source_target_pairs={{0,2},{1,3},{2,0},{3,1},{4,6},{5,7},{6,4},{7,5},{8,10},{9,11},{10,... | collective-permute-start | bytes 196616 | tf_op jit(solution)/shard_map/ppermute | solution.py:50
  33.9 12.9 %collective-permute-start.8 = (bf16[4,128,256]{2,1,0:T(8,128)(2,1)S(1)}, bf16[4,128,256]{2,1,0:T(8,128)(2,1)S(1)}, u32[]{:S(2)}, u32[]{:S(2)}) collective-permute-start(bf16[4,128,256]{2,1,0:T(8,128)(2,1)S(1)} %get-tuple-element.20.v), channel_id=1, source_target_pairs={{0,225},{1,224},{2,227},{3,226},{4,229},{5,228},{6,231},{7,230},{8... | collective-permute-start | bytes 786440 | tf_op jit(solution)/shard_map/ppermute | solution.py:50
  35.6 11.1 %collective-permute-start.7 = (bf16[4,128,256]{2,1,0:T(8,128)(2,1)S(1)}, bf16[4,128,256]{2,1,0:T(8,128)(2,1)S(1)}, u32[]{:S(2)}, u32[]{:S(2)}) collective-permute-start(bf16[4,128,256]{2,1,0:T(8,128)(2,1)S(1)} %get-tuple-element.20.v), channel_id=1, source_target_pairs={{0,32},{1,33},{2,34},{3,35},{4,36},{5,37},{6,38},{7,39},{8,40},{9,... | collective-permute-start | bytes 786440 | tf_op jit(solution)/shard_map/ppermute | solution.py:50
  35.6 4.0 %collective-permute-start.10 = (bf16[1,128,256]{2,1,0:T(8,128)(2,1)S(1)}, bf16[1,128,256]{2,1,0:T(8,128)(2,1)S(1)}, u32[]{:S(2)}, u32[]{:S(2)}) collective-permute-start(bf16[1,128,256]{2,1,0:T(8,128)(2,1)S(1)} %get-tuple-element.22), channel_id=1, source_target_pairs={{0,30},{1,31},{2,4},{3,5},{4,2},{5,3},{6,8},{7,9},{8,6},{9,7},{10,... | collective-permute-start | bytes 196616 | tf_op jit(solution)/shard_map/ppermute | solution.py:50
  39.6 7.1 %collective-permute-start.12 = (bf16[2,128,256]{2,1,0:T(8,128)(2,1)S(1)}, bf16[2,128,256]{2,1,0:T(8,128)(2,1)S(1)}, u32[]{:S(2)}, u32[]{:S(2)}) collective-permute-start(bf16[2,128,256]{2,1,0:T(8,128)(2,1)S(1)} %constant_dynamic-update-slice_fusion.2), channel_id=1, source_target_pairs={{0,225},{1,224},{2,227},{3,226},{4,229},{5,228},{6,231},{7,230},{8... | collective-permute-start | bytes 393224 | tf_op jit(solution)/shard_map/ppermute | solution.py:50
  42.7 4.1 %collective-permute-start.11 = (bf16[2,128,256]{2,1,0:T(8,128)(2,1)S(1)}, bf16[2,128,256]{2,1,0:T(8,128)(2,1)S(1)}, u32[]{:S(2)}, u32[]{:S(2)}) collective-permute-start(bf16[2,128,256]{2,1,0:T(8,128)(2,1)S(1)} %constant_dynamic-update-slice_fusion.2), channel_id=1, source_target_pairs={{0,32},{1,33},{2,34},{3,35},{4,36},{5,37},{6,38},{7,39},{8,40},{9,... | collective-permute-start | bytes 393224 | tf_op jit(solution)/shard_map/ppermute | solution.py:50
  47.8 10.6 %collective-permute-start.14 = (bf16[4,128,256]{2,1,0:T(8,128)(2,1)S(1)}, bf16[4,128,256]{2,1,0:T(8,128)(2,1)S(1)}, u32[]{:S(2)}, u32[]{:S(2)}) collective-permute-start(bf16[4,128,256]{2,1,0:T(8,128)(2,1)S(1)} %get-tuple-element.23.s), channel_id=1, source_target_pairs={{0,225},{1,224},{2,227},{3,226},{4,229},{5,228},{6,231},{7,230},{8... | collective-permute-start | bytes 786440 | tf_op jit(solution)/shard_map/ppermute | solution.py:54
  50.9 7.5 %collective-permute-start.15 = (bf16[1,128,256]{2,1,0:T(8,128)(2,1)S(1)}, bf16[1,128,256]{2,1,0:T(8,128)(2,1)S(1)}, u32[]{:S(2)}, u32[]{:S(2)}) collective-permute-start(bf16[1,128,256]{2,1,0:T(8,128)(2,1)S(1)} %get-tuple-element.25), channel_id=1, source_target_pairs={{0,227},{1,226},{2,229},{3,228},{4,231},{5,230},{6,233},{7,232},{8... | collective-permute-start | bytes 196616 | tf_op jit(solution)/shard_map/ppermute | solution.py:54
  51.6 6.8 %collective-permute-start.16 = (bf16[1,128,256]{2,1,0:T(8,128)(2,1)S(1)}, bf16[1,128,256]{2,1,0:T(8,128)(2,1)S(1)}, u32[]{:S(2)}, u32[]{:S(2)}) collective-permute-start(bf16[1,128,256]{2,1,0:T(8,128)(2,1)S(1)} %get-tuple-element.24), channel_id=1, source_target_pairs={{0,255},{1,254},{2,225},{3,224},{4,227},{5,226},{6,229},{7,228},{8... | collective-permute-start | bytes 196616 | tf_op jit(solution)/shard_map/ppermute | solution.py:54
  53.6 4.8 %collective-permute-start.13 = (bf16[1,128,256]{2,1,0:T(8,128)(2,1)S(1)}, bf16[1,128,256]{2,1,0:T(8,128)(2,1)S(1)}, u32[]{:S(2)}, u32[]{:S(2)}) collective-permute-start(bf16[1,128,256]{2,1,0:T(8,128)(2,1)S(1)} %get-tuple-element.24), channel_id=1, source_target_pairs={{0,30},{1,31},{2,0},{3,1},{4,2},{5,3},{6,4},{7,5},{8,6},{9,7},{10,... | collective-permute-start | bytes 196616 | tf_op jit(solution)/shard_map/ppermute | solution.py:54
  152.8 6.4 %collective-permute-start.17 = (bf16[4,128,128]{2,1,0:T(8,128)(2,1)S(1)}, bf16[4,128,128]{2,1,0:T(8,128)(2,1)S(1)}, u32[]{:S(2)}, u32[]{:S(2)}) collective-permute-start(bf16[4,128,128]{2,1,0:T(8,128)(2,1)S(1)} %get-tuple-element.29), channel_id=1, source_target_pairs={{0,1},{1,0},{2,3},{3,2},{4,5},{5,4},{6,7},{7,6},{8,9},{9,8},{10,11... | collective-permute-start | bytes 393224 | tf_op jit(solution)/shard_map/ppermute | solution.py:59
  152.9 9.1 %collective-permute-start.18 = (f32[256,128]{1,0:T(8,128)S(1)}, f32[256,128]{1,0:T(8,128)S(1)}, u32[]{:S(2)}, u32[]{:S(2)}) collective-permute-start(f32[256,128]{1,0:T(8,128)S(1)} %get-tuple-element.31), channel_id=1, source_target_pairs={{0,1},{1,0},{2,3},{3,2},{4,5},{5,4},{6,7},{7,6},{8,9},{9,8},{10,11... | collective-permute-start | bytes 393224 | tf_op jit(solution)/shard_map/ppermute | solution.py:59

commit v2 on v1

--- a/solution.py
+++ b/solution.py
@@ -61,8 +61,13 @@
 
 def exchange(sizes, pieces):
     groups = [
-        [device(sizes, gx, gy, col_of(gx, spin)) for gx in range(sizes[0]) for gy in range(sizes[1])]
+        [
+            device(sizes, gx, gy, col_of(gx, spin))
+            for gx in range(sizes[0])
+            for gy in range(core, sizes[1], 2)
+        ]
         for spin in range(2)
+        for core in range(2)
     ]
     return lax.all_to_all(pieces, AXES, 0, 0, axis_index_groups=groups, tiled=True)
 
@@ -104,11 +109,10 @@
     q_ref[...] = ref[pl.ds(jnp.where(par == 0, 0, 3), 1)]
 
 
-def join_kernel(m, start, other, v, p, q):
-    own = start[pl.ds(m[SPIN], 1)][0, 0]
+def join_kernel(m, own, other, v, p, q):
     first_col = m[COL] == 0
-    v[:, :, :T] = jnp.where(first_col, own, other[...])
-    v[:, :, T:] = jnp.where(first_col, other[...], own)
+    v[:, :, :T] = jnp.where(first_col, own[...], other[...])
+    v[:, :, T:] = jnp.where(first_col, other[...], own[...])
     store_sides(m, v, p, q)
 
 
@@ -157,7 +161,7 @@
     return lax.broadcasted_iota(jnp.int32, shape, 0), lax.broadcasted_iota(jnp.int32, shape, 1)
 
 
-def gram_kernel(m, h, s, above, right, right_low, right_high, acc, corr, out, ext):
+def gram_kernel(m, h, s, above, right, right_low, right_high, acc, corr, mine, theirs, ext):
     ext[0:1] = right_low[...]
     ext[1:5] = right[...]
     ext[5:6] = right_high[...]
@@ -175,20 +179,35 @@
     rows, cols = places()
     both = jnp.where(rows >= cols, corr[...], coupling)
     diagonal = jnp.sum(jnp.where(rows == cols, coupling, 0.0), axis=1, keepdims=True)
-    lane = lax.broadcasted_iota(jnp.int32, (T, T), 1)
-    extra = jnp.where(lane == 0, diagonal[:T], jnp.where(lane == 1, diagonal[T:], 0.0))
-    out[:, 0, :] = jnp.concatenate([both[:T], both[T:], extra], axis=1)
+    first, second = pack(both[:T], diagonal[:T]), pack(both[T:], diagonal[T:])
+    even = m[PAR_Y] == 0
+    mine[:, 0, :] = jnp.where(even, first, second)
+    theirs[:, 0, :] = jnp.where(even, second, first)
+
+
+def pack(square, diagonal):
+    lane = lax.broadcasted_iota(jnp.int32, (T // 2, T), 1)
+    extra = jnp.where(lane == 0, diagonal[: T // 2], jnp.where(lane == 1, diagonal[T // 2 :], 0.0))
+    return jnp.concatenate([square[: T // 2], square[T // 2 :], extra], axis=1)
+
+
+def unpack(table):
+    square = jnp.concatenate([table[:, : 2 * T], table[:, 2 * T : 4 * T]], axis=0)
+    return square, jnp.concatenate([table[:, 4 * T : 4 * T + 1], table[:, 4 * T + 1 : 4 * T + 2]], axis=0)
 
 
 def lower_part(e, rows, cols):
     return jnp.where(rows > cols, e, jnp.where(rows == cols, 0.5 * e, 0.0))
 
 
-def final_kernel(m, packed, s, keep, send, p_keep, p_send, x_ref, a_ref):
+def final_kernel(m, mine, theirs, s, keep, send, p_keep, p_send, x_ref, a_ref):
     rows, cols = places()
-    table = packed[:, 0, :]
-    both = jnp.concatenate([table[:, : 2 * T], table[:, 2 * T : 4 * T]], axis=0)
-    diagonal = jnp.concatenate([table[:, 4 * T : 4 * T + 1], table[:, 4 * T + 1 : 4 * T + 2]], axis=0)
+    even = m[PAR_Y] == 0
+    first, second = mine[:, 0, :], theirs[:, 0, :]
+    top = unpack(jnp.where(even, first, second))
+    bottom = unpack(jnp.where(even, second, first))
+    both = jnp.concatenate([top[0], bottom[0]], axis=0)
+    diagonal = jnp.concatenate([top[1], bottom[1]], axis=0)
     turned = both.T
     corr = jnp.where(rows >= cols, both, turned)
     coupling = jnp.where(rows < cols, both, jnp.where(rows == cols, diagonal, turned))
@@ -302,8 +321,9 @@
     spin, col, m = table(neighbour_index, block_count)
 
     other = swap_col(sizes, lax.dynamic_index_in_dim(start_block, 1 - spin, 0, keepdims=False)[0])
+    own = lax.dynamic_index_in_dim(start_block, spin, 0, keepdims=False)[0]
     v, p, q = call(
-        join_kernel, m, [start_block, other],
+        join_kernel, m, [own, other],
         [shaped(block, BF), shaped(tile, BF), shaped(tile, BF)], name="join",
     )
 
@@ -335,19 +355,21 @@
         inner_kernel, m, [second], [shaped(full, F32), shaped(block, F32)], (), hamiltonian,
         2 * 15 * T * T * 2 * T, "inner",
     )
-    (packed,) = call(
+    piece = shaped((members // 2, 1, 5 * T), F32)
+    mine, theirs = call(
         gram_kernel, m, [second, above, right, right_low, right_high, acc, corr],
-        [shaped((members, 1, 5 * T), F32)], [ext], hamiltonian, 2 * 21 * T * T * 2 * T, "gram",
+        [piece, piece], [ext], hamiltonian, 2 * 21 * T * T * 2 * T, "gram",
     )
 
     rows = members * second.shape[0] * second.shape[1]
-    mine = exchange(sizes, packed).sum(axis=0, keepdims=True) / rows
-    spread = jnp.broadcast_to(mine, packed.shape)
-    gathered = exchange(sizes, spread)
+    partial = mine + swap(sizes, theirs, 0, 1)
+    total = exchange(sizes, partial).sum(axis=0, keepdims=True) / rows
+    mine = exchange(sizes, jnp.broadcast_to(total, partial.shape))
+    theirs = swap(sizes, mine, 0, 1)
 
     half = (4, T, T)
     keep, send, p_keep, p_send = call(
-        final_kernel, m, [gathered, second],
+        final_kernel, m, [mine, theirs, second],
         [shaped(half, BF), shaped(half, BF), shaped((2 * T, T), F32), shaped((2 * T, T), F32)],
         [pltpu.VMEM(full, F32), pltpu.VMEM(full, F32)], None, 0, "final",
     )

time: 163 us -> 156 us (0.957)
  blocking collectives: 52.5 us -> 40.2 us
  starting transfers between devices: 36.9 us -> 41.5 us
  waiting for transfers between devices: 18.2 us -> 20.2 us
    all_to_all x2, blocking collectives: 52.5 us -> 40.2 us  [exchange(): lax.all_to_all(pieces, AXES, 0, 0, axis_index_groups=groups, tiled=True)]
    ppermute x12 -> x14, starting transfers between devices: 20.9 us -> 25.5 us  [swap(): return lax.ppermute(block, AXES, perm)]
    ppermute x12 -> x14, waiting for transfers between devices: 12.2 us -> 14.3 us  [swap(): return lax.ppermute(block, AXES, perm)]
  transfers between devices with their start and end apart: 19 -> 21, of which waited for: 8 -> 10; matrix products, arithmetic and copies ran while one was open for 2% -> 2% of each run, Pallas kernels for 2% -> 2%
where the time goes in v2:
time: 156 us
  Pallas kernels  46.7 us (30%)
  starting transfers between devices  41.5 us (27%)
  blocking collectives  40.2 us (26%)
  waiting for transfers between devices  20.2 us (13%)
  other arithmetic  3.64 us (2%)
  local copies, waits for them, and re-layouts  3.06 us (2%)
    pallas_call x8, Pallas kernels, call(): pl.pallas_call(kernel, out_shape=outs, grid_spec=pltpu.PrefetchScalarGrid...  46.7 us
    all_to_all x2, blocking collectives, exchange(): lax.all_to_all(pieces, AXES, 0, 0, axis_index_groups=groups, tiled=True)  40.2 us
    ppermute x14, starting transfers between devices, swap(): return lax.ppermute(block, AXES, perm)  25.5 us
    ppermute x14, waiting for transfers between devices, swap(): return lax.ppermute(block, AXES, perm)  14.3 us
    ppermute x4, starting transfers between devices, shift(): lax.ppermute(block, AXES, pairs(sizes, lambda gx, gy: (gx + dx, gy + dy)))  9.28 us
    ppermute x3, starting transfers between devices, swap_col(): return lax.ppermute(block, AXES, perm)  6.71 us
    ppermute x3, waiting for transfers between devices, swap_col(): return lax.ppermute(block, AXES, perm)  5.48 us
  transfers between devices with their start and end apart: 21, of which 10 were waited for; matrix products, arithmetic and copies ran while one was open for 2% of the time, Pallas kernels for 2%

profile of v2, /device:TPU:1, one launch (start us, length us, event | category | flops | bytes accessed | tf_op | source)
XLA Modules:
  0.0 156.1 jit_solution(9931247779462919723)
XLA Ops:
  0.6 1.0 dynamic-slice_bitcast_fusion
  1.6 3.7 %collective-permute-start = (bf16[4,128,128]{2,1,0:T(8,128)(2,1)S(1)}, bf16[4,128,128]{2,1,0:T(8,128)(2,1)S(1)}, u32[]{:S(2)}, u32[]{:S(2)}) collective-permute-start(bf16[4,128,128]{2,1,0:T(8,128)(2,1)S(1)} %get-tuple-element.36), channel_id=1, source_target_pairs={{0,1},{1,0},{2,3},{3,2},{4,5},{5,4},{6,7},{7,6},{8,9},{9,8},{10,11... | collective-permute-start | bytes 393224 | tf_op jit(solution)/shard_map/ppermute | solution.py:59
  6.2 1.0 select_reduce_fusion
  8.3 3.9 %collective-permute-start.3 = (bf16[1,128,256]{2,1,0:T(8,128)(2,1)S(1)}, bf16[1,128,256]{2,1,0:T(8,128)(2,1)S(1)}, u32[]{:S(2)}, u32[]{:S(2)}) collective-permute-start(bf16[1,128,256]{2,1,0:T(8,128)(2,1)S(1)} %get-tuple-element.20), channel_id=1, source_target_pairs={{0,2},{1,3},{2,0},{3,1},{4,6},{5,7},{6,4},{7,5},{8,10},{9,11},{10,... | collective-permute-start | bytes 196616 | tf_op jit(solution)/shard_map/ppermute | solution.py:50
  12.1 3.5 %collective-permute-start.2 = (bf16[4,128,256]{2,1,0:T(8,128)(2,1)S(1)}, bf16[4,128,256]{2,1,0:T(8,128)(2,1)S(1)}, u32[]{:S(2)}, u32[]{:S(2)}) collective-permute-start(bf16[4,128,256]{2,1,0:T(8,128)(2,1)S(1)} %get-tuple-element.19.v.rest_0_), channel_id=1, source_target_pairs={{0,225},{1,224},{2,227},{3,226},{4,229},{5,228},{6,231},{7,230},{8... | collective-permute-start | bytes 786440 | tf_op jit(solution)/shard_map/ppermute | solution.py:50
  15.6 1.9 %collective-permute-start.4 = (bf16[1,128,256]{2,1,0:T(8,128)(2,1)S(1)}, bf16[1,128,256]{2,1,0:T(8,128)(2,1)S(1)}, u32[]{:S(2)}, u32[]{:S(2)}) collective-permute-start(bf16[1,128,256]{2,1,0:T(8,128)(2,1)S(1)} %get-tuple-element.21), channel_id=1, source_target_pairs={{0,30},{1,31},{2,4},{3,5},{4,2},{5,3},{6,8},{7,9},{8,6},{9,7},{10,... | collective-permute-start | bytes 196616 | tf_op jit(solution)/shard_map/ppermute | solution.py:50
  17.5 2.2 %collective-permute-done.4.q = bf16[1,128,256]{2,1,0:T(8,128)(2,1)S(1)} collective-permute-done((bf16[1,128,256]{2,1,0:T(8,128)(2,1)S(1)}, bf16[1,128,256]{2,1,0:T(8,128)(2,1)S(1)}, u32[]{:S(2)}, u32[]{:S(2)}) %collective-permute-start.4) | collective-permute-done | bytes 65568 | tf_op jit(solution)/shard_map/ppermute | solution.py:50
  19.8 1.3 collective-permute-start.6
  21.6 1.7 %copy-done = bf16[2,1,4,9,128,128]{5,4,3,2,1,0:T(8,128)(2,1)S(1)} copy-done((bf16[2,1,4,9,128,128]{5,4,3,2,1,0:T(8,128)(2,1)S(1)}, bf16[2,1,4,9,128,128]{5,4,3,2,1,0:T(8,128)(2,1)}, u32[]{:S(2)}) %copy-start) | copy-done | bytes 2359320
  24.1 2.8 %collective-permute-done.6.cb = bf16[2,128,256]{2,1,0:T(8,128)(2,1)S(1)} collective-permute-done((bf16[2,128,256]{2,1,0:T(8,128)(2,1)S(1)}, bf16[2,128,256]{2,1,0:T(8,128)(2,1)S(1)}, u32[]{:S(2)}, u32[]{:S(2)}) %collective-permute-start.6) | collective-permute-done | bytes 131104 | tf_op jit(solution)/shard_map/ppermute | solution.py:50
  26.9 1.0 sides.2
  28.0 5.0 %collective-permute-start.9 = (bf16[1,128,256]{2,1,0:T(8,128)(2,1)S(1)}, bf16[1,128,256]{2,1,0:T(8,128)(2,1)S(1)}, u32[]{:S(2)}, u32[]{:S(2)}) collective-permute-start(bf16[1,128,256]{2,1,0:T(8,128)(2,1)S(1)} %get-tuple-element.23), channel_id=1, source_target_pairs={{0,2},{1,3},{2,0},{3,1},{4,6},{5,7},{6,4},{7,5},{8,10},{9,11},{10,... | collective-permute-start | bytes 196616 | tf_op jit(solution)/shard_map/ppermute | solution.py:50
  33.0 1.8 %collective-permute-start.8 = (bf16[4,128,256]{2,1,0:T(8,128)(2,1)S(1)}, bf16[4,128,256]{2,1,0:T(8,128)(2,1)S(1)}, u32[]{:S(2)}, u32[]{:S(2)}) collective-permute-start(bf16[4,128,256]{2,1,0:T(8,128)(2,1)S(1)} %get-tuple-element.22.v), channel_id=1, source_target_pairs={{0,225},{1,224},{2,227},{3,226},{4,229},{5,228},{6,231},{7,230},{8... | collective-permute-start | bytes 786440 | tf_op jit(solution)/shard_map/ppermute | solution.py:50
  34.8 4.0 %collective-permute-done.10.q = bf16[1,128,256]{2,1,0:T(8,128)(2,1)S(1)} collective-permute-done((bf16[1,128,256]{2,1,0:T(8,128)(2,1)S(1)}, bf16[1,128,256]{2,1,0:T(8,128)(2,1)S(1)}, u32[]{:S(2)}, u32[]{:S(2)}) %collective-permute-start.10) | collective-permute-done | bytes 65568 | tf_op jit(solution)/shard_map/ppermute | solution.py:50
  38.7 3.0 %collective-permute-start.12 = (bf16[2,128,256]{2,1,0:T(8,128)(2,1)S(1)}, bf16[2,128,256]{2,1,0:T(8,128)(2,1)S(1)}, u32[]{:S(2)}, u32[]{:S(2)}) collective-permute-start(bf16[2,128,256]{2,1,0:T(8,128)(2,1)S(1)} %constant_dynamic-update-slice_fusion.2), channel_id=1, source_target_pairs={{0,225},{1,224},{2,227},{3,226},{4,229},{5,228},{6,231},{7,230},{8... | collective-permute-start | bytes 393224 | tf_op jit(solution)/shard_map/ppermute | solution.py:50
  42.6 3.2 %collective-permute-done.12.cb = bf16[2,128,256]{2,1,0:T(8,128)(2,1)S(1)} collective-permute-done((bf16[2,128,256]{2,1,0:T(8,128)(2,1)S(1)}, bf16[2,128,256]{2,1,0:T(8,128)(2,1)S(1)}, u32[]{:S(2)}, u32[]{:S(2)}) %collective-permute-start.12) | collective-permute-done | bytes 131104 | tf_op jit(solution)/shard_map/ppermute | solution.py:50
  45.9 1.0 sides.3
  46.9 3.1 %collective-permute-start.14 = (bf16[4,128,256]{2,1,0:T(8,128)(2,1)S(1)}, bf16[4,128,256]{2,1,0:T(8,128)(2,1)S(1)}, u32[]{:S(2)}, u32[]{:S(2)}) collective-permute-start(bf16[4,128,256]{2,1,0:T(8,128)(2,1)S(1)} %get-tuple-element.25.s), channel_id=1, source_target_pairs={{0,225},{1,224},{2,227},{3,226},{4,229},{5,228},{6,231},{7,230},{8... | collective-permute-start | bytes 786440 | tf_op jit(solution)/shard_map/ppermute | solution.py:54
  50.7 2.0 %collective-permute-start.16 = (bf16[1,128,256]{2,1,0:T(8,128)(2,1)S(1)}, bf16[1,128,256]{2,1,0:T(8,128)(2,1)S(1)}, u32[]{:S(2)}, u32[]{:S(2)}) collective-permute-start(bf16[1,128,256]{2,1,0:T(8,128)(2,1)S(1)} %get-tuple-element.26), channel_id=1, source_target_pairs={{0,255},{1,254},{2,225},{3,224},{4,227},{5,226},{6,229},{7,228},{8... | collective-permute-start | bytes 196616 | tf_op jit(solution)/shard_map/ppermute | solution.py:54
  52.7 3.5 %collective-permute-start.13 = (bf16[1,128,256]{2,1,0:T(8,128)(2,1)S(1)}, bf16[1,128,256]{2,1,0:T(8,128)(2,1)S(1)}, u32[]{:S(2)}, u32[]{:S(2)}) collective-permute-start(bf16[1,128,256]{2,1,0:T(8,128)(2,1)S(1)} %get-tuple-element.26), channel_id=1, source_target_pairs={{0,30},{1,31},{2,0},{3,1},{4,2},{5,3},{6,4},{7,5},{8,6},{9,7},{10,... | collective-permute-start | bytes 196616 | tf_op jit(solution)/shard_map/ppermute | solution.py:54
  56.2 0.9 inner.1
  57.5 1.8 %gram.1 = (f32[64,1,640]{2,1,0:T(1,128)S(1)}, f32[64,1,640]{2,1,0:T(1,128)S(1)}) custom-call(s32[40]{0:T(128)S(1)} %concatenate.27.m, bf16[2,1,4,9,128,128]{5,4,3,2,1,0:T(8,128)(2,1)S(1)} %copy-done.1, bf16[4,128,256]{2,1,0:T(8,128)(2,1)S(1)} %get-tuple-element.25.s, bf16[1,128,256]{2,1,0:T(8,128)(2,1)S(1)} %collective-permute-done.13.above, ...), custom_call_target="tpu_custom_call" | custom-call | flops 176160768 | bytes 4194304 | tf_op jit(solution)/shard_map/gram/pallas_call | solution.py:280
  59.3 1.9 %collective-permute-start.17 = (f32[64,1,640]{2,1,0:T(1,128)S(1)}, f32[64,1,640]{2,1,0:T(1,128)S(1)}, u32[]{:S(2)}, u32[]{:S(2)}) collective-permute-start(f32[64,1,640]{2,1,0:T(1,128)S(1)} %get-tuple-element.31), channel_id=1, source_target_pairs={{0,2},{1,3},{2,0},{3,1},{4,6},{5,7},{6,4},{7,5},{8,10},{9,11},{10,... | collective-permute-start | bytes 491528 | tf_op jit(solution)/shard_map/ppermute | solution.py:50
  61.2 1.0 collective-permute-done.17
  62.4 23.6 %all_to_all.10 = f32[64,1,640]{2,1,0:T(1,128)S(1)} all-to-all(f32[64,1,640]{2,1,0:T(1,128)S(1)} %add.59), channel_id=1, replica_groups={{0,4,8,12,16,20,24,28,32,36,40,44,48,52,56,60,65,69,73,77,81,85,89,93,9..., dimensions={0} | all-to-all | bytes 327680 | tf_op jit(solution)/shard_map/all_to_all | solution.py:72
  86.3 16.6 %all_to_all.11.mine = f32[64,1,640]{2,1,0:T(1,128)S(1)} all-to-all(f32[64,1,640]{2,1,0:T(1,128)S(1)} %broadcast_in_dim.12), channel_id=1, replica_groups={{0,4,8,12,16,20,24,28,32,36,40,44,48,52,56,60,65,69,73,77,81,85,89,93,9..., dimensions={0} | all-to-all | bytes 327680 | tf_op jit(solution)/shard_map/all_to_all | solution.py:72
  102.8 2.7 %collective-permute-start.18 = (f32[64,1,640]{2,1,0:T(1,128)S(1)}, f32[64,1,640]{2,1,0:T(1,128)S(1)}, u32[]{:S(2)}, u32[]{:S(2)}) collective-permute-start(f32[64,1,640]{2,1,0:T(1,128)S(1)} %all_to_all.11.mine), channel_id=1, source_target_pairs={{0,2},{1,3},{2,0},{3,1},{4,6},{5,7},{6,4},{7,5},{8,10},{9,11},{10,... | collective-permute-start | bytes 491528 | tf_op jit(solution)/shard_map/ppermute | solution.py:50
  105.5 1.0 collective-permute-done.18.theirs
  106.6 39.7 %final.1 = (bf16[4,128,128]{2,1,0:T(8,128)(2,1)S(1)}, bf16[4,128,128]{2,1,0:T(8,128)(2,1)S(1)}, f32[256,128]{1,0:T(8,128)S(1)}, f32[256,128]{1,0:T(8,128)S(1)}) custom-call(s32[40]{0:T(128)S(1)} %concatenate.27.m, f32[64,1,640]{2,1,0:T(1,128)S(1)} %all_to_all.11.mine, f32[64,1,640]{2,1,0:T(1,128)S(1)} %collective-permute-done.18.theirs, ...), custom_call_target="tpu_custom_call" | custom-call | bytes 1114112 | tf_op jit(solution)/shard_map/final/pallas_call | solution.py:280
  146.4 3.0 %collective-permute-start.20 = (f32[256,128]{1,0:T(8,128)S(1)}, f32[256,128]{1,0:T(8,128)S(1)}, u32[]{:S(2)}, u32[]{:S(2)}) collective-permute-start(f32[256,128]{1,0:T(8,128)S(1)} %get-tuple-element.35), channel_id=1, source_target_pairs={{0,1},{1,0},{2,3},{3,2},{4,5},{5,4},{6,7},{7,6},{8,9},{9,8},{10,11... | collective-permute-start | bytes 393224 | tf_op jit(solution)/shard_map/ppermute | solution.py:59
  149.3 3.2 %collective-permute-done.19 = bf16[4,128,128]{2,1,0:T(8,128)(2,1)S(1)} collective-permute-done((bf16[4,128,128]{2,1,0:T(8,128)(2,1)S(1)}, bf16[4,128,128]{2,1,0:T(8,128)(2,1)S(1)}, u32[]{:S(2)}, u32[]{:S(2)}) %collective-permute-start.19) | collective-permute-done | bytes 131104 | tf_op jit(solution)/shard_map/ppermute | solution.py:59
  153.3 2.1 %collective-permute-done.20 = f32[256,128]{1,0:T(8,128)S(1)} collective-permute-done((f32[256,128]{1,0:T(8,128)S(1)}, f32[256,128]{1,0:T(8,128)S(1)}, u32[]{:S(2)}, u32[]{:S(2)}) %collective-permute-start.20) | collective-permute-done | bytes 131104 | tf_op jit(solution)/shard_map/ppermute | solution.py:59
  (44 shorter events, 7.4 us)
Async XLA Ops:
  1.6 6.0 %collective-permute-start = (bf16[4,128,128]{2,1,0:T(8,128)(2,1)S(1)}, bf16[4,128,128]{2,1,0:T(8,128)(2,1)S(1)}, u32[]{:S(2)}, u32[]{:S(2)}) collective-permute-start(bf16[4,128,128]{2,1,0:T(8,128)(2,1)S(1)} %get-tuple-element.36), channel_id=1, source_target_pairs={{0,1},{1,0},{2,3},{3,2},{4,5},{5,4},{6,7},{7,6},{8,9},{9,8},{10,11... | collective-permute-start | bytes 393224 | tf_op jit(solution)/shard_map/ppermute | solution.py:59
  8.3 9.2 %collective-permute-start.3 = (bf16[1,128,256]{2,1,0:T(8,128)(2,1)S(1)}, bf16[1,128,256]{2,1,0:T(8,128)(2,1)S(1)}, u32[]{:S(2)}, u32[]{:S(2)}) collective-permute-start(bf16[1,128,256]{2,1,0:T(8,128)(2,1)S(1)} %get-tuple-element.20), channel_id=1, source_target_pairs={{0,2},{1,3},{2,0},{3,1},{4,6},{5,7},{6,4},{7,5},{8,10},{9,11},{10,... | collective-permute-start | bytes 196616 | tf_op jit(solution)/shard_map/ppermute | solution.py:50
  12.1 14.8 %collective-permute-start.2 = (bf16[4,128,256]{2,1,0:T(8,128)(2,1)S(1)}, bf16[4,128,256]{2,1,0:T(8,128)(2,1)S(1)}, u32[]{:S(2)}, u32[]{:S(2)}) collective-permute-start(bf16[4,128,256]{2,1,0:T(8,128)(2,1)S(1)} %get-tuple-element.19.v.rest_0_), channel_id=1, source_target_pairs={{0,225},{1,224},{2,227},{3,226},{4,229},{5,228},{6,231},{7,230},{8... | collective-permute-start | bytes 786440 | tf_op jit(solution)/shard_map/ppermute | solution.py:50
  15.6 11.3 %collective-permute-start.1 = (bf16[4,128,256]{2,1,0:T(8,128)(2,1)S(1)}, bf16[4,128,256]{2,1,0:T(8,128)(2,1)S(1)}, u32[]{:S(2)}, u32[]{:S(2)}) collective-permute-start(bf16[4,128,256]{2,1,0:T(8,128)(2,1)S(1)} %get-tuple-element.19.v.rest_0_), channel_id=1, source_target_pairs={{0,32},{1,33},{2,34},{3,35},{4,36},{5,37},{6,38},{7,39},{8,40},{9,... | collective-permute-start | bytes 786440 | tf_op jit(solution)/shard_map/ppermute | solution.py:50
  15.6 4.1 %collective-permute-start.4 = (bf16[1,128,256]{2,1,0:T(8,128)(2,1)S(1)}, bf16[1,128,256]{2,1,0:T(8,128)(2,1)S(1)}, u32[]{:S(2)}, u32[]{:S(2)}) collective-permute-start(bf16[1,128,256]{2,1,0:T(8,128)(2,1)S(1)} %get-tuple-element.21), channel_id=1, source_target_pairs={{0,30},{1,31},{2,4},{3,5},{4,2},{5,3},{6,8},{7,9},{8,6},{9,7},{10,... | collective-permute-start | bytes 196616 | tf_op jit(solution)/shard_map/ppermute | solution.py:50
  19.8 7.1 %collective-permute-start.6 = (bf16[2,128,256]{2,1,0:T(8,128)(2,1)S(1)}, bf16[2,128,256]{2,1,0:T(8,128)(2,1)S(1)}, u32[]{:S(2)}, u32[]{:S(2)}) collective-permute-start(bf16[2,128,256]{2,1,0:T(8,128)(2,1)S(1)} %constant_dynamic-update-slice_fusion), channel_id=1, source_target_pairs={{0,225},{1,224},{2,227},{3,226},{4,229},{5,228},{6,231},{7,230},{8... | collective-permute-start | bytes 393224 | tf_op jit(solution)/shard_map/ppermute | solution.py:50
  21.0 5.9 %collective-permute-start.5 = (bf16[2,128,256]{2,1,0:T(8,128)(2,1)S(1)}, bf16[2,128,256]{2,1,0:T(8,128)(2,1)S(1)}, u32[]{:S(2)}, u32[]{:S(2)}) collective-permute-start(bf16[2,128,256]{2,1,0:T(8,128)(2,1)S(1)} %constant_dynamic-update-slice_fusion), channel_id=1, source_target_pairs={{0,32},{1,33},{2,34},{3,35},{4,36},{5,37},{6,38},{7,39},{8,40},{9,... | collective-permute-start | bytes 393224 | tf_op jit(solution)/shard_map/ppermute | solution.py:50
  21.6 1.7 %copy-start = (bf16[2,1,4,9,128,128]{5,4,3,2,1,0:T(8,128)(2,1)S(1)}, bf16[2,1,4,9,128,128]{5,4,3,2,1,0:T(8,128)(2,1)}, u32[]{:S(2)}) copy-start(bf16[2,1,4,9,128,128]{5,4,3,2,1,0:T(8,128)(2,1)} %h.11) | copy-start | bytes 7077892
  23.3 3.6 %copy-start.1 = (bf16[2,1,4,9,128,128]{5,4,3,2,1,0:T(8,128)(2,1)S(1)}, bf16[2,1,4,9,128,128]{5,4,3,2,1,0:T(8,128)(2,1)}, u32[]{:S(2)}) copy-start(bf16[2,1,4,9,128,128]{5,4,3,2,1,0:T(8,128)(2,1)} %h.11) | copy-start | bytes 7077892
  28.0 6.8 %collective-permute-start.9 = (bf16[1,128,256]{2,1,0:T(8,128)(2,1)S(1)}, bf16[1,128,256]{2,1,0:T(8,128)(2,1)S(1)}, u32[]{:S(2)}, u32[]{:S(2)}) collective-permute-start(bf16[1,128,256]{2,1,0:T(8,128)(2,1)S(1)} %get-tuple-element.23), channel_id=1, source_target_pairs={{0,2},{1,3},{2,0},{3,1},{4,6},{5,7},{6,4},{7,5},{8,10},{9,11},{10,... | collective-permute-start | bytes 196616 | tf_op jit(solution)/shard_map/ppermute | solution.py:50
  33.0 12.9 %collective-permute-start.8 = (bf16[4,128,256]{2,1,0:T(8,128)(2,1)S(1)}, bf16[4,128,256]{2,1,0:T(8,128)(2,1)S(1)}, u32[]{:S(2)}, u32[]{:S(2)}) collective-permute-start(bf16[4,128,256]{2,1,0:T(8,128)(2,1)S(1)} %get-tuple-element.22.v), channel_id=1, source_target_pairs={{0,225},{1,224},{2,227},{3,226},{4,229},{5,228},{6,231},{7,230},{8... | collective-permute-start | bytes 786440 | tf_op jit(solution)/shard_map/ppermute | solution.py:50
  34.7 11.1 %collective-permute-start.7 = (bf16[4,128,256]{2,1,0:T(8,128)(2,1)S(1)}, bf16[4,128,256]{2,1,0:T(8,128)(2,1)S(1)}, u32[]{:S(2)}, u32[]{:S(2)}) collective-permute-start(bf16[4,128,256]{2,1,0:T(8,128)(2,1)S(1)} %get-tuple-element.22.v), channel_id=1, source_target_pairs={{0,32},{1,33},{2,34},{3,35},{4,36},{5,37},{6,38},{7,39},{8,40},{9,... | collective-permute-start | bytes 786440 | tf_op jit(solution)/shard_map/ppermute | solution.py:50
  34.7 4.0 %collective-permute-start.10 = (bf16[1,128,256]{2,1,0:T(8,128)(2,1)S(1)}, bf16[1,128,256]{2,1,0:T(8,128)(2,1)S(1)}, u32[]{:S(2)}, u32[]{:S(2)}) collective-permute-start(bf16[1,128,256]{2,1,0:T(8,128)(2,1)S(1)} %get-tuple-element.24), channel_id=1, source_target_pairs={{0,30},{1,31},{2,4},{3,5},{4,2},{5,3},{6,8},{7,9},{8,6},{9,7},{10,... | collective-permute-start | bytes 196616 | tf_op jit(solution)/shard_map/ppermute | solution.py:50
  38.7 7.1 %collective-permute-start.12 = (bf16[2,128,256]{2,1,0:T(8,128)(2,1)S(1)}, bf16[2,128,256]{2,1,0:T(8,128)(2,1)S(1)}, u32[]{:S(2)}, u32[]{:S(2)}) collective-permute-start(bf16[2,128,256]{2,1,0:T(8,128)(2,1)S(1)} %constant_dynamic-update-slice_fusion.2), channel_id=1, source_target_pairs={{0,225},{1,224},{2,227},{3,226},{4,229},{5,228},{6,231},{7,230},{8... | collective-permute-start | bytes 393224 | tf_op jit(solution)/shard_map/ppermute | solution.py:50
  41.8 4.1 %collective-permute-start.11 = (bf16[2,128,256]{2,1,0:T(8,128)(2,1)S(1)}, bf16[2,128,256]{2,1,0:T(8,128)(2,1)S(1)}, u32[]{:S(2)}, u32[]{:S(2)}) collective-permute-start(bf16[2,128,256]{2,1,0:T(8,128)(2,1)S(1)} %constant_dynamic-update-slice_fusion.2), channel_id=1, source_target_pairs={{0,32},{1,33},{2,34},{3,35},{4,36},{5,37},{6,38},{7,39},{8,40},{9,... | collective-permute-start | bytes 393224 | tf_op jit(solution)/shard_map/ppermute | solution.py:50
  46.9 10.6 %collective-permute-start.14 = (bf16[4,128,256]{2,1,0:T(8,128)(2,1)S(1)}, bf16[4,128,256]{2,1,0:T(8,128)(2,1)S(1)}, u32[]{:S(2)}, u32[]{:S(2)}) collective-permute-start(bf16[4,128,256]{2,1,0:T(8,128)(2,1)S(1)} %get-tuple-element.25.s), channel_id=1, source_target_pairs={{0,225},{1,224},{2,227},{3,226},{4,229},{5,228},{6,231},{7,230},{8... | collective-permute-start | bytes 786440 | tf_op jit(solution)/shard_map/ppermute | solution.py:54
  50.0 7.5 %collective-permute-start.15 = (bf16[1,128,256]{2,1,0:T(8,128)(2,1)S(1)}, bf16[1,128,256]{2,1,0:T(8,128)(2,1)S(1)}, u32[]{:S(2)}, u32[]{:S(2)}) collective-permute-start(bf16[1,128,256]{2,1,0:T(8,128)(2,1)S(1)} %get-tuple-element.27), channel_id=1, source_target_pairs={{0,227},{1,226},{2,229},{3,228},{4,231},{5,230},{6,233},{7,232},{8... | collective-permute-start | bytes 196616 | tf_op jit(solution)/shard_map/ppermute | solution.py:54
  50.7 6.8 %collective-permute-start.16 = (bf16[1,128,256]{2,1,0:T(8,128)(2,1)S(1)}, bf16[1,128,256]{2,1,0:T(8,128)(2,1)S(1)}, u32[]{:S(2)}, u32[]{:S(2)}) collective-permute-start(bf16[1,128,256]{2,1,0:T(8,128)(2,1)S(1)} %get-tuple-element.26), channel_id=1, source_target_pairs={{0,255},{1,254},{2,225},{3,224},{4,227},{5,226},{6,229},{7,228},{8... | collective-permute-start | bytes 196616 | tf_op jit(solution)/shard_map/ppermute | solution.py:54
  52.7 4.8 %collective-permute-start.13 = (bf16[1,128,256]{2,1,0:T(8,128)(2,1)S(1)}, bf16[1,128,256]{2,1,0:T(8,128)(2,1)S(1)}, u32[]{:S(2)}, u32[]{:S(2)}) collective-permute-start(bf16[1,128,256]{2,1,0:T(8,128)(2,1)S(1)} %get-tuple-element.26), channel_id=1, source_target_pairs={{0,30},{1,31},{2,0},{3,1},{4,2},{5,3},{6,4},{7,5},{8,6},{9,7},{10,... | collective-permute-start | bytes 196616 | tf_op jit(solution)/shard_map/ppermute | solution.py:54
  59.3 3.0 %collective-permute-start.17 = (f32[64,1,640]{2,1,0:T(1,128)S(1)}, f32[64,1,640]{2,1,0:T(1,128)S(1)}, u32[]{:S(2)}, u32[]{:S(2)}) collective-permute-start(f32[64,1,640]{2,1,0:T(1,128)S(1)} %get-tuple-element.31), channel_id=1, source_target_pairs={{0,2},{1,3},{2,0},{3,1},{4,6},{5,7},{6,4},{7,5},{8,10},{9,11},{10,... | collective-permute-start | bytes 491528 | tf_op jit(solution)/shard_map/ppermute | solution.py:50
  102.8 3.7 %collective-permute-start.18 = (f32[64,1,640]{2,1,0:T(1,128)S(1)}, f32[64,1,640]{2,1,0:T(1,128)S(1)}, u32[]{:S(2)}, u32[]{:S(2)}) collective-permute-start(f32[64,1,640]{2,1,0:T(1,128)S(1)} %all_to_all.11.mine), channel_id=1, source_target_pairs={{0,2},{1,3},{2,0},{3,1},{4,6},{5,7},{6,4},{7,5},{8,10},{9,11},{10,... | collective-permute-start | bytes 491528 | tf_op jit(solution)/shard_map/ppermute | solution.py:50
  146.3 6.3 %collective-permute-start.19 = (bf16[4,128,128]{2,1,0:T(8,128)(2,1)S(1)}, bf16[4,128,128]{2,1,0:T(8,128)(2,1)S(1)}, u32[]{:S(2)}, u32[]{:S(2)}) collective-permute-start(bf16[4,128,128]{2,1,0:T(8,128)(2,1)S(1)} %get-tuple-element.33), channel_id=1, source_target_pairs={{0,1},{1,0},{2,3},{3,2},{4,5},{5,4},{6,7},{7,6},{8,9},{9,8},{10,11... | collective-permute-start | bytes 393224 | tf_op jit(solution)/shard_map/ppermute | solution.py:59
  146.4 9.0 %collective-permute-start.20 = (f32[256,128]{1,0:T(8,128)S(1)}, f32[256,128]{1,0:T(8,128)S(1)}, u32[]{:S(2)}, u32[]{:S(2)}) collective-permute-start(f32[256,128]{1,0:T(8,128)S(1)} %get-tuple-element.35), channel_id=1, source_target_pairs={{0,1},{1,0},{2,3},{3,2},{4,5},{5,4},{6,7},{7,6},{8,9},{9,8},{10,11... | collective-permute-start | bytes 393224 | tf_op jit(solution)/shard_map/ppermute | solution.py:59

commit v3 on v2

--- a/solution.py
+++ b/solution.py
@@ -96,40 +96,42 @@
     return jnp.concatenate([h_block(m, h, tile, side, dy) for dy in dys], axis=1)
 
 
-def fill(m, ext, middle, p, q):
-    par = m[PAR_Y]
-    ext[1:5] = middle
-    ext[pl.ds(jnp.where(par == 0, 5, 0), 1)] = p
-    ext[pl.ds(jnp.where(par == 0, 0, 5), 1)] = q
-
-
-def store_sides(m, ref, p_ref, q_ref):
-    par = m[PAR_Y]
-    p_ref[...] = ref[pl.ds(jnp.where(par == 0, 3, 0), 1)]
-    q_ref[...] = ref[pl.ds(jnp.where(par == 0, 0, 3), 1)]
-
-
-def join_kernel(m, own, other, v, p, q):
+def fill(m, ext, mid, ends):
+    even = m[PAR_Y] == 0
+    ext[1:2] = ends[1:2]
+    ext[2:5] = mid[...]
+    ext[pl.ds(jnp.where(even, 5, 0), 1)] = ends[0:1]
+    ext[pl.ds(jnp.where(even, 0, 5), 1)] = ends[2:3]
+
+
+def store_sides(m, ref, mid, p_ref, q_ref):
+    even = m[PAR_Y] == 0
+    p_ref[...] = ref[pl.ds(jnp.where(even, 3, 0), 1)]
+    q_ref[...] = ref[pl.ds(jnp.where(even, 0, 3), 1)]
+    mid[...] = ref[1:4]
+
+
+def join_kernel(m, own, other, v, mid, p, q):
     first_col = m[COL] == 0
     v[:, :, :T] = jnp.where(first_col, own[...], other[...])
     v[:, :, T:] = jnp.where(first_col, other[...], own[...])
-    store_sides(m, v, p, q)
-
-
-def own_kernel(m, h, v, p, q, acc, ext):
-    fill(m, ext, v[...], p[...], q[...])
+    store_sides(m, v, mid, p, q)
+
+
+def own_kernel(m, h, mid, ends, acc, ext):
+    fill(m, ext, mid, ends)
     for tile in range(4):
         row = h_row(m, h, tile, 0, range(3))
         acc[tile] = dot(row, ext[tile : tile + 3].reshape(3 * T, 2 * T))
 
 
-def side_kernel(m, h, a, b, ca, cb, acc, *rest, last):
+def side_kernel(m, h, a, a_ends, b, b_ends, acc, *rest, last):
     if last:
-        v, out, low, high, ext_a, ext_b = rest
+        v, out, mid, p, q, ext_a, ext_b = rest
     else:
-        out, p, q, ext_a, ext_b = rest
-    fill(m, ext_a, a[...], ca[0:1], ca[1:2])
-    fill(m, ext_b, b[...], cb[0:1], cb[1:2])
+        out, mid, p, q, ext_a, ext_b = rest
+    fill(m, ext_a, a, a_ends)
+    fill(m, ext_b, b, b_ends)
     for tile in range(4):
         total = acc[tile]
         for side, ext in ((1, ext_a), (2, ext_b)):
@@ -139,11 +141,7 @@
             out[tile] = (total - v[tile].astype(F32)).astype(BF)
         else:
             out[tile] = (0.5 * total).astype(BF)
-    if last:
-        low[...] = out[0:1]
-        high[...] = out[3:4]
-    else:
-        store_sides(m, out, p, q)
+    store_sides(m, out, mid, p, q)
 
 
 def inner_kernel(m, h, s, corr, acc):
@@ -161,16 +159,15 @@
     return lax.broadcasted_iota(jnp.int32, shape, 0), lax.broadcasted_iota(jnp.int32, shape, 1)
 
 
-def gram_kernel(m, h, s, above, right, right_low, right_high, acc, corr, mine, theirs, ext):
-    ext[0:1] = right_low[...]
-    ext[1:5] = right[...]
-    ext[5:6] = right_high[...]
+def gram_kernel(m, h, s, ends, right, right_ends, acc, corr, mine, theirs, ext):
+    fill(m, ext, right, right_ends)
+    above = jnp.where(m[PAR_Y] == 0, ends[0], ends[2])
     side = 1 + m[PAR_X]
     half = jnp.zeros((2 * T, 2 * T), F32)
     for tile in range(4):
         total = acc[tile]
         if tile == 3:
-            total += dot(h_block(m, h, tile, 0, 2), above[0])
+            total += dot(h_block(m, h, tile, 0, 2), above)
         row = h_row(m, h, tile, side, range(3))
         total += dot(row, ext[tile : tile + 3].reshape(3 * T, 2 * T))
         high, low = split(total)
@@ -316,48 +313,47 @@
 def per_device(start_block, hamiltonian, neighbour_index, block_count):
     sizes = tuple(lax.axis_size(a) for a in AXES)
     members = sizes[0] * sizes[1]
-    block, tile, full = (4, T, 2 * T), (1, T, 2 * T), (2 * T, 2 * T)
+    block, middle, tile, full = (4, T, 2 * T), (3, T, 2 * T), (1, T, 2 * T), (2 * T, 2 * T)
     ext = pltpu.VMEM((6, T, 2 * T), BF)
     spin, col, m = table(neighbour_index, block_count)
 
     other = swap_col(sizes, lax.dynamic_index_in_dim(start_block, 1 - spin, 0, keepdims=False)[0])
     own = lax.dynamic_index_in_dim(start_block, spin, 0, keepdims=False)[0]
-    v, p, q = call(
-        join_kernel, m, [own, other],
-        [shaped(block, BF), shaped(tile, BF), shaped(tile, BF)], name="join",
-    )
-
-    def apply_ham(x, p, q, before):
+    parts = [shaped(block, BF), shaped(middle, BF), shaped(tile, BF), shaped(tile, BF)]
+    v, mid, p, q = call(join_kernel, m, [own, other], parts, name="join")
+
+    def along_y(x, p, q):
         p, q = swap(sizes, p, 0, 1), swap(sizes, q, 0, 2)
-        a, b = swap(sizes, x, 1, 0), swap(sizes, x, 2, 0)
-        ends = jnp.concatenate([p, q], axis=0)
-        ca, cb = swap(sizes, ends, 1, 0), swap(sizes, ends, 2, 0)
+        return jnp.concatenate([p, x[:1], q], axis=0)
+
+    def apply_ham(x, mid, p, q, before):
+        ends = along_y(x, p, q)
+        a, b = swap(sizes, mid, 1, 0), swap(sizes, mid, 2, 0)
+        a_ends, b_ends = swap(sizes, ends, 1, 0), swap(sizes, ends, 2, 0)
         (acc,) = call(
-            own_kernel, m, [x, p, q], [shaped(block, F32)], [ext], hamiltonian,
+            own_kernel, m, [mid, ends], [shaped(block, F32)], [ext], hamiltonian,
             2 * 12 * T * T * 2 * T, "own",
         )
         last = before is not None
-        arrays = [a, b, ca, cb, acc] + ([before] if last else [])
+        arrays = [a, a_ends, b, b_ends, acc] + ([before] if last else [])
         return call(
-            functools.partial(side_kernel, last=last), m, arrays,
-            [shaped(block, BF), shaped(tile, BF), shaped(tile, BF)], [ext, ext], hamiltonian,
+            functools.partial(side_kernel, last=last), m, arrays, parts, [ext, ext], hamiltonian,
             2 * 24 * T * T * 2 * T, "sides",
         )
 
-    first, p, q = apply_ham(v, p, q, None)
-    second, low, high = apply_ham(first, p, q, v)
-
-    above = shift(sizes, low, 0, -1)
-    right_high = shift(sizes, low, -1, -1)
-    right_low = shift(sizes, high, -1, 1)
-    right = shift(sizes, second, -1, 0)
+    first, mid, p, q = apply_ham(v, mid, p, q, None)
+    second, mid, p, q = apply_ham(first, mid, p, q, v)
+
+    ends = along_y(second, p, q)
+    right = shift(sizes, mid, -1, 0)
+    right_ends = shift(sizes, ends, -1, 0)
     corr, acc = call(
         inner_kernel, m, [second], [shaped(full, F32), shaped(block, F32)], (), hamiltonian,
         2 * 15 * T * T * 2 * T, "inner",
     )
     piece = shaped((members // 2, 1, 5 * T), F32)
     mine, theirs = call(
-        gram_kernel, m, [second, above, right, right_low, right_high, acc, corr],
+        gram_kernel, m, [second, ends, right, right_ends, acc, corr],
         [piece, piece], [ext], hamiltonian, 2 * 21 * T * T * 2 * T, "gram",
     )
 

time: 156 us -> 158 us (1.013)
  waiting for transfers between devices: 20.2 us -> 26.7 us
  starting transfers between devices: 41.5 us -> 36.7 us
    ppermute x14 -> x16, waiting for transfers between devices: 14.3 us -> 18.1 us  [swap(): return lax.ppermute(block, AXES, perm)]
    ppermute x4 -> x2, starting transfers between devices: 9.28 us -> 5.81 us  [shift(): lax.ppermute(block, AXES, pairs(sizes, lambda gx, gy: (gx + dx, gy + dy)))]
    ppermute x4 -> x2, waiting for transfers between devices: 0.42 us -> 3.15 us  [shift(): lax.ppermute(block, AXES, pairs(sizes, lambda gx, gy: (gx + dx, gy + dy)))]
    ppermute x14 -> x16, starting transfers between devices: 25.5 us -> 24.2 us  [swap(): return lax.ppermute(block, AXES, perm)]
  transfers between devices with their start and end apart: 21 -> 21, of which waited for: 10 -> 11; matrix products, arithmetic and copies ran while one was open for 2% -> 2% of each run, Pallas kernels for 2% -> 2%
where the time goes in v3:
time: 158 us
  Pallas kernels  46.8 us (30%)
  blocking collectives  40.3 us (26%)
  starting transfers between devices  36.7 us (23%)
  waiting for transfers between devices  26.7 us (17%)
  other arithmetic  3.72 us (2%)
  local copies, waits for them, and re-layouts  3.05 us (2%)
    pallas_call x8, Pallas kernels, call(): pl.pallas_call(kernel, out_shape=outs, grid_spec=pltpu.PrefetchScalarGrid...  46.8 us
    all_to_all x2, blocking collectives, exchange(): lax.all_to_all(pieces, AXES, 0, 0, axis_index_groups=groups, tiled=True)  40.3 us
    ppermute x16, starting transfers between devices, swap(): return lax.ppermute(block, AXES, perm)  24.2 us
    ppermute x16, waiting for transfers between devices, swap(): return lax.ppermute(block, AXES, perm)  18.1 us
    ppermute x3, starting transfers between devices, swap_col(): return lax.ppermute(block, AXES, perm)  6.71 us
    ppermute x2, starting transfers between devices, shift(): lax.ppermute(block, AXES, pairs(sizes, lambda gx, gy: (gx + dx, gy + dy)))  5.81 us
    ppermute x3, waiting for transfers between devices, swap_col(): return lax.ppermute(block, AXES, perm)  5.49 us
  transfers between devices with their start and end apart: 21, of which 11 were waited for; matrix products, arithmetic and copies ran while one was open for 2% of the time, Pallas kernels for 2%

profile of v3, /device:TPU:1, one launch (start us, length us, event | category | flops | bytes accessed | tf_op | source)
XLA Modules:
  0.0 158.1 jit_solution(16162145881554547320)
XLA Ops:
  0.6 1.0 dynamic-slice_bitcast_fusion
  1.6 3.7 %collective-permute-start = (bf16[4,128,128]{2,1,0:T(8,128)(2,1)S(1)}, bf16[4,128,128]{2,1,0:T(8,128)(2,1)S(1)}, u32[]{:S(2)}, u32[]{:S(2)}) collective-permute-start(bf16[4,128,128]{2,1,0:T(8,128)(2,1)S(1)} %get-tuple-element.42), channel_id=1, source_target_pairs={{0,1},{1,0},{2,3},{3,2},{4,5},{5,4},{6,7},{7,6},{8,9},{9,8},{10,11... | collective-permute-start | bytes 393224 | tf_op jit(solution)/shard_map/ppermute | solution.py:59
  6.2 1.0 select_reduce_fusion
  8.3 3.9 %collective-permute-start.2 = (bf16[1,128,256]{2,1,0:T(8,128)(2,1)S(1)}, bf16[1,128,256]{2,1,0:T(8,128)(2,1)S(1)}, u32[]{:S(2)}, u32[]{:S(2)}) collective-permute-start(bf16[1,128,256]{2,1,0:T(8,128)(2,1)S(1)} %get-tuple-element.23), channel_id=1, source_target_pairs={{0,2},{1,3},{2,0},{3,1},{4,6},{5,7},{6,4},{7,5},{8,10},{9,11},{10,... | collective-permute-start | bytes 196616 | tf_op jit(solution)/shard_map/ppermute | solution.py:50
  12.3 4.9 %collective-permute-start.5 = (bf16[3,128,256]{2,1,0:T(8,128)(2,1)S(1)}, bf16[3,128,256]{2,1,0:T(8,128)(2,1)S(1)}, u32[]{:S(2)}, u32[]{:S(2)}) collective-permute-start(bf16[3,128,256]{2,1,0:T(8,128)(2,1)S(1)} %get-tuple-element.22.mid), channel_id=1, source_target_pairs={{0,225},{1,224},{2,227},{3,226},{4,229},{5,228},{6,231},{7,230},{8... | collective-permute-start | bytes 589832 | tf_op jit(solution)/shard_map/ppermute | solution.py:50
  17.3 2.1 %collective-permute-start.6 = (bf16[3,128,256]{2,1,0:T(8,128)(2,1)S(1)}, bf16[3,128,256]{2,1,0:T(8,128)(2,1)S(1)}, u32[]{:S(2)}, u32[]{:S(2)}) collective-permute-start(bf16[3,128,256]{2,1,0:T(8,128)(2,1)S(1)} %pad_maximum_fusion.ends), channel_id=1, source_target_pairs={{0,225},{1,224},{2,227},{3,226},{4,229},{5,228},{6,231},{7,230},{8... | collective-permute-start | bytes 589832 | tf_op jit(solution)/shard_map/ppermute | solution.py:50
  19.4 1.7 %copy-done = bf16[2,1,4,9,128,128]{5,4,3,2,1,0:T(8,128)(2,1)S(1)} copy-done((bf16[2,1,4,9,128,128]{5,4,3,2,1,0:T(8,128)(2,1)S(1)}, bf16[2,1,4,9,128,128]{5,4,3,2,1,0:T(8,128)(2,1)}, u32[]{:S(2)}) %copy-start) | copy-done | bytes 2359320
  22.0 5.1 %collective-permute-done.6.b_ends = bf16[3,128,256]{2,1,0:T(8,128)(2,1)S(1)} collective-permute-done((bf16[3,128,256]{2,1,0:T(8,128)(2,1)S(1)}, bf16[3,128,256]{2,1,0:T(8,128)(2,1)S(1)}, u32[]{:S(2)}, u32[]{:S(2)}) %collective-permute-start.6) | collective-permute-done | bytes 196640 | tf_op jit(solution)/shard_map/ppermute | solution.py:50
  27.1 1.0 sides.2
  28.1 4.0 %collective-permute-start.8 = (bf16[1,128,256]{2,1,0:T(8,128)(2,1)S(1)}, bf16[1,128,256]{2,1,0:T(8,128)(2,1)S(1)}, u32[]{:S(2)}, u32[]{:S(2)}) collective-permute-start(bf16[1,128,256]{2,1,0:T(8,128)(2,1)S(1)} %get-tuple-element.27), channel_id=1, source_target_pairs={{0,2},{1,3},{2,0},{3,1},{4,6},{5,7},{6,4},{7,5},{8,10},{9,11},{10,... | collective-permute-start | bytes 196616 | tf_op jit(solution)/shard_map/ppermute | solution.py:50
  32.1 1.7 %collective-permute-start.11 = (bf16[3,128,256]{2,1,0:T(8,128)(2,1)S(1)}, bf16[3,128,256]{2,1,0:T(8,128)(2,1)S(1)}, u32[]{:S(2)}, u32[]{:S(2)}) collective-permute-start(bf16[3,128,256]{2,1,0:T(8,128)(2,1)S(1)} %get-tuple-element.26.mid), channel_id=1, source_target_pairs={{0,225},{1,224},{2,227},{3,226},{4,229},{5,228},{6,231},{7,230},{8... | collective-permute-start | bytes 589832 | tf_op jit(solution)/shard_map/ppermute | solution.py:50
  33.9 2.2 %collective-permute-done.9 = bf16[1,128,256]{2,1,0:T(8,128)(2,1)S(1)} collective-permute-done((bf16[1,128,256]{2,1,0:T(8,128)(2,1)S(1)}, bf16[1,128,256]{2,1,0:T(8,128)(2,1)S(1)}, u32[]{:S(2)}, u32[]{:S(2)}) %collective-permute-start.9) | collective-permute-done | bytes 65568 | tf_op jit(solution)/shard_map/ppermute | solution.py:50
  36.2 1.5 collective-permute-start.12
  38.5 1.4 collective-permute-done.11.b
  40.0 6.1 %collective-permute-done.12.b_ends = bf16[3,128,256]{2,1,0:T(8,128)(2,1)S(1)} collective-permute-done((bf16[3,128,256]{2,1,0:T(8,128)(2,1)S(1)}, bf16[3,128,256]{2,1,0:T(8,128)(2,1)S(1)}, u32[]{:S(2)}, u32[]{:S(2)}) %collective-permute-start.12) | collective-permute-done | bytes 196640 | tf_op jit(solution)/shard_map/ppermute | solution.py:50
  46.1 1.0 sides.3
  47.1 1.6 %collective-permute-start.13 = (bf16[1,128,256]{2,1,0:T(8,128)(2,1)S(1)}, bf16[1,128,256]{2,1,0:T(8,128)(2,1)S(1)}, u32[]{:S(2)}, u32[]{:S(2)}) collective-permute-start(bf16[1,128,256]{2,1,0:T(8,128)(2,1)S(1)} %get-tuple-element.31), channel_id=1, source_target_pairs={{0,2},{1,3},{2,0},{3,1},{4,6},{5,7},{6,4},{7,5},{8,10},{9,11},{10,... | collective-permute-start | bytes 196616 | tf_op jit(solution)/shard_map/ppermute | solution.py:50
  48.7 2.8 %collective-permute-start.15 = (bf16[3,128,256]{2,1,0:T(8,128)(2,1)S(1)}, bf16[3,128,256]{2,1,0:T(8,128)(2,1)S(1)}, u32[]{:S(2)}, u32[]{:S(2)}) collective-permute-start(bf16[3,128,256]{2,1,0:T(8,128)(2,1)S(1)} %get-tuple-element.33), channel_id=1, source_target_pairs={{0,225},{1,224},{2,227},{3,226},{4,229},{5,228},{6,231},{7,230},{8... | collective-permute-start | bytes 589832 | tf_op jit(solution)/shard_map/ppermute | solution.py:54
  51.6 1.2 collective-permute-done.14
  52.7 3.0 %collective-permute-start.16 = (bf16[3,128,256]{2,1,0:T(8,128)(2,1)S(1)}, bf16[3,128,256]{2,1,0:T(8,128)(2,1)S(1)}, u32[]{:S(2)}, u32[]{:S(2)}) collective-permute-start(bf16[3,128,256]{2,1,0:T(8,128)(2,1)S(1)} %pad_maximum_fusion.2.ends), channel_id=1, source_target_pairs={{0,225},{1,224},{2,227},{3,226},{4,229},{5,228},{6,231},{7,230},{8... | collective-permute-start | bytes 589832 | tf_op jit(solution)/shard_map/ppermute | solution.py:54
  56.6 3.2 %collective-permute-done.16.right_ends = bf16[3,128,256]{2,1,0:T(8,128)(2,1)S(1)} collective-permute-done((bf16[3,128,256]{2,1,0:T(8,128)(2,1)S(1)}, bf16[3,128,256]{2,1,0:T(8,128)(2,1)S(1)}, u32[]{:S(2)}, u32[]{:S(2)}) %collective-permute-start.16) | collective-permute-done | bytes 196640 | tf_op jit(solution)/shard_map/ppermute | solution.py:54
  59.8 1.8 %gram.1 = (f32[64,1,640]{2,1,0:T(1,128)S(1)}, f32[64,1,640]{2,1,0:T(1,128)S(1)}) custom-call(s32[40]{0:T(128)S(1)} %concatenate.30.m, bf16[2,1,4,9,128,128]{5,4,3,2,1,0:T(8,128)(2,1)S(1)} %copy-done.1, bf16[4,128,256]{2,1,0:T(8,128)(2,1)S(1)} %get-tuple-element.30.s, bf16[3,128,256]{2,1,0:T(8,128)(2,1)S(1)} %pad_maximum_fusion.2.ends, ...), custom_call_target="tpu_custom_call" | custom-call | flops 176160768 | bytes 4325376 | tf_op jit(solution)/shard_map/gram/pallas_call | solution.py:277
  61.6 1.5 collective-permute-start.17
  63.1 1.0 collective-permute-done.17
  64.3 23.5 %all_to_all.10 = f32[64,1,640]{2,1,0:T(1,128)S(1)} all-to-all(f32[64,1,640]{2,1,0:T(1,128)S(1)} %add.59), channel_id=1, replica_groups={{0,4,8,12,16,20,24,28,32,36,40,44,48,52,56,60,65,69,73,77,81,85,89,93,9..., dimensions={0} | all-to-all | bytes 327680 | tf_op jit(solution)/shard_map/all_to_all | solution.py:72
  88.1 16.8 %all_to_all.11.mine = f32[64,1,640]{2,1,0:T(1,128)S(1)} all-to-all(f32[64,1,640]{2,1,0:T(1,128)S(1)} %broadcast_in_dim.12), channel_id=1, replica_groups={{0,4,8,12,16,20,24,28,32,36,40,44,48,52,56,60,65,69,73,77,81,85,89,93,9..., dimensions={0} | all-to-all | bytes 327680 | tf_op jit(solution)/shard_map/all_to_all | solution.py:72
  104.9 2.7 %collective-permute-start.18 = (f32[64,1,640]{2,1,0:T(1,128)S(1)}, f32[64,1,640]{2,1,0:T(1,128)S(1)}, u32[]{:S(2)}, u32[]{:S(2)}) collective-permute-start(f32[64,1,640]{2,1,0:T(1,128)S(1)} %all_to_all.11.mine), channel_id=1, source_target_pairs={{0,2},{1,3},{2,0},{3,1},{4,6},{5,7},{6,4},{7,5},{8,10},{9,11},{10,... | collective-permute-start | bytes 491528 | tf_op jit(solution)/shard_map/ppermute | solution.py:50
  107.5 1.0 collective-permute-done.18.theirs
  108.6 39.7 %final.1 = (bf16[4,128,128]{2,1,0:T(8,128)(2,1)S(1)}, bf16[4,128,128]{2,1,0:T(8,128)(2,1)S(1)}, f32[256,128]{1,0:T(8,128)S(1)}, f32[256,128]{1,0:T(8,128)S(1)}) custom-call(s32[40]{0:T(128)S(1)} %concatenate.30.m, f32[64,1,640]{2,1,0:T(1,128)S(1)} %all_to_all.11.mine, f32[64,1,640]{2,1,0:T(1,128)S(1)} %collective-permute-done.18.theirs, ...), custom_call_target="tpu_custom_call" | custom-call | bytes 1114112 | tf_op jit(solution)/shard_map/final/pallas_call | solution.py:277
  148.4 3.0 %collective-permute-start.20 = (f32[256,128]{1,0:T(8,128)S(1)}, f32[256,128]{1,0:T(8,128)S(1)}, u32[]{:S(2)}, u32[]{:S(2)}) collective-permute-start(f32[256,128]{1,0:T(8,128)S(1)} %get-tuple-element.41), channel_id=1, source_target_pairs={{0,1},{1,0},{2,3},{3,2},{4,5},{5,4},{6,7},{7,6},{8,9},{9,8},{10,11... | collective-permute-start | bytes 393224 | tf_op jit(solution)/shard_map/ppermute | solution.py:59
  151.4 3.2 %collective-permute-done.19 = bf16[4,128,128]{2,1,0:T(8,128)(2,1)S(1)} collective-permute-done((bf16[4,128,128]{2,1,0:T(8,128)(2,1)S(1)}, bf16[4,128,128]{2,1,0:T(8,128)(2,1)S(1)}, u32[]{:S(2)}, u32[]{:S(2)}) %collective-permute-start.19) | collective-permute-done | bytes 131104 | tf_op jit(solution)/shard_map/ppermute | solution.py:59
  155.3 2.1 %collective-permute-done.20 = f32[256,128]{1,0:T(8,128)S(1)} collective-permute-done((f32[256,128]{1,0:T(8,128)S(1)}, f32[256,128]{1,0:T(8,128)S(1)}, u32[]{:S(2)}, u32[]{:S(2)}) %collective-permute-start.20) | collective-permute-done | bytes 131104 | tf_op jit(solution)/shard_map/ppermute | solution.py:59
  (46 shorter events, 6.8 us)
Async XLA Ops:
  1.6 6.0 %collective-permute-start = (bf16[4,128,128]{2,1,0:T(8,128)(2,1)S(1)}, bf16[4,128,128]{2,1,0:T(8,128)(2,1)S(1)}, u32[]{:S(2)}, u32[]{:S(2)}) collective-permute-start(bf16[4,128,128]{2,1,0:T(8,128)(2,1)S(1)} %get-tuple-element.42), channel_id=1, source_target_pairs={{0,1},{1,0},{2,3},{3,2},{4,5},{5,4},{6,7},{7,6},{8,9},{9,8},{10,11... | collective-permute-start | bytes 393224 | tf_op jit(solution)/shard_map/ppermute | solution.py:59
  8.3 9.0 %collective-permute-start.2 = (bf16[1,128,256]{2,1,0:T(8,128)(2,1)S(1)}, bf16[1,128,256]{2,1,0:T(8,128)(2,1)S(1)}, u32[]{:S(2)}, u32[]{:S(2)}) collective-permute-start(bf16[1,128,256]{2,1,0:T(8,128)(2,1)S(1)} %get-tuple-element.23), channel_id=1, source_target_pairs={{0,2},{1,3},{2,0},{3,1},{4,6},{5,7},{6,4},{7,5},{8,10},{9,11},{10,... | collective-permute-start | bytes 196616 | tf_op jit(solution)/shard_map/ppermute | solution.py:50
  12.2 5.1 %collective-permute-start.3 = (bf16[1,128,256]{2,1,0:T(8,128)(2,1)S(1)}, bf16[1,128,256]{2,1,0:T(8,128)(2,1)S(1)}, u32[]{:S(2)}, u32[]{:S(2)}) collective-permute-start(bf16[1,128,256]{2,1,0:T(8,128)(2,1)S(1)} %get-tuple-element.25), channel_id=1, source_target_pairs={{0,30},{1,31},{2,4},{3,5},{4,2},{5,3},{6,8},{7,9},{8,6},{9,7},{10,... | collective-permute-start | bytes 196616 | tf_op jit(solution)/shard_map/ppermute | solution.py:50
  12.3 9.6 %collective-permute-start.5 = (bf16[3,128,256]{2,1,0:T(8,128)(2,1)S(1)}, bf16[3,128,256]{2,1,0:T(8,128)(2,1)S(1)}, u32[]{:S(2)}, u32[]{:S(2)}) collective-permute-start(bf16[3,128,256]{2,1,0:T(8,128)(2,1)S(1)} %get-tuple-element.22.mid), channel_id=1, source_target_pairs={{0,225},{1,224},{2,227},{3,226},{4,229},{5,228},{6,231},{7,230},{8... | collective-permute-start | bytes 589832 | tf_op jit(solution)/shard_map/ppermute | solution.py:50
  17.2 4.7 %collective-permute-start.1 = (bf16[3,128,256]{2,1,0:T(8,128)(2,1)S(1)}, bf16[3,128,256]{2,1,0:T(8,128)(2,1)S(1)}, u32[]{:S(2)}, u32[]{:S(2)}) collective-permute-start(bf16[3,128,256]{2,1,0:T(8,128)(2,1)S(1)} %get-tuple-element.22.mid), channel_id=1, source_target_pairs={{0,32},{1,33},{2,34},{3,35},{4,36},{5,37},{6,38},{7,39},{8,40},{9,... | collective-permute-start | bytes 589832 | tf_op jit(solution)/shard_map/ppermute | solution.py:50
  17.3 9.8 %collective-permute-start.6 = (bf16[3,128,256]{2,1,0:T(8,128)(2,1)S(1)}, bf16[3,128,256]{2,1,0:T(8,128)(2,1)S(1)}, u32[]{:S(2)}, u32[]{:S(2)}) collective-permute-start(bf16[3,128,256]{2,1,0:T(8,128)(2,1)S(1)} %pad_maximum_fusion.ends), channel_id=1, source_target_pairs={{0,225},{1,224},{2,227},{3,226},{4,229},{5,228},{6,231},{7,230},{8... | collective-permute-start | bytes 589832 | tf_op jit(solution)/shard_map/ppermute | solution.py:50
  19.4 7.7 %collective-permute-start.4 = (bf16[3,128,256]{2,1,0:T(8,128)(2,1)S(1)}, bf16[3,128,256]{2,1,0:T(8,128)(2,1)S(1)}, u32[]{:S(2)}, u32[]{:S(2)}) collective-permute-start(bf16[3,128,256]{2,1,0:T(8,128)(2,1)S(1)} %pad_maximum_fusion.ends), channel_id=1, source_target_pairs={{0,32},{1,33},{2,34},{3,35},{4,36},{5,37},{6,38},{7,39},{8,40},{9,... | collective-permute-start | bytes 589832 | tf_op jit(solution)/shard_map/ppermute | solution.py:50
  19.4 1.7 %copy-start = (bf16[2,1,4,9,128,128]{5,4,3,2,1,0:T(8,128)(2,1)S(1)}, bf16[2,1,4,9,128,128]{5,4,3,2,1,0:T(8,128)(2,1)}, u32[]{:S(2)}) copy-start(bf16[2,1,4,9,128,128]{5,4,3,2,1,0:T(8,128)(2,1)} %h.11) | copy-start | bytes 7077892
  21.1 6.0 %copy-start.1 = (bf16[2,1,4,9,128,128]{5,4,3,2,1,0:T(8,128)(2,1)S(1)}, bf16[2,1,4,9,128,128]{5,4,3,2,1,0:T(8,128)(2,1)}, u32[]{:S(2)}) copy-start(bf16[2,1,4,9,128,128]{5,4,3,2,1,0:T(8,128)(2,1)} %h.11) | copy-start | bytes 7077892
  28.1 5.8 %collective-permute-start.8 = (bf16[1,128,256]{2,1,0:T(8,128)(2,1)S(1)}, bf16[1,128,256]{2,1,0:T(8,128)(2,1)S(1)}, u32[]{:S(2)}, u32[]{:S(2)}) collective-permute-start(bf16[1,128,256]{2,1,0:T(8,128)(2,1)S(1)} %get-tuple-element.27), channel_id=1, source_target_pairs={{0,2},{1,3},{2,0},{3,1},{4,6},{5,7},{6,4},{7,5},{8,10},{9,11},{10,... | collective-permute-start | bytes 196616 | tf_op jit(solution)/shard_map/ppermute | solution.py:50
  32.1 4.0 %collective-permute-start.9 = (bf16[1,128,256]{2,1,0:T(8,128)(2,1)S(1)}, bf16[1,128,256]{2,1,0:T(8,128)(2,1)S(1)}, u32[]{:S(2)}, u32[]{:S(2)}) collective-permute-start(bf16[1,128,256]{2,1,0:T(8,128)(2,1)S(1)} %get-tuple-element.29), channel_id=1, source_target_pairs={{0,30},{1,31},{2,4},{3,5},{4,2},{5,3},{6,8},{7,9},{8,6},{9,7},{10,... | collective-permute-start | bytes 196616 | tf_op jit(solution)/shard_map/ppermute | solution.py:50
  32.1 7.8 %collective-permute-start.11 = (bf16[3,128,256]{2,1,0:T(8,128)(2,1)S(1)}, bf16[3,128,256]{2,1,0:T(8,128)(2,1)S(1)}, u32[]{:S(2)}, u32[]{:S(2)}) collective-permute-start(bf16[3,128,256]{2,1,0:T(8,128)(2,1)S(1)} %get-tuple-element.26.mid), channel_id=1, source_target_pairs={{0,225},{1,224},{2,227},{3,226},{4,229},{5,228},{6,231},{7,230},{8... | collective-permute-start | bytes 589832 | tf_op jit(solution)/shard_map/ppermute | solution.py:50
  33.9 6.1 %collective-permute-start.7 = (bf16[3,128,256]{2,1,0:T(8,128)(2,1)S(1)}, bf16[3,128,256]{2,1,0:T(8,128)(2,1)S(1)}, u32[]{:S(2)}, u32[]{:S(2)}) collective-permute-start(bf16[3,128,256]{2,1,0:T(8,128)(2,1)S(1)} %get-tuple-element.26.mid), channel_id=1, source_target_pairs={{0,32},{1,33},{2,34},{3,35},{4,36},{5,37},{6,38},{7,39},{8,40},{9,... | collective-permute-start | bytes 589832 | tf_op jit(solution)/shard_map/ppermute | solution.py:50
  36.2 9.9 %collective-permute-start.12 = (bf16[3,128,256]{2,1,0:T(8,128)(2,1)S(1)}, bf16[3,128,256]{2,1,0:T(8,128)(2,1)S(1)}, u32[]{:S(2)}, u32[]{:S(2)}) collective-permute-start(bf16[3,128,256]{2,1,0:T(8,128)(2,1)S(1)} %pad_maximum_fusion.1.ends), channel_id=1, source_target_pairs={{0,225},{1,224},{2,227},{3,226},{4,229},{5,228},{6,231},{7,230},{8... | collective-permute-start | bytes 589832 | tf_op jit(solution)/shard_map/ppermute | solution.py:50
  37.7 8.4 %collective-permute-start.10 = (bf16[3,128,256]{2,1,0:T(8,128)(2,1)S(1)}, bf16[3,128,256]{2,1,0:T(8,128)(2,1)S(1)}, u32[]{:S(2)}, u32[]{:S(2)}) collective-permute-start(bf16[3,128,256]{2,1,0:T(8,128)(2,1)S(1)} %pad_maximum_fusion.1.ends), channel_id=1, source_target_pairs={{0,32},{1,33},{2,34},{3,35},{4,36},{5,37},{6,38},{7,39},{8,40},{9,... | collective-permute-start | bytes 589832 | tf_op jit(solution)/shard_map/ppermute | solution.py:50
  47.1 4.4 %collective-permute-start.13 = (bf16[1,128,256]{2,1,0:T(8,128)(2,1)S(1)}, bf16[1,128,256]{2,1,0:T(8,128)(2,1)S(1)}, u32[]{:S(2)}, u32[]{:S(2)}) collective-permute-start(bf16[1,128,256]{2,1,0:T(8,128)(2,1)S(1)} %get-tuple-element.31), channel_id=1, source_target_pairs={{0,2},{1,3},{2,0},{3,1},{4,6},{5,7},{6,4},{7,5},{8,10},{9,11},{10,... | collective-permute-start | bytes 196616 | tf_op jit(solution)/shard_map/ppermute | solution.py:50
  48.7 4.0 %collective-permute-start.14 = (bf16[1,128,256]{2,1,0:T(8,128)(2,1)S(1)}, bf16[1,128,256]{2,1,0:T(8,128)(2,1)S(1)}, u32[]{:S(2)}, u32[]{:S(2)}) collective-permute-start(bf16[1,128,256]{2,1,0:T(8,128)(2,1)S(1)} %get-tuple-element.32), channel_id=1, source_target_pairs={{0,30},{1,31},{2,4},{3,5},{4,2},{5,3},{6,8},{7,9},{8,6},{9,7},{10,... | collective-permute-start | bytes 196616 | tf_op jit(solution)/shard_map/ppermute | solution.py:50
  48.7 7.9 %collective-permute-start.15 = (bf16[3,128,256]{2,1,0:T(8,128)(2,1)S(1)}, bf16[3,128,256]{2,1,0:T(8,128)(2,1)S(1)}, u32[]{:S(2)}, u32[]{:S(2)}) collective-permute-start(bf16[3,128,256]{2,1,0:T(8,128)(2,1)S(1)} %get-tuple-element.33), channel_id=1, source_target_pairs={{0,225},{1,224},{2,227},{3,226},{4,229},{5,228},{6,231},{7,230},{8... | collective-permute-start | bytes 589832 | tf_op jit(solution)/shard_map/ppermute | solution.py:54
  52.7 7.1 %collective-permute-start.16 = (bf16[3,128,256]{2,1,0:T(8,128)(2,1)S(1)}, bf16[3,128,256]{2,1,0:T(8,128)(2,1)S(1)}, u32[]{:S(2)}, u32[]{:S(2)}) collective-permute-start(bf16[3,128,256]{2,1,0:T(8,128)(2,1)S(1)} %pad_maximum_fusion.2.ends), channel_id=1, source_target_pairs={{0,225},{1,224},{2,227},{3,226},{4,229},{5,228},{6,231},{7,230},{8... | collective-permute-start | bytes 589832 | tf_op jit(solution)/shard_map/ppermute | solution.py:54
  61.6 2.5 %collective-permute-start.17 = (f32[64,1,640]{2,1,0:T(1,128)S(1)}, f32[64,1,640]{2,1,0:T(1,128)S(1)}, u32[]{:S(2)}, u32[]{:S(2)}) collective-permute-start(f32[64,1,640]{2,1,0:T(1,128)S(1)} %get-tuple-element.37), channel_id=1, source_target_pairs={{0,2},{1,3},{2,0},{3,1},{4,6},{5,7},{6,4},{7,5},{8,10},{9,11},{10,... | collective-permute-start | bytes 491528 | tf_op jit(solution)/shard_map/ppermute | solution.py:50
  104.9 3.7 %collective-permute-start.18 = (f32[64,1,640]{2,1,0:T(1,128)S(1)}, f32[64,1,640]{2,1,0:T(1,128)S(1)}, u32[]{:S(2)}, u32[]{:S(2)}) collective-permute-start(f32[64,1,640]{2,1,0:T(1,128)S(1)} %all_to_all.11.mine), channel_id=1, source_target_pairs={{0,2},{1,3},{2,0},{3,1},{4,6},{5,7},{6,4},{7,5},{8,10},{9,11},{10,... | collective-permute-start | bytes 491528 | tf_op jit(solution)/shard_map/ppermute | solution.py:50
  148.3 6.3 %collective-permute-start.19 = (bf16[4,128,128]{2,1,0:T(8,128)(2,1)S(1)}, bf16[4,128,128]{2,1,0:T(8,128)(2,1)S(1)}, u32[]{:S(2)}, u32[]{:S(2)}) collective-permute-start(bf16[4,128,128]{2,1,0:T(8,128)(2,1)S(1)} %get-tuple-element.39), channel_id=1, source_target_pairs={{0,1},{1,0},{2,3},{3,2},{4,5},{5,4},{6,7},{7,6},{8,9},{9,8},{10,11... | collective-permute-start | bytes 393224 | tf_op jit(solution)/shard_map/ppermute | solution.py:59
  148.4 9.0 %collective-permute-start.20 = (f32[256,128]{1,0:T(8,128)S(1)}, f32[256,128]{1,0:T(8,128)S(1)}, u32[]{:S(2)}, u32[]{:S(2)}) collective-permute-start(f32[256,128]{1,0:T(8,128)S(1)} %get-tuple-element.41), channel_id=1, source_target_pairs={{0,1},{1,0},{2,3},{3,2},{4,5},{5,4},{6,7},{7,6},{8,9},{9,8},{10,11... | collective-permute-start | bytes 393224 | tf_op jit(solution)/shard_map/ppermute | solution.py:59

commit v4 on v3

--- a/solution.py
+++ b/solution.py
@@ -86,72 +86,99 @@
     return dot(ah, bh, dims) + (dot(ah, bl, dims) + dot(al, bh, dims))
 
 
-def h_block(m, h, tile, side, dy):
-    slot = m[(tile * 3 + side) * 3 + dy]
-    block = h[0, 0, tile, jnp.maximum(slot, 0)]
-    return jnp.where(slot >= 0, block, jnp.zeros_like(block))
-
-
-def h_row(m, h, tile, side, dys):
-    return jnp.concatenate([h_block(m, h, tile, side, dy) for dy in dys], axis=1)
-
-
-def fill(m, ext, mid, ends):
-    even = m[PAR_Y] == 0
-    ext[1:2] = ends[1:2]
-    ext[2:5] = mid[...]
-    ext[pl.ds(jnp.where(even, 5, 0), 1)] = ends[0:1]
-    ext[pl.ds(jnp.where(even, 0, 5), 1)] = ends[2:3]
-
-
-def store_sides(m, ref, mid, p_ref, q_ref):
-    even = m[PAR_Y] == 0
-    p_ref[...] = ref[pl.ds(jnp.where(even, 3, 0), 1)]
-    q_ref[...] = ref[pl.ds(jnp.where(even, 0, 3), 1)]
-    mid[...] = ref[1:4]
-
-
-def join_kernel(m, own, other, v, mid, p, q):
+def order_kernel(m, h, o):
+    for tile in range(4):
+        for at in range(9):
+            slot = m[tile * 9 + at]
+            block = h[0, 0, tile, jnp.maximum(slot, 0)]
+            o[tile, :, at * T : (at + 1) * T] = jnp.where(slot >= 0, block, jnp.zeros_like(block))
+
+
+def blocks(o, tile, sides, dys):
+    out = []
+    for side in sides:
+        at = (side * 3 + dys[0]) * T
+        if not isinstance(side, int):
+            at = pl.multiple_of(at, T)
+        out.append(o[tile, :, pl.ds(at, len(dys) * T)])
+    return out[0] if len(out) == 1 else jnp.concatenate(out, axis=1)
+
+
+def join_kernel(m, own, other, v):
     first_col = m[COL] == 0
     v[:, :, :T] = jnp.where(first_col, own[...], other[...])
     v[:, :, T:] = jnp.where(first_col, other[...], own[...])
-    store_sides(m, v, mid, p, q)
-
-
-def own_kernel(m, h, mid, ends, acc, ext):
-    fill(m, ext, mid, ends)
-    for tile in range(4):
-        row = h_row(m, h, tile, 0, range(3))
-        acc[tile] = dot(row, ext[tile : tile + 3].reshape(3 * T, 2 * T))
-
-
-def side_kernel(m, h, a, a_ends, b, b_ends, acc, *rest, last):
-    if last:
-        v, out, mid, p, q, ext_a, ext_b = rest
-    else:
-        out, mid, p, q, ext_a, ext_b = rest
-    fill(m, ext_a, a, a_ends)
-    fill(m, ext_b, b, b_ends)
+
+
+def edges_kernel(m, *refs):
+    *sources, p, q = refs
+    even = m[PAR_Y] == 0
+    for at, x in enumerate(sources):
+        p[at : at + 1] = x[pl.ds(jnp.where(even, 3, 0), 1)]
+        q[at : at + 1] = x[pl.ds(jnp.where(even, 0, 3), 1)]
+
+
+def inside(o, tile, sides, sources):
+    dys = [dy for dy in range(3) if 0 <= tile + dy - 1 < 4]
+    at = tile + dys[0] - 1
+    rhs = [x[at : at + len(dys)].reshape(len(dys) * T, 2 * T) for x in sources]
+    return dot(blocks(o, tile, sides, dys), rhs[0] if len(rhs) == 1 else jnp.concatenate(rhs, axis=0))
+
+
+def ends(m, p, q):
+    even = m[PAR_Y] == 0
+    return jnp.where(even, q[...], p[...]), jnp.where(even, p[...], q[...])
+
+
+def outside(o, tile, sides, dy, tiles):
+    return dot(blocks(o, tile, sides, (dy,)), tiles.reshape(len(sides) * T, 2 * T))
+
+
+def core_kernel(m, o, x, a, b, acc):
+    for tile in range(4):
+        acc[tile] = inside(o, tile, range(3), (x, a, b))
+
+
+def rim_kernel(m, o, p, q, acc, *rest):
+    *before, out = rest
+    low, high = ends(m, p, q)
     for tile in range(4):
         total = acc[tile]
-        for side, ext in ((1, ext_a), (2, ext_b)):
-            row = h_row(m, h, tile, side, range(3))
-            total += dot(row, ext[tile : tile + 3].reshape(3 * T, 2 * T))
-        if last:
-            out[tile] = (total - v[tile].astype(F32)).astype(BF)
+        if tile == 0:
+            total += outside(o, tile, range(3), 0, low)
+        if tile == 3:
+            total += outside(o, tile, range(3), 2, high)
+        if before:
+            out[tile] = (total - before[0][tile].astype(F32)).astype(BF)
         else:
             out[tile] = (0.5 * total).astype(BF)
-    store_sides(m, out, mid, p, q)
-
-
-def inner_kernel(m, h, s, corr, acc):
+
+
+def corr_kernel(m, o, s, corr, acc):
     flat = s[...].reshape(4 * T, 2 * T)
     corr[...] = dot(flat, flat, ((0,), (0,)))
     for tile in range(4):
-        total = 0.5 * dot(h_block(m, h, tile, 0, 1), s[tile])
+        total = 0.5 * dot(blocks(o, tile, (0,), (1,)), s[tile])
         if tile < 3:
-            total += dot(h_block(m, h, tile, 0, 2), s[tile + 1])
+            total += dot(blocks(o, tile, (0,), (2,)), s[tile + 1])
         acc[tile] = total
+
+
+def coupled(s_tile, total):
+    high, low = split(total)
+    return dot(s_tile, high, ((0,), (0,))) + dot(s_tile, low, ((0,), (0,)))
+
+
+def right_kernel(m, o, s, right, acc, out, half):
+    side = 1 + m[PAR_X]
+    total = jnp.zeros((2 * T, 2 * T), F32)
+    for tile in range(4):
+        part = acc[tile] + inside(o, tile, (side,), (right,))
+        if tile in (1, 2):
+            total += coupled(s[tile], part)
+        else:
+            out[tile // 3] = part
+    half[...] = total
 
 
 def places():
@@ -159,19 +186,12 @@
     return lax.broadcasted_iota(jnp.int32, shape, 0), lax.broadcasted_iota(jnp.int32, shape, 1)
 
 
-def gram_kernel(m, h, s, ends, right, right_ends, acc, corr, mine, theirs, ext):
-    fill(m, ext, right, right_ends)
-    above = jnp.where(m[PAR_Y] == 0, ends[0], ends[2])
+def gram_kernel(m, o, s, p, q, acc, partial, corr, mine, theirs):
     side = 1 + m[PAR_X]
-    half = jnp.zeros((2 * T, 2 * T), F32)
-    for tile in range(4):
-        total = acc[tile]
-        if tile == 3:
-            total += dot(h_block(m, h, tile, 0, 2), above)
-        row = h_row(m, h, tile, side, range(3))
-        total += dot(row, ext[tile : tile + 3].reshape(3 * T, 2 * T))
-        high, low = split(total)
-        half += dot(s[tile], high, ((0,), (0,))) + dot(s[tile], low, ((0,), (0,)))
+    low, high = ends(m, p, q)
+    half = partial[...]
+    half += coupled(s[0], acc[0] + outside(o, 0, (side,), 0, low[1:2]))
+    half += coupled(s[3], acc[1] + outside(o, 3, (0, side), 2, high))
     coupling = half + half.T
     rows, cols = places()
     both = jnp.where(rows >= cols, corr[...], coupling)
@@ -267,25 +287,21 @@
     return pl.BlockSpec(shape, lambda i, m, n=len(shape): (0,) * n)
 
 
-def call(kernel, m, arrays, outs, scratch=(), with_h=None, flops=0, name=None):
-    specs = [whole(a.shape) for a in arrays]
-    if with_h is not None:
-        shape = (1,) + with_h.shape[1:]
-        specs.insert(0, pl.BlockSpec(shape, lambda i, m: (m[SPIN], 0, 0, 0, 0, 0)))
-        arrays = [with_h, *arrays]
-    moved = sum(a.size * a.dtype.itemsize for a in arrays) + sum(o.size * o.dtype.itemsize for o in outs)
+def call(kernel, m, arrays, outs, name, flops=0, specs=None, scratch=()):
+    arrays = list(arrays)
+    moved = sum(a.size * a.dtype.itemsize for a in [*arrays, *outs])
     return pl.pallas_call(
         kernel,
         out_shape=outs,
         grid_spec=pltpu.PrefetchScalarGridSpec(
             num_scalar_prefetch=1,
             grid=(1,),
-            in_specs=specs,
+            in_specs=specs or [whole(a.shape) for a in arrays],
             out_specs=[whole(o.shape) for o in outs],
             scratch_shapes=list(scratch),
         ),
         compiler_params=pltpu.CompilerParams(vmem_limit_bytes=32 * 1024 * 1024),
-        cost_estimate=pl.CostEstimate(flops=flops, bytes_accessed=moved, transcendentals=0),
+        cost_estimate=pl.CostEstimate(flops=2 * T * T * 2 * T * flops, bytes_accessed=moved, transcendentals=0),
         name=name,
     )(m, *arrays)
 
@@ -313,49 +329,39 @@
 def per_device(start_block, hamiltonian, neighbour_index, block_count):
     sizes = tuple(lax.axis_size(a) for a in AXES)
     members = sizes[0] * sizes[1]
-    block, middle, tile, full = (4, T, 2 * T), (3, T, 2 * T), (1, T, 2 * T), (2 * T, 2 * T)
-    ext = pltpu.VMEM((6, T, 2 * T), BF)
+    block, full = (4, T, 2 * T), (2 * T, 2 * T)
     spin, col, m = table(neighbour_index, block_count)
 
     other = swap_col(sizes, lax.dynamic_index_in_dim(start_block, 1 - spin, 0, keepdims=False)[0])
     own = lax.dynamic_index_in_dim(start_block, spin, 0, keepdims=False)[0]
-    parts = [shaped(block, BF), shaped(middle, BF), shaped(tile, BF), shaped(tile, BF)]
-    v, mid, p, q = call(join_kernel, m, [own, other], parts, name="join")
-
-    def along_y(x, p, q):
-        p, q = swap(sizes, p, 0, 1), swap(sizes, q, 0, 2)
-        return jnp.concatenate([p, x[:1], q], axis=0)
-
-    def apply_ham(x, mid, p, q, before):
-        ends = along_y(x, p, q)
-        a, b = swap(sizes, mid, 1, 0), swap(sizes, mid, 2, 0)
-        a_ends, b_ends = swap(sizes, ends, 1, 0), swap(sizes, ends, 2, 0)
-        (acc,) = call(
-            own_kernel, m, [mid, ends], [shaped(block, F32)], [ext], hamiltonian,
-            2 * 12 * T * T * 2 * T, "own",
-        )
-        last = before is not None
-        arrays = [a, a_ends, b, b_ends, acc] + ([before] if last else [])
-        return call(
-            functools.partial(side_kernel, last=last), m, arrays, parts, [ext, ext], hamiltonian,
-            2 * 24 * T * T * 2 * T, "sides",
-        )
-
-    first, mid, p, q = apply_ham(v, mid, p, q, None)
-    second, mid, p, q = apply_ham(first, mid, p, q, v)
-
-    ends = along_y(second, p, q)
-    right = shift(sizes, mid, -1, 0)
-    right_ends = shift(sizes, ends, -1, 0)
-    corr, acc = call(
-        inner_kernel, m, [second], [shaped(full, F32), shaped(block, F32)], (), hamiltonian,
-        2 * 15 * T * T * 2 * T, "inner",
+    spin_block = pl.BlockSpec((1,) + hamiltonian.shape[1:], lambda i, m: (m[SPIN], 0, 0, 0, 0, 0))
+    (o,) = call(order_kernel, m, [hamiltonian], [shaped((4, T, NB * T), BF)], "order", specs=[spin_block])
+    (v,) = call(join_kernel, m, [own, other], [shaped(block, BF)], "join")
+
+    def along_y(*sources):
+        edge = shaped((len(sources), T, 2 * T), BF)
+        p, q = call(edges_kernel, m, sources, [edge, edge], "edges")
+        return swap(sizes, p, 0, 1), swap(sizes, q, 0, 2)
+
+    def apply_ham(o, x, before):
+        a, b = swap(sizes, x, 1, 0), swap(sizes, x, 2, 0)
+        o, a, b = lax.optimization_barrier((o, a, b))
+        p, q = along_y(x, a, b)
+        (acc,) = call(core_kernel, m, [o, x, a, b], [shaped(block, F32)], "core", 30)
+        (out,) = call(rim_kernel, m, [o, p, q, acc, *before], [shaped(block, BF)], "rim", 6)
+        return o, out
+
+    o, first = apply_ham(o, v, [])
+    o, second = apply_ham(o, first, [v])
+
+    right = shift(sizes, second, -1, 0)
+    corr, acc = call(corr_kernel, m, [o, second], [shaped(full, F32), shaped(block, F32)], "corr", 15)
+    p, q = along_y(second, right)
+    acc, half = call(
+        right_kernel, m, [o, second, right, acc], [shaped((2, T, 2 * T), F32), shaped(full, F32)], "right", 18
     )
     piece = shaped((members // 2, 1, 5 * T), F32)
-    mine, theirs = call(
-        gram_kernel, m, [second, ends, right, right_ends, acc, corr],
-        [piece, piece], [ext], hamiltonian, 2 * 21 * T * T * 2 * T, "gram",
-    )
+    mine, theirs = call(gram_kernel, m, [o, second, p, q, acc, half, corr], [piece, piece], "gram", 11)
 
     rows = members * second.shape[0] * second.shape[1]
     partial = mine + swap(sizes, theirs, 0, 1)
@@ -366,8 +372,8 @@
     half = (4, T, T)
     keep, send, p_keep, p_send = call(
         final_kernel, m, [mine, theirs, second],
-        [shaped(half, BF), shaped(half, BF), shaped((2 * T, T), F32), shaped((2 * T, T), F32)],
-        [pltpu.VMEM(full, F32), pltpu.VMEM(full, F32)], None, 0, "final",
+        [shaped(half, BF), shaped(half, BF), shaped((2 * T, T), F32), shaped((2 * T, T), F32)], "final", 80,
+        scratch=[pltpu.VMEM(full, F32), pltpu.VMEM(full, F32)],
     )
     got, p_got = swap_col(sizes, send), swap_col(sizes, p_send)
     ritz = jnp.where(spin == 0, jnp.stack([keep, got]), jnp.stack([got, keep]))

time: 158 us -> 165 us (1.044)
  starting transfers between devices: 36.7 us -> 40.2 us
  Pallas kernels: 46.8 us -> 50 us
    ppermute x16 -> x12, starting transfers between devices: 24.2 us -> 29.2 us  [swap(): return lax.ppermute(block, AXES, perm)]
    pallas_call x8 -> x13, Pallas kernels: 46.8 us -> 50 us  [call(): pl.pallas_call(kernel, out_shape=outs, grid_spec=pltpu.PrefetchScalarGrid...]
    ppermute x2 -> x1, starting transfers between devices: 5.81 us -> 4.34 us  [shift(): lax.ppermute(block, AXES, pairs(sizes, lambda gx, gy: (gx + dx, gy + dy)))]
    ppermute x2 -> x1, waiting for transfers between devices: 3.15 us -> 3.57 us  [shift(): lax.ppermute(block, AXES, pairs(sizes, lambda gx, gy: (gx + dx, gy + dy)))]
    ppermute x16 -> x12, waiting for transfers between devices: 18.1 us -> 17.8 us  [swap(): return lax.ppermute(block, AXES, perm)]
  transfers between devices with their start and end apart: 21 -> 16, of which waited for: 11 -> 13; matrix products, arithmetic and copies ran while one was open for 2% -> 2% of each run, Pallas kernels for 2% -> 3%
where the time goes in v4:
time: 165 us; the launch traced here: 164 us
  Pallas kernels  50 us (30%)
  starting transfers between devices  40.2 us (24%)
  blocking collectives  39.7 us (24%)
  waiting for transfers between devices  26.9 us (16%)
  other arithmetic  3.64 us (2%)
  local copies, waits for them, and re-layouts  3.03 us (2%)
    pallas_call x13, Pallas kernels, call(): pl.pallas_call(kernel, out_shape=outs, grid_spec=pltpu.PrefetchScalarGrid...  50 us
    all_to_all x2, blocking collectives, exchange(): lax.all_to_all(pieces, AXES, 0, 0, axis_index_groups=groups, tiled=True)  39.7 us
    ppermute x12, starting transfers between devices, swap(): return lax.ppermute(block, AXES, perm)  29.2 us
    ppermute x12, waiting for transfers between devices, swap(): return lax.ppermute(block, AXES, perm)  17.8 us
    ppermute x3, starting transfers between devices, swap_col(): return lax.ppermute(block, AXES, perm)  6.71 us
    ppermute x3, waiting for transfers between devices, swap_col(): return lax.ppermute(block, AXES, perm)  5.49 us
    ppermute x1, starting transfers between devices, shift(): lax.ppermute(block, AXES, pairs(sizes, lambda gx, gy: (gx + dx, gy + dy)))  4.34 us
    ppermute x1, waiting for transfers between devices, shift(): lax.ppermute(block, AXES, pairs(sizes, lambda gx, gy: (gx + dx, gy + dy)))  3.57 us
  transfers between devices with their start and end apart: 16, of which 13 were waited for; matrix products, arithmetic and copies ran while one was open for 2% of the time, Pallas kernels for 3%

profile of v4, /device:TPU:1, one launch (start us, length us, event | category | flops | bytes accessed | tf_op | source)
XLA Modules:
  0.0 164.4 jit_solution(4395758070728797447)
XLA Ops:
  0.6 1.0 dynamic-slice_bitcast_fusion
  1.6 3.7 %collective-permute-start = (bf16[4,128,128]{2,1,0:T(8,128)(2,1)S(1)}, bf16[4,128,128]{2,1,0:T(8,128)(2,1)S(1)}, u32[]{:S(2)}, u32[]{:S(2)}) collective-permute-start(bf16[4,128,128]{2,1,0:T(8,128)(2,1)S(1)} %get-tuple-element.46), channel_id=1, source_target_pairs={{0,1},{1,0},{2,3},{3,2},{4,5},{5,4},{6,7},{7,6},{8,9},{9,8},{10,11... | collective-permute-start | bytes 393224 | tf_op jit(solution)/shard_map/ppermute | solution.py:59
  6.2 1.0 select_reduce_fusion
  8.3 2.1 %collective-permute-start.1 = (bf16[4,128,256]{2,1,0:T(8,128)(2,1)S(1)}, bf16[4,128,256]{2,1,0:T(8,128)(2,1)S(1)}, u32[]{:S(2)}, u32[]{:S(2)}) collective-permute-start(bf16[4,128,256]{2,1,0:T(8,128)(2,1)S(1)} %join.1.refs_0_.x.rest_0_), channel_id=1, source_target_pairs={{0,32},{1,33},{2,34},{3,35},{4,36},{5,37},{6,38},{7,39},{8,40},{9,... | collective-permute-start | bytes 786440 | tf_op jit(solution)/shard_map/ppermute | solution.py:50
  10.3 4.3 %collective-permute-start.2 = (bf16[4,128,256]{2,1,0:T(8,128)(2,1)S(1)}, bf16[4,128,256]{2,1,0:T(8,128)(2,1)S(1)}, u32[]{:S(2)}, u32[]{:S(2)}) collective-permute-start(bf16[4,128,256]{2,1,0:T(8,128)(2,1)S(1)} %join.1.refs_0_.x.rest_0_), channel_id=1, source_target_pairs={{0,225},{1,224},{2,227},{3,226},{4,229},{5,228},{6,231},{7,230},{8... | collective-permute-start | bytes 786440 | tf_op jit(solution)/shard_map/ppermute | solution.py:50
  14.6 1.7 %copy-done = bf16[2,1,4,9,128,128]{5,4,3,2,1,0:T(8,128)(2,1)S(1)} copy-done((bf16[2,1,4,9,128,128]{5,4,3,2,1,0:T(8,128)(2,1)S(1)}, bf16[2,1,4,9,128,128]{5,4,3,2,1,0:T(8,128)(2,1)}, u32[]{:S(2)}) %copy-start) | copy-done | bytes 2359320
  17.1 2.4 %collective-permute-done.2.refs_2_.b = bf16[4,128,256]{2,1,0:T(8,128)(2,1)S(1)} collective-permute-done((bf16[4,128,256]{2,1,0:T(8,128)(2,1)S(1)}, bf16[4,128,256]{2,1,0:T(8,128)(2,1)S(1)}, u32[]{:S(2)}, u32[]{:S(2)}) %collective-permute-start.2) | collective-permute-done | bytes 262176 | tf_op jit(solution)/shard_map/ppermute | solution.py:50
  20.1 2.9 %collective-permute-start.3 = (bf16[3,128,256]{2,1,0:T(8,128)(2,1)S(1)}, bf16[3,128,256]{2,1,0:T(8,128)(2,1)S(1)}, u32[]{:S(2)}, u32[]{:S(2)}) collective-permute-start(bf16[3,128,256]{2,1,0:T(8,128)(2,1)S(1)} %get-tuple-element.27), channel_id=1, source_target_pairs={{0,2},{1,3},{2,0},{3,1},{4,6},{5,7},{6,4},{7,5},{8,10},{9,11},{10,... | collective-permute-start | bytes 589832 | tf_op jit(solution)/shard_map/ppermute | solution.py:50
  23.0 1.6 collective-permute-start.4
  24.6 1.0 core.2.acc
  25.6 2.5 %collective-permute-done.4.q = bf16[3,128,256]{2,1,0:T(8,128)(2,1)S(1)} collective-permute-done((bf16[3,128,256]{2,1,0:T(8,128)(2,1)S(1)}, bf16[3,128,256]{2,1,0:T(8,128)(2,1)S(1)}, u32[]{:S(2)}, u32[]{:S(2)}) %collective-permute-start.4) | collective-permute-done | bytes 196640 | tf_op jit(solution)/shard_map/ppermute | solution.py:50
  29.0 4.4 %collective-permute-start.6 = (bf16[4,128,256]{2,1,0:T(8,128)(2,1)S(1)}, bf16[4,128,256]{2,1,0:T(8,128)(2,1)S(1)}, u32[]{:S(2)}, u32[]{:S(2)}) collective-permute-start(bf16[4,128,256]{2,1,0:T(8,128)(2,1)S(1)} %rim.2.refs_0_.x), channel_id=1, source_target_pairs={{0,225},{1,224},{2,227},{3,226},{4,229},{5,228},{6,231},{7,230},{8... | collective-permute-start | bytes 786440 | tf_op jit(solution)/shard_map/ppermute | solution.py:50
  34.2 3.4 %collective-permute-done.6.refs_2_.b = bf16[4,128,256]{2,1,0:T(8,128)(2,1)S(1)} collective-permute-done((bf16[4,128,256]{2,1,0:T(8,128)(2,1)S(1)}, bf16[4,128,256]{2,1,0:T(8,128)(2,1)S(1)}, u32[]{:S(2)}, u32[]{:S(2)}) %collective-permute-start.6) | collective-permute-done | bytes 262176 | tf_op jit(solution)/shard_map/ppermute | solution.py:50
  38.2 5.5 %collective-permute-start.7 = (bf16[3,128,256]{2,1,0:T(8,128)(2,1)S(1)}, bf16[3,128,256]{2,1,0:T(8,128)(2,1)S(1)}, u32[]{:S(2)}, u32[]{:S(2)}) collective-permute-start(bf16[3,128,256]{2,1,0:T(8,128)(2,1)S(1)} %get-tuple-element.32), channel_id=1, source_target_pairs={{0,2},{1,3},{2,0},{3,1},{4,6},{5,7},{6,4},{7,5},{8,10},{9,11},{10,... | collective-permute-start | bytes 589832 | tf_op jit(solution)/shard_map/ppermute | solution.py:50
  43.7 1.0 core.3.acc
  44.8 4.3 %collective-permute-done.8.q = bf16[3,128,256]{2,1,0:T(8,128)(2,1)S(1)} collective-permute-done((bf16[3,128,256]{2,1,0:T(8,128)(2,1)S(1)}, bf16[3,128,256]{2,1,0:T(8,128)(2,1)S(1)}, u32[]{:S(2)}, u32[]{:S(2)}) %collective-permute-start.8) | collective-permute-done | bytes 196640 | tf_op jit(solution)/shard_map/ppermute | solution.py:50
  49.9 4.3 %collective-permute-start.9 = (bf16[4,128,256]{2,1,0:T(8,128)(2,1)S(1)}, bf16[4,128,256]{2,1,0:T(8,128)(2,1)S(1)}, u32[]{:S(2)}, u32[]{:S(2)}) collective-permute-start(bf16[4,128,256]{2,1,0:T(8,128)(2,1)S(1)} %rim.3.refs_0_.s), channel_id=1, source_target_pairs={{0,225},{1,224},{2,227},{3,226},{4,229},{5,228},{6,231},{7,230},{8... | collective-permute-start | bytes 786440 | tf_op jit(solution)/shard_map/ppermute | solution.py:54
  54.2 3.6 %collective-permute-done.9.refs_1_.right = bf16[4,128,256]{2,1,0:T(8,128)(2,1)S(1)} collective-permute-done((bf16[4,128,256]{2,1,0:T(8,128)(2,1)S(1)}, bf16[4,128,256]{2,1,0:T(8,128)(2,1)S(1)}, u32[]{:S(2)}, u32[]{:S(2)}) %collective-permute-start.9) | collective-permute-done | bytes 262176 | tf_op jit(solution)/shard_map/ppermute | solution.py:54
  58.4 3.0 %collective-permute-start.10 = (bf16[2,128,256]{2,1,0:T(8,128)(2,1)S(1)}, bf16[2,128,256]{2,1,0:T(8,128)(2,1)S(1)}, u32[]{:S(2)}, u32[]{:S(2)}) collective-permute-start(bf16[2,128,256]{2,1,0:T(8,128)(2,1)S(1)} %get-tuple-element.34), channel_id=1, source_target_pairs={{0,2},{1,3},{2,0},{3,1},{4,6},{5,7},{6,4},{7,5},{8,10},{9,11},{10,... | collective-permute-start | bytes 393224 | tf_op jit(solution)/shard_map/ppermute | solution.py:50
  62.3 1.3 right.1
  63.6 2.2 %collective-permute-done.11.q = bf16[2,128,256]{2,1,0:T(8,128)(2,1)S(1)} collective-permute-done((bf16[2,128,256]{2,1,0:T(8,128)(2,1)S(1)}, bf16[2,128,256]{2,1,0:T(8,128)(2,1)S(1)}, u32[]{:S(2)}, u32[]{:S(2)}) %collective-permute-start.11) | collective-permute-done | bytes 131104 | tf_op jit(solution)/shard_map/ppermute | solution.py:50
  65.8 1.4 gram.1
  67.2 2.7 %collective-permute-start.12 = (f32[64,1,640]{2,1,0:T(1,128)S(1)}, f32[64,1,640]{2,1,0:T(1,128)S(1)}, u32[]{:S(2)}, u32[]{:S(2)}) collective-permute-start(f32[64,1,640]{2,1,0:T(1,128)S(1)} %get-tuple-element.41), channel_id=1, source_target_pairs={{0,2},{1,3},{2,0},{3,1},{4,6},{5,7},{6,4},{7,5},{8,10},{9,11},{10,... | collective-permute-start | bytes 491528 | tf_op jit(solution)/shard_map/ppermute | solution.py:50
  69.9 1.0 collective-permute-done.12
  71.1 23.0 %all_to_all.10 = f32[64,1,640]{2,1,0:T(1,128)S(1)} all-to-all(f32[64,1,640]{2,1,0:T(1,128)S(1)} %add.59), channel_id=1, replica_groups={{0,4,8,12,16,20,24,28,32,36,40,44,48,52,56,60,65,69,73,77,81,85,89,93,9..., dimensions={0} | all-to-all | bytes 327680 | tf_op jit(solution)/shard_map/all_to_all | solution.py:72
  94.3 16.8 %all_to_all.11.mine = f32[64,1,640]{2,1,0:T(1,128)S(1)} all-to-all(f32[64,1,640]{2,1,0:T(1,128)S(1)} %broadcast_in_dim.12), channel_id=1, replica_groups={{0,4,8,12,16,20,24,28,32,36,40,44,48,52,56,60,65,69,73,77,81,85,89,93,9..., dimensions={0} | all-to-all | bytes 327680 | tf_op jit(solution)/shard_map/all_to_all | solution.py:72
  111.1 2.7 %collective-permute-start.13 = (f32[64,1,640]{2,1,0:T(1,128)S(1)}, f32[64,1,640]{2,1,0:T(1,128)S(1)}, u32[]{:S(2)}, u32[]{:S(2)}) collective-permute-start(f32[64,1,640]{2,1,0:T(1,128)S(1)} %all_to_all.11.mine), channel_id=1, source_target_pairs={{0,2},{1,3},{2,0},{3,1},{4,6},{5,7},{6,4},{7,5},{8,10},{9,11},{10,... | collective-permute-start | bytes 491528 | tf_op jit(solution)/shard_map/ppermute | solution.py:50
  113.8 1.0 collective-permute-done.13.theirs
  114.8 39.7 %final.1 = (bf16[4,128,128]{2,1,0:T(8,128)(2,1)S(1)}, bf16[4,128,128]{2,1,0:T(8,128)(2,1)S(1)}, f32[256,128]{1,0:T(8,128)S(1)}, f32[256,128]{1,0:T(8,128)S(1)}) custom-call(s32[40]{0:T(128)S(1)} %concatenate.21.m, f32[64,1,640]{2,1,0:T(1,128)S(1)} %all_to_all.11.mine, f32[64,1,640]{2,1,0:T(1,128)S(1)} %collective-permute-done.13.theirs, ...), custom_call_target="tpu_custom_call" | custom-call | flops 671088640 | bytes 1114112 | tf_op jit(solution)/shard_map/final/pallas_call | solution.py:293
  154.6 3.0 %collective-permute-start.14 = (bf16[4,128,128]{2,1,0:T(8,128)(2,1)S(1)}, bf16[4,128,128]{2,1,0:T(8,128)(2,1)S(1)}, u32[]{:S(2)}, u32[]{:S(2)}) collective-permute-start(bf16[4,128,128]{2,1,0:T(8,128)(2,1)S(1)} %get-tuple-element.43), channel_id=1, source_target_pairs={{0,1},{1,0},{2,3},{3,2},{4,5},{5,4},{6,7},{7,6},{8,9},{9,8},{10,11... | collective-permute-start | bytes 393224 | tf_op jit(solution)/shard_map/ppermute | solution.py:59
  157.6 3.2 %collective-permute-done.15 = f32[256,128]{1,0:T(8,128)S(1)} collective-permute-done((f32[256,128]{1,0:T(8,128)S(1)}, f32[256,128]{1,0:T(8,128)S(1)}, u32[]{:S(2)}, u32[]{:S(2)}) %collective-permute-start.15) | collective-permute-done | bytes 131104 | tf_op jit(solution)/shard_map/ppermute | solution.py:59
  161.6 2.1 %collective-permute-done.14 = bf16[4,128,128]{2,1,0:T(8,128)(2,1)S(1)} collective-permute-done((bf16[4,128,128]{2,1,0:T(8,128)(2,1)S(1)}, bf16[4,128,128]{2,1,0:T(8,128)(2,1)S(1)}, u32[]{:S(2)}, u32[]{:S(2)}) %collective-permute-start.14) | collective-permute-done | bytes 131104 | tf_op jit(solution)/shard_map/ppermute | solution.py:59
  (33 shorter events, 9.9 us)
Async XLA Ops:
  1.6 6.0 %collective-permute-start = (bf16[4,128,128]{2,1,0:T(8,128)(2,1)S(1)}, bf16[4,128,128]{2,1,0:T(8,128)(2,1)S(1)}, u32[]{:S(2)}, u32[]{:S(2)}) collective-permute-start(bf16[4,128,128]{2,1,0:T(8,128)(2,1)S(1)} %get-tuple-element.46), channel_id=1, source_target_pairs={{0,1},{1,0},{2,3},{3,2},{4,5},{5,4},{6,7},{7,6},{8,9},{9,8},{10,11... | collective-permute-start | bytes 393224 | tf_op jit(solution)/shard_map/ppermute | solution.py:59
  8.3 8.8 %collective-permute-start.1 = (bf16[4,128,256]{2,1,0:T(8,128)(2,1)S(1)}, bf16[4,128,256]{2,1,0:T(8,128)(2,1)S(1)}, u32[]{:S(2)}, u32[]{:S(2)}) collective-permute-start(bf16[4,128,256]{2,1,0:T(8,128)(2,1)S(1)} %join.1.refs_0_.x.rest_0_), channel_id=1, source_target_pairs={{0,32},{1,33},{2,34},{3,35},{4,36},{5,37},{6,38},{7,39},{8,40},{9,... | collective-permute-start | bytes 786440 | tf_op jit(solution)/shard_map/ppermute | solution.py:50
  10.3 9.2 %collective-permute-start.2 = (bf16[4,128,256]{2,1,0:T(8,128)(2,1)S(1)}, bf16[4,128,256]{2,1,0:T(8,128)(2,1)S(1)}, u32[]{:S(2)}, u32[]{:S(2)}) collective-permute-start(bf16[4,128,256]{2,1,0:T(8,128)(2,1)S(1)} %join.1.refs_0_.x.rest_0_), channel_id=1, source_target_pairs={{0,225},{1,224},{2,227},{3,226},{4,229},{5,228},{6,231},{7,230},{8... | collective-permute-start | bytes 786440 | tf_op jit(solution)/shard_map/ppermute | solution.py:50
  14.6 1.7 %copy-start = (bf16[2,1,4,9,128,128]{5,4,3,2,1,0:T(8,128)(2,1)S(1)}, bf16[2,1,4,9,128,128]{5,4,3,2,1,0:T(8,128)(2,1)}, u32[]{:S(2)}) copy-start(bf16[2,1,4,9,128,128]{5,4,3,2,1,0:T(8,128)(2,1)} %h.1) | copy-start | bytes 7077892
  20.1 5.5 %collective-permute-start.3 = (bf16[3,128,256]{2,1,0:T(8,128)(2,1)S(1)}, bf16[3,128,256]{2,1,0:T(8,128)(2,1)S(1)}, u32[]{:S(2)}, u32[]{:S(2)}) collective-permute-start(bf16[3,128,256]{2,1,0:T(8,128)(2,1)S(1)} %get-tuple-element.27), channel_id=1, source_target_pairs={{0,2},{1,3},{2,0},{3,1},{4,6},{5,7},{6,4},{7,5},{8,10},{9,11},{10,... | collective-permute-start | bytes 589832 | tf_op jit(solution)/shard_map/ppermute | solution.py:50
  23.0 5.1 %collective-permute-start.4 = (bf16[3,128,256]{2,1,0:T(8,128)(2,1)S(1)}, bf16[3,128,256]{2,1,0:T(8,128)(2,1)S(1)}, u32[]{:S(2)}, u32[]{:S(2)}) collective-permute-start(bf16[3,128,256]{2,1,0:T(8,128)(2,1)S(1)} %get-tuple-element.28), channel_id=1, source_target_pairs={{0,30},{1,31},{2,4},{3,5},{4,2},{5,3},{6,8},{7,9},{8,6},{9,7},{10,... | collective-permute-start | bytes 589832 | tf_op jit(solution)/shard_map/ppermute | solution.py:50
  28.9 5.3 %collective-permute-start.5 = (bf16[4,128,256]{2,1,0:T(8,128)(2,1)S(1)}, bf16[4,128,256]{2,1,0:T(8,128)(2,1)S(1)}, u32[]{:S(2)}, u32[]{:S(2)}) collective-permute-start(bf16[4,128,256]{2,1,0:T(8,128)(2,1)S(1)} %rim.2.refs_0_.x), channel_id=1, source_target_pairs={{0,32},{1,33},{2,34},{3,35},{4,36},{5,37},{6,38},{7,39},{8,40},{9,... | collective-permute-start | bytes 786440 | tf_op jit(solution)/shard_map/ppermute | solution.py:50
  29.0 8.6 %collective-permute-start.6 = (bf16[4,128,256]{2,1,0:T(8,128)(2,1)S(1)}, bf16[4,128,256]{2,1,0:T(8,128)(2,1)S(1)}, u32[]{:S(2)}, u32[]{:S(2)}) collective-permute-start(bf16[4,128,256]{2,1,0:T(8,128)(2,1)S(1)} %rim.2.refs_0_.x), channel_id=1, source_target_pairs={{0,225},{1,224},{2,227},{3,226},{4,229},{5,228},{6,231},{7,230},{8... | collective-permute-start | bytes 786440 | tf_op jit(solution)/shard_map/ppermute | solution.py:50
  38.2 6.5 %collective-permute-start.7 = (bf16[3,128,256]{2,1,0:T(8,128)(2,1)S(1)}, bf16[3,128,256]{2,1,0:T(8,128)(2,1)S(1)}, u32[]{:S(2)}, u32[]{:S(2)}) collective-permute-start(bf16[3,128,256]{2,1,0:T(8,128)(2,1)S(1)} %get-tuple-element.32), channel_id=1, source_target_pairs={{0,2},{1,3},{2,0},{3,1},{4,6},{5,7},{6,4},{7,5},{8,10},{9,11},{10,... | collective-permute-start | bytes 589832 | tf_op jit(solution)/shard_map/ppermute | solution.py:50
  43.7 5.4 %collective-permute-start.8 = (bf16[3,128,256]{2,1,0:T(8,128)(2,1)S(1)}, bf16[3,128,256]{2,1,0:T(8,128)(2,1)S(1)}, u32[]{:S(2)}, u32[]{:S(2)}) collective-permute-start(bf16[3,128,256]{2,1,0:T(8,128)(2,1)S(1)} %get-tuple-element.33), channel_id=1, source_target_pairs={{0,30},{1,31},{2,4},{3,5},{4,2},{5,3},{6,8},{7,9},{8,6},{9,7},{10,... | collective-permute-start | bytes 589832 | tf_op jit(solution)/shard_map/ppermute | solution.py:50
  49.9 7.9 %collective-permute-start.9 = (bf16[4,128,256]{2,1,0:T(8,128)(2,1)S(1)}, bf16[4,128,256]{2,1,0:T(8,128)(2,1)S(1)}, u32[]{:S(2)}, u32[]{:S(2)}) collective-permute-start(bf16[4,128,256]{2,1,0:T(8,128)(2,1)S(1)} %rim.3.refs_0_.s), channel_id=1, source_target_pairs={{0,225},{1,224},{2,227},{3,226},{4,229},{5,228},{6,231},{7,230},{8... | collective-permute-start | bytes 786440 | tf_op jit(solution)/shard_map/ppermute | solution.py:54
  58.4 5.2 %collective-permute-start.10 = (bf16[2,128,256]{2,1,0:T(8,128)(2,1)S(1)}, bf16[2,128,256]{2,1,0:T(8,128)(2,1)S(1)}, u32[]{:S(2)}, u32[]{:S(2)}) collective-permute-start(bf16[2,128,256]{2,1,0:T(8,128)(2,1)S(1)} %get-tuple-element.34), channel_id=1, source_target_pairs={{0,2},{1,3},{2,0},{3,1},{4,6},{5,7},{6,4},{7,5},{8,10},{9,11},{10,... | collective-permute-start | bytes 393224 | tf_op jit(solution)/shard_map/ppermute | solution.py:50
  61.4 4.4 %collective-permute-start.11 = (bf16[2,128,256]{2,1,0:T(8,128)(2,1)S(1)}, bf16[2,128,256]{2,1,0:T(8,128)(2,1)S(1)}, u32[]{:S(2)}, u32[]{:S(2)}) collective-permute-start(bf16[2,128,256]{2,1,0:T(8,128)(2,1)S(1)} %get-tuple-element.35), channel_id=1, source_target_pairs={{0,30},{1,31},{2,4},{3,5},{4,2},{5,3},{6,8},{7,9},{8,6},{9,7},{10,... | collective-permute-start | bytes 393224 | tf_op jit(solution)/shard_map/ppermute | solution.py:50
  67.2 3.7 %collective-permute-start.12 = (f32[64,1,640]{2,1,0:T(1,128)S(1)}, f32[64,1,640]{2,1,0:T(1,128)S(1)}, u32[]{:S(2)}, u32[]{:S(2)}) collective-permute-start(f32[64,1,640]{2,1,0:T(1,128)S(1)} %get-tuple-element.41), channel_id=1, source_target_pairs={{0,2},{1,3},{2,0},{3,1},{4,6},{5,7},{6,4},{7,5},{8,10},{9,11},{10,... | collective-permute-start | bytes 491528 | tf_op jit(solution)/shard_map/ppermute | solution.py:50
  111.1 3.7 %collective-permute-start.13 = (f32[64,1,640]{2,1,0:T(1,128)S(1)}, f32[64,1,640]{2,1,0:T(1,128)S(1)}, u32[]{:S(2)}, u32[]{:S(2)}) collective-permute-start(f32[64,1,640]{2,1,0:T(1,128)S(1)} %all_to_all.11.mine), channel_id=1, source_target_pairs={{0,2},{1,3},{2,0},{3,1},{4,6},{5,7},{6,4},{7,5},{8,10},{9,11},{10,... | collective-permute-start | bytes 491528 | tf_op jit(solution)/shard_map/ppermute | solution.py:50
  154.5 6.3 %collective-permute-start.15 = (f32[256,128]{1,0:T(8,128)S(1)}, f32[256,128]{1,0:T(8,128)S(1)}, u32[]{:S(2)}, u32[]{:S(2)}) collective-permute-start(f32[256,128]{1,0:T(8,128)S(1)} %get-tuple-element.45), channel_id=1, source_target_pairs={{0,1},{1,0},{2,3},{3,2},{4,5},{5,4},{6,7},{7,6},{8,9},{9,8},{10,11... | collective-permute-start | bytes 393224 | tf_op jit(solution)/shard_map/ppermute | solution.py:59
  154.6 9.0 %collective-permute-start.14 = (bf16[4,128,128]{2,1,0:T(8,128)(2,1)S(1)}, bf16[4,128,128]{2,1,0:T(8,128)(2,1)S(1)}, u32[]{:S(2)}, u32[]{:S(2)}) collective-permute-start(bf16[4,128,128]{2,1,0:T(8,128)(2,1)S(1)} %get-tuple-element.43), channel_id=1, source_target_pairs={{0,1},{1,0},{2,3},{3,2},{4,5},{5,4},{6,7},{7,6},{8,9},{9,8},{10,11... | collective-permute-start | bytes 393224 | tf_op jit(solution)/shard_map/ppermute | solution.py:59

commit v5 on v4

--- a/solution.py
+++ b/solution.py
@@ -104,54 +104,69 @@
     return out[0] if len(out) == 1 else jnp.concatenate(out, axis=1)
 
 
-def join_kernel(m, own, other, v):
+def store_parts(m, ref, mid, p, q):
+    even = m[PAR_Y] == 0
+    p[...] = ref[pl.ds(jnp.where(even, 3, 0), 1)]
+    q[...] = ref[pl.ds(jnp.where(even, 0, 3), 1)]
+    mid[...] = ref[1:4]
+
+
+def join_kernel(m, own, other, v, mid, p, q):
     first_col = m[COL] == 0
     v[:, :, :T] = jnp.where(first_col, own[...], other[...])
     v[:, :, T:] = jnp.where(first_col, other[...], own[...])
-
-
-def edges_kernel(m, *refs):
-    *sources, p, q = refs
+    store_parts(m, v, mid, p, q)
+
+
+def fill(m, ext, mid, ends):
     even = m[PAR_Y] == 0
-    for at, x in enumerate(sources):
-        p[at : at + 1] = x[pl.ds(jnp.where(even, 3, 0), 1)]
-        q[at : at + 1] = x[pl.ds(jnp.where(even, 0, 3), 1)]
-
-
-def inside(o, tile, sides, sources):
-    dys = [dy for dy in range(3) if 0 <= tile + dy - 1 < 4]
-    at = tile + dys[0] - 1
-    rhs = [x[at : at + len(dys)].reshape(len(dys) * T, 2 * T) for x in sources]
-    return dot(blocks(o, tile, sides, dys), rhs[0] if len(rhs) == 1 else jnp.concatenate(rhs, axis=0))
-
-
-def ends(m, p, q):
+    ext[1:2] = ends[1:2]
+    ext[2:5] = mid[...]
+    ext[pl.ds(jnp.where(even, 5, 0), 1)] = ends[0:1]
+    ext[pl.ds(jnp.where(even, 0, 5), 1)] = ends[2:3]
+
+
+def product(o, tile, sides, at, sources):
+    row = blocks(o, tile, sides, [place - tile for place in at])
+    return dot(row, jnp.concatenate([x.reshape(len(at) * T, 2 * T) for x in sources], axis=0))
+
+
+def core_kernel(m, o, mid, ends, a, b, acc, ext):
+    fill(m, ext, mid, ends)
+    for tile in range(4):
+        total = product(o, tile, (0,), range(tile, tile + 3), [ext[tile : tile + 3]])
+        at = [place for place in range(tile, tile + 3) if 2 <= place <= 4]
+        sources = [x[at[0] - 2 : at[-1] - 1] for x in (a, b)]
+        acc[tile] = total + product(o, tile, (1, 2), at, sources)
+
+
+def rim_kernel(m, o, a_ends, b_ends, acc, *rest, last):
+    if last:
+        before, out, first_out, last_out = rest
+    else:
+        out, mid, p, q = rest
     even = m[PAR_Y] == 0
-    return jnp.where(even, q[...], p[...]), jnp.where(even, p[...], q[...])
-
-
-def outside(o, tile, sides, dy, tiles):
-    return dot(blocks(o, tile, sides, (dy,)), tiles.reshape(len(sides) * T, 2 * T))
-
-
-def core_kernel(m, o, x, a, b, acc):
-    for tile in range(4):
-        acc[tile] = inside(o, tile, range(3), (x, a, b))
-
-
-def rim_kernel(m, o, p, q, acc, *rest):
-    *before, out = rest
-    low, high = ends(m, p, q)
+    low = [jnp.where(even, x[2:3], x[0:1]) for x in (a_ends, b_ends)]
+    first = [x[1:2] for x in (a_ends, b_ends)]
+    high = [jnp.where(even, x[0:1], x[2:3]) for x in (a_ends, b_ends)]
     for tile in range(4):
         total = acc[tile]
         if tile == 0:
-            total += outside(o, tile, range(3), 0, low)
+            pair = [jnp.concatenate([x, y], axis=0) for x, y in zip(low, first)]
+            total += product(o, tile, (1, 2), (0, 1), pair)
+        if tile == 1:
+            total += product(o, tile, (1, 2), (1,), first)
         if tile == 3:
-            total += outside(o, tile, range(3), 2, high)
-        if before:
-            out[tile] = (total - before[0][tile].astype(F32)).astype(BF)
+            total += product(o, tile, (1, 2), (5,), high)
+        if last:
+            out[tile] = (total - before[tile].astype(F32)).astype(BF)
         else:
             out[tile] = (0.5 * total).astype(BF)
+    if last:
+        first_out[...] = out[0:1]
+        last_out[...] = out[3:4]
+    else:
+        store_parts(m, out, mid, p, q)
 
 
 def corr_kernel(m, o, s, corr, acc):
@@ -169,29 +184,22 @@
     return dot(s_tile, high, ((0,), (0,))) + dot(s_tile, low, ((0,), (0,)))
 
 
-def right_kernel(m, o, s, right, acc, out, half):
-    side = 1 + m[PAR_X]
-    total = jnp.zeros((2 * T, 2 * T), F32)
-    for tile in range(4):
-        part = acc[tile] + inside(o, tile, (side,), (right,))
-        if tile in (1, 2):
-            total += coupled(s[tile], part)
-        else:
-            out[tile // 3] = part
-    half[...] = total
-
-
 def places():
     shape = (2 * T, 2 * T)
     return lax.broadcasted_iota(jnp.int32, shape, 0), lax.broadcasted_iota(jnp.int32, shape, 1)
 
 
-def gram_kernel(m, o, s, p, q, acc, partial, corr, mine, theirs):
+def gram_kernel(m, o, s, above, right_low, right, right_high, acc, corr, mine, theirs, ext):
+    ext[0:1] = right_low[...]
+    ext[1:5] = right[...]
+    ext[5:6] = right_high[...]
     side = 1 + m[PAR_X]
-    low, high = ends(m, p, q)
-    half = partial[...]
-    half += coupled(s[0], acc[0] + outside(o, 0, (side,), 0, low[1:2]))
-    half += coupled(s[3], acc[1] + outside(o, 3, (0, side), 2, high))
+    half = jnp.zeros((2 * T, 2 * T), F32)
+    for tile in range(4):
+        part = acc[tile] + product(o, tile, (side,), range(tile, tile + 3), [ext[tile : tile + 3]])
+        if tile == 3:
+            part += product(o, tile, (0,), (5,), [above[...]])
+        half += coupled(s[tile], part)
     coupling = half + half.T
     rows, cols = places()
     both = jnp.where(rows >= cols, corr[...], coupling)
@@ -217,7 +225,7 @@
     return jnp.where(rows > cols, e, jnp.where(rows == cols, 0.5 * e, 0.0))
 
 
-def final_kernel(m, mine, theirs, s, keep, send, p_keep, p_send, x_ref, a_ref):
+def final_kernel(m, mine, theirs, s, keep, p_keep, send, x_ref, a_ref):
     rows, cols = places()
     even = m[PAR_Y] == 0
     first, second = mine[:, 0, :], theirs[:, 0, :]
@@ -278,9 +286,20 @@
     projected = dot3(dot3(x, coupling), x, ((1,), (1,)))
     first_col = m[COL] == 0
     keep[...] = jnp.where(first_col, ritz[:, :, :T], ritz[:, :, T:])
-    send[...] = jnp.where(first_col, ritz[:, :, T:], ritz[:, :, :T])
+    send[0:4] = jnp.where(first_col, ritz[:, :, T:], ritz[:, :, :T])
     p_keep[...] = jnp.where(first_col, projected[:, :T], projected[:, T:])
-    p_send[...] = jnp.where(first_col, projected[:, T:], projected[:, :T])
+    high, low = split(jnp.where(first_col, projected[:, T:], projected[:, :T]))
+    send[4:6] = high.reshape(2, T, T)
+    send[6:8] = low.reshape(2, T, T)
+
+
+def assemble_kernel(m, keep, p_keep, got, ritz, projected):
+    spin = m[SPIN]
+    ritz[pl.ds(spin, 1)] = keep[...][None, None]
+    ritz[pl.ds(1 - spin, 1)] = got[0:4][None, None]
+    projected[pl.ds(spin, 1)] = p_keep[...][None]
+    received = got[4:6].astype(F32) + got[6:8].astype(F32)
+    projected[pl.ds(1 - spin, 1)] = received.reshape(1, 2 * T, T)
 
 
 def whole(shape):
@@ -336,32 +355,36 @@
     own = lax.dynamic_index_in_dim(start_block, spin, 0, keepdims=False)[0]
     spin_block = pl.BlockSpec((1,) + hamiltonian.shape[1:], lambda i, m: (m[SPIN], 0, 0, 0, 0, 0))
     (o,) = call(order_kernel, m, [hamiltonian], [shaped((4, T, NB * T), BF)], "order", specs=[spin_block])
-    (v,) = call(join_kernel, m, [own, other], [shaped(block, BF)], "join")
-
-    def along_y(*sources):
-        edge = shaped((len(sources), T, 2 * T), BF)
-        p, q = call(edges_kernel, m, sources, [edge, edge], "edges")
-        return swap(sizes, p, 0, 1), swap(sizes, q, 0, 2)
-
-    def apply_ham(o, x, before):
-        a, b = swap(sizes, x, 1, 0), swap(sizes, x, 2, 0)
+    tile, middle = shaped((1, T, 2 * T), BF), shaped((3, T, 2 * T), BF)
+    parts = [shaped(block, BF), middle, tile, tile]
+    ext = pltpu.VMEM((6, T, 2 * T), BF)
+    v, mid, p, q = call(join_kernel, m, [own, other], parts, "join")
+
+    def apply_ham(o, x, mid, p, q, before):
+        last = before is not None
+        p, q = swap(sizes, p, 0, 1), swap(sizes, q, 0, 2)
+        ends = jnp.concatenate([p, x[:1], q], axis=0)
+        a, b = swap(sizes, mid, 1, 0), swap(sizes, mid, 2, 0)
         o, a, b = lax.optimization_barrier((o, a, b))
-        p, q = along_y(x, a, b)
-        (acc,) = call(core_kernel, m, [o, x, a, b], [shaped(block, F32)], "core", 30)
-        (out,) = call(rim_kernel, m, [o, p, q, acc, *before], [shaped(block, BF)], "rim", 6)
-        return o, out
-
-    o, first = apply_ham(o, v, [])
-    o, second = apply_ham(o, first, [v])
-
+        a_ends, b_ends = swap(sizes, ends, 1, 0), swap(sizes, ends, 2, 0)
+        (acc,) = call(core_kernel, m, [o, mid, ends, a, b], [shaped(block, F32)], "core", 28, scratch=[ext])
+        arrays = [o, a_ends, b_ends, acc] + ([before] if last else [])
+        outs = [shaped(block, BF), tile, tile] if last else parts
+        return o, call(functools.partial(rim_kernel, last=last), m, arrays, outs, "rim", 8)
+
+    o, (first, mid, p, q) = apply_ham(o, v, mid, p, q, None)
+    o, (second, low, high) = apply_ham(o, first, mid, p, q, v)
+
+    above = shift(sizes, low, 0, -1)
+    right_high = shift(sizes, low, -1, -1)
+    right_low = shift(sizes, high, -1, 1)
     right = shift(sizes, second, -1, 0)
     corr, acc = call(corr_kernel, m, [o, second], [shaped(full, F32), shaped(block, F32)], "corr", 15)
-    p, q = along_y(second, right)
-    acc, half = call(
-        right_kernel, m, [o, second, right, acc], [shaped((2, T, 2 * T), F32), shaped(full, F32)], "right", 18
+    piece = shaped((members // 2, 1, 5 * T), F32)
+    mine, theirs = call(
+        gram_kernel, m, [o, second, above, right_low, right, right_high, acc, corr], [piece, piece], "gram", 29,
+        scratch=[ext],
     )
-    piece = shaped((members // 2, 1, 5 * T), F32)
-    mine, theirs = call(gram_kernel, m, [o, second, p, q, acc, half, corr], [piece, piece], "gram", 11)
 
     rows = members * second.shape[0] * second.shape[1]
     partial = mine + swap(sizes, theirs, 0, 1)
@@ -369,16 +392,16 @@
     mine = exchange(sizes, jnp.broadcast_to(total, partial.shape))
     theirs = swap(sizes, mine, 0, 1)
 
-    half = (4, T, T)
-    keep, send, p_keep, p_send = call(
+    keep, p_keep, send = call(
         final_kernel, m, [mine, theirs, second],
-        [shaped(half, BF), shaped(half, BF), shaped((2 * T, T), F32), shaped((2 * T, T), F32)], "final", 80,
+        [shaped((4, T, T), BF), shaped((2 * T, T), F32), shaped((8, T, T), BF)], "final", 80,
         scratch=[pltpu.VMEM(full, F32), pltpu.VMEM(full, F32)],
     )
-    got, p_got = swap_col(sizes, send), swap_col(sizes, p_send)
-    ritz = jnp.where(spin == 0, jnp.stack([keep, got]), jnp.stack([got, keep]))
-    projected = jnp.where(spin == 0, jnp.stack([p_keep, p_got]), jnp.stack([p_got, p_keep]))
-    return ritz[:, None], projected
+    got = swap_col(sizes, send)
+    ritz = shaped((2, 1, 4, T, T), BF)
+    return tuple(
+        call(assemble_kernel, m, [keep, p_keep, got], [ritz, shaped((2, 2 * T, T), F32)], "assemble")
+    )
 
 
 def solution(mesh):

time: 165 us -> 157 us (0.952)
  starting transfers between devices: 40.2 us -> 36.3 us
  blocking collectives: 39.7 us -> 37.3 us
    ppermute x12 -> x14, waiting for transfers between devices: 17.8 us -> 13.5 us  [swap(): return lax.ppermute(block, AXES, perm)]
    ppermute x3 -> x2, waiting for transfers between devices: 5.49 us -> 9.17 us  [swap_col(): return lax.ppermute(block, AXES, perm)]
    ppermute x3 -> x2, starting transfers between devices: 6.71 us -> 3.75 us  [swap_col(): return lax.ppermute(block, AXES, perm)]
    ppermute x12 -> x14, starting transfers between devices: 29.2 us -> 26.7 us  [swap(): return lax.ppermute(block, AXES, perm)]
    all_to_all x2, blocking collectives: 39.7 us -> 37.3 us  [exchange(): lax.all_to_all(pieces, AXES, 0, 0, axis_index_groups=groups, tiled=True)]
    ppermute x1 -> x4, waiting for transfers between devices: 3.57 us -> 5.26 us  [shift(): lax.ppermute(block, AXES, pairs(sizes, lambda gx, gy: (gx + dx, gy + dy)))]
    ppermute x1 -> x4, starting transfers between devices: 4.34 us -> 5.86 us  [shift(): lax.ppermute(block, AXES, pairs(sizes, lambda gx, gy: (gx + dx, gy + dy)))]
    pallas_call x13 -> x10, Pallas kernels: 50 us -> 48.8 us  [call(): pl.pallas_call(kernel, out_shape=outs, grid_spec=pltpu.PrefetchScalarGrid...]
  transfers between devices with their start and end apart: 16 -> 20, of which waited for: 13 -> 13; matrix products, arithmetic and copies ran while one was open for 2% -> 1% of each run, Pallas kernels for 3% -> 2%
where the time goes in v5:
time: 157 us
  Pallas kernels  48.8 us (31%)
  blocking collectives  37.3 us (24%)
  starting transfers between devices  36.3 us (23%)
  waiting for transfers between devices  27.9 us (18%)
  local copies, waits for them, and re-layouts  3.04 us (2%)
  other arithmetic  2.24 us (1%)
    pallas_call x10, Pallas kernels, call(): pl.pallas_call(kernel, out_shape=outs, grid_spec=pltpu.PrefetchScalarGrid...  48.8 us
    all_to_all x2, blocking collectives, exchange(): lax.all_to_all(pieces, AXES, 0, 0, axis_index_groups=groups, tiled=True)  37.3 us
    ppermute x14, starting transfers between devices, swap(): return lax.ppermute(block, AXES, perm)  26.7 us
    ppermute x14, waiting for transfers between devices, swap(): return lax.ppermute(block, AXES, perm)  13.5 us
    ppermute x2, waiting for transfers between devices, swap_col(): return lax.ppermute(block, AXES, perm)  9.17 us
    ppermute x4, starting transfers between devices, shift(): lax.ppermute(block, AXES, pairs(sizes, lambda gx, gy: (gx + dx, gy + dy)))  5.86 us
    ppermute x4, waiting for transfers between devices, shift(): lax.ppermute(block, AXES, pairs(sizes, lambda gx, gy: (gx + dx, gy + dy)))  5.26 us
    ppermute x2, starting transfers between devices, swap_col(): return lax.ppermute(block, AXES, perm)  3.75 us
  transfers between devices with their start and end apart: 20, of which 13 were waited for; matrix products, arithmetic and copies ran while one was open for 1% of the time, Pallas kernels for 2%

profile of v5, /device:TPU:1, one launch (start us, length us, event | category | flops | bytes accessed | tf_op | source)
XLA Modules:
  0.0 156.5 jit_solution(4543146337026593928)
XLA Ops:
  0.6 1.0 dynamic-slice_bitcast_fusion
  1.6 3.7 %collective-permute-start = (bf16[4,128,128]{2,1,0:T(8,128)(2,1)S(1)}, bf16[4,128,128]{2,1,0:T(8,128)(2,1)S(1)}, u32[]{:S(2)}, u32[]{:S(2)}) collective-permute-start(bf16[4,128,128]{2,1,0:T(8,128)(2,1)S(1)} %get-tuple-element.50), channel_id=1, source_target_pairs={{0,1},{1,0},{2,3},{3,2},{4,5},{5,4},{6,7},{7,6},{8,9},{9,8},{10,11... | collective-permute-start | bytes 393224 | tf_op jit(solution)/shard_map/ppermute | solution.py:59
  6.2 1.0 select_reduce_fusion
  8.3 3.9 %collective-permute-start.3 = (bf16[1,128,256]{2,1,0:T(8,128)(2,1)S(1)}, bf16[1,128,256]{2,1,0:T(8,128)(2,1)S(1)}, u32[]{:S(2)}, u32[]{:S(2)}) collective-permute-start(bf16[1,128,256]{2,1,0:T(8,128)(2,1)S(1)} %get-tuple-element.28), channel_id=1, source_target_pairs={{0,2},{1,3},{2,0},{3,1},{4,6},{5,7},{6,4},{7,5},{8,10},{9,11},{10,... | collective-permute-start | bytes 196616 | tf_op jit(solution)/shard_map/ppermute | solution.py:50
  12.3 1.2 collective-permute-start.1
  13.5 4.3 %collective-permute-start.2 = (bf16[3,128,256]{2,1,0:T(8,128)(2,1)S(1)}, bf16[3,128,256]{2,1,0:T(8,128)(2,1)S(1)}, u32[]{:S(2)}, u32[]{:S(2)}) collective-permute-start(bf16[3,128,256]{2,1,0:T(8,128)(2,1)S(1)} %get-tuple-element.26.mid), channel_id=1, source_target_pairs={{0,225},{1,224},{2,227},{3,226},{4,229},{5,228},{6,231},{7,230},{8... | collective-permute-start | bytes 589832 | tf_op jit(solution)/shard_map/ppermute | solution.py:50
  18.0 2.0 %collective-permute-start.6 = (bf16[3,128,256]{2,1,0:T(8,128)(2,1)S(1)}, bf16[3,128,256]{2,1,0:T(8,128)(2,1)S(1)}, u32[]{:S(2)}, u32[]{:S(2)}) collective-permute-start(bf16[3,128,256]{2,1,0:T(8,128)(2,1)S(1)} %pad_maximum_fusion.ends), channel_id=1, source_target_pairs={{0,225},{1,224},{2,227},{3,226},{4,229},{5,228},{6,231},{7,230},{8... | collective-permute-start | bytes 589832 | tf_op jit(solution)/shard_map/ppermute | solution.py:50
  20.0 1.7 %copy-done = bf16[2,1,4,9,128,128]{5,4,3,2,1,0:T(8,128)(2,1)S(1)} copy-done((bf16[2,1,4,9,128,128]{5,4,3,2,1,0:T(8,128)(2,1)S(1)}, bf16[2,1,4,9,128,128]{5,4,3,2,1,0:T(8,128)(2,1)}, u32[]{:S(2)}) %copy-start) | copy-done | bytes 2359320
  22.5 1.0 core.2.acc
  23.8 4.0 %collective-permute-done.6.b_ends = bf16[3,128,256]{2,1,0:T(8,128)(2,1)S(1)} collective-permute-done((bf16[3,128,256]{2,1,0:T(8,128)(2,1)S(1)}, bf16[3,128,256]{2,1,0:T(8,128)(2,1)S(1)}, u32[]{:S(2)}, u32[]{:S(2)}) %collective-permute-start.6) | collective-permute-done | bytes 196640 | tf_op jit(solution)/shard_map/ppermute | solution.py:50
  28.5 1.9 %collective-permute-start.10 = (bf16[1,128,256]{2,1,0:T(8,128)(2,1)S(1)}, bf16[1,128,256]{2,1,0:T(8,128)(2,1)S(1)}, u32[]{:S(2)}, u32[]{:S(2)}) collective-permute-start(bf16[1,128,256]{2,1,0:T(8,128)(2,1)S(1)} %get-tuple-element.37), channel_id=1, source_target_pairs={{0,30},{1,31},{2,4},{3,5},{4,2},{5,3},{6,8},{7,9},{8,6},{9,7},{10,... | collective-permute-start | bytes 196616 | tf_op jit(solution)/shard_map/ppermute | solution.py:50
  30.4 2.5 %collective-permute-start.9 = (bf16[1,128,256]{2,1,0:T(8,128)(2,1)S(1)}, bf16[1,128,256]{2,1,0:T(8,128)(2,1)S(1)}, u32[]{:S(2)}, u32[]{:S(2)}) collective-permute-start(bf16[1,128,256]{2,1,0:T(8,128)(2,1)S(1)} %get-tuple-element.35), channel_id=1, source_target_pairs={{0,2},{1,3},{2,0},{3,1},{4,6},{5,7},{6,4},{7,5},{8,10},{9,11},{10,... | collective-permute-start | bytes 196616 | tf_op jit(solution)/shard_map/ppermute | solution.py:50
  32.9 4.7 %collective-permute-start.8 = (bf16[3,128,256]{2,1,0:T(8,128)(2,1)S(1)}, bf16[3,128,256]{2,1,0:T(8,128)(2,1)S(1)}, u32[]{:S(2)}, u32[]{:S(2)}) collective-permute-start(bf16[3,128,256]{2,1,0:T(8,128)(2,1)S(1)} %get-tuple-element.33.mid), channel_id=1, source_target_pairs={{0,225},{1,224},{2,227},{3,226},{4,229},{5,228},{6,231},{7,230},{8... | collective-permute-start | bytes 589832 | tf_op jit(solution)/shard_map/ppermute | solution.py:50
  37.8 1.5 collective-permute-start.12
  39.4 3.2 %collective-permute-done.8.b = bf16[3,128,256]{2,1,0:T(8,128)(2,1)S(1)} collective-permute-done((bf16[3,128,256]{2,1,0:T(8,128)(2,1)S(1)}, bf16[3,128,256]{2,1,0:T(8,128)(2,1)S(1)}, u32[]{:S(2)}, u32[]{:S(2)}) %collective-permute-start.8) | collective-permute-done | bytes 196640 | tf_op jit(solution)/shard_map/ppermute | solution.py:50
  42.6 1.0 core.3.acc
  44.0 3.4 %collective-permute-done.12.b_ends = bf16[3,128,256]{2,1,0:T(8,128)(2,1)S(1)} collective-permute-done((bf16[3,128,256]{2,1,0:T(8,128)(2,1)S(1)}, bf16[3,128,256]{2,1,0:T(8,128)(2,1)S(1)}, u32[]{:S(2)}, u32[]{:S(2)}) %collective-permute-start.12) | collective-permute-done | bytes 196640 | tf_op jit(solution)/shard_map/ppermute | solution.py:50
  48.2 4.4 %collective-permute-start.15 = (bf16[4,128,256]{2,1,0:T(8,128)(2,1)S(1)}, bf16[4,128,256]{2,1,0:T(8,128)(2,1)S(1)}, u32[]{:S(2)}, u32[]{:S(2)}) collective-permute-start(bf16[4,128,256]{2,1,0:T(8,128)(2,1)S(1)} %get-tuple-element.40.s), channel_id=1, source_target_pairs={{0,225},{1,224},{2,227},{3,226},{4,229},{5,228},{6,231},{7,230},{8... | collective-permute-start | bytes 786440 | tf_op jit(solution)/shard_map/ppermute | solution.py:54
  52.6 1.1 collective-permute-start.13
  55.0 1.6 %collective-permute-done.13.above = bf16[1,128,256]{2,1,0:T(8,128)(2,1)S(1)} collective-permute-done((bf16[1,128,256]{2,1,0:T(8,128)(2,1)S(1)}, bf16[1,128,256]{2,1,0:T(8,128)(2,1)S(1)}, u32[]{:S(2)}, u32[]{:S(2)}) %collective-permute-start.13) | collective-permute-done | bytes 65568 | tf_op jit(solution)/shard_map/ppermute | solution.py:54
  56.6 1.6 %collective-permute-done.14.right_low = bf16[1,128,256]{2,1,0:T(8,128)(2,1)S(1)} collective-permute-done((bf16[1,128,256]{2,1,0:T(8,128)(2,1)S(1)}, bf16[1,128,256]{2,1,0:T(8,128)(2,1)S(1)}, u32[]{:S(2)}, u32[]{:S(2)}) %collective-permute-start.14) | collective-permute-done | bytes 65568 | tf_op jit(solution)/shard_map/ppermute | solution.py:54
  58.2 2.1 %collective-permute-done.16.right_high = bf16[1,128,256]{2,1,0:T(8,128)(2,1)S(1)} collective-permute-done((bf16[1,128,256]{2,1,0:T(8,128)(2,1)S(1)}, bf16[1,128,256]{2,1,0:T(8,128)(2,1)S(1)}, u32[]{:S(2)}, u32[]{:S(2)}) %collective-permute-start.16) | collective-permute-done | bytes 65568 | tf_op jit(solution)/shard_map/ppermute | solution.py:54
  60.3 1.8 %gram.1 = (f32[64,1,640]{2,1,0:T(1,128)S(1)}, f32[64,1,640]{2,1,0:T(1,128)S(1)}) custom-call(s32[40]{0:T(128)S(1)} %concatenate.13.m, bf16[4,128,1152]{2,1,0:T(8,128)(2,1)S(1)} %order.1.o, bf16[4,128,256]{2,1,0:T(8,128)(2,1)S(1)} %get-tuple-element.40.s, bf16[1,128,256]{2,1,0:T(8,128)(2,1)S(1)} %collective-permute-done.13.above, ...), custom_call_target="tpu_custom_call" | custom-call | flops 243269632 | bytes 3014656 | tf_op jit(solution)/shard_map/gram/pallas_call | solution.py:312
  62.0 1.8 %collective-permute-start.17 = (f32[64,1,640]{2,1,0:T(1,128)S(1)}, f32[64,1,640]{2,1,0:T(1,128)S(1)}, u32[]{:S(2)}, u32[]{:S(2)}) collective-permute-start(f32[64,1,640]{2,1,0:T(1,128)S(1)} %get-tuple-element.46), channel_id=1, source_target_pairs={{0,2},{1,3},{2,0},{3,1},{4,6},{5,7},{6,4},{7,5},{8,10},{9,11},{10,... | collective-permute-start | bytes 491528 | tf_op jit(solution)/shard_map/ppermute | solution.py:50
  63.8 1.0 collective-permute-done.17
  65.0 20.8 %all_to_all.10 = f32[64,1,640]{2,1,0:T(1,128)S(1)} all-to-all(f32[64,1,640]{2,1,0:T(1,128)S(1)} %add.59), channel_id=1, replica_groups={{0,4,8,12,16,20,24,28,32,36,40,44,48,52,56,60,65,69,73,77,81,85,89,93,9..., dimensions={0} | all-to-all | bytes 327680 | tf_op jit(solution)/shard_map/all_to_all | solution.py:72
  86.0 16.6 %all_to_all.11.mine = f32[64,1,640]{2,1,0:T(1,128)S(1)} all-to-all(f32[64,1,640]{2,1,0:T(1,128)S(1)} %broadcast_in_dim.20), channel_id=1, replica_groups={{0,4,8,12,16,20,24,28,32,36,40,44,48,52,56,60,65,69,73,77,81,85,89,93,9..., dimensions={0} | all-to-all | bytes 327680 | tf_op jit(solution)/shard_map/all_to_all | solution.py:72
  102.6 2.7 %collective-permute-start.18 = (f32[64,1,640]{2,1,0:T(1,128)S(1)}, f32[64,1,640]{2,1,0:T(1,128)S(1)}, u32[]{:S(2)}, u32[]{:S(2)}) collective-permute-start(f32[64,1,640]{2,1,0:T(1,128)S(1)} %all_to_all.11.mine), channel_id=1, source_target_pairs={{0,2},{1,3},{2,0},{3,1},{4,6},{5,7},{6,4},{7,5},{8,10},{9,11},{10,... | collective-permute-start | bytes 491528 | tf_op jit(solution)/shard_map/ppermute | solution.py:50
  105.3 1.0 collective-permute-done.18.theirs
  106.3 39.7 %final.1 = (bf16[4,128,128]{2,1,0:T(8,128)(2,1)S(1)}, f32[256,128]{1,0:T(8,128)S(1)}, bf16[8,128,128]{2,1,0:T(8,128)(2,1)S(1)}) custom-call(s32[40]{0:T(128)S(1)} %concatenate.13.m, f32[64,1,640]{2,1,0:T(1,128)S(1)} %all_to_all.11.mine, f32[64,1,640]{2,1,0:T(1,128)S(1)} %collective-permute-done.18.theirs, bf16[4,128,256]{2,1,0:T(8,128)(2,1)S(1)} %get-tuple-element.40.s), custom_call_target="tpu_custom_call" | custom-call | flops 671088640 | bytes 1114112 | tf_op jit(solution)/shard_map/final/pallas_call | solution.py:312
  146.1 9.0 %collective-permute-done.19.got = bf16[8,128,128]{2,1,0:T(8,128)(2,1)S(1)} collective-permute-done((bf16[8,128,128]{2,1,0:T(8,128)(2,1)S(1)}, bf16[8,128,128]{2,1,0:T(8,128)(2,1)S(1)}, u32[]{:S(2)}, u32[]{:S(2)}) %collective-permute-start.19) | collective-permute-done | bytes 262176 | tf_op jit(solution)/shard_map/ppermute | solution.py:59
  155.1 1.4 assemble.1
  (40 shorter events, 7.5 us)
Async XLA Ops:
  1.6 6.0 %collective-permute-start = (bf16[4,128,128]{2,1,0:T(8,128)(2,1)S(1)}, bf16[4,128,128]{2,1,0:T(8,128)(2,1)S(1)}, u32[]{:S(2)}, u32[]{:S(2)}) collective-permute-start(bf16[4,128,128]{2,1,0:T(8,128)(2,1)S(1)} %get-tuple-element.50), channel_id=1, source_target_pairs={{0,1},{1,0},{2,3},{3,2},{4,5},{5,4},{6,7},{7,6},{8,9},{9,8},{10,11... | collective-permute-start | bytes 393224 | tf_op jit(solution)/shard_map/ppermute | solution.py:59
  8.3 9.5 %collective-permute-start.3 = (bf16[1,128,256]{2,1,0:T(8,128)(2,1)S(1)}, bf16[1,128,256]{2,1,0:T(8,128)(2,1)S(1)}, u32[]{:S(2)}, u32[]{:S(2)}) collective-permute-start(bf16[1,128,256]{2,1,0:T(8,128)(2,1)S(1)} %get-tuple-element.28), channel_id=1, source_target_pairs={{0,2},{1,3},{2,0},{3,1},{4,6},{5,7},{6,4},{7,5},{8,10},{9,11},{10,... | collective-permute-start | bytes 196616 | tf_op jit(solution)/shard_map/ppermute | solution.py:50
  12.2 5.6 %collective-permute-start.4 = (bf16[1,128,256]{2,1,0:T(8,128)(2,1)S(1)}, bf16[1,128,256]{2,1,0:T(8,128)(2,1)S(1)}, u32[]{:S(2)}, u32[]{:S(2)}) collective-permute-start(bf16[1,128,256]{2,1,0:T(8,128)(2,1)S(1)} %get-tuple-element.30), channel_id=1, source_target_pairs={{0,30},{1,31},{2,4},{3,5},{4,2},{5,3},{6,8},{7,9},{8,6},{9,7},{10,... | collective-permute-start | bytes 196616 | tf_op jit(solution)/shard_map/ppermute | solution.py:50
  12.3 10.2 %collective-permute-start.1 = (bf16[3,128,256]{2,1,0:T(8,128)(2,1)S(1)}, bf16[3,128,256]{2,1,0:T(8,128)(2,1)S(1)}, u32[]{:S(2)}, u32[]{:S(2)}) collective-permute-start(bf16[3,128,256]{2,1,0:T(8,128)(2,1)S(1)} %get-tuple-element.26.mid), channel_id=1, source_target_pairs={{0,32},{1,33},{2,34},{3,35},{4,36},{5,37},{6,38},{7,39},{8,40},{9,... | collective-permute-start | bytes 589832 | tf_op jit(solution)/shard_map/ppermute | solution.py:50
  13.5 9.0 %collective-permute-start.2 = (bf16[3,128,256]{2,1,0:T(8,128)(2,1)S(1)}, bf16[3,128,256]{2,1,0:T(8,128)(2,1)S(1)}, u32[]{:S(2)}, u32[]{:S(2)}) collective-permute-start(bf16[3,128,256]{2,1,0:T(8,128)(2,1)S(1)} %get-tuple-element.26.mid), channel_id=1, source_target_pairs={{0,225},{1,224},{2,227},{3,226},{4,229},{5,228},{6,231},{7,230},{8... | collective-permute-start | bytes 589832 | tf_op jit(solution)/shard_map/ppermute | solution.py:50
  17.9 5.9 %collective-permute-start.5 = (bf16[3,128,256]{2,1,0:T(8,128)(2,1)S(1)}, bf16[3,128,256]{2,1,0:T(8,128)(2,1)S(1)}, u32[]{:S(2)}, u32[]{:S(2)}) collective-permute-start(bf16[3,128,256]{2,1,0:T(8,128)(2,1)S(1)} %pad_maximum_fusion.ends), channel_id=1, source_target_pairs={{0,32},{1,33},{2,34},{3,35},{4,36},{5,37},{6,38},{7,39},{8,40},{9,... | collective-permute-start | bytes 589832 | tf_op jit(solution)/shard_map/ppermute | solution.py:50
  18.0 9.8 %collective-permute-start.6 = (bf16[3,128,256]{2,1,0:T(8,128)(2,1)S(1)}, bf16[3,128,256]{2,1,0:T(8,128)(2,1)S(1)}, u32[]{:S(2)}, u32[]{:S(2)}) collective-permute-start(bf16[3,128,256]{2,1,0:T(8,128)(2,1)S(1)} %pad_maximum_fusion.ends), channel_id=1, source_target_pairs={{0,225},{1,224},{2,227},{3,226},{4,229},{5,228},{6,231},{7,230},{8... | collective-permute-start | bytes 589832 | tf_op jit(solution)/shard_map/ppermute | solution.py:50
  20.0 1.7 %copy-start = (bf16[2,1,4,9,128,128]{5,4,3,2,1,0:T(8,128)(2,1)S(1)}, bf16[2,1,4,9,128,128]{5,4,3,2,1,0:T(8,128)(2,1)}, u32[]{:S(2)}) copy-start(bf16[2,1,4,9,128,128]{5,4,3,2,1,0:T(8,128)(2,1)} %h.1) | copy-start | bytes 7077892
  28.5 9.1 %collective-permute-start.10 = (bf16[1,128,256]{2,1,0:T(8,128)(2,1)S(1)}, bf16[1,128,256]{2,1,0:T(8,128)(2,1)S(1)}, u32[]{:S(2)}, u32[]{:S(2)}) collective-permute-start(bf16[1,128,256]{2,1,0:T(8,128)(2,1)S(1)} %get-tuple-element.37), channel_id=1, source_target_pairs={{0,30},{1,31},{2,4},{3,5},{4,2},{5,3},{6,8},{7,9},{8,6},{9,7},{10,... | collective-permute-start | bytes 196616 | tf_op jit(solution)/shard_map/ppermute | solution.py:50
  30.4 7.2 %collective-permute-start.9 = (bf16[1,128,256]{2,1,0:T(8,128)(2,1)S(1)}, bf16[1,128,256]{2,1,0:T(8,128)(2,1)S(1)}, u32[]{:S(2)}, u32[]{:S(2)}) collective-permute-start(bf16[1,128,256]{2,1,0:T(8,128)(2,1)S(1)} %get-tuple-element.35), channel_id=1, source_target_pairs={{0,2},{1,3},{2,0},{3,1},{4,6},{5,7},{6,4},{7,5},{8,10},{9,11},{10,... | collective-permute-start | bytes 196616 | tf_op jit(solution)/shard_map/ppermute | solution.py:50
  32.9 6.5 %collective-permute-start.7 = (bf16[3,128,256]{2,1,0:T(8,128)(2,1)S(1)}, bf16[3,128,256]{2,1,0:T(8,128)(2,1)S(1)}, u32[]{:S(2)}, u32[]{:S(2)}) collective-permute-start(bf16[3,128,256]{2,1,0:T(8,128)(2,1)S(1)} %get-tuple-element.33.mid), channel_id=1, source_target_pairs={{0,32},{1,33},{2,34},{3,35},{4,36},{5,37},{6,38},{7,39},{8,40},{9,... | collective-permute-start | bytes 589832 | tf_op jit(solution)/shard_map/ppermute | solution.py:50
  32.9 9.6 %collective-permute-start.8 = (bf16[3,128,256]{2,1,0:T(8,128)(2,1)S(1)}, bf16[3,128,256]{2,1,0:T(8,128)(2,1)S(1)}, u32[]{:S(2)}, u32[]{:S(2)}) collective-permute-start(bf16[3,128,256]{2,1,0:T(8,128)(2,1)S(1)} %get-tuple-element.33.mid), channel_id=1, source_target_pairs={{0,225},{1,224},{2,227},{3,226},{4,229},{5,228},{6,231},{7,230},{8... | collective-permute-start | bytes 589832 | tf_op jit(solution)/shard_map/ppermute | solution.py:50
  37.7 6.3 %collective-permute-start.11 = (bf16[3,128,256]{2,1,0:T(8,128)(2,1)S(1)}, bf16[3,128,256]{2,1,0:T(8,128)(2,1)S(1)}, u32[]{:S(2)}, u32[]{:S(2)}) collective-permute-start(bf16[3,128,256]{2,1,0:T(8,128)(2,1)S(1)} %pad_maximum_fusion.1.ends), channel_id=1, source_target_pairs={{0,32},{1,33},{2,34},{3,35},{4,36},{5,37},{6,38},{7,39},{8,40},{9,... | collective-permute-start | bytes 589832 | tf_op jit(solution)/shard_map/ppermute | solution.py:50
  37.8 9.6 %collective-permute-start.12 = (bf16[3,128,256]{2,1,0:T(8,128)(2,1)S(1)}, bf16[3,128,256]{2,1,0:T(8,128)(2,1)S(1)}, u32[]{:S(2)}, u32[]{:S(2)}) collective-permute-start(bf16[3,128,256]{2,1,0:T(8,128)(2,1)S(1)} %pad_maximum_fusion.1.ends), channel_id=1, source_target_pairs={{0,225},{1,224},{2,227},{3,226},{4,229},{5,228},{6,231},{7,230},{8... | collective-permute-start | bytes 589832 | tf_op jit(solution)/shard_map/ppermute | solution.py:50
  48.2 12.0 %collective-permute-start.15 = (bf16[4,128,256]{2,1,0:T(8,128)(2,1)S(1)}, bf16[4,128,256]{2,1,0:T(8,128)(2,1)S(1)}, u32[]{:S(2)}, u32[]{:S(2)}) collective-permute-start(bf16[4,128,256]{2,1,0:T(8,128)(2,1)S(1)} %get-tuple-element.40.s), channel_id=1, source_target_pairs={{0,225},{1,224},{2,227},{3,226},{4,229},{5,228},{6,231},{7,230},{8... | collective-permute-start | bytes 786440 | tf_op jit(solution)/shard_map/ppermute | solution.py:54
  52.6 4.0 %collective-permute-start.13 = (bf16[1,128,256]{2,1,0:T(8,128)(2,1)S(1)}, bf16[1,128,256]{2,1,0:T(8,128)(2,1)S(1)}, u32[]{:S(2)}, u32[]{:S(2)}) collective-permute-start(bf16[1,128,256]{2,1,0:T(8,128)(2,1)S(1)} %get-tuple-element.41), channel_id=1, source_target_pairs={{0,30},{1,31},{2,0},{3,1},{4,2},{5,3},{6,4},{7,5},{8,6},{9,7},{10,... | collective-permute-start | bytes 196616 | tf_op jit(solution)/shard_map/ppermute | solution.py:54
  53.7 4.5 %collective-permute-start.14 = (bf16[1,128,256]{2,1,0:T(8,128)(2,1)S(1)}, bf16[1,128,256]{2,1,0:T(8,128)(2,1)S(1)}, u32[]{:S(2)}, u32[]{:S(2)}) collective-permute-start(bf16[1,128,256]{2,1,0:T(8,128)(2,1)S(1)} %get-tuple-element.42), channel_id=1, source_target_pairs={{0,227},{1,226},{2,229},{3,228},{4,231},{5,230},{6,233},{7,232},{8... | collective-permute-start | bytes 196616 | tf_op jit(solution)/shard_map/ppermute | solution.py:54
  54.1 6.2 %collective-permute-start.16 = (bf16[1,128,256]{2,1,0:T(8,128)(2,1)S(1)}, bf16[1,128,256]{2,1,0:T(8,128)(2,1)S(1)}, u32[]{:S(2)}, u32[]{:S(2)}) collective-permute-start(bf16[1,128,256]{2,1,0:T(8,128)(2,1)S(1)} %get-tuple-element.41), channel_id=1, source_target_pairs={{0,255},{1,254},{2,225},{3,224},{4,227},{5,226},{6,229},{7,228},{8... | collective-permute-start | bytes 196616 | tf_op jit(solution)/shard_map/ppermute | solution.py:54
  62.0 2.8 %collective-permute-start.17 = (f32[64,1,640]{2,1,0:T(1,128)S(1)}, f32[64,1,640]{2,1,0:T(1,128)S(1)}, u32[]{:S(2)}, u32[]{:S(2)}) collective-permute-start(f32[64,1,640]{2,1,0:T(1,128)S(1)} %get-tuple-element.46), channel_id=1, source_target_pairs={{0,2},{1,3},{2,0},{3,1},{4,6},{5,7},{6,4},{7,5},{8,10},{9,11},{10,... | collective-permute-start | bytes 491528 | tf_op jit(solution)/shard_map/ppermute | solution.py:50
  102.6 3.7 %collective-permute-start.18 = (f32[64,1,640]{2,1,0:T(1,128)S(1)}, f32[64,1,640]{2,1,0:T(1,128)S(1)}, u32[]{:S(2)}, u32[]{:S(2)}) collective-permute-start(f32[64,1,640]{2,1,0:T(1,128)S(1)} %all_to_all.11.mine), channel_id=1, source_target_pairs={{0,2},{1,3},{2,0},{3,1},{4,6},{5,7},{6,4},{7,5},{8,10},{9,11},{10,... | collective-permute-start | bytes 491528 | tf_op jit(solution)/shard_map/ppermute | solution.py:50
  146.0 9.1 %collective-permute-start.19 = (bf16[8,128,128]{2,1,0:T(8,128)(2,1)S(1)}, bf16[8,128,128]{2,1,0:T(8,128)(2,1)S(1)}, u32[]{:S(2)}, u32[]{:S(2)}) collective-permute-start(bf16[8,128,128]{2,1,0:T(8,128)(2,1)S(1)} %get-tuple-element.49), channel_id=1, source_target_pairs={{0,1},{1,0},{2,3},{3,2},{4,5},{5,4},{6,7},{7,6},{8,9},{9,8},{10,11... | collective-permute-start | bytes 786440 | tf_op jit(solution)/shard_map/ppermute | solution.py:59

commit v6 on v5

--- a/solution.py
+++ b/solution.py
@@ -104,26 +104,23 @@
     return out[0] if len(out) == 1 else jnp.concatenate(out, axis=1)
 
 
-def store_parts(m, ref, mid, p, q):
+def store_edges(m, ref, p, q):
     even = m[PAR_Y] == 0
     p[...] = ref[pl.ds(jnp.where(even, 3, 0), 1)]
-    q[...] = ref[pl.ds(jnp.where(even, 0, 3), 1)]
-    mid[...] = ref[1:4]
-
-
-def join_kernel(m, own, other, v, mid, p, q):
+    q[0:1] = ref[pl.ds(jnp.where(even, 0, 3), 1)]
+    q[1:2] = ref[1:2]
+
+
+def join_kernel(m, own, other, v, p, q):
     first_col = m[COL] == 0
     v[:, :, :T] = jnp.where(first_col, own[...], other[...])
     v[:, :, T:] = jnp.where(first_col, other[...], own[...])
-    store_parts(m, v, mid, p, q)
-
-
-def fill(m, ext, mid, ends):
+    store_edges(m, v, p, q)
+
+
+def ends_of(m, ends):
     even = m[PAR_Y] == 0
-    ext[1:2] = ends[1:2]
-    ext[2:5] = mid[...]
-    ext[pl.ds(jnp.where(even, 5, 0), 1)] = ends[0:1]
-    ext[pl.ds(jnp.where(even, 0, 5), 1)] = ends[2:3]
+    return jnp.where(even, ends[1:2], ends[0:1]), jnp.where(even, ends[0:1], ends[1:2])
 
 
 def product(o, tile, sides, at, sources):
@@ -131,12 +128,15 @@
     return dot(row, jnp.concatenate([x.reshape(len(at) * T, 2 * T) for x in sources], axis=0))
 
 
-def core_kernel(m, o, mid, ends, a, b, acc, ext):
-    fill(m, ext, mid, ends)
+def core_kernel(m, o, x, ends, a, b, acc, ext):
+    low, high = ends_of(m, ends)
+    ext[0:1] = low
+    ext[1:5] = x[...]
+    ext[5:6] = high
     for tile in range(4):
         total = product(o, tile, (0,), range(tile, tile + 3), [ext[tile : tile + 3]])
-        at = [place for place in range(tile, tile + 3) if 2 <= place <= 4]
-        sources = [x[at[0] - 2 : at[-1] - 1] for x in (a, b)]
+        at = [place for place in range(tile, tile + 3) if 1 <= place <= 4]
+        sources = [y[at[0] - 1 : at[-1]] for y in (a, b)]
         acc[tile] = total + product(o, tile, (1, 2), at, sources)
 
 
@@ -144,18 +144,12 @@
     if last:
         before, out, first_out, last_out = rest
     else:
-        out, mid, p, q = rest
-    even = m[PAR_Y] == 0
-    low = [jnp.where(even, x[2:3], x[0:1]) for x in (a_ends, b_ends)]
-    first = [x[1:2] for x in (a_ends, b_ends)]
-    high = [jnp.where(even, x[0:1], x[2:3]) for x in (a_ends, b_ends)]
+        out, p, q = rest
+    low, high = zip(ends_of(m, a_ends), ends_of(m, b_ends))
     for tile in range(4):
         total = acc[tile]
         if tile == 0:
-            pair = [jnp.concatenate([x, y], axis=0) for x, y in zip(low, first)]
-            total += product(o, tile, (1, 2), (0, 1), pair)
-        if tile == 1:
-            total += product(o, tile, (1, 2), (1,), first)
+            total += product(o, tile, (1, 2), (0,), low)
         if tile == 3:
             total += product(o, tile, (1, 2), (5,), high)
         if last:
@@ -166,12 +160,13 @@
         first_out[...] = out[0:1]
         last_out[...] = out[3:4]
     else:
-        store_parts(m, out, mid, p, q)
-
-
-def corr_kernel(m, o, s, corr, acc):
+        store_edges(m, out, p, q)
+
+
+def corr_kernel(m, o, s, corr, turned, acc):
     flat = s[...].reshape(4 * T, 2 * T)
-    corr[...] = dot(flat, flat, ((0,), (0,)))
+    turned[...] = flat.T
+    corr[...] = dot(turned[...], flat)
     for tile in range(4):
         total = 0.5 * dot(blocks(o, tile, (0,), (1,)), s[tile])
         if tile < 3:
@@ -179,27 +174,24 @@
         acc[tile] = total
 
 
-def coupled(s_tile, total):
-    high, low = split(total)
-    return dot(s_tile, high, ((0,), (0,))) + dot(s_tile, low, ((0,), (0,)))
-
-
 def places():
     shape = (2 * T, 2 * T)
     return lax.broadcasted_iota(jnp.int32, shape, 0), lax.broadcasted_iota(jnp.int32, shape, 1)
 
 
-def gram_kernel(m, o, s, above, right_low, right, right_high, acc, corr, mine, theirs, ext):
+def gram_kernel(m, o, turned, above, right_low, right, right_high, acc, corr, mine, theirs, ext):
     ext[0:1] = right_low[...]
     ext[1:5] = right[...]
     ext[5:6] = right_high[...]
     side = 1 + m[PAR_X]
-    half = jnp.zeros((2 * T, 2 * T), F32)
+    parts = []
     for tile in range(4):
         part = acc[tile] + product(o, tile, (side,), range(tile, tile + 3), [ext[tile : tile + 3]])
         if tile == 3:
             part += product(o, tile, (0,), (5,), [above[...]])
-        half += coupled(s[tile], part)
+        parts.append(part)
+    high, low = split(jnp.concatenate(parts, axis=0))
+    half = dot(turned[...], high) + dot(turned[...], low)
     coupling = half + half.T
     rows, cols = places()
     both = jnp.where(rows >= cols, corr[...], coupling)
@@ -225,17 +217,19 @@
     return jnp.where(rows > cols, e, jnp.where(rows == cols, 0.5 * e, 0.0))
 
 
-def final_kernel(m, mine, theirs, s, keep, p_keep, send, x_ref, a_ref):
-    rows, cols = places()
+def square_of(m, mine, theirs):
     even = m[PAR_Y] == 0
     first, second = mine[:, 0, :], theirs[:, 0, :]
     top = unpack(jnp.where(even, first, second))
     bottom = unpack(jnp.where(even, second, first))
-    both = jnp.concatenate([top[0], bottom[0]], axis=0)
-    diagonal = jnp.concatenate([top[1], bottom[1]], axis=0)
+    return jnp.concatenate([top[0], bottom[0]], axis=0), jnp.concatenate([top[1], bottom[1]], axis=0)
+
+
+def inverse_kernel(m, mine, theirs, s, keep, send, x_out, x_ref, a_ref):
+    rows, cols = places()
+    both, _ = square_of(m, mine, theirs)
     turned = both.T
     corr = jnp.where(rows >= cols, both, turned)
-    coupling = jnp.where(rows < cols, both, jnp.where(rows == cols, diagonal, turned))
     on_diagonal = jnp.where(rows == cols, corr, 0.0)
     scale_row = 1.0 / jnp.sqrt(jnp.sum(on_diagonal, axis=0, keepdims=True))
     scale_col = 1.0 / jnp.sqrt(jnp.sum(on_diagonal, axis=1, keepdims=True))
@@ -280,26 +274,23 @@
         x_ref[...] = x_ref[...] / jnp.sqrt(pivots)
 
     x = x_ref[...] * scale_row
-    rotation = x.astype(BF)
-    ritz = dot(s[...].reshape(4 * T, 2 * T), rotation, ((1,), (1,))).astype(BF)
+    x_out[...] = x
+    ritz = dot(s[...].reshape(4 * T, 2 * T), x.astype(BF), ((1,), (1,))).astype(BF)
     ritz = ritz.reshape(4, T, 2 * T)
+    first_col = m[COL] == 0
+    keep[...] = jnp.where(first_col, ritz[:, :, :T], ritz[:, :, T:])
+    send[...] = jnp.where(first_col, ritz[:, :, T:], ritz[:, :, :T])
+
+
+def project_kernel(m, mine, theirs, x_ref, keep, send):
+    rows, cols = places()
+    both, diagonal = square_of(m, mine, theirs)
+    coupling = jnp.where(rows < cols, both, jnp.where(rows == cols, diagonal, both.T))
+    x = x_ref[...]
     projected = dot3(dot3(x, coupling), x, ((1,), (1,)))
     first_col = m[COL] == 0
-    keep[...] = jnp.where(first_col, ritz[:, :, :T], ritz[:, :, T:])
-    send[0:4] = jnp.where(first_col, ritz[:, :, T:], ritz[:, :, :T])
-    p_keep[...] = jnp.where(first_col, projected[:, :T], projected[:, T:])
-    high, low = split(jnp.where(first_col, projected[:, T:], projected[:, :T]))
-    send[4:6] = high.reshape(2, T, T)
-    send[6:8] = low.reshape(2, T, T)
-
-
-def assemble_kernel(m, keep, p_keep, got, ritz, projected):
-    spin = m[SPIN]
-    ritz[pl.ds(spin, 1)] = keep[...][None, None]
-    ritz[pl.ds(1 - spin, 1)] = got[0:4][None, None]
-    projected[pl.ds(spin, 1)] = p_keep[...][None]
-    received = got[4:6].astype(F32) + got[6:8].astype(F32)
-    projected[pl.ds(1 - spin, 1)] = received.reshape(1, 2 * T, T)
+    keep[...] = jnp.where(first_col, projected[:, :T], projected[:, T:])
+    send[...] = jnp.where(first_col, projected[:, T:], projected[:, :T]).astype(BF)
 
 
 def whole(shape):
@@ -355,34 +346,36 @@
     own = lax.dynamic_index_in_dim(start_block, spin, 0, keepdims=False)[0]
     spin_block = pl.BlockSpec((1,) + hamiltonian.shape[1:], lambda i, m: (m[SPIN], 0, 0, 0, 0, 0))
     (o,) = call(order_kernel, m, [hamiltonian], [shaped((4, T, NB * T), BF)], "order", specs=[spin_block])
-    tile, middle = shaped((1, T, 2 * T), BF), shaped((3, T, 2 * T), BF)
-    parts = [shaped(block, BF), middle, tile, tile]
+    tile = shaped((1, T, 2 * T), BF)
+    parts = [shaped(block, BF), tile, shaped((2, T, 2 * T), BF)]
     ext = pltpu.VMEM((6, T, 2 * T), BF)
-    v, mid, p, q = call(join_kernel, m, [own, other], parts, "join")
-
-    def apply_ham(o, x, mid, p, q, before):
+    v, p, q = call(join_kernel, m, [own, other], parts, "join")
+
+    def apply_ham(o, x, p, q, before):
         last = before is not None
         p, q = swap(sizes, p, 0, 1), swap(sizes, q, 0, 2)
-        ends = jnp.concatenate([p, x[:1], q], axis=0)
-        a, b = swap(sizes, mid, 1, 0), swap(sizes, mid, 2, 0)
+        ends = jnp.concatenate([p, q[:1]], axis=0)
+        a, b = swap(sizes, x, 1, 0), swap(sizes, x, 2, 0)
         o, a, b = lax.optimization_barrier((o, a, b))
         a_ends, b_ends = swap(sizes, ends, 1, 0), swap(sizes, ends, 2, 0)
-        (acc,) = call(core_kernel, m, [o, mid, ends, a, b], [shaped(block, F32)], "core", 28, scratch=[ext])
+        (acc,) = call(core_kernel, m, [o, x, ends, a, b], [shaped(block, F32)], "core", 32, scratch=[ext])
         arrays = [o, a_ends, b_ends, acc] + ([before] if last else [])
         outs = [shaped(block, BF), tile, tile] if last else parts
-        return o, call(functools.partial(rim_kernel, last=last), m, arrays, outs, "rim", 8)
-
-    o, (first, mid, p, q) = apply_ham(o, v, mid, p, q, None)
-    o, (second, low, high) = apply_ham(o, first, mid, p, q, v)
+        return o, call(functools.partial(rim_kernel, last=last), m, arrays, outs, "rim", 4)
+
+    o, (first, p, q) = apply_ham(o, v, p, q, None)
+    o, (second, low, high) = apply_ham(o, first, p, q, v)
 
     above = shift(sizes, low, 0, -1)
     right_high = shift(sizes, low, -1, -1)
     right_low = shift(sizes, high, -1, 1)
     right = shift(sizes, second, -1, 0)
-    corr, acc = call(corr_kernel, m, [o, second], [shaped(full, F32), shaped(block, F32)], "corr", 15)
+    corr, turned, acc = call(
+        corr_kernel, m, [o, second], [shaped(full, F32), shaped((2 * T, 4 * T), BF), shaped(block, F32)], "corr", 15
+    )
     piece = shaped((members // 2, 1, 5 * T), F32)
     mine, theirs = call(
-        gram_kernel, m, [o, second, above, right_low, right, right_high, acc, corr], [piece, piece], "gram", 29,
+        gram_kernel, m, [o, turned, above, right_low, right, right_high, acc, corr], [piece, piece], "gram", 29,
         scratch=[ext],
     )
 
@@ -392,16 +385,21 @@
     mine = exchange(sizes, jnp.broadcast_to(total, partial.shape))
     theirs = swap(sizes, mine, 0, 1)
 
-    keep, p_keep, send = call(
-        final_kernel, m, [mine, theirs, second],
-        [shaped((4, T, T), BF), shaped((2 * T, T), F32), shaped((8, T, T), BF)], "final", 80,
+    half = (4, T, T)
+    keep, send, x = call(
+        inverse_kernel, m, [mine, theirs, second],
+        [shaped(half, BF), shaped(half, BF), shaped(full, F32)], "inverse", 80,
         scratch=[pltpu.VMEM(full, F32), pltpu.VMEM(full, F32)],
     )
     got = swap_col(sizes, send)
-    ritz = shaped((2, 1, 4, T, T), BF)
-    return tuple(
-        call(assemble_kernel, m, [keep, p_keep, got], [ritz, shaped((2, 2 * T, T), F32)], "assemble")
-    )
+    p_shape = (2 * T, T)
+    p_keep, p_send = call(
+        project_kernel, m, [mine, theirs, x], [shaped(p_shape, F32), shaped(p_shape, BF)], "project", 24
+    )
+    p_got = swap_col(sizes, p_send).astype(F32)
+    ritz = jnp.where(spin == 0, jnp.stack([keep, got]), jnp.stack([got, keep]))
+    projected = jnp.where(spin == 0, jnp.stack([p_keep, p_got]), jnp.stack([p_got, p_keep]))
+    return ritz[:, None], projected
 
 
 def solution(mesh):

time: 157 us -> 155 us (0.987)
  waiting for transfers between devices: 27.9 us -> 22.6 us
  starting transfers between devices: 36.3 us -> 38.4 us
    ppermute x2 -> x3, waiting for transfers between devices: 9.17 us -> 4.08 us  [swap_col(): return lax.ppermute(block, AXES, perm)]
    ppermute x2 -> x3, starting transfers between devices: 3.75 us -> 6.7 us  [swap_col(): return lax.ppermute(block, AXES, perm)]
  transfers between devices with their start and end apart: 20 -> 21, of which waited for: 13 -> 13; matrix products, arithmetic and copies ran while one was open for 1% -> 2% of each run, Pallas kernels for 2% -> 2%
where the time goes in v6:
time: 155 us
  Pallas kernels  47.9 us (31%)
  blocking collectives  38.5 us (25%)
  starting transfers between devices  38.4 us (25%)
  waiting for transfers between devices  22.6 us (15%)
  other arithmetic  3.69 us (2%)
  local copies, waits for them, and re-layouts  3.04 us (2%)
    pallas_call x10, Pallas kernels, call(): pl.pallas_call(kernel, out_shape=outs, grid_spec=pltpu.PrefetchScalarGrid...  47.9 us
    all_to_all x2, blocking collectives, exchange(): lax.all_to_all(pieces, AXES, 0, 0, axis_index_groups=groups, tiled=True)  38.5 us
    ppermute x14, starting transfers between devices, swap(): return lax.ppermute(block, AXES, perm)  26.3 us
    ppermute x14, waiting for transfers between devices, swap(): return lax.ppermute(block, AXES, perm)  13.4 us
    ppermute x3, starting transfers between devices, swap_col(): return lax.ppermute(block, AXES, perm)  6.7 us
    ppermute x4, starting transfers between devices, shift(): lax.ppermute(block, AXES, pairs(sizes, lambda gx, gy: (gx + dx, gy + dy)))  5.39 us
    ppermute x4, waiting for transfers between devices, shift(): lax.ppermute(block, AXES, pairs(sizes, lambda gx, gy: (gx + dx, gy + dy)))  5.09 us
    ppermute x3, waiting for transfers between devices, swap_col(): return lax.ppermute(block, AXES, perm)  4.08 us
  transfers between devices with their start and end apart: 21, of which 13 were waited for; matrix products, arithmetic and copies ran while one was open for 2% of the time, Pallas kernels for 2%

profile of v6, /device:TPU:1, one launch (start us, length us, event | category | flops | bytes accessed | tf_op | source)
XLA Modules:
  0.0 155.0 jit_solution(15385001772037330457)
XLA Ops:
  0.6 1.0 dynamic-slice_bitcast_fusion
  1.6 3.7 %collective-permute-start = (bf16[4,128,128]{2,1,0:T(8,128)(2,1)S(1)}, bf16[4,128,128]{2,1,0:T(8,128)(2,1)S(1)}, u32[]{:S(2)}, u32[]{:S(2)}) collective-permute-start(bf16[4,128,128]{2,1,0:T(8,128)(2,1)S(1)} %get-tuple-element.52), channel_id=1, source_target_pairs={{0,1},{1,0},{2,3},{3,2},{4,5},{5,4},{6,7},{7,6},{8,9},{9,8},{10,11... | collective-permute-start | bytes 393224 | tf_op jit(solution)/shard_map/ppermute | solution.py:59
  6.2 1.0 select_reduce_fusion
  8.3 3.9 %collective-permute-start.4 = (bf16[2,128,256]{2,1,0:T(8,128)(2,1)S(1)}, bf16[2,128,256]{2,1,0:T(8,128)(2,1)S(1)}, u32[]{:S(2)}, u32[]{:S(2)}) collective-permute-start(bf16[2,128,256]{2,1,0:T(8,128)(2,1)S(1)} %get-tuple-element.30), channel_id=1, source_target_pairs={{0,30},{1,31},{2,4},{3,5},{4,2},{5,3},{6,8},{7,9},{8,6},{9,7},{10,... | collective-permute-start | bytes 393224 | tf_op jit(solution)/shard_map/ppermute | solution.py:50
  12.2 2.9 %collective-permute-start.3 = (bf16[1,128,256]{2,1,0:T(8,128)(2,1)S(1)}, bf16[1,128,256]{2,1,0:T(8,128)(2,1)S(1)}, u32[]{:S(2)}, u32[]{:S(2)}) collective-permute-start(bf16[1,128,256]{2,1,0:T(8,128)(2,1)S(1)} %get-tuple-element.29), channel_id=1, source_target_pairs={{0,2},{1,3},{2,0},{3,1},{4,6},{5,7},{6,4},{7,5},{8,10},{9,11},{10,... | collective-permute-start | bytes 196616 | tf_op jit(solution)/shard_map/ppermute | solution.py:50
  15.1 4.9 %collective-permute-start.2 = (bf16[4,128,256]{2,1,0:T(8,128)(2,1)S(1)}, bf16[4,128,256]{2,1,0:T(8,128)(2,1)S(1)}, u32[]{:S(2)}, u32[]{:S(2)}) collective-permute-start(bf16[4,128,256]{2,1,0:T(8,128)(2,1)S(1)} %get-tuple-element.27.x.rest_0_), channel_id=1, source_target_pairs={{0,225},{1,224},{2,227},{3,226},{4,229},{5,228},{6,231},{7,230},{8... | collective-permute-start | bytes 786440 | tf_op jit(solution)/shard_map/ppermute | solution.py:50
  20.1 1.1 collective-permute-start.6
  21.7 1.7 %copy-done = bf16[2,1,4,9,128,128]{5,4,3,2,1,0:T(8,128)(2,1)S(1)} copy-done((bf16[2,1,4,9,128,128]{5,4,3,2,1,0:T(8,128)(2,1)S(1)}, bf16[2,1,4,9,128,128]{5,4,3,2,1,0:T(8,128)(2,1)}, u32[]{:S(2)}) %copy-start) | copy-done | bytes 2359320
  24.2 2.3 %collective-permute-done.2.b = bf16[4,128,256]{2,1,0:T(8,128)(2,1)S(1)} collective-permute-done((bf16[4,128,256]{2,1,0:T(8,128)(2,1)S(1)}, bf16[4,128,256]{2,1,0:T(8,128)(2,1)S(1)}, u32[]{:S(2)}, u32[]{:S(2)}) %collective-permute-start.2) | collective-permute-done | bytes 262176 | tf_op jit(solution)/shard_map/ppermute | solution.py:50
  26.6 1.1 collective-permute-done.1.a
  27.7 1.0 core.2.acc
  29.4 1.1 collective-permute-done.5.a_ends
  31.3 1.6 %collective-permute-start.9 = (bf16[1,128,256]{2,1,0:T(8,128)(2,1)S(1)}, bf16[1,128,256]{2,1,0:T(8,128)(2,1)S(1)}, u32[]{:S(2)}, u32[]{:S(2)}) collective-permute-start(bf16[1,128,256]{2,1,0:T(8,128)(2,1)S(1)} %get-tuple-element.35), channel_id=1, source_target_pairs={{0,2},{1,3},{2,0},{3,1},{4,6},{5,7},{6,4},{7,5},{8,10},{9,11},{10,... | collective-permute-start | bytes 196616 | tf_op jit(solution)/shard_map/ppermute | solution.py:50
  32.9 3.6 %collective-permute-start.8 = (bf16[4,128,256]{2,1,0:T(8,128)(2,1)S(1)}, bf16[4,128,256]{2,1,0:T(8,128)(2,1)S(1)}, u32[]{:S(2)}, u32[]{:S(2)}) collective-permute-start(bf16[4,128,256]{2,1,0:T(8,128)(2,1)S(1)} %get-tuple-element.33.x), channel_id=1, source_target_pairs={{0,225},{1,224},{2,227},{3,226},{4,229},{5,228},{6,231},{7,230},{8... | collective-permute-start | bytes 786440 | tf_op jit(solution)/shard_map/ppermute | solution.py:50
  36.6 3.2 %collective-permute-start.12 = (bf16[2,128,256]{2,1,0:T(8,128)(2,1)S(1)}, bf16[2,128,256]{2,1,0:T(8,128)(2,1)S(1)}, u32[]{:S(2)}, u32[]{:S(2)}) collective-permute-start(bf16[2,128,256]{2,1,0:T(8,128)(2,1)S(1)} %pad_maximum_fusion.1.ends), channel_id=1, source_target_pairs={{0,225},{1,224},{2,227},{3,226},{4,229},{5,228},{6,231},{7,230},{8... | collective-permute-start | bytes 393224 | tf_op jit(solution)/shard_map/ppermute | solution.py:50
  39.8 4.4 %collective-permute-done.8.b = bf16[4,128,256]{2,1,0:T(8,128)(2,1)S(1)} collective-permute-done((bf16[4,128,256]{2,1,0:T(8,128)(2,1)S(1)}, bf16[4,128,256]{2,1,0:T(8,128)(2,1)S(1)}, u32[]{:S(2)}, u32[]{:S(2)}) %collective-permute-start.8) | collective-permute-done | bytes 262176 | tf_op jit(solution)/shard_map/ppermute | solution.py:50
  44.2 1.0 core.3.acc
  45.2 1.8 %collective-permute-done.12.b_ends = bf16[2,128,256]{2,1,0:T(8,128)(2,1)S(1)} collective-permute-done((bf16[2,128,256]{2,1,0:T(8,128)(2,1)S(1)}, bf16[2,128,256]{2,1,0:T(8,128)(2,1)S(1)}, u32[]{:S(2)}, u32[]{:S(2)}) %collective-permute-start.12) | collective-permute-done | bytes 131104 | tf_op jit(solution)/shard_map/ppermute | solution.py:50
  47.7 3.7 %collective-permute-start.15 = (bf16[4,128,256]{2,1,0:T(8,128)(2,1)S(1)}, bf16[4,128,256]{2,1,0:T(8,128)(2,1)S(1)}, u32[]{:S(2)}, u32[]{:S(2)}) collective-permute-start(bf16[4,128,256]{2,1,0:T(8,128)(2,1)S(1)} %get-tuple-element.39.s), channel_id=1, source_target_pairs={{0,225},{1,224},{2,227},{3,226},{4,229},{5,228},{6,231},{7,230},{8... | collective-permute-start | bytes 786440 | tf_op jit(solution)/shard_map/ppermute | solution.py:54
  54.0 4.6 %collective-permute-done.14.right_low = bf16[1,128,256]{2,1,0:T(8,128)(2,1)S(1)} collective-permute-done((bf16[1,128,256]{2,1,0:T(8,128)(2,1)S(1)}, bf16[1,128,256]{2,1,0:T(8,128)(2,1)S(1)}, u32[]{:S(2)}, u32[]{:S(2)}) %collective-permute-start.14) | collective-permute-done | bytes 65568 | tf_op jit(solution)/shard_map/ppermute | solution.py:54
  59.1 1.4 gram.1
  60.6 1.8 %collective-permute-start.17 = (f32[64,1,640]{2,1,0:T(1,128)S(1)}, f32[64,1,640]{2,1,0:T(1,128)S(1)}, u32[]{:S(2)}, u32[]{:S(2)}) collective-permute-start(f32[64,1,640]{2,1,0:T(1,128)S(1)} %get-tuple-element.46), channel_id=1, source_target_pairs={{0,2},{1,3},{2,0},{3,1},{4,6},{5,7},{6,4},{7,5},{8,10},{9,11},{10,... | collective-permute-start | bytes 491528 | tf_op jit(solution)/shard_map/ppermute | solution.py:50
  62.3 1.0 collective-permute-done.17
  63.5 21.9 %all_to_all.10 = f32[64,1,640]{2,1,0:T(1,128)S(1)} all-to-all(f32[64,1,640]{2,1,0:T(1,128)S(1)} %add.59), channel_id=1, replica_groups={{0,4,8,12,16,20,24,28,32,36,40,44,48,52,56,60,65,69,73,77,81,85,89,93,9..., dimensions={0} | all-to-all | bytes 327680 | tf_op jit(solution)/shard_map/all_to_all | solution.py:72
  85.7 16.6 %all_to_all.11.mine = f32[64,1,640]{2,1,0:T(1,128)S(1)} all-to-all(f32[64,1,640]{2,1,0:T(1,128)S(1)} %broadcast_in_dim.12), channel_id=1, replica_groups={{0,4,8,12,16,20,24,28,32,36,40,44,48,52,56,60,65,69,73,77,81,85,89,93,9..., dimensions={0} | all-to-all | bytes 327680 | tf_op jit(solution)/shard_map/all_to_all | solution.py:72
  102.2 2.7 %collective-permute-start.18 = (f32[64,1,640]{2,1,0:T(1,128)S(1)}, f32[64,1,640]{2,1,0:T(1,128)S(1)}, u32[]{:S(2)}, u32[]{:S(2)}) collective-permute-start(f32[64,1,640]{2,1,0:T(1,128)S(1)} %all_to_all.11.mine), channel_id=1, source_target_pairs={{0,2},{1,3},{2,0},{3,1},{4,6},{5,7},{6,4},{7,5},{8,10},{9,11},{10,... | collective-permute-start | bytes 491528 | tf_op jit(solution)/shard_map/ppermute | solution.py:50
  104.9 1.0 collective-permute-done.18.theirs
  106.0 39.2 %inverse.1 = (bf16[4,128,128]{2,1,0:T(8,128)(2,1)S(1)}, bf16[4,128,128]{2,1,0:T(8,128)(2,1)S(1)}, f32[256,256]{1,0:T(8,128)S(1)}) custom-call(s32[40]{0:T(128)S(1)} %concatenate.27.m, f32[64,1,640]{2,1,0:T(1,128)S(1)} %all_to_all.11.mine, f32[64,1,640]{2,1,0:T(1,128)S(1)} %collective-permute-done.18.theirs, bf16[4,128,256]{2,1,0:T(8,128)(2,1)S(1)} %get-tuple-element.39.s), custom_call_target="tpu_custom_call" | custom-call | flops 671088640 | bytes 1114112 | tf_op jit(solution)/shard_map/inverse/pallas_call | solution.py:303
  145.2 1.4 project.1
  146.7 3.0 %collective-permute-start.19 = (bf16[4,128,128]{2,1,0:T(8,128)(2,1)S(1)}, bf16[4,128,128]{2,1,0:T(8,128)(2,1)S(1)}, u32[]{:S(2)}, u32[]{:S(2)}) collective-permute-start(bf16[4,128,128]{2,1,0:T(8,128)(2,1)S(1)} %get-tuple-element.48), channel_id=1, source_target_pairs={{0,1},{1,0},{2,3},{3,2},{4,5},{5,4},{6,7},{7,6},{8,9},{9,8},{10,11... | collective-permute-start | bytes 393224 | tf_op jit(solution)/shard_map/ppermute | solution.py:59
  149.6 1.6 %collective-permute-done.20 = bf16[256,128]{1,0:T(8,128)(2,1)S(1)} collective-permute-done((bf16[256,128]{1,0:T(8,128)(2,1)S(1)}, bf16[256,128]{1,0:T(8,128)(2,1)S(1)}, u32[]{:S(2)}, u32[]{:S(2)}) %collective-permute-start.20) | collective-permute-done | bytes 65568 | tf_op jit(solution)/shard_map/ppermute | solution.py:59
  152.0 2.3 %collective-permute-done.19 = bf16[4,128,128]{2,1,0:T(8,128)(2,1)S(1)} collective-permute-done((bf16[4,128,128]{2,1,0:T(8,128)(2,1)S(1)}, bf16[4,128,128]{2,1,0:T(8,128)(2,1)S(1)}, u32[]{:S(2)}, u32[]{:S(2)}) %collective-permute-start.19) | collective-permute-done | bytes 131104 | tf_op jit(solution)/shard_map/ppermute | solution.py:59
  (45 shorter events, 10.7 us)
Async XLA Ops:
  1.6 6.0 %collective-permute-start = (bf16[4,128,128]{2,1,0:T(8,128)(2,1)S(1)}, bf16[4,128,128]{2,1,0:T(8,128)(2,1)S(1)}, u32[]{:S(2)}, u32[]{:S(2)}) collective-permute-start(bf16[4,128,128]{2,1,0:T(8,128)(2,1)S(1)} %get-tuple-element.52), channel_id=1, source_target_pairs={{0,1},{1,0},{2,3},{3,2},{4,5},{5,4},{6,7},{7,6},{8,9},{9,8},{10,11... | collective-permute-start | bytes 393224 | tf_op jit(solution)/shard_map/ppermute | solution.py:59
  8.3 11.8 %collective-permute-start.4 = (bf16[2,128,256]{2,1,0:T(8,128)(2,1)S(1)}, bf16[2,128,256]{2,1,0:T(8,128)(2,1)S(1)}, u32[]{:S(2)}, u32[]{:S(2)}) collective-permute-start(bf16[2,128,256]{2,1,0:T(8,128)(2,1)S(1)} %get-tuple-element.30), channel_id=1, source_target_pairs={{0,30},{1,31},{2,4},{3,5},{4,2},{5,3},{6,8},{7,9},{8,6},{9,7},{10,... | collective-permute-start | bytes 393224 | tf_op jit(solution)/shard_map/ppermute | solution.py:50
  12.2 7.8 %collective-permute-start.3 = (bf16[1,128,256]{2,1,0:T(8,128)(2,1)S(1)}, bf16[1,128,256]{2,1,0:T(8,128)(2,1)S(1)}, u32[]{:S(2)}, u32[]{:S(2)}) collective-permute-start(bf16[1,128,256]{2,1,0:T(8,128)(2,1)S(1)} %get-tuple-element.29), channel_id=1, source_target_pairs={{0,2},{1,3},{2,0},{3,1},{4,6},{5,7},{6,4},{7,5},{8,10},{9,11},{10,... | collective-permute-start | bytes 196616 | tf_op jit(solution)/shard_map/ppermute | solution.py:50
  15.1 11.5 %collective-permute-start.2 = (bf16[4,128,256]{2,1,0:T(8,128)(2,1)S(1)}, bf16[4,128,256]{2,1,0:T(8,128)(2,1)S(1)}, u32[]{:S(2)}, u32[]{:S(2)}) collective-permute-start(bf16[4,128,256]{2,1,0:T(8,128)(2,1)S(1)} %get-tuple-element.27.x.rest_0_), channel_id=1, source_target_pairs={{0,225},{1,224},{2,227},{3,226},{4,229},{5,228},{6,231},{7,230},{8... | collective-permute-start | bytes 786440 | tf_op jit(solution)/shard_map/ppermute | solution.py:50
  20.0 7.6 %collective-permute-start.1 = (bf16[4,128,256]{2,1,0:T(8,128)(2,1)S(1)}, bf16[4,128,256]{2,1,0:T(8,128)(2,1)S(1)}, u32[]{:S(2)}, u32[]{:S(2)}) collective-permute-start(bf16[4,128,256]{2,1,0:T(8,128)(2,1)S(1)} %get-tuple-element.27.x.rest_0_), channel_id=1, source_target_pairs={{0,32},{1,33},{2,34},{3,35},{4,36},{5,37},{6,38},{7,39},{8,40},{9,... | collective-permute-start | bytes 786440 | tf_op jit(solution)/shard_map/ppermute | solution.py:50
  20.1 9.3 %collective-permute-start.6 = (bf16[2,128,256]{2,1,0:T(8,128)(2,1)S(1)}, bf16[2,128,256]{2,1,0:T(8,128)(2,1)S(1)}, u32[]{:S(2)}, u32[]{:S(2)}) collective-permute-start(bf16[2,128,256]{2,1,0:T(8,128)(2,1)S(1)} %pad_maximum_fusion.ends), channel_id=1, source_target_pairs={{0,225},{1,224},{2,227},{3,226},{4,229},{5,228},{6,231},{7,230},{8... | collective-permute-start | bytes 393224 | tf_op jit(solution)/shard_map/ppermute | solution.py:50
  21.2 9.3 %collective-permute-start.5 = (bf16[2,128,256]{2,1,0:T(8,128)(2,1)S(1)}, bf16[2,128,256]{2,1,0:T(8,128)(2,1)S(1)}, u32[]{:S(2)}, u32[]{:S(2)}) collective-permute-start(bf16[2,128,256]{2,1,0:T(8,128)(2,1)S(1)} %pad_maximum_fusion.ends), channel_id=1, source_target_pairs={{0,32},{1,33},{2,34},{3,35},{4,36},{5,37},{6,38},{7,39},{8,40},{9,... | collective-permute-start | bytes 393224 | tf_op jit(solution)/shard_map/ppermute | solution.py:50
  21.7 1.7 %copy-start = (bf16[2,1,4,9,128,128]{5,4,3,2,1,0:T(8,128)(2,1)S(1)}, bf16[2,1,4,9,128,128]{5,4,3,2,1,0:T(8,128)(2,1)}, u32[]{:S(2)}) copy-start(bf16[2,1,4,9,128,128]{5,4,3,2,1,0:T(8,128)(2,1)} %h.1) | copy-start | bytes 7077892
  31.2 5.3 %collective-permute-start.10 = (bf16[2,128,256]{2,1,0:T(8,128)(2,1)S(1)}, bf16[2,128,256]{2,1,0:T(8,128)(2,1)S(1)}, u32[]{:S(2)}, u32[]{:S(2)}) collective-permute-start(bf16[2,128,256]{2,1,0:T(8,128)(2,1)S(1)} %get-tuple-element.36), channel_id=1, source_target_pairs={{0,30},{1,31},{2,4},{3,5},{4,2},{5,3},{6,8},{7,9},{8,6},{9,7},{10,... | collective-permute-start | bytes 393224 | tf_op jit(solution)/shard_map/ppermute | solution.py:50
  31.3 5.2 %collective-permute-start.9 = (bf16[1,128,256]{2,1,0:T(8,128)(2,1)S(1)}, bf16[1,128,256]{2,1,0:T(8,128)(2,1)S(1)}, u32[]{:S(2)}, u32[]{:S(2)}) collective-permute-start(bf16[1,128,256]{2,1,0:T(8,128)(2,1)S(1)} %get-tuple-element.35), channel_id=1, source_target_pairs={{0,2},{1,3},{2,0},{3,1},{4,6},{5,7},{6,4},{7,5},{8,10},{9,11},{10,... | collective-permute-start | bytes 196616 | tf_op jit(solution)/shard_map/ppermute | solution.py:50
  32.9 11.3 %collective-permute-start.8 = (bf16[4,128,256]{2,1,0:T(8,128)(2,1)S(1)}, bf16[4,128,256]{2,1,0:T(8,128)(2,1)S(1)}, u32[]{:S(2)}, u32[]{:S(2)}) collective-permute-start(bf16[4,128,256]{2,1,0:T(8,128)(2,1)S(1)} %get-tuple-element.33.x), channel_id=1, source_target_pairs={{0,225},{1,224},{2,227},{3,226},{4,229},{5,228},{6,231},{7,230},{8... | collective-permute-start | bytes 786440 | tf_op jit(solution)/shard_map/ppermute | solution.py:50
  36.5 7.6 %collective-permute-start.7 = (bf16[4,128,256]{2,1,0:T(8,128)(2,1)S(1)}, bf16[4,128,256]{2,1,0:T(8,128)(2,1)S(1)}, u32[]{:S(2)}, u32[]{:S(2)}) collective-permute-start(bf16[4,128,256]{2,1,0:T(8,128)(2,1)S(1)} %get-tuple-element.33.x), channel_id=1, source_target_pairs={{0,32},{1,33},{2,34},{3,35},{4,36},{5,37},{6,38},{7,39},{8,40},{9,... | collective-permute-start | bytes 786440 | tf_op jit(solution)/shard_map/ppermute | solution.py:50
  36.6 10.4 %collective-permute-start.12 = (bf16[2,128,256]{2,1,0:T(8,128)(2,1)S(1)}, bf16[2,128,256]{2,1,0:T(8,128)(2,1)S(1)}, u32[]{:S(2)}, u32[]{:S(2)}) collective-permute-start(bf16[2,128,256]{2,1,0:T(8,128)(2,1)S(1)} %pad_maximum_fusion.1.ends), channel_id=1, source_target_pairs={{0,225},{1,224},{2,227},{3,226},{4,229},{5,228},{6,231},{7,230},{8... | collective-permute-start | bytes 393224 | tf_op jit(solution)/shard_map/ppermute | solution.py:50
  39.8 7.2 %collective-permute-start.11 = (bf16[2,128,256]{2,1,0:T(8,128)(2,1)S(1)}, bf16[2,128,256]{2,1,0:T(8,128)(2,1)S(1)}, u32[]{:S(2)}, u32[]{:S(2)}) collective-permute-start(bf16[2,128,256]{2,1,0:T(8,128)(2,1)S(1)} %pad_maximum_fusion.1.ends), channel_id=1, source_target_pairs={{0,32},{1,33},{2,34},{3,35},{4,36},{5,37},{6,38},{7,39},{8,40},{9,... | collective-permute-start | bytes 393224 | tf_op jit(solution)/shard_map/ppermute | solution.py:50
  47.7 11.4 %collective-permute-start.15 = (bf16[4,128,256]{2,1,0:T(8,128)(2,1)S(1)}, bf16[4,128,256]{2,1,0:T(8,128)(2,1)S(1)}, u32[]{:S(2)}, u32[]{:S(2)}) collective-permute-start(bf16[4,128,256]{2,1,0:T(8,128)(2,1)S(1)} %get-tuple-element.39.s), channel_id=1, source_target_pairs={{0,225},{1,224},{2,227},{3,226},{4,229},{5,228},{6,231},{7,230},{8... | collective-permute-start | bytes 786440 | tf_op jit(solution)/shard_map/ppermute | solution.py:54
  51.5 7.2 %collective-permute-start.14 = (bf16[1,128,256]{2,1,0:T(8,128)(2,1)S(1)}, bf16[1,128,256]{2,1,0:T(8,128)(2,1)S(1)}, u32[]{:S(2)}, u32[]{:S(2)}) collective-permute-start(bf16[1,128,256]{2,1,0:T(8,128)(2,1)S(1)} %get-tuple-element.42), channel_id=1, source_target_pairs={{0,227},{1,226},{2,229},{3,228},{4,231},{5,230},{6,233},{7,232},{8... | collective-permute-start | bytes 196616 | tf_op jit(solution)/shard_map/ppermute | solution.py:54
  52.2 6.9 %collective-permute-start.16 = (bf16[1,128,256]{2,1,0:T(8,128)(2,1)S(1)}, bf16[1,128,256]{2,1,0:T(8,128)(2,1)S(1)}, u32[]{:S(2)}, u32[]{:S(2)}) collective-permute-start(bf16[1,128,256]{2,1,0:T(8,128)(2,1)S(1)} %get-tuple-element.41), channel_id=1, source_target_pairs={{0,255},{1,254},{2,225},{3,224},{4,227},{5,226},{6,229},{7,228},{8... | collective-permute-start | bytes 196616 | tf_op jit(solution)/shard_map/ppermute | solution.py:54
  52.5 6.6 %collective-permute-start.13 = (bf16[1,128,256]{2,1,0:T(8,128)(2,1)S(1)}, bf16[1,128,256]{2,1,0:T(8,128)(2,1)S(1)}, u32[]{:S(2)}, u32[]{:S(2)}) collective-permute-start(bf16[1,128,256]{2,1,0:T(8,128)(2,1)S(1)} %get-tuple-element.41), channel_id=1, source_target_pairs={{0,30},{1,31},{2,0},{3,1},{4,2},{5,3},{6,4},{7,5},{8,6},{9,7},{10,... | collective-permute-start | bytes 196616 | tf_op jit(solution)/shard_map/ppermute | solution.py:54
  60.6 2.8 %collective-permute-start.17 = (f32[64,1,640]{2,1,0:T(1,128)S(1)}, f32[64,1,640]{2,1,0:T(1,128)S(1)}, u32[]{:S(2)}, u32[]{:S(2)}) collective-permute-start(f32[64,1,640]{2,1,0:T(1,128)S(1)} %get-tuple-element.46), channel_id=1, source_target_pairs={{0,2},{1,3},{2,0},{3,1},{4,6},{5,7},{6,4},{7,5},{8,10},{9,11},{10,... | collective-permute-start | bytes 491528 | tf_op jit(solution)/shard_map/ppermute | solution.py:50
  102.2 3.7 %collective-permute-start.18 = (f32[64,1,640]{2,1,0:T(1,128)S(1)}, f32[64,1,640]{2,1,0:T(1,128)S(1)}, u32[]{:S(2)}, u32[]{:S(2)}) collective-permute-start(f32[64,1,640]{2,1,0:T(1,128)S(1)} %all_to_all.11.mine), channel_id=1, source_target_pairs={{0,2},{1,3},{2,0},{3,1},{4,6},{5,7},{6,4},{7,5},{8,10},{9,11},{10,... | collective-permute-start | bytes 491528 | tf_op jit(solution)/shard_map/ppermute | solution.py:50
  146.6 4.7 %collective-permute-start.20 = (bf16[256,128]{1,0:T(8,128)(2,1)S(1)}, bf16[256,128]{1,0:T(8,128)(2,1)S(1)}, u32[]{:S(2)}, u32[]{:S(2)}) collective-permute-start(bf16[256,128]{1,0:T(8,128)(2,1)S(1)} %get-tuple-element.51), channel_id=1, source_target_pairs={{0,1},{1,0},{2,3},{3,2},{4,5},{5,4},{6,7},{7,6},{8,9},{9,8},{10,11... | collective-permute-start | bytes 196616 | tf_op jit(solution)/shard_map/ppermute | solution.py:59
  146.7 7.6 %collective-permute-start.19 = (bf16[4,128,128]{2,1,0:T(8,128)(2,1)S(1)}, bf16[4,128,128]{2,1,0:T(8,128)(2,1)S(1)}, u32[]{:S(2)}, u32[]{:S(2)}) collective-permute-start(bf16[4,128,128]{2,1,0:T(8,128)(2,1)S(1)} %get-tuple-element.48), channel_id=1, source_target_pairs={{0,1},{1,0},{2,3},{3,2},{4,5},{5,4},{6,7},{7,6},{8,9},{9,8},{10,11... | collective-permute-start | bytes 393224 | tf_op jit(solution)/shard_map/ppermute | solution.py:59

commit v7 on v6

--- a/solution.py
+++ b/solution.py
@@ -1,5 +1,3 @@
-import functools
-
 import jax
 import jax.numpy as jnp
 from jax import lax
@@ -86,12 +84,20 @@
     return dot(ah, bh, dims) + (dot(ah, bl, dims) + dot(al, bh, dims))
 
 
-def order_kernel(m, h, o):
+def order_kernel(m, h, o, p, q):
+    def block(tile, at):
+        slot = m[tile * 9 + at]
+        found = h[0, 0, tile, jnp.maximum(slot, 0)]
+        return jnp.where(slot >= 0, found, jnp.zeros_like(found))
+
     for tile in range(4):
         for at in range(9):
-            slot = m[tile * 9 + at]
-            block = h[0, 0, tile, jnp.maximum(slot, 0)]
-            o[tile, :, at * T : (at + 1) * T] = jnp.where(slot >= 0, block, jnp.zeros_like(block))
+            o[tile, :, at * T : (at + 1) * T] = block(tile, at)
+    even = m[PAR_Y] == 0
+    side = 1 + m[PAR_X]
+    down, up = block(0, side * 3), block(3, side * 3 + 2)
+    p[...] = jnp.where(even, up, down)
+    q[...] = jnp.where(even, down, up)
 
 
 def blocks(o, tile, sides, dys):
@@ -140,11 +146,8 @@
         acc[tile] = total + product(o, tile, (1, 2), at, sources)
 
 
-def rim_kernel(m, o, a_ends, b_ends, acc, *rest, last):
-    if last:
-        before, out, first_out, last_out = rest
-    else:
-        out, p, q = rest
+def rim_kernel(m, o, a_ends, b_ends, acc, *rest):
+    *before, out, p, q = rest
     low, high = zip(ends_of(m, a_ends), ends_of(m, b_ends))
     for tile in range(4):
         total = acc[tile]
@@ -152,26 +155,23 @@
             total += product(o, tile, (1, 2), (0,), low)
         if tile == 3:
             total += product(o, tile, (1, 2), (5,), high)
-        if last:
-            out[tile] = (total - before[tile].astype(F32)).astype(BF)
+        if before:
+            out[tile] = (total - before[0][tile].astype(F32)).astype(BF)
         else:
             out[tile] = (0.5 * total).astype(BF)
-    if last:
-        first_out[...] = out[0:1]
-        last_out[...] = out[3:4]
-    else:
-        store_edges(m, out, p, q)
-
-
-def corr_kernel(m, o, s, corr, turned, acc):
+    store_edges(m, out, p, q)
+
+
+def corr_kernel(m, o, s, p, q, corr, turned, acc):
     flat = s[...].reshape(4 * T, 2 * T)
-    turned[...] = flat.T
-    corr[...] = dot(turned[...], flat)
+    turned[:, : 4 * T] = flat.T
+    turned[:, 4 * T : 5 * T] = p[0].T
+    turned[:, 5 * T :] = q[0].T
+    corr[...] = dot(turned[:, : 4 * T], flat)
+    above = jnp.where(m[PAR_Y] == 0, p[0], q[0])
     for tile in range(4):
         total = 0.5 * dot(blocks(o, tile, (0,), (1,)), s[tile])
-        if tile < 3:
-            total += dot(blocks(o, tile, (0,), (2,)), s[tile + 1])
-        acc[tile] = total
+        acc[tile] = total + dot(blocks(o, tile, (0,), (2,)), s[tile + 1] if tile < 3 else above)
 
 
 def places():
@@ -179,17 +179,15 @@
     return lax.broadcasted_iota(jnp.int32, shape, 0), lax.broadcasted_iota(jnp.int32, shape, 1)
 
 
-def gram_kernel(m, o, turned, above, right_low, right, right_high, acc, corr, mine, theirs, ext):
-    ext[0:1] = right_low[...]
-    ext[1:5] = right[...]
-    ext[5:6] = right_high[...]
+def gram_kernel(m, o, turned, right, h_p, h_q, acc, corr, mine, theirs):
     side = 1 + m[PAR_X]
     parts = []
     for tile in range(4):
-        part = acc[tile] + product(o, tile, (side,), range(tile, tile + 3), [ext[tile : tile + 3]])
-        if tile == 3:
-            part += product(o, tile, (0,), (5,), [above[...]])
-        parts.append(part)
+        at = [place for place in range(tile, tile + 3) if 1 <= place <= 4]
+        parts.append(acc[tile] + product(o, tile, (side,), at, [right[at[0] - 1 : at[-1]]]))
+    even = m[PAR_Y] == 0
+    parts.append(dot(h_p[...], right[jnp.where(even, 3, 0)]))
+    parts.append(dot(h_q[...], right[jnp.where(even, 0, 3)]))
     high, low = split(jnp.concatenate(parts, axis=0))
     half = dot(turned[...], high) + dot(turned[...], low)
     coupling = half + half.T
@@ -345,38 +343,39 @@
     other = swap_col(sizes, lax.dynamic_index_in_dim(start_block, 1 - spin, 0, keepdims=False)[0])
     own = lax.dynamic_index_in_dim(start_block, spin, 0, keepdims=False)[0]
     spin_block = pl.BlockSpec((1,) + hamiltonian.shape[1:], lambda i, m: (m[SPIN], 0, 0, 0, 0, 0))
-    (o,) = call(order_kernel, m, [hamiltonian], [shaped((4, T, NB * T), BF)], "order", specs=[spin_block])
+    corner = shaped((T, T), BF)
+    o, h_p, h_q = call(
+        order_kernel, m, [hamiltonian], [shaped((4, T, NB * T), BF), corner, corner], "order", specs=[spin_block]
+    )
+    h_p, h_q = swap(sizes, h_p, 0, 1), swap(sizes, h_q, 0, 2)
     tile = shaped((1, T, 2 * T), BF)
     parts = [shaped(block, BF), tile, shaped((2, T, 2 * T), BF)]
     ext = pltpu.VMEM((6, T, 2 * T), BF)
     v, p, q = call(join_kernel, m, [own, other], parts, "join")
 
-    def apply_ham(o, x, p, q, before):
-        last = before is not None
+    def apply_ham(o, x, p, q, before, *kept):
         p, q = swap(sizes, p, 0, 1), swap(sizes, q, 0, 2)
         ends = jnp.concatenate([p, q[:1]], axis=0)
         a, b = swap(sizes, x, 1, 0), swap(sizes, x, 2, 0)
         o, a, b = lax.optimization_barrier((o, a, b))
         a_ends, b_ends = swap(sizes, ends, 1, 0), swap(sizes, ends, 2, 0)
         (acc,) = call(core_kernel, m, [o, x, ends, a, b], [shaped(block, F32)], "core", 32, scratch=[ext])
-        arrays = [o, a_ends, b_ends, acc] + ([before] if last else [])
-        outs = [shaped(block, BF), tile, tile] if last else parts
-        return o, call(functools.partial(rim_kernel, last=last), m, arrays, outs, "rim", 4)
-
-    o, (first, p, q) = apply_ham(o, v, p, q, None)
-    o, (second, low, high) = apply_ham(o, first, p, q, v)
-
-    above = shift(sizes, low, 0, -1)
-    right_high = shift(sizes, low, -1, -1)
-    right_low = shift(sizes, high, -1, 1)
+        acc, *kept = lax.optimization_barrier((acc, *kept))
+        out = call(rim_kernel, m, [o, a_ends, b_ends, acc, *before], parts, "rim", 4)
+        return o, kept, out
+
+    o, _, (first, p, q) = apply_ham(o, v, p, q, [])
+    o, (h_p, h_q), (second, p, q) = apply_ham(o, first, p, q, [v], h_p, h_q)
+
     right = shift(sizes, second, -1, 0)
+    p, q = swap(sizes, p, 0, 1), swap(sizes, q, 0, 2)
     corr, turned, acc = call(
-        corr_kernel, m, [o, second], [shaped(full, F32), shaped((2 * T, 4 * T), BF), shaped(block, F32)], "corr", 15
+        corr_kernel, m, [o, second, p, q],
+        [shaped(full, F32), shaped((2 * T, 6 * T), BF), shaped(block, F32)], "corr", 16,
     )
     piece = shaped((members // 2, 1, 5 * T), F32)
     mine, theirs = call(
-        gram_kernel, m, [o, turned, above, right_low, right, right_high, acc, corr], [piece, piece], "gram", 29,
-        scratch=[ext],
+        gram_kernel, m, [o, turned, right, h_p, h_q, acc, corr], [piece, piece], "gram", 30
     )
 
     rows = members * second.shape[0] * second.shape[1]

time: 155 us -> 154 us (level)
  starting transfers between devices: 38.4 us -> 44.6 us
  waiting for transfers between devices: 22.6 us -> 16.7 us
  blocking collectives: 38.5 us -> 36.6 us
    ppermute x14 -> x18, starting transfers between devices: 26.3 us -> 34.4 us  [swap(): return lax.ppermute(block, AXES, perm)]
    ppermute x4 -> x1, waiting for transfers between devices: 5.09 us -> 0.01 us  [shift(): lax.ppermute(block, AXES, pairs(sizes, lambda gx, gy: (gx + dx, gy + dy)))]
    all_to_all x2, blocking collectives: 38.5 us -> 36.6 us  [exchange(): lax.all_to_all(pieces, AXES, 0, 0, axis_index_groups=groups, tiled=True)]
    ppermute x4 -> x1, starting transfers between devices: 5.39 us -> 3.54 us  [shift(): lax.ppermute(block, AXES, pairs(sizes, lambda gx, gy: (gx + dx, gy + dy)))]
    ppermute x14 -> x18, waiting for transfers between devices: 13.4 us -> 12.7 us  [swap(): return lax.ppermute(block, AXES, perm)]
  transfers between devices with their start and end apart: 21 -> 22, of which waited for: 13 -> 13; matrix products, arithmetic and copies ran while one was open for 2% -> 2% of each run, Pallas kernels for 2% -> 2%
where the time goes in v7:
time: 154 us; the launch traced here: 153 us
  Pallas kernels  47.9 us (31%)
  starting transfers between devices  44.6 us (29%)
  blocking collectives  36.6 us (24%)
  waiting for transfers between devices  16.7 us (11%)
  other arithmetic  3.69 us (2%)
  local copies, waits for them, and re-layouts  3.04 us (2%)
    pallas_call x10, Pallas kernels, call(): pl.pallas_call(kernel, out_shape=outs, grid_spec=pltpu.PrefetchScalarGrid...  47.9 us
    all_to_all x2, blocking collectives, exchange(): lax.all_to_all(pieces, AXES, 0, 0, axis_index_groups=groups, tiled=True)  36.6 us
    ppermute x18, starting transfers between devices, swap(): return lax.ppermute(block, AXES, perm)  34.4 us
    ppermute x18, waiting for transfers between devices, swap(): return lax.ppermute(block, AXES, perm)  12.7 us
    ppermute x3, starting transfers between devices, swap_col(): return lax.ppermute(block, AXES, perm)  6.7 us
    ppermute x3, waiting for transfers between devices, swap_col(): return lax.ppermute(block, AXES, perm)  4.07 us
    ppermute x1, starting transfers between devices, shift(): lax.ppermute(block, AXES, pairs(sizes, lambda gx, gy: (gx + dx, gy + dy)))  3.54 us
  transfers between devices with their start and end apart: 22, of which 13 were waited for; matrix products, arithmetic and copies ran while one was open for 2% of the time, Pallas kernels for 2%

profile of v7, /device:TPU:1, one launch (start us, length us, event | category | flops | bytes accessed | tf_op | source)
XLA Modules:
  0.0 153.5 jit_solution(18013480965280387034)
XLA Ops:
  1.6 3.7 %collective-permute-start = (bf16[4,128,128]{2,1,0:T(8,128)(2,1)S(1)}, bf16[4,128,128]{2,1,0:T(8,128)(2,1)S(1)}, u32[]{:S(2)}, u32[]{:S(2)}) collective-permute-start(bf16[4,128,128]{2,1,0:T(8,128)(2,1)S(1)} %get-tuple-element.64), channel_id=1, source_target_pairs={{0,1},{1,0},{2,3},{3,2},{4,5},{5,4},{6,7},{7,6},{8,9},{9,8},{10,11... | collective-permute-start | bytes 393224 | tf_op jit(solution)/shard_map/ppermute | solution.py:57
  8.3 3.9 %collective-permute-start.4 = (bf16[2,128,256]{2,1,0:T(8,128)(2,1)S(1)}, bf16[2,128,256]{2,1,0:T(8,128)(2,1)S(1)}, u32[]{:S(2)}, u32[]{:S(2)}) collective-permute-start(bf16[2,128,256]{2,1,0:T(8,128)(2,1)S(1)} %get-tuple-element.37), channel_id=1, source_target_pairs={{0,30},{1,31},{2,4},{3,5},{4,2},{5,3},{6,8},{7,9},{8,6},{9,7},{10,... | collective-permute-start | bytes 393224 | tf_op jit(solution)/shard_map/ppermute | solution.py:48
  12.2 2.9 %collective-permute-start.3 = (bf16[1,128,256]{2,1,0:T(8,128)(2,1)S(1)}, bf16[1,128,256]{2,1,0:T(8,128)(2,1)S(1)}, u32[]{:S(2)}, u32[]{:S(2)}) collective-permute-start(bf16[1,128,256]{2,1,0:T(8,128)(2,1)S(1)} %get-tuple-element.36), channel_id=1, source_target_pairs={{0,2},{1,3},{2,0},{3,1},{4,6},{5,7},{6,4},{7,5},{8,10},{9,11},{10,... | collective-permute-start | bytes 196616 | tf_op jit(solution)/shard_map/ppermute | solution.py:48
  15.1 4.9 %collective-permute-start.2 = (bf16[4,128,256]{2,1,0:T(8,128)(2,1)S(1)}, bf16[4,128,256]{2,1,0:T(8,128)(2,1)S(1)}, u32[]{:S(2)}, u32[]{:S(2)}) collective-permute-start(bf16[4,128,256]{2,1,0:T(8,128)(2,1)S(1)} %get-tuple-element.34.x.rest_0_), channel_id=1, source_target_pairs={{0,225},{1,224},{2,227},{3,226},{4,229},{5,228},{6,231},{7,230},{8... | collective-permute-start | bytes 786440 | tf_op jit(solution)/shard_map/ppermute | solution.py:48
  20.1 1.1 collective-permute-start.6
  21.7 1.7 %copy-done = bf16[2,1,4,9,128,128]{5,4,3,2,1,0:T(8,128)(2,1)S(1)} copy-done((bf16[2,1,4,9,128,128]{5,4,3,2,1,0:T(8,128)(2,1)S(1)}, bf16[2,1,4,9,128,128]{5,4,3,2,1,0:T(8,128)(2,1)}, u32[]{:S(2)}) %copy-start) | copy-done | bytes 2359320
  24.3 2.3 %collective-permute-done.2.b = bf16[4,128,256]{2,1,0:T(8,128)(2,1)S(1)} collective-permute-done((bf16[4,128,256]{2,1,0:T(8,128)(2,1)S(1)}, bf16[4,128,256]{2,1,0:T(8,128)(2,1)S(1)}, u32[]{:S(2)}, u32[]{:S(2)}) %collective-permute-start.2) | collective-permute-done | bytes 262176 | tf_op jit(solution)/shard_map/ppermute | solution.py:48
  26.6 1.1 collective-permute-done.1.a
  27.7 1.0 core.2.acc
  29.4 1.1 collective-permute-done.5.a_ends
  31.3 1.6 %collective-permute-start.9 = (bf16[1,128,256]{2,1,0:T(8,128)(2,1)S(1)}, bf16[1,128,256]{2,1,0:T(8,128)(2,1)S(1)}, u32[]{:S(2)}, u32[]{:S(2)}) collective-permute-start(bf16[1,128,256]{2,1,0:T(8,128)(2,1)S(1)} %get-tuple-element.42), channel_id=1, source_target_pairs={{0,2},{1,3},{2,0},{3,1},{4,6},{5,7},{6,4},{7,5},{8,10},{9,11},{10,... | collective-permute-start | bytes 196616 | tf_op jit(solution)/shard_map/ppermute | solution.py:48
  32.9 3.6 %collective-permute-start.8 = (bf16[4,128,256]{2,1,0:T(8,128)(2,1)S(1)}, bf16[4,128,256]{2,1,0:T(8,128)(2,1)S(1)}, u32[]{:S(2)}, u32[]{:S(2)}) collective-permute-start(bf16[4,128,256]{2,1,0:T(8,128)(2,1)S(1)} %get-tuple-element.40.x), channel_id=1, source_target_pairs={{0,225},{1,224},{2,227},{3,226},{4,229},{5,228},{6,231},{7,230},{8... | collective-permute-start | bytes 786440 | tf_op jit(solution)/shard_map/ppermute | solution.py:48
  36.6 3.2 %collective-permute-start.12 = (bf16[2,128,256]{2,1,0:T(8,128)(2,1)S(1)}, bf16[2,128,256]{2,1,0:T(8,128)(2,1)S(1)}, u32[]{:S(2)}, u32[]{:S(2)}) collective-permute-start(bf16[2,128,256]{2,1,0:T(8,128)(2,1)S(1)} %pad_maximum_fusion.1.ends), channel_id=1, source_target_pairs={{0,225},{1,224},{2,227},{3,226},{4,229},{5,228},{6,231},{7,230},{8... | collective-permute-start | bytes 393224 | tf_op jit(solution)/shard_map/ppermute | solution.py:48
  39.8 2.0 %collective-permute-start.13 = (bf16[128,128]{1,0:T(8,128)(2,1)S(1)}, bf16[128,128]{1,0:T(8,128)(2,1)S(1)}, u32[]{:S(2)}, u32[]{:S(2)}) collective-permute-start(bf16[128,128]{1,0:T(8,128)(2,1)S(1)} %get-tuple-element.46), channel_id=1, source_target_pairs={{0,2},{1,3},{2,0},{3,1},{4,6},{5,7},{6,4},{7,5},{8,10},{9,11},{10,... | collective-permute-start | bytes 98312 | tf_op jit(solution)/shard_map/ppermute | solution.py:48
  41.8 2.4 %collective-permute-done.8.b = bf16[4,128,256]{2,1,0:T(8,128)(2,1)S(1)} collective-permute-done((bf16[4,128,256]{2,1,0:T(8,128)(2,1)S(1)}, bf16[4,128,256]{2,1,0:T(8,128)(2,1)S(1)}, u32[]{:S(2)}, u32[]{:S(2)}) %collective-permute-start.8) | collective-permute-done | bytes 262176 | tf_op jit(solution)/shard_map/ppermute | solution.py:48
  44.2 1.3 collective-permute-start.14
  46.5 1.1 collective-permute-done.14.h_q
  48.5 3.5 %collective-permute-start.17 = (bf16[4,128,256]{2,1,0:T(8,128)(2,1)S(1)}, bf16[4,128,256]{2,1,0:T(8,128)(2,1)S(1)}, u32[]{:S(2)}, u32[]{:S(2)}) collective-permute-start(bf16[4,128,256]{2,1,0:T(8,128)(2,1)S(1)} %get-tuple-element.49.s), channel_id=1, source_target_pairs={{0,225},{1,224},{2,227},{3,226},{4,229},{5,228},{6,231},{7,230},{8... | collective-permute-start | bytes 786440 | tf_op jit(solution)/shard_map/ppermute | solution.py:52
  52.0 1.6 %collective-permute-start.16 = (bf16[2,128,256]{2,1,0:T(8,128)(2,1)S(1)}, bf16[2,128,256]{2,1,0:T(8,128)(2,1)S(1)}, u32[]{:S(2)}, u32[]{:S(2)}) collective-permute-start(bf16[2,128,256]{2,1,0:T(8,128)(2,1)S(1)} %get-tuple-element.51), channel_id=1, source_target_pairs={{0,30},{1,31},{2,4},{3,5},{4,2},{5,3},{6,8},{7,9},{8,6},{9,7},{10,... | collective-permute-start | bytes 393224 | tf_op jit(solution)/shard_map/ppermute | solution.py:48
  53.6 1.2 collective-permute-start.15
  57.6 1.3 gram.1
  59.0 3.7 %collective-permute-start.18 = (f32[64,1,640]{2,1,0:T(1,128)S(1)}, f32[64,1,640]{2,1,0:T(1,128)S(1)}, u32[]{:S(2)}, u32[]{:S(2)}) collective-permute-start(f32[64,1,640]{2,1,0:T(1,128)S(1)} %get-tuple-element.58), channel_id=1, source_target_pairs={{0,2},{1,3},{2,0},{3,1},{4,6},{5,7},{6,4},{7,5},{8,10},{9,11},{10,... | collective-permute-start | bytes 491528 | tf_op jit(solution)/shard_map/ppermute | solution.py:48
  62.6 1.0 collective-permute-done.18
  63.8 19.8 %all_to_all.10 = f32[64,1,640]{2,1,0:T(1,128)S(1)} all-to-all(f32[64,1,640]{2,1,0:T(1,128)S(1)} %add.59), channel_id=1, replica_groups={{0,4,8,12,16,20,24,28,32,36,40,44,48,52,56,60,65,69,73,77,81,85,89,93,9..., dimensions={0} | all-to-all | bytes 327680 | tf_op jit(solution)/shard_map/all_to_all | solution.py:70
  83.9 16.8 %all_to_all.11.mine = f32[64,1,640]{2,1,0:T(1,128)S(1)} all-to-all(f32[64,1,640]{2,1,0:T(1,128)S(1)} %broadcast_in_dim.12), channel_id=1, replica_groups={{0,4,8,12,16,20,24,28,32,36,40,44,48,52,56,60,65,69,73,77,81,85,89,93,9..., dimensions={0} | all-to-all | bytes 327680 | tf_op jit(solution)/shard_map/all_to_all | solution.py:70
  100.7 2.7 %collective-permute-start.19 = (f32[64,1,640]{2,1,0:T(1,128)S(1)}, f32[64,1,640]{2,1,0:T(1,128)S(1)}, u32[]{:S(2)}, u32[]{:S(2)}) collective-permute-start(f32[64,1,640]{2,1,0:T(1,128)S(1)} %all_to_all.11.mine), channel_id=1, source_target_pairs={{0,2},{1,3},{2,0},{3,1},{4,6},{5,7},{6,4},{7,5},{8,10},{9,11},{10,... | collective-permute-start | bytes 491528 | tf_op jit(solution)/shard_map/ppermute | solution.py:48
  103.4 1.0 collective-permute-done.19.theirs
  104.4 39.2 %inverse.1 = (bf16[4,128,128]{2,1,0:T(8,128)(2,1)S(1)}, bf16[4,128,128]{2,1,0:T(8,128)(2,1)S(1)}, f32[256,256]{1,0:T(8,128)S(1)}) custom-call(s32[40]{0:T(128)S(1)} %concatenate.27.m, f32[64,1,640]{2,1,0:T(1,128)S(1)} %all_to_all.11.mine, f32[64,1,640]{2,1,0:T(1,128)S(1)} %collective-permute-done.19.theirs, bf16[4,128,256]{2,1,0:T(8,128)(2,1)S(1)} %get-tuple-element.49.s), custom_call_target="tpu_custom_call" | custom-call | flops 671088640 | bytes 1114112 | tf_op jit(solution)/shard_map/inverse/pallas_call | solution.py:301
  143.6 1.4 project.1
  145.1 3.0 %collective-permute-start.20 = (bf16[4,128,128]{2,1,0:T(8,128)(2,1)S(1)}, bf16[4,128,128]{2,1,0:T(8,128)(2,1)S(1)}, u32[]{:S(2)}, u32[]{:S(2)}) collective-permute-start(bf16[4,128,128]{2,1,0:T(8,128)(2,1)S(1)} %get-tuple-element.60), channel_id=1, source_target_pairs={{0,1},{1,0},{2,3},{3,2},{4,5},{5,4},{6,7},{7,6},{8,9},{9,8},{10,11... | collective-permute-start | bytes 393224 | tf_op jit(solution)/shard_map/ppermute | solution.py:57
  148.1 1.6 %collective-permute-done.21 = bf16[256,128]{1,0:T(8,128)(2,1)S(1)} collective-permute-done((bf16[256,128]{1,0:T(8,128)(2,1)S(1)}, bf16[256,128]{1,0:T(8,128)(2,1)S(1)}, u32[]{:S(2)}, u32[]{:S(2)}) %collective-permute-start.21) | collective-permute-done | bytes 65568 | tf_op jit(solution)/shard_map/ppermute | solution.py:57
  150.5 2.3 %collective-permute-done.20 = bf16[4,128,128]{2,1,0:T(8,128)(2,1)S(1)} collective-permute-done((bf16[4,128,128]{2,1,0:T(8,128)(2,1)S(1)}, bf16[4,128,128]{2,1,0:T(8,128)(2,1)S(1)}, u32[]{:S(2)}, u32[]{:S(2)}) %collective-permute-start.20) | collective-permute-done | bytes 131104 | tf_op jit(solution)/shard_map/ppermute | solution.py:57
  (47 shorter events, 13.6 us)
Async XLA Ops:
  1.6 6.0 %collective-permute-start = (bf16[4,128,128]{2,1,0:T(8,128)(2,1)S(1)}, bf16[4,128,128]{2,1,0:T(8,128)(2,1)S(1)}, u32[]{:S(2)}, u32[]{:S(2)}) collective-permute-start(bf16[4,128,128]{2,1,0:T(8,128)(2,1)S(1)} %get-tuple-element.64), channel_id=1, source_target_pairs={{0,1},{1,0},{2,3},{3,2},{4,5},{5,4},{6,7},{7,6},{8,9},{9,8},{10,11... | collective-permute-start | bytes 393224 | tf_op jit(solution)/shard_map/ppermute | solution.py:57
  8.3 11.8 %collective-permute-start.4 = (bf16[2,128,256]{2,1,0:T(8,128)(2,1)S(1)}, bf16[2,128,256]{2,1,0:T(8,128)(2,1)S(1)}, u32[]{:S(2)}, u32[]{:S(2)}) collective-permute-start(bf16[2,128,256]{2,1,0:T(8,128)(2,1)S(1)} %get-tuple-element.37), channel_id=1, source_target_pairs={{0,30},{1,31},{2,4},{3,5},{4,2},{5,3},{6,8},{7,9},{8,6},{9,7},{10,... | collective-permute-start | bytes 393224 | tf_op jit(solution)/shard_map/ppermute | solution.py:48
  12.2 7.8 %collective-permute-start.3 = (bf16[1,128,256]{2,1,0:T(8,128)(2,1)S(1)}, bf16[1,128,256]{2,1,0:T(8,128)(2,1)S(1)}, u32[]{:S(2)}, u32[]{:S(2)}) collective-permute-start(bf16[1,128,256]{2,1,0:T(8,128)(2,1)S(1)} %get-tuple-element.36), channel_id=1, source_target_pairs={{0,2},{1,3},{2,0},{3,1},{4,6},{5,7},{6,4},{7,5},{8,10},{9,11},{10,... | collective-permute-start | bytes 196616 | tf_op jit(solution)/shard_map/ppermute | solution.py:48
  15.1 11.5 %collective-permute-start.2 = (bf16[4,128,256]{2,1,0:T(8,128)(2,1)S(1)}, bf16[4,128,256]{2,1,0:T(8,128)(2,1)S(1)}, u32[]{:S(2)}, u32[]{:S(2)}) collective-permute-start(bf16[4,128,256]{2,1,0:T(8,128)(2,1)S(1)} %get-tuple-element.34.x.rest_0_), channel_id=1, source_target_pairs={{0,225},{1,224},{2,227},{3,226},{4,229},{5,228},{6,231},{7,230},{8... | collective-permute-start | bytes 786440 | tf_op jit(solution)/shard_map/ppermute | solution.py:48
  20.0 7.6 %collective-permute-start.1 = (bf16[4,128,256]{2,1,0:T(8,128)(2,1)S(1)}, bf16[4,128,256]{2,1,0:T(8,128)(2,1)S(1)}, u32[]{:S(2)}, u32[]{:S(2)}) collective-permute-start(bf16[4,128,256]{2,1,0:T(8,128)(2,1)S(1)} %get-tuple-element.34.x.rest_0_), channel_id=1, source_target_pairs={{0,32},{1,33},{2,34},{3,35},{4,36},{5,37},{6,38},{7,39},{8,40},{9,... | collective-permute-start | bytes 786440 | tf_op jit(solution)/shard_map/ppermute | solution.py:48
  20.1 9.3 %collective-permute-start.6 = (bf16[2,128,256]{2,1,0:T(8,128)(2,1)S(1)}, bf16[2,128,256]{2,1,0:T(8,128)(2,1)S(1)}, u32[]{:S(2)}, u32[]{:S(2)}) collective-permute-start(bf16[2,128,256]{2,1,0:T(8,128)(2,1)S(1)} %pad_maximum_fusion.ends), channel_id=1, source_target_pairs={{0,225},{1,224},{2,227},{3,226},{4,229},{5,228},{6,231},{7,230},{8... | collective-permute-start | bytes 393224 | tf_op jit(solution)/shard_map/ppermute | solution.py:48
  21.2 9.3 %collective-permute-start.5 = (bf16[2,128,256]{2,1,0:T(8,128)(2,1)S(1)}, bf16[2,128,256]{2,1,0:T(8,128)(2,1)S(1)}, u32[]{:S(2)}, u32[]{:S(2)}) collective-permute-start(bf16[2,128,256]{2,1,0:T(8,128)(2,1)S(1)} %pad_maximum_fusion.ends), channel_id=1, source_target_pairs={{0,32},{1,33},{2,34},{3,35},{4,36},{5,37},{6,38},{7,39},{8,40},{9,... | collective-permute-start | bytes 393224 | tf_op jit(solution)/shard_map/ppermute | solution.py:48
  21.7 1.7 %copy-start = (bf16[2,1,4,9,128,128]{5,4,3,2,1,0:T(8,128)(2,1)S(1)}, bf16[2,1,4,9,128,128]{5,4,3,2,1,0:T(8,128)(2,1)}, u32[]{:S(2)}) copy-start(bf16[2,1,4,9,128,128]{5,4,3,2,1,0:T(8,128)(2,1)} %h.1) | copy-start | bytes 7077892
  31.2 5.3 %collective-permute-start.10 = (bf16[2,128,256]{2,1,0:T(8,128)(2,1)S(1)}, bf16[2,128,256]{2,1,0:T(8,128)(2,1)S(1)}, u32[]{:S(2)}, u32[]{:S(2)}) collective-permute-start(bf16[2,128,256]{2,1,0:T(8,128)(2,1)S(1)} %get-tuple-element.43), channel_id=1, source_target_pairs={{0,30},{1,31},{2,4},{3,5},{4,2},{5,3},{6,8},{7,9},{8,6},{9,7},{10,... | collective-permute-start | bytes 393224 | tf_op jit(solution)/shard_map/ppermute | solution.py:48
  31.3 5.2 %collective-permute-start.9 = (bf16[1,128,256]{2,1,0:T(8,128)(2,1)S(1)}, bf16[1,128,256]{2,1,0:T(8,128)(2,1)S(1)}, u32[]{:S(2)}, u32[]{:S(2)}) collective-permute-start(bf16[1,128,256]{2,1,0:T(8,128)(2,1)S(1)} %get-tuple-element.42), channel_id=1, source_target_pairs={{0,2},{1,3},{2,0},{3,1},{4,6},{5,7},{6,4},{7,5},{8,10},{9,11},{10,... | collective-permute-start | bytes 196616 | tf_op jit(solution)/shard_map/ppermute | solution.py:48
  32.9 11.3 %collective-permute-start.8 = (bf16[4,128,256]{2,1,0:T(8,128)(2,1)S(1)}, bf16[4,128,256]{2,1,0:T(8,128)(2,1)S(1)}, u32[]{:S(2)}, u32[]{:S(2)}) collective-permute-start(bf16[4,128,256]{2,1,0:T(8,128)(2,1)S(1)} %get-tuple-element.40.x), channel_id=1, source_target_pairs={{0,225},{1,224},{2,227},{3,226},{4,229},{5,228},{6,231},{7,230},{8... | collective-permute-start | bytes 786440 | tf_op jit(solution)/shard_map/ppermute | solution.py:48
  36.5 9.0 %collective-permute-start.7 = (bf16[4,128,256]{2,1,0:T(8,128)(2,1)S(1)}, bf16[4,128,256]{2,1,0:T(8,128)(2,1)S(1)}, u32[]{:S(2)}, u32[]{:S(2)}) collective-permute-start(bf16[4,128,256]{2,1,0:T(8,128)(2,1)S(1)} %get-tuple-element.40.x), channel_id=1, source_target_pairs={{0,32},{1,33},{2,34},{3,35},{4,36},{5,37},{6,38},{7,39},{8,40},{9,... | collective-permute-start | bytes 786440 | tf_op jit(solution)/shard_map/ppermute | solution.py:48
  36.6 11.1 %collective-permute-start.12 = (bf16[2,128,256]{2,1,0:T(8,128)(2,1)S(1)}, bf16[2,128,256]{2,1,0:T(8,128)(2,1)S(1)}, u32[]{:S(2)}, u32[]{:S(2)}) collective-permute-start(bf16[2,128,256]{2,1,0:T(8,128)(2,1)S(1)} %pad_maximum_fusion.1.ends), channel_id=1, source_target_pairs={{0,225},{1,224},{2,227},{3,226},{4,229},{5,228},{6,231},{7,230},{8... | collective-permute-start | bytes 393224 | tf_op jit(solution)/shard_map/ppermute | solution.py:48
  39.8 7.9 %collective-permute-start.11 = (bf16[2,128,256]{2,1,0:T(8,128)(2,1)S(1)}, bf16[2,128,256]{2,1,0:T(8,128)(2,1)S(1)}, u32[]{:S(2)}, u32[]{:S(2)}) collective-permute-start(bf16[2,128,256]{2,1,0:T(8,128)(2,1)S(1)} %pad_maximum_fusion.1.ends), channel_id=1, source_target_pairs={{0,32},{1,33},{2,34},{3,35},{4,36},{5,37},{6,38},{7,39},{8,40},{9,... | collective-permute-start | bytes 393224 | tf_op jit(solution)/shard_map/ppermute | solution.py:48
  39.8 6.7 %collective-permute-start.13 = (bf16[128,128]{1,0:T(8,128)(2,1)S(1)}, bf16[128,128]{1,0:T(8,128)(2,1)S(1)}, u32[]{:S(2)}, u32[]{:S(2)}) collective-permute-start(bf16[128,128]{1,0:T(8,128)(2,1)S(1)} %get-tuple-element.46), channel_id=1, source_target_pairs={{0,2},{1,3},{2,0},{3,1},{4,6},{5,7},{6,4},{7,5},{8,10},{9,11},{10,... | collective-permute-start | bytes 98312 | tf_op jit(solution)/shard_map/ppermute | solution.py:48
  44.2 3.5 %collective-permute-start.14 = (bf16[128,128]{1,0:T(8,128)(2,1)S(1)}, bf16[128,128]{1,0:T(8,128)(2,1)S(1)}, u32[]{:S(2)}, u32[]{:S(2)}) collective-permute-start(bf16[128,128]{1,0:T(8,128)(2,1)S(1)} %get-tuple-element.47), channel_id=1, source_target_pairs={{0,30},{1,31},{2,4},{3,5},{4,2},{5,3},{6,8},{7,9},{8,6},{9,7},{10,... | collective-permute-start | bytes 98312 | tf_op jit(solution)/shard_map/ppermute | solution.py:48
  48.5 9.1 %collective-permute-start.17 = (bf16[4,128,256]{2,1,0:T(8,128)(2,1)S(1)}, bf16[4,128,256]{2,1,0:T(8,128)(2,1)S(1)}, u32[]{:S(2)}, u32[]{:S(2)}) collective-permute-start(bf16[4,128,256]{2,1,0:T(8,128)(2,1)S(1)} %get-tuple-element.49.s), channel_id=1, source_target_pairs={{0,225},{1,224},{2,227},{3,226},{4,229},{5,228},{6,231},{7,230},{8... | collective-permute-start | bytes 786440 | tf_op jit(solution)/shard_map/ppermute | solution.py:52
  52.0 4.7 %collective-permute-start.16 = (bf16[2,128,256]{2,1,0:T(8,128)(2,1)S(1)}, bf16[2,128,256]{2,1,0:T(8,128)(2,1)S(1)}, u32[]{:S(2)}, u32[]{:S(2)}) collective-permute-start(bf16[2,128,256]{2,1,0:T(8,128)(2,1)S(1)} %get-tuple-element.51), channel_id=1, source_target_pairs={{0,30},{1,31},{2,4},{3,5},{4,2},{5,3},{6,8},{7,9},{8,6},{9,7},{10,... | collective-permute-start | bytes 393224 | tf_op jit(solution)/shard_map/ppermute | solution.py:48
  53.6 2.1 %collective-permute-start.15 = (bf16[1,128,256]{2,1,0:T(8,128)(2,1)S(1)}, bf16[1,128,256]{2,1,0:T(8,128)(2,1)S(1)}, u32[]{:S(2)}, u32[]{:S(2)}) collective-permute-start(bf16[1,128,256]{2,1,0:T(8,128)(2,1)S(1)} %get-tuple-element.50), channel_id=1, source_target_pairs={{0,2},{1,3},{2,0},{3,1},{4,6},{5,7},{6,4},{7,5},{8,10},{9,11},{10,... | collective-permute-start | bytes 196616 | tf_op jit(solution)/shard_map/ppermute | solution.py:48
  59.0 4.7 %collective-permute-start.18 = (f32[64,1,640]{2,1,0:T(1,128)S(1)}, f32[64,1,640]{2,1,0:T(1,128)S(1)}, u32[]{:S(2)}, u32[]{:S(2)}) collective-permute-start(f32[64,1,640]{2,1,0:T(1,128)S(1)} %get-tuple-element.58), channel_id=1, source_target_pairs={{0,2},{1,3},{2,0},{3,1},{4,6},{5,7},{6,4},{7,5},{8,10},{9,11},{10,... | collective-permute-start | bytes 491528 | tf_op jit(solution)/shard_map/ppermute | solution.py:48
  100.7 3.7 %collective-permute-start.19 = (f32[64,1,640]{2,1,0:T(1,128)S(1)}, f32[64,1,640]{2,1,0:T(1,128)S(1)}, u32[]{:S(2)}, u32[]{:S(2)}) collective-permute-start(f32[64,1,640]{2,1,0:T(1,128)S(1)} %all_to_all.11.mine), channel_id=1, source_target_pairs={{0,2},{1,3},{2,0},{3,1},{4,6},{5,7},{6,4},{7,5},{8,10},{9,11},{10,... | collective-permute-start | bytes 491528 | tf_op jit(solution)/shard_map/ppermute | solution.py:48
  145.0 4.7 %collective-permute-start.21 = (bf16[256,128]{1,0:T(8,128)(2,1)S(1)}, bf16[256,128]{1,0:T(8,128)(2,1)S(1)}, u32[]{:S(2)}, u32[]{:S(2)}) collective-permute-start(bf16[256,128]{1,0:T(8,128)(2,1)S(1)} %get-tuple-element.63), channel_id=1, source_target_pairs={{0,1},{1,0},{2,3},{3,2},{4,5},{5,4},{6,7},{7,6},{8,9},{9,8},{10,11... | collective-permute-start | bytes 196616 | tf_op jit(solution)/shard_map/ppermute | solution.py:57
  145.1 7.6 %collective-permute-start.20 = (bf16[4,128,128]{2,1,0:T(8,128)(2,1)S(1)}, bf16[4,128,128]{2,1,0:T(8,128)(2,1)S(1)}, u32[]{:S(2)}, u32[]{:S(2)}) collective-permute-start(bf16[4,128,128]{2,1,0:T(8,128)(2,1)S(1)} %get-tuple-element.60), channel_id=1, source_target_pairs={{0,1},{1,0},{2,3},{3,2},{4,5},{5,4},{6,7},{7,6},{8,9},{9,8},{10,11... | collective-permute-start | bytes 393224 | tf_op jit(solution)/shard_map/ppermute | solution.py:57

commit v8 on v7

--- a/solution.py
+++ b/solution.py
@@ -1,3 +1,5 @@
+import functools
+
 import jax
 import jax.numpy as jnp
 from jax import lax
@@ -112,9 +114,8 @@
 
 def store_edges(m, ref, p, q):
     even = m[PAR_Y] == 0
-    p[...] = ref[pl.ds(jnp.where(even, 3, 0), 1)]
+    p[0:1] = ref[pl.ds(jnp.where(even, 3, 0), 1)]
     q[0:1] = ref[pl.ds(jnp.where(even, 0, 3), 1)]
-    q[1:2] = ref[1:2]
 
 
 def join_kernel(m, own, other, v, p, q):
@@ -122,6 +123,7 @@
     v[:, :, :T] = jnp.where(first_col, own[...], other[...])
     v[:, :, T:] = jnp.where(first_col, other[...], own[...])
     store_edges(m, v, p, q)
+    q[1:2] = v[1:2]
 
 
 def ends_of(m, ends):
@@ -146,8 +148,8 @@
         acc[tile] = total + product(o, tile, (1, 2), at, sources)
 
 
-def rim_kernel(m, o, a_ends, b_ends, acc, *rest):
-    *before, out, p, q = rest
+def rim_kernel(m, o, a_ends, b_ends, acc, *rest, last):
+    *more, out, p, q = rest
     low, high = zip(ends_of(m, a_ends), ends_of(m, b_ends))
     for tile in range(4):
         total = acc[tile]
@@ -155,11 +157,15 @@
             total += product(o, tile, (1, 2), (0,), low)
         if tile == 3:
             total += product(o, tile, (1, 2), (5,), high)
-        if before:
-            out[tile] = (total - before[0][tile].astype(F32)).astype(BF)
+        if last:
+            out[tile] = (total - more[0][tile].astype(F32)).astype(BF)
         else:
             out[tile] = (0.5 * total).astype(BF)
     store_edges(m, out, p, q)
+    if not last:
+        for to, block in zip((p, q), more):
+            to[1, :, :T] = block[...]
+            to[1, :, T:] = block[...]
 
 
 def corr_kernel(m, o, s, p, q, corr, turned, acc):
@@ -186,8 +192,8 @@
         at = [place for place in range(tile, tile + 3) if 1 <= place <= 4]
         parts.append(acc[tile] + product(o, tile, (side,), at, [right[at[0] - 1 : at[-1]]]))
     even = m[PAR_Y] == 0
-    parts.append(dot(h_p[...], right[jnp.where(even, 3, 0)]))
-    parts.append(dot(h_q[...], right[jnp.where(even, 0, 3)]))
+    parts.append(dot(h_p[1, :, :T], right[jnp.where(even, 3, 0)]))
+    parts.append(dot(h_q[1, :, :T], right[jnp.where(even, 0, 3)]))
     high, low = split(jnp.concatenate(parts, axis=0))
     half = dot(turned[...], high) + dot(turned[...], low)
     coupling = half + half.T
@@ -347,31 +353,31 @@
     o, h_p, h_q = call(
         order_kernel, m, [hamiltonian], [shaped((4, T, NB * T), BF), corner, corner], "order", specs=[spin_block]
     )
-    h_p, h_q = swap(sizes, h_p, 0, 1), swap(sizes, h_q, 0, 2)
-    tile = shaped((1, T, 2 * T), BF)
-    parts = [shaped(block, BF), tile, shaped((2, T, 2 * T), BF)]
+    tile, two = shaped((1, T, 2 * T), BF), shaped((2, T, 2 * T), BF)
     ext = pltpu.VMEM((6, T, 2 * T), BF)
-    v, p, q = call(join_kernel, m, [own, other], parts, "join")
-
-    def apply_ham(o, x, p, q, before, *kept):
+    v, p, q = call(join_kernel, m, [own, other], [shaped(block, BF), tile, two], "join")
+
+    def apply_ham(o, x, p, q, more, edges, last):
         p, q = swap(sizes, p, 0, 1), swap(sizes, q, 0, 2)
-        ends = jnp.concatenate([p, q[:1]], axis=0)
+        ends = jnp.concatenate([p[:1], q[:1]], axis=0)
         a, b = swap(sizes, x, 1, 0), swap(sizes, x, 2, 0)
         o, a, b = lax.optimization_barrier((o, a, b))
         a_ends, b_ends = swap(sizes, ends, 1, 0), swap(sizes, ends, 2, 0)
         (acc,) = call(core_kernel, m, [o, x, ends, a, b], [shaped(block, F32)], "core", 32, scratch=[ext])
-        acc, *kept = lax.optimization_barrier((acc, *kept))
-        out = call(rim_kernel, m, [o, a_ends, b_ends, acc, *before], parts, "rim", 4)
-        return o, kept, out
-
-    o, _, (first, p, q) = apply_ham(o, v, p, q, [])
-    o, (h_p, h_q), (second, p, q) = apply_ham(o, first, p, q, [v], h_p, h_q)
+        out = call(
+            functools.partial(rim_kernel, last=last), m, [o, a_ends, b_ends, acc, *more],
+            [shaped(block, BF), edges, edges], "rim", 4,
+        )
+        return o, p, q, out
+
+    o, _, _, (first, p, q) = apply_ham(o, v, p, q, [h_p, h_q], two, False)
+    o, h_p, h_q, (second, p, q) = apply_ham(o, first, p, q, [v], tile, True)
 
     right = shift(sizes, second, -1, 0)
     p, q = swap(sizes, p, 0, 1), swap(sizes, q, 0, 2)
     corr, turned, acc = call(
         corr_kernel, m, [o, second, p, q],
-        [shaped(full, F32), shaped((2 * T, 6 * T), BF), shaped(block, F32)], "corr", 16,
+        [shaped(full, F32), shaped((2 * T, 6 * T), BF), shaped(block, F32)], "corr", 400,
     )
     piece = shaped((members // 2, 1, 5 * T), F32)
     mine, theirs = call(

time: 154 us -> 154 us (level)
  starting transfers between devices: 44.6 us -> 39.5 us
  blocking collectives: 36.6 us -> 39.6 us
  waiting for transfers between devices: 16.7 us -> 19.6 us
    ppermute x18 -> x16, starting transfers between devices: 34.4 us -> 29.4 us  [swap(): return lax.ppermute(block, AXES, perm)]
    all_to_all x2, blocking collectives: 36.6 us -> 39.6 us  [exchange(): lax.all_to_all(pieces, AXES, 0, 0, axis_index_groups=groups, tiled=True)]
    ppermute x1, waiting for transfers between devices: 0.01 us -> 2.09 us  [shift(): lax.ppermute(block, AXES, pairs(sizes, lambda gx, gy: (gx + dx, gy + dy)))]
    ppermute x18 -> x16, waiting for transfers between devices: 12.7 us -> 13.4 us  [swap(): return lax.ppermute(block, AXES, perm)]
  transfers between devices with their start and end apart: 22 -> 20, of which waited for: 13 -> 14; matrix products, arithmetic and copies ran while one was open for 2% -> 2% of each run, Pallas kernels for 2% -> 2%
where the time goes in v8:
time: 154 us
  Pallas kernels  47.9 us (31%)
  blocking collectives  39.6 us (26%)
  starting transfers between devices  39.5 us (26%)
  waiting for transfers between devices  19.6 us (13%)
  other arithmetic  3.69 us (2%)
  local copies, waits for them, and re-layouts  3.05 us (2%)
    pallas_call x10, Pallas kernels, call(): pl.pallas_call(kernel, out_shape=outs, grid_spec=pltpu.PrefetchScalarGrid...  47.9 us
    all_to_all x2, blocking collectives, exchange(): lax.all_to_all(pieces, AXES, 0, 0, axis_index_groups=groups, tiled=True)  39.6 us
    ppermute x16, starting transfers between devices, swap(): return lax.ppermute(block, AXES, perm)  29.4 us
    ppermute x16, waiting for transfers between devices, swap(): return lax.ppermute(block, AXES, perm)  13.4 us
    ppermute x3, starting transfers between devices, swap_col(): return lax.ppermute(block, AXES, perm)  6.7 us
    ppermute x3, waiting for transfers between devices, swap_col(): return lax.ppermute(block, AXES, perm)  4.08 us
    ppermute x1, starting transfers between devices, shift(): lax.ppermute(block, AXES, pairs(sizes, lambda gx, gy: (gx + dx, gy + dy)))  3.32 us
  transfers between devices with their start and end apart: 20, of which 14 were waited for; matrix products, arithmetic and copies ran while one was open for 2% of the time, Pallas kernels for 2%

profile of v8, /device:TPU:1, one launch (start us, length us, event | category | flops | bytes accessed | tf_op | source)
XLA Modules:
  0.0 154.1 jit_solution(12759764360974098345)
XLA Ops:
  1.6 3.7 %collective-permute-start = (bf16[4,128,128]{2,1,0:T(8,128)(2,1)S(1)}, bf16[4,128,128]{2,1,0:T(8,128)(2,1)S(1)}, u32[]{:S(2)}, u32[]{:S(2)}) collective-permute-start(bf16[4,128,128]{2,1,0:T(8,128)(2,1)S(1)} %get-tuple-element.58), channel_id=1, source_target_pairs={{0,1},{1,0},{2,3},{3,2},{4,5},{5,4},{6,7},{7,6},{8,9},{9,8},{10,11... | collective-permute-start | bytes 393224 | tf_op jit(solution)/shard_map/ppermute | solution.py:59
  8.3 3.9 %collective-permute-start.4 = (bf16[2,128,256]{2,1,0:T(8,128)(2,1)S(1)}, bf16[2,128,256]{2,1,0:T(8,128)(2,1)S(1)}, u32[]{:S(2)}, u32[]{:S(2)}) collective-permute-start(bf16[2,128,256]{2,1,0:T(8,128)(2,1)S(1)} %get-tuple-element.34), channel_id=1, source_target_pairs={{0,30},{1,31},{2,4},{3,5},{4,2},{5,3},{6,8},{7,9},{8,6},{9,7},{10,... | collective-permute-start | bytes 393224 | tf_op jit(solution)/shard_map/ppermute | solution.py:50
  12.2 2.9 %collective-permute-start.3 = (bf16[1,128,256]{2,1,0:T(8,128)(2,1)S(1)}, bf16[1,128,256]{2,1,0:T(8,128)(2,1)S(1)}, u32[]{:S(2)}, u32[]{:S(2)}) collective-permute-start(bf16[1,128,256]{2,1,0:T(8,128)(2,1)S(1)} %get-tuple-element.33), channel_id=1, source_target_pairs={{0,2},{1,3},{2,0},{3,1},{4,6},{5,7},{6,4},{7,5},{8,10},{9,11},{10,... | collective-permute-start | bytes 196616 | tf_op jit(solution)/shard_map/ppermute | solution.py:50
  15.1 4.9 %collective-permute-start.2 = (bf16[4,128,256]{2,1,0:T(8,128)(2,1)S(1)}, bf16[4,128,256]{2,1,0:T(8,128)(2,1)S(1)}, u32[]{:S(2)}, u32[]{:S(2)}) collective-permute-start(bf16[4,128,256]{2,1,0:T(8,128)(2,1)S(1)} %get-tuple-element.31.x.rest_0_), channel_id=1, source_target_pairs={{0,225},{1,224},{2,227},{3,226},{4,229},{5,228},{6,231},{7,230},{8... | collective-permute-start | bytes 786440 | tf_op jit(solution)/shard_map/ppermute | solution.py:50
  20.1 1.1 collective-permute-start.6
  21.7 1.7 %copy-done = bf16[2,1,4,9,128,128]{5,4,3,2,1,0:T(8,128)(2,1)S(1)} copy-done((bf16[2,1,4,9,128,128]{5,4,3,2,1,0:T(8,128)(2,1)S(1)}, bf16[2,1,4,9,128,128]{5,4,3,2,1,0:T(8,128)(2,1)}, u32[]{:S(2)}) %copy-start) | copy-done | bytes 2359320
  24.3 2.3 %collective-permute-done.2.b = bf16[4,128,256]{2,1,0:T(8,128)(2,1)S(1)} collective-permute-done((bf16[4,128,256]{2,1,0:T(8,128)(2,1)S(1)}, bf16[4,128,256]{2,1,0:T(8,128)(2,1)S(1)}, u32[]{:S(2)}, u32[]{:S(2)}) %collective-permute-start.2) | collective-permute-done | bytes 262176 | tf_op jit(solution)/shard_map/ppermute | solution.py:50
  26.6 1.1 collective-permute-done.1.a
  27.7 1.0 core.2.acc
  29.4 1.1 collective-permute-done.5.a_ends
  31.2 1.2 collective-permute-start.9
  32.4 3.3 %collective-permute-start.8 = (bf16[4,128,256]{2,1,0:T(8,128)(2,1)S(1)}, bf16[4,128,256]{2,1,0:T(8,128)(2,1)S(1)}, u32[]{:S(2)}, u32[]{:S(2)}) collective-permute-start(bf16[4,128,256]{2,1,0:T(8,128)(2,1)S(1)} %get-tuple-element.39.x), channel_id=1, source_target_pairs={{0,225},{1,224},{2,227},{3,226},{4,229},{5,228},{6,231},{7,230},{8... | collective-permute-start | bytes 786440 | tf_op jit(solution)/shard_map/ppermute | solution.py:50
  35.8 1.3 collective-permute-done.10.h_q
  37.1 3.4 %collective-permute-start.12 = (bf16[2,128,256]{2,1,0:T(8,128)(2,1)S(1)}, bf16[2,128,256]{2,1,0:T(8,128)(2,1)S(1)}, u32[]{:S(2)}, u32[]{:S(2)}) collective-permute-start(bf16[2,128,256]{2,1,0:T(8,128)(2,1)S(1)} %pad_maximum_fusion.1.ends), channel_id=1, source_target_pairs={{0,225},{1,224},{2,227},{3,226},{4,229},{5,228},{6,231},{7,230},{8... | collective-permute-start | bytes 393224 | tf_op jit(solution)/shard_map/ppermute | solution.py:50
  40.6 1.3 collective-permute-done.8.b
  41.9 1.0 core.3.acc
  42.9 3.2 %collective-permute-done.12.b_ends = bf16[2,128,256]{2,1,0:T(8,128)(2,1)S(1)} collective-permute-done((bf16[2,128,256]{2,1,0:T(8,128)(2,1)S(1)}, bf16[2,128,256]{2,1,0:T(8,128)(2,1)S(1)}, u32[]{:S(2)}, u32[]{:S(2)}) %collective-permute-start.12) | collective-permute-done | bytes 131104 | tf_op jit(solution)/shard_map/ppermute | solution.py:50
  46.9 1.2 collective-permute-start.13
  48.5 3.3 %collective-permute-start.15 = (bf16[4,128,256]{2,1,0:T(8,128)(2,1)S(1)}, bf16[4,128,256]{2,1,0:T(8,128)(2,1)S(1)}, u32[]{:S(2)}, u32[]{:S(2)}) collective-permute-start(bf16[4,128,256]{2,1,0:T(8,128)(2,1)S(1)} %get-tuple-element.45.s), channel_id=1, source_target_pairs={{0,225},{1,224},{2,227},{3,226},{4,229},{5,228},{6,231},{7,230},{8... | collective-permute-start | bytes 786440 | tf_op jit(solution)/shard_map/ppermute | solution.py:54
  53.1 2.1 %collective-permute-done.15.right = bf16[4,128,256]{2,1,0:T(8,128)(2,1)S(1)} collective-permute-done((bf16[4,128,256]{2,1,0:T(8,128)(2,1)S(1)}, bf16[4,128,256]{2,1,0:T(8,128)(2,1)S(1)}, u32[]{:S(2)}, u32[]{:S(2)}) %collective-permute-start.15) | collective-permute-done | bytes 262176 | tf_op jit(solution)/shard_map/ppermute | solution.py:54
  55.2 1.3 gram.1
  56.5 3.8 %collective-permute-start.16 = (f32[64,1,640]{2,1,0:T(1,128)S(1)}, f32[64,1,640]{2,1,0:T(1,128)S(1)}, u32[]{:S(2)}, u32[]{:S(2)}) collective-permute-start(f32[64,1,640]{2,1,0:T(1,128)S(1)} %get-tuple-element.52), channel_id=1, source_target_pairs={{0,2},{1,3},{2,0},{3,1},{4,6},{5,7},{6,4},{7,5},{8,10},{9,11},{10,... | collective-permute-start | bytes 491528 | tf_op jit(solution)/shard_map/ppermute | solution.py:50
  60.3 1.0 collective-permute-done.16
  61.5 22.8 %all_to_all.10 = f32[64,1,640]{2,1,0:T(1,128)S(1)} all-to-all(f32[64,1,640]{2,1,0:T(1,128)S(1)} %add.59), channel_id=1, replica_groups={{0,4,8,12,16,20,24,28,32,36,40,44,48,52,56,60,65,69,73,77,81,85,89,93,9..., dimensions={0} | all-to-all | bytes 327680 | tf_op jit(solution)/shard_map/all_to_all | solution.py:72
  84.5 16.8 %all_to_all.11.mine = f32[64,1,640]{2,1,0:T(1,128)S(1)} all-to-all(f32[64,1,640]{2,1,0:T(1,128)S(1)} %broadcast_in_dim.12), channel_id=1, replica_groups={{0,4,8,12,16,20,24,28,32,36,40,44,48,52,56,60,65,69,73,77,81,85,89,93,9..., dimensions={0} | all-to-all | bytes 327680 | tf_op jit(solution)/shard_map/all_to_all | solution.py:72
  101.3 2.7 %collective-permute-start.17 = (f32[64,1,640]{2,1,0:T(1,128)S(1)}, f32[64,1,640]{2,1,0:T(1,128)S(1)}, u32[]{:S(2)}, u32[]{:S(2)}) collective-permute-start(f32[64,1,640]{2,1,0:T(1,128)S(1)} %all_to_all.11.mine), channel_id=1, source_target_pairs={{0,2},{1,3},{2,0},{3,1},{4,6},{5,7},{6,4},{7,5},{8,10},{9,11},{10,... | collective-permute-start | bytes 491528 | tf_op jit(solution)/shard_map/ppermute | solution.py:50
  104.0 1.0 collective-permute-done.17.theirs
  105.0 39.2 %inverse.1 = (bf16[4,128,128]{2,1,0:T(8,128)(2,1)S(1)}, bf16[4,128,128]{2,1,0:T(8,128)(2,1)S(1)}, f32[256,256]{1,0:T(8,128)S(1)}) custom-call(s32[40]{0:T(128)S(1)} %concatenate.27.m, f32[64,1,640]{2,1,0:T(1,128)S(1)} %all_to_all.11.mine, f32[64,1,640]{2,1,0:T(1,128)S(1)} %collective-permute-done.17.theirs, bf16[4,128,256]{2,1,0:T(8,128)(2,1)S(1)} %get-tuple-element.45.s), custom_call_target="tpu_custom_call" | custom-call | flops 671088640 | bytes 1114112 | tf_op jit(solution)/shard_map/inverse/pallas_call | solution.py:307
  144.2 1.4 project.1
  145.8 3.0 %collective-permute-start.18 = (bf16[4,128,128]{2,1,0:T(8,128)(2,1)S(1)}, bf16[4,128,128]{2,1,0:T(8,128)(2,1)S(1)}, u32[]{:S(2)}, u32[]{:S(2)}) collective-permute-start(bf16[4,128,128]{2,1,0:T(8,128)(2,1)S(1)} %get-tuple-element.54), channel_id=1, source_target_pairs={{0,1},{1,0},{2,3},{3,2},{4,5},{5,4},{6,7},{7,6},{8,9},{9,8},{10,11... | collective-permute-start | bytes 393224 | tf_op jit(solution)/shard_map/ppermute | solution.py:59
  148.7 1.6 %collective-permute-done.19 = bf16[256,128]{1,0:T(8,128)(2,1)S(1)} collective-permute-done((bf16[256,128]{1,0:T(8,128)(2,1)S(1)}, bf16[256,128]{1,0:T(8,128)(2,1)S(1)}, u32[]{:S(2)}, u32[]{:S(2)}) %collective-permute-start.19) | collective-permute-done | bytes 65568 | tf_op jit(solution)/shard_map/ppermute | solution.py:59
  151.1 2.3 %collective-permute-done.18 = bf16[4,128,128]{2,1,0:T(8,128)(2,1)S(1)} collective-permute-done((bf16[4,128,128]{2,1,0:T(8,128)(2,1)S(1)}, bf16[4,128,128]{2,1,0:T(8,128)(2,1)S(1)}, u32[]{:S(2)}, u32[]{:S(2)}) %collective-permute-start.18) | collective-permute-done | bytes 131104 | tf_op jit(solution)/shard_map/ppermute | solution.py:59
  (44 shorter events, 11.2 us)
Async XLA Ops:
  1.6 6.0 %collective-permute-start = (bf16[4,128,128]{2,1,0:T(8,128)(2,1)S(1)}, bf16[4,128,128]{2,1,0:T(8,128)(2,1)S(1)}, u32[]{:S(2)}, u32[]{:S(2)}) collective-permute-start(bf16[4,128,128]{2,1,0:T(8,128)(2,1)S(1)} %get-tuple-element.58), channel_id=1, source_target_pairs={{0,1},{1,0},{2,3},{3,2},{4,5},{5,4},{6,7},{7,6},{8,9},{9,8},{10,11... | collective-permute-start | bytes 393224 | tf_op jit(solution)/shard_map/ppermute | solution.py:59
  8.3 11.8 %collective-permute-start.4 = (bf16[2,128,256]{2,1,0:T(8,128)(2,1)S(1)}, bf16[2,128,256]{2,1,0:T(8,128)(2,1)S(1)}, u32[]{:S(2)}, u32[]{:S(2)}) collective-permute-start(bf16[2,128,256]{2,1,0:T(8,128)(2,1)S(1)} %get-tuple-element.34), channel_id=1, source_target_pairs={{0,30},{1,31},{2,4},{3,5},{4,2},{5,3},{6,8},{7,9},{8,6},{9,7},{10,... | collective-permute-start | bytes 393224 | tf_op jit(solution)/shard_map/ppermute | solution.py:50
  12.2 7.8 %collective-permute-start.3 = (bf16[1,128,256]{2,1,0:T(8,128)(2,1)S(1)}, bf16[1,128,256]{2,1,0:T(8,128)(2,1)S(1)}, u32[]{:S(2)}, u32[]{:S(2)}) collective-permute-start(bf16[1,128,256]{2,1,0:T(8,128)(2,1)S(1)} %get-tuple-element.33), channel_id=1, source_target_pairs={{0,2},{1,3},{2,0},{3,1},{4,6},{5,7},{6,4},{7,5},{8,10},{9,11},{10,... | collective-permute-start | bytes 196616 | tf_op jit(solution)/shard_map/ppermute | solution.py:50
  15.1 11.5 %collective-permute-start.2 = (bf16[4,128,256]{2,1,0:T(8,128)(2,1)S(1)}, bf16[4,128,256]{2,1,0:T(8,128)(2,1)S(1)}, u32[]{:S(2)}, u32[]{:S(2)}) collective-permute-start(bf16[4,128,256]{2,1,0:T(8,128)(2,1)S(1)} %get-tuple-element.31.x.rest_0_), channel_id=1, source_target_pairs={{0,225},{1,224},{2,227},{3,226},{4,229},{5,228},{6,231},{7,230},{8... | collective-permute-start | bytes 786440 | tf_op jit(solution)/shard_map/ppermute | solution.py:50
  20.0 7.6 %collective-permute-start.1 = (bf16[4,128,256]{2,1,0:T(8,128)(2,1)S(1)}, bf16[4,128,256]{2,1,0:T(8,128)(2,1)S(1)}, u32[]{:S(2)}, u32[]{:S(2)}) collective-permute-start(bf16[4,128,256]{2,1,0:T(8,128)(2,1)S(1)} %get-tuple-element.31.x.rest_0_), channel_id=1, source_target_pairs={{0,32},{1,33},{2,34},{3,35},{4,36},{5,37},{6,38},{7,39},{8,40},{9,... | collective-permute-start | bytes 786440 | tf_op jit(solution)/shard_map/ppermute | solution.py:50
  20.1 9.3 %collective-permute-start.6 = (bf16[2,128,256]{2,1,0:T(8,128)(2,1)S(1)}, bf16[2,128,256]{2,1,0:T(8,128)(2,1)S(1)}, u32[]{:S(2)}, u32[]{:S(2)}) collective-permute-start(bf16[2,128,256]{2,1,0:T(8,128)(2,1)S(1)} %pad_maximum_fusion.ends), channel_id=1, source_target_pairs={{0,225},{1,224},{2,227},{3,226},{4,229},{5,228},{6,231},{7,230},{8... | collective-permute-start | bytes 393224 | tf_op jit(solution)/shard_map/ppermute | solution.py:50
  21.2 9.3 %collective-permute-start.5 = (bf16[2,128,256]{2,1,0:T(8,128)(2,1)S(1)}, bf16[2,128,256]{2,1,0:T(8,128)(2,1)S(1)}, u32[]{:S(2)}, u32[]{:S(2)}) collective-permute-start(bf16[2,128,256]{2,1,0:T(8,128)(2,1)S(1)} %pad_maximum_fusion.ends), channel_id=1, source_target_pairs={{0,32},{1,33},{2,34},{3,35},{4,36},{5,37},{6,38},{7,39},{8,40},{9,... | collective-permute-start | bytes 393224 | tf_op jit(solution)/shard_map/ppermute | solution.py:50
  21.7 1.7 %copy-start = (bf16[2,1,4,9,128,128]{5,4,3,2,1,0:T(8,128)(2,1)S(1)}, bf16[2,1,4,9,128,128]{5,4,3,2,1,0:T(8,128)(2,1)}, u32[]{:S(2)}) copy-start(bf16[2,1,4,9,128,128]{5,4,3,2,1,0:T(8,128)(2,1)} %h.1) | copy-start | bytes 7077892
  31.2 4.5 %collective-permute-start.9 = (bf16[2,128,256]{2,1,0:T(8,128)(2,1)S(1)}, bf16[2,128,256]{2,1,0:T(8,128)(2,1)S(1)}, u32[]{:S(2)}, u32[]{:S(2)}) collective-permute-start(bf16[2,128,256]{2,1,0:T(8,128)(2,1)S(1)} %get-tuple-element.41), channel_id=1, source_target_pairs={{0,2},{1,3},{2,0},{3,1},{4,6},{5,7},{6,4},{7,5},{8,10},{9,11},{10,... | collective-permute-start | bytes 393224 | tf_op jit(solution)/shard_map/ppermute | solution.py:50
  32.4 4.7 %collective-permute-start.10 = (bf16[2,128,256]{2,1,0:T(8,128)(2,1)S(1)}, bf16[2,128,256]{2,1,0:T(8,128)(2,1)S(1)}, u32[]{:S(2)}, u32[]{:S(2)}) collective-permute-start(bf16[2,128,256]{2,1,0:T(8,128)(2,1)S(1)} %get-tuple-element.42), channel_id=1, source_target_pairs={{0,30},{1,31},{2,4},{3,5},{4,2},{5,3},{6,8},{7,9},{8,6},{9,7},{10,... | collective-permute-start | bytes 393224 | tf_op jit(solution)/shard_map/ppermute | solution.py:50
  32.4 9.5 %collective-permute-start.8 = (bf16[4,128,256]{2,1,0:T(8,128)(2,1)S(1)}, bf16[4,128,256]{2,1,0:T(8,128)(2,1)S(1)}, u32[]{:S(2)}, u32[]{:S(2)}) collective-permute-start(bf16[4,128,256]{2,1,0:T(8,128)(2,1)S(1)} %get-tuple-element.39.x), channel_id=1, source_target_pairs={{0,225},{1,224},{2,227},{3,226},{4,229},{5,228},{6,231},{7,230},{8... | collective-permute-start | bytes 786440 | tf_op jit(solution)/shard_map/ppermute | solution.py:50
  35.8 6.1 %collective-permute-start.7 = (bf16[4,128,256]{2,1,0:T(8,128)(2,1)S(1)}, bf16[4,128,256]{2,1,0:T(8,128)(2,1)S(1)}, u32[]{:S(2)}, u32[]{:S(2)}) collective-permute-start(bf16[4,128,256]{2,1,0:T(8,128)(2,1)S(1)} %get-tuple-element.39.x), channel_id=1, source_target_pairs={{0,32},{1,33},{2,34},{3,35},{4,36},{5,37},{6,38},{7,39},{8,40},{9,... | collective-permute-start | bytes 786440 | tf_op jit(solution)/shard_map/ppermute | solution.py:50
  37.1 9.0 %collective-permute-start.12 = (bf16[2,128,256]{2,1,0:T(8,128)(2,1)S(1)}, bf16[2,128,256]{2,1,0:T(8,128)(2,1)S(1)}, u32[]{:S(2)}, u32[]{:S(2)}) collective-permute-start(bf16[2,128,256]{2,1,0:T(8,128)(2,1)S(1)} %pad_maximum_fusion.1.ends), channel_id=1, source_target_pairs={{0,225},{1,224},{2,227},{3,226},{4,229},{5,228},{6,231},{7,230},{8... | collective-permute-start | bytes 393224 | tf_op jit(solution)/shard_map/ppermute | solution.py:50
  40.6 5.6 %collective-permute-start.11 = (bf16[2,128,256]{2,1,0:T(8,128)(2,1)S(1)}, bf16[2,128,256]{2,1,0:T(8,128)(2,1)S(1)}, u32[]{:S(2)}, u32[]{:S(2)}) collective-permute-start(bf16[2,128,256]{2,1,0:T(8,128)(2,1)S(1)} %pad_maximum_fusion.1.ends), channel_id=1, source_target_pairs={{0,32},{1,33},{2,34},{3,35},{4,36},{5,37},{6,38},{7,39},{8,40},{9,... | collective-permute-start | bytes 393224 | tf_op jit(solution)/shard_map/ppermute | solution.py:50
  46.9 4.9 %collective-permute-start.13 = (bf16[1,128,256]{2,1,0:T(8,128)(2,1)S(1)}, bf16[1,128,256]{2,1,0:T(8,128)(2,1)S(1)}, u32[]{:S(2)}, u32[]{:S(2)}) collective-permute-start(bf16[1,128,256]{2,1,0:T(8,128)(2,1)S(1)} %get-tuple-element.46), channel_id=1, source_target_pairs={{0,2},{1,3},{2,0},{3,1},{4,6},{5,7},{6,4},{7,5},{8,10},{9,11},{10,... | collective-permute-start | bytes 196616 | tf_op jit(solution)/shard_map/ppermute | solution.py:50
  48.2 4.0 %collective-permute-start.14 = (bf16[1,128,256]{2,1,0:T(8,128)(2,1)S(1)}, bf16[1,128,256]{2,1,0:T(8,128)(2,1)S(1)}, u32[]{:S(2)}, u32[]{:S(2)}) collective-permute-start(bf16[1,128,256]{2,1,0:T(8,128)(2,1)S(1)} %get-tuple-element.47), channel_id=1, source_target_pairs={{0,30},{1,31},{2,4},{3,5},{4,2},{5,3},{6,8},{7,9},{8,6},{9,7},{10,... | collective-permute-start | bytes 196616 | tf_op jit(solution)/shard_map/ppermute | solution.py:50
  48.5 6.6 %collective-permute-start.15 = (bf16[4,128,256]{2,1,0:T(8,128)(2,1)S(1)}, bf16[4,128,256]{2,1,0:T(8,128)(2,1)S(1)}, u32[]{:S(2)}, u32[]{:S(2)}) collective-permute-start(bf16[4,128,256]{2,1,0:T(8,128)(2,1)S(1)} %get-tuple-element.45.s), channel_id=1, source_target_pairs={{0,225},{1,224},{2,227},{3,226},{4,229},{5,228},{6,231},{7,230},{8... | collective-permute-start | bytes 786440 | tf_op jit(solution)/shard_map/ppermute | solution.py:54
  56.5 4.9 %collective-permute-start.16 = (f32[64,1,640]{2,1,0:T(1,128)S(1)}, f32[64,1,640]{2,1,0:T(1,128)S(1)}, u32[]{:S(2)}, u32[]{:S(2)}) collective-permute-start(f32[64,1,640]{2,1,0:T(1,128)S(1)} %get-tuple-element.52), channel_id=1, source_target_pairs={{0,2},{1,3},{2,0},{3,1},{4,6},{5,7},{6,4},{7,5},{8,10},{9,11},{10,... | collective-permute-start | bytes 491528 | tf_op jit(solution)/shard_map/ppermute | solution.py:50
  101.3 3.7 %collective-permute-start.17 = (f32[64,1,640]{2,1,0:T(1,128)S(1)}, f32[64,1,640]{2,1,0:T(1,128)S(1)}, u32[]{:S(2)}, u32[]{:S(2)}) collective-permute-start(f32[64,1,640]{2,1,0:T(1,128)S(1)} %all_to_all.11.mine), channel_id=1, source_target_pairs={{0,2},{1,3},{2,0},{3,1},{4,6},{5,7},{6,4},{7,5},{8,10},{9,11},{10,... | collective-permute-start | bytes 491528 | tf_op jit(solution)/shard_map/ppermute | solution.py:50
  145.7 4.7 %collective-permute-start.19 = (bf16[256,128]{1,0:T(8,128)(2,1)S(1)}, bf16[256,128]{1,0:T(8,128)(2,1)S(1)}, u32[]{:S(2)}, u32[]{:S(2)}) collective-permute-start(bf16[256,128]{1,0:T(8,128)(2,1)S(1)} %get-tuple-element.57), channel_id=1, source_target_pairs={{0,1},{1,0},{2,3},{3,2},{4,5},{5,4},{6,7},{7,6},{8,9},{9,8},{10,11... | collective-permute-start | bytes 196616 | tf_op jit(solution)/shard_map/ppermute | solution.py:59
  145.8 7.6 %collective-permute-start.18 = (bf16[4,128,128]{2,1,0:T(8,128)(2,1)S(1)}, bf16[4,128,128]{2,1,0:T(8,128)(2,1)S(1)}, u32[]{:S(2)}, u32[]{:S(2)}) collective-permute-start(bf16[4,128,128]{2,1,0:T(8,128)(2,1)S(1)} %get-tuple-element.54), channel_id=1, source_target_pairs={{0,1},{1,0},{2,3},{3,2},{4,5},{5,4},{6,7},{7,6},{8,9},{9,8},{10,11... | collective-permute-start | bytes 393224 | tf_op jit(solution)/shard_map/ppermute | solution.py:59

commit v9 on v8

--- a/solution.py
+++ b/solution.py
@@ -59,16 +59,18 @@
     return lax.ppermute(block, AXES, perm)
 
 
-def exchange(sizes, pieces):
+def exchange(sizes, pieces, joint):
     groups = [
         [
             device(sizes, gx, gy, col_of(gx, spin))
             for gx in range(sizes[0])
             for gy in range(core, sizes[1], 2)
         ]
+        for core in range(2)
         for spin in range(2)
-        for core in range(2)
     ]
+    if joint:
+        groups = [groups[0] + groups[1], groups[2] + groups[3]]
     return lax.all_to_all(pieces, AXES, 0, 0, axis_index_groups=groups, tiled=True)
 
 
@@ -221,80 +223,80 @@
     return jnp.where(rows > cols, e, jnp.where(rows == cols, 0.5 * e, 0.0))
 
 
-def square_of(m, mine, theirs):
-    even = m[PAR_Y] == 0
-    first, second = mine[:, 0, :], theirs[:, 0, :]
+def squares(m, mine, theirs, spin):
+    even = m[PAR_Y] == 0
+    half = slice(spin * T // 2, (spin + 1) * T // 2)
+    first, second = mine[half, 0, :], theirs[half, 0, :]
     top = unpack(jnp.where(even, first, second))
     bottom = unpack(jnp.where(even, second, first))
-    return jnp.concatenate([top[0], bottom[0]], axis=0), jnp.concatenate([top[1], bottom[1]], axis=0)
-
-
-def inverse_kernel(m, mine, theirs, s, keep, send, x_out, x_ref, a_ref):
+    both = jnp.concatenate([top[0], bottom[0]], axis=0)
+    diagonal = jnp.concatenate([top[1], bottom[1]], axis=0)
     rows, cols = places()
-    both, _ = square_of(m, mine, theirs)
     turned = both.T
     corr = jnp.where(rows >= cols, both, turned)
-    on_diagonal = jnp.where(rows == cols, corr, 0.0)
-    scale_row = 1.0 / jnp.sqrt(jnp.sum(on_diagonal, axis=0, keepdims=True))
-    scale_col = 1.0 / jnp.sqrt(jnp.sum(on_diagonal, axis=1, keepdims=True))
-    scaled = corr * scale_row * scale_col
+    return corr, jnp.where(rows < cols, both, jnp.where(rows == cols, diagonal, turned))
+
+
+def final_kernel(m, mine, theirs, s, other, ritz, projected, x_ref, a_ref, k_ref):
+    rows, cols = places()
     unit = (rows == cols).astype(F32)
-
-    a_ref[...] = scaled
-    x_ref[...] = unit - lower_part(scaled - unit, rows, cols)
+    scales = []
+    for spin in range(2):
+        corr, k_ref[spin] = squares(m, mine, theirs, spin)
+        on_diagonal = jnp.where(rows == cols, corr, 0.0)
+        scale_row = 1.0 / jnp.sqrt(jnp.sum(on_diagonal, axis=0, keepdims=True))
+        scale_col = 1.0 / jnp.sqrt(jnp.sum(on_diagonal, axis=1, keepdims=True))
+        scaled = corr * scale_row * scale_col
+        scales.append(scale_row)
+        a_ref[spin] = scaled
+        x_ref[spin] = unit - lower_part(scaled - unit, rows, cols)
 
     def step(state):
-        count, _ = state
-        x = x_ref[...]
-        e = dot3(dot3(x, a_ref[...]), x, ((1,), (1,))) - unit
-        x_ref[...] = x - dot3(lower_part(e, rows, cols), x)
-        return count + 1, jnp.sum(e * e)
+        count, _, _ = state
+        xs = [x_ref[spin] for spin in range(2)]
+        es = [dot3(xs[spin], a_ref[spin]) for spin in range(2)]
+        es = [dot3(es[spin], xs[spin], ((1,), (1,))) - unit for spin in range(2)]
+        for spin in range(2):
+            x_ref[spin] = xs[spin] - dot3(lower_part(es[spin], rows, cols), xs[spin])
+        return count + 1, jnp.sum(es[0] * es[0]), jnp.sum(es[1] * es[1])
 
     def more(state):
-        count, size = state
-        return (count < 12) & (size >= 4e-6) & (size < 1e4)
-
-    _, size = lax.while_loop(more, step, (0, F32(1.0)))
-
-    @pl.when(jnp.logical_not(size < 4e-6))
-    def _():
-        a_ref[...] = scaled
-        x_ref[...] = unit
-
-        def eliminate(j, carry):
-            row = a_ref[pl.ds(j, 1), :]
-            pivot = jnp.sum(jnp.where(cols[:1] == j, row, 0.0), axis=1, keepdims=True)
-            a = a_ref[...]
-            column = jnp.sum(jnp.where(cols == j, a, 0.0), axis=1, keepdims=True)
-            factor = jnp.where(rows[:, :1] > j, column / pivot, 0.0)
-            x = x_ref[...]
-            x_row = x_ref[pl.ds(j, 1), :]
-            a_ref[...] = a - factor * row
-            x_ref[...] = x - factor * x_row
-            return carry
-
-        lax.fori_loop(0, 2 * T, eliminate, 0)
-        pivots = jnp.sum(jnp.where(rows == cols, a_ref[...], 0.0), axis=1, keepdims=True)
-        x_ref[...] = x_ref[...] / jnp.sqrt(pivots)
-
-    x = x_ref[...] * scale_row
-    x_out[...] = x
-    ritz = dot(s[...].reshape(4 * T, 2 * T), x.astype(BF), ((1,), (1,))).astype(BF)
-    ritz = ritz.reshape(4, T, 2 * T)
+        count, *sizes = state
+        largest = jnp.maximum(*sizes)
+        return (count < 12) & (largest >= 4e-6) & (largest < 1e4)
+
+    _, *sizes = lax.while_loop(more, step, (0, F32(1.0), F32(1.0)))
+
+    for spin in range(2):
+
+        @pl.when(jnp.logical_not(sizes[spin] < 4e-6))
+        def _(spin=spin):
+            x_ref[spin] = unit
+
+            def eliminate(j, carry):
+                row = a_ref[spin, pl.ds(j, 1), :]
+                pivot = jnp.sum(jnp.where(cols[:1] == j, row, 0.0), axis=1, keepdims=True)
+                a = a_ref[spin]
+                column = jnp.sum(jnp.where(cols == j, a, 0.0), axis=1, keepdims=True)
+                factor = jnp.where(rows[:, :1] > j, column / pivot, 0.0)
+                x = x_ref[spin]
+                x_row = x_ref[spin, pl.ds(j, 1), :]
+                a_ref[spin] = a - factor * row
+                x_ref[spin] = x - factor * x_row
+                return carry
+
+            lax.fori_loop(0, 2 * T, eliminate, 0)
+            pivots = jnp.sum(jnp.where(rows == cols, a_ref[spin], 0.0), axis=1, keepdims=True)
+            x_ref[spin] = x_ref[spin] / jnp.sqrt(pivots)
+
+    mine_first = m[SPIN] == 0
     first_col = m[COL] == 0
-    keep[...] = jnp.where(first_col, ritz[:, :, :T], ritz[:, :, T:])
-    send[...] = jnp.where(first_col, ritz[:, :, T:], ritz[:, :, :T])
-
-
-def project_kernel(m, mine, theirs, x_ref, keep, send):
-    rows, cols = places()
-    both, diagonal = square_of(m, mine, theirs)
-    coupling = jnp.where(rows < cols, both, jnp.where(rows == cols, diagonal, both.T))
-    x = x_ref[...]
-    projected = dot3(dot3(x, coupling), x, ((1,), (1,)))
-    first_col = m[COL] == 0
-    keep[...] = jnp.where(first_col, projected[:, :T], projected[:, T:])
-    send[...] = jnp.where(first_col, projected[:, T:], projected[:, :T]).astype(BF)
+    for spin in range(2):
+        x = x_ref[spin] * scales[spin]
+        part = jnp.where(first_col, x[:T], x[T:])
+        block = jnp.where(mine_first == (spin == 0), s[...], other[...]).reshape(4 * T, 2 * T)
+        ritz[spin, 0] = dot(block, part.astype(BF), ((1,), (1,))).astype(BF).reshape(4, T, T)
+        projected[spin] = dot3(dot3(x, k_ref[spin]), part, ((1,), (1,)))
 
 
 def whole(shape):
@@ -377,7 +379,7 @@
     p, q = swap(sizes, p, 0, 1), swap(sizes, q, 0, 2)
     corr, turned, acc = call(
         corr_kernel, m, [o, second, p, q],
-        [shaped(full, F32), shaped((2 * T, 6 * T), BF), shaped(block, F32)], "corr", 400,
+        [shaped(full, F32), shaped((2 * T, 6 * T), BF), shaped(block, F32)], "corr", 16,
     )
     piece = shaped((members // 2, 1, 5 * T), F32)
     mine, theirs = call(
@@ -386,25 +388,19 @@
 
     rows = members * second.shape[0] * second.shape[1]
     partial = mine + swap(sizes, theirs, 0, 1)
-    total = exchange(sizes, partial).sum(axis=0, keepdims=True) / rows
-    mine = exchange(sizes, jnp.broadcast_to(total, partial.shape))
+    partner_second = swap_col(sizes, second)
+    total = exchange(sizes, partial, False).sum(axis=0, keepdims=True) / rows
+    total, partner_second = lax.optimization_barrier((total, partner_second))
+    mine = exchange(sizes, jnp.broadcast_to(total, (members, 1, 5 * T)), True)
     theirs = swap(sizes, mine, 0, 1)
-
-    half = (4, T, T)
-    keep, send, x = call(
-        inverse_kernel, m, [mine, theirs, second],
-        [shaped(half, BF), shaped(half, BF), shaped(full, F32)], "inverse", 80,
-        scratch=[pltpu.VMEM(full, F32), pltpu.VMEM(full, F32)],
-    )
-    got = swap_col(sizes, send)
-    p_shape = (2 * T, T)
-    p_keep, p_send = call(
-        project_kernel, m, [mine, theirs, x], [shaped(p_shape, F32), shaped(p_shape, BF)], "project", 24
-    )
-    p_got = swap_col(sizes, p_send).astype(F32)
-    ritz = jnp.where(spin == 0, jnp.stack([keep, got]), jnp.stack([got, keep]))
-    projected = jnp.where(spin == 0, jnp.stack([p_keep, p_got]), jnp.stack([p_got, p_keep]))
-    return ritz[:, None], projected
+    squared = pltpu.VMEM((2, *full), F32)
+    return tuple(
+        call(
+            final_kernel, m, [mine, theirs, second, partner_second],
+            [shaped((2, 1, 4, T, T), BF), shaped((2, 2 * T, T), F32)], "final", 200,
+            scratch=[squared, squared, squared],
+        )
+    )
 
 
 def solution(mesh):

time: 154 us -> 192 us (1.25)
  Pallas kernels: 47.9 us -> 85.8 us
  blocking collectives: 39.6 us -> 24.1 us
  starting transfers between devices: 39.5 us -> 49.1 us
  waiting for transfers between devices: 19.6 us -> 25.9 us
    pallas_call x10 -> x9, Pallas kernels: 47.9 us -> 85.8 us  [call(): pl.pallas_call(kernel, out_shape=outs, grid_spec=pltpu.PrefetchScalarGrid...]
    all_to_all x2 -> x1, blocking collectives: 39.6 us -> 24.1 us  [exchange(): lax.all_to_all(pieces, AXES, 0, 0, axis_index_groups=groups, tiled=True)]
    all_to_all x0 -> x1, waiting for transfers between devices: none -> 11.5 us  [exchange(): lax.all_to_all(pieces, AXES, 0, 0, axis_index_groups=groups, tiled=True)]
    all_to_all x0 -> x1, starting transfers between devices: none -> 10.8 us  [exchange(): lax.all_to_all(pieces, AXES, 0, 0, axis_index_groups=groups, tiled=True)]
    ppermute x3 -> x2, waiting for transfers between devices: 4.08 us -> 0.16 us  [swap_col(): return lax.ppermute(block, AXES, perm)]
    ppermute x3 -> x2, starting transfers between devices: 6.7 us -> 3.75 us  [swap_col(): return lax.ppermute(block, AXES, perm)]
    ppermute x1, waiting for transfers between devices: 2.09 us -> 0.01 us  [shift(): lax.ppermute(block, AXES, pairs(sizes, lambda gx, gy: (gx + dx, gy + dy)))]
  transfers between devices with their start and end apart: 20 -> 20, of which waited for: 14 -> 11; matrix products, arithmetic and copies ran while one was open for 2% -> 1% of each run, Pallas kernels for 2% -> 2%
where the time goes in v9:
time: 192 us
  Pallas kernels  85.8 us (45%)
  starting transfers between devices  49.1 us (26%)
  waiting for transfers between devices  25.9 us (13%)
  blocking collectives  24.1 us (13%)
  local copies, waits for them, and re-layouts  3.13 us (2%)
  other arithmetic  2.9 us (2%)
    pallas_call x9, Pallas kernels, call(): pl.pallas_call(kernel, out_shape=outs, grid_spec=pltpu.PrefetchScalarGrid...  85.8 us
    ppermute x16, starting transfers between devices, swap(): return lax.ppermute(block, AXES, perm)  29.7 us
    all_to_all x1, blocking collectives, exchange(): lax.all_to_all(pieces, AXES, 0, 0, axis_index_groups=groups, tiled=True)  24.1 us
    ppermute x16, waiting for transfers between devices, swap(): return lax.ppermute(block, AXES, perm)  14.2 us
    all_to_all x1, waiting for transfers between devices, exchange(): lax.all_to_all(pieces, AXES, 0, 0, axis_index_groups=groups, tiled=True)  11.5 us
    all_to_all x1, starting transfers between devices, exchange(): lax.all_to_all(pieces, AXES, 0, 0, axis_index_groups=groups, tiled=True)  10.8 us
    ppermute x1, starting transfers between devices, shift(): lax.ppermute(block, AXES, pairs(sizes, lambda gx, gy: (gx + dx, gy + dy)))  4.89 us
  transfers between devices with their start and end apart: 20, of which 11 were waited for; matrix products, arithmetic and copies ran while one was open for 1% of the time, Pallas kernels for 2%

profile of v9, /device:TPU:1, one launch (start us, length us, event | category | flops | bytes accessed | tf_op | source)
XLA Modules:
  0.0 191.8 jit_solution(8479061432006924246)
XLA Ops:
  0.6 1.0 dynamic-slice_bitcast_fusion
  1.6 3.7 %collective-permute-start = (bf16[4,128,128]{2,1,0:T(8,128)(2,1)S(1)}, bf16[4,128,128]{2,1,0:T(8,128)(2,1)S(1)}, u32[]{:S(2)}, u32[]{:S(2)}) collective-permute-start(bf16[4,128,128]{2,1,0:T(8,128)(2,1)S(1)} %get-tuple-element.52), channel_id=1, source_target_pairs={{0,1},{1,0},{2,3},{3,2},{4,5},{5,4},{6,7},{7,6},{8,9},{9,8},{10,11... | collective-permute-start | bytes 393224 | tf_op jit(solution)/shard_map/ppermute | solution.py:59
  6.2 1.0 select_reduce_fusion
  8.3 3.9 %collective-permute-start.4 = (bf16[2,128,256]{2,1,0:T(8,128)(2,1)S(1)}, bf16[2,128,256]{2,1,0:T(8,128)(2,1)S(1)}, u32[]{:S(2)}, u32[]{:S(2)}) collective-permute-start(bf16[2,128,256]{2,1,0:T(8,128)(2,1)S(1)} %get-tuple-element.31), channel_id=1, source_target_pairs={{0,30},{1,31},{2,4},{3,5},{4,2},{5,3},{6,8},{7,9},{8,6},{9,7},{10,... | collective-permute-start | bytes 393224 | tf_op jit(solution)/shard_map/ppermute | solution.py:50
  12.2 2.9 %collective-permute-start.3 = (bf16[1,128,256]{2,1,0:T(8,128)(2,1)S(1)}, bf16[1,128,256]{2,1,0:T(8,128)(2,1)S(1)}, u32[]{:S(2)}, u32[]{:S(2)}) collective-permute-start(bf16[1,128,256]{2,1,0:T(8,128)(2,1)S(1)} %get-tuple-element.30), channel_id=1, source_target_pairs={{0,2},{1,3},{2,0},{3,1},{4,6},{5,7},{6,4},{7,5},{8,10},{9,11},{10,... | collective-permute-start | bytes 196616 | tf_op jit(solution)/shard_map/ppermute | solution.py:50
  15.1 1.2 collective-permute-start.1
  16.3 4.3 %collective-permute-start.2 = (bf16[4,128,256]{2,1,0:T(8,128)(2,1)S(1)}, bf16[4,128,256]{2,1,0:T(8,128)(2,1)S(1)}, u32[]{:S(2)}, u32[]{:S(2)}) collective-permute-start(bf16[4,128,256]{2,1,0:T(8,128)(2,1)S(1)} %get-tuple-element.28.x.rest_0_), channel_id=1, source_target_pairs={{0,225},{1,224},{2,227},{3,226},{4,229},{5,228},{6,231},{7,230},{8... | collective-permute-start | bytes 786440 | tf_op jit(solution)/shard_map/ppermute | solution.py:50
  20.7 0.9 collective-permute-start.6
  21.6 1.7 copy-done
  23.3 0.9 order.1
  24.2 3.1 %collective-permute-done.2.b = bf16[4,128,256]{2,1,0:T(8,128)(2,1)S(1)} collective-permute-done((bf16[4,128,256]{2,1,0:T(8,128)(2,1)S(1)}, bf16[4,128,256]{2,1,0:T(8,128)(2,1)S(1)}, u32[]{:S(2)}, u32[]{:S(2)}) %collective-permute-start.2) | collective-permute-done | bytes 262176 | tf_op jit(solution)/shard_map/ppermute | solution.py:50
  27.3 1.0 core.2.acc
  28.3 1.8 collective-permute-done.6.b_ends
  30.8 1.2 collective-permute-start.9
  32.0 4.3 %collective-permute-start.8 = (bf16[4,128,256]{2,1,0:T(8,128)(2,1)S(1)}, bf16[4,128,256]{2,1,0:T(8,128)(2,1)S(1)}, u32[]{:S(2)}, u32[]{:S(2)}) collective-permute-start(bf16[4,128,256]{2,1,0:T(8,128)(2,1)S(1)} %get-tuple-element.36.x), channel_id=1, source_target_pairs={{0,225},{1,224},{2,227},{3,226},{4,229},{5,228},{6,231},{7,230},{8... | collective-permute-start | bytes 786440 | tf_op jit(solution)/shard_map/ppermute | solution.py:50
  36.8 4.4 %collective-permute-start.12 = (bf16[2,128,256]{2,1,0:T(8,128)(2,1)S(1)}, bf16[2,128,256]{2,1,0:T(8,128)(2,1)S(1)}, u32[]{:S(2)}, u32[]{:S(2)}) collective-permute-start(bf16[2,128,256]{2,1,0:T(8,128)(2,1)S(1)} %pad_maximum_fusion.1.ends), channel_id=1, source_target_pairs={{0,225},{1,224},{2,227},{3,226},{4,229},{5,228},{6,231},{7,230},{8... | collective-permute-start | bytes 393224 | tf_op jit(solution)/shard_map/ppermute | solution.py:50
  41.5 1.0 core.3.acc
  42.5 2.6 %collective-permute-done.12.b_ends = bf16[2,128,256]{2,1,0:T(8,128)(2,1)S(1)} collective-permute-done((bf16[2,128,256]{2,1,0:T(8,128)(2,1)S(1)}, bf16[2,128,256]{2,1,0:T(8,128)(2,1)S(1)}, u32[]{:S(2)}, u32[]{:S(2)}) %collective-permute-start.12) | collective-permute-done | bytes 131104 | tf_op jit(solution)/shard_map/ppermute | solution.py:50
  45.9 4.9 %collective-permute-start.15 = (bf16[4,128,256]{2,1,0:T(8,128)(2,1)S(1)}, bf16[4,128,256]{2,1,0:T(8,128)(2,1)S(1)}, u32[]{:S(2)}, u32[]{:S(2)}) collective-permute-start(bf16[4,128,256]{2,1,0:T(8,128)(2,1)S(1)} %get-tuple-element.42.s), channel_id=1, source_target_pairs={{0,225},{1,224},{2,227},{3,226},{4,229},{5,228},{6,231},{7,230},{8... | collective-permute-start | bytes 786440 | tf_op jit(solution)/shard_map/ppermute | solution.py:54
  50.8 1.5 collective-permute-start.13
  53.2 3.1 %collective-permute-done.14.q = bf16[1,128,256]{2,1,0:T(8,128)(2,1)S(1)} collective-permute-done((bf16[1,128,256]{2,1,0:T(8,128)(2,1)S(1)}, bf16[1,128,256]{2,1,0:T(8,128)(2,1)S(1)}, u32[]{:S(2)}, u32[]{:S(2)}) %collective-permute-start.14) | collective-permute-done | bytes 65568 | tf_op jit(solution)/shard_map/ppermute | solution.py:50
  56.3 0.9 corr.1
  57.2 1.3 gram.1
  58.6 1.3 collective-permute-start.16
  59.8 1.0 collective-permute-done.16
  60.9 0.8 add.59
  61.7 10.8 %all-to-all-start = ((f32[64,1,640]{2,1,0:T(1,128)}), f32[64,1,640]{2,1,0:T(1,128)S(1)}, u32[]{:S(2)}, u32[]{:S(2)}) async-start(f32[64,1,640]{2,1,0:T(1,128)} %add.59), calls=%async_computation | async-start | bytes 327680 | tf_op jit(solution)/shard_map/all_to_all | solution.py:74
  72.6 11.5 %all-to-all-done = f32[64,1,640]{2,1,0:T(1,128)S(1)} async-done(((f32[64,1,640]{2,1,0:T(1,128)}), f32[64,1,640]{2,1,0:T(1,128)S(1)}, u32[]{:S(2)}, u32[]{:S(2)}) %all-to-all-start) | async-done | bytes 163872 | tf_op jit(solution)/shard_map/all_to_all | solution.py:74
  84.5 24.1 %all_to_all.10.mine = f32[128,1,640]{2,1,0:T(1,128)S(1)} all-to-all(f32[128,1,640]{2,1,0:T(1,128)S(1)} %broadcast_in_dim.23), channel_id=1, replica_groups={{0,4,8,12,16,20,24,28,32,36,40,44,48,52,56,60,65,69,73,77,81,85,89,93,9..., dimensions={0} | all-to-all | bytes 655360 | tf_op jit(solution)/shard_map/all_to_all | solution.py:74
  108.6 3.4 %collective-permute-start.18 = (f32[128,1,640]{2,1,0:T(1,128)S(1)}, f32[128,1,640]{2,1,0:T(1,128)S(1)}, u32[]{:S(2)}, u32[]{:S(2)}) collective-permute-start(f32[128,1,640]{2,1,0:T(1,128)S(1)} %all_to_all.10.mine), channel_id=1, source_target_pairs={{0,2},{1,3},{2,0},{3,1},{4,6},{5,7},{6,4},{7,5},{8,10},{9,11},{10,... | collective-permute-start | bytes 983048 | tf_op jit(solution)/shard_map/ppermute | solution.py:50
  112.0 1.3 collective-permute-done.18.theirs
  113.3 78.5 %final.1 = (bf16[2,1,4,128,128]{4,3,2,1,0:T(8,128)(2,1)}, f32[2,256,128]{2,1,0:T(8,128)}) custom-call(s32[40]{0:T(128)S(1)} %concatenate.13.m, f32[128,1,640]{2,1,0:T(1,128)S(1)} %all_to_all.10.mine, f32[128,1,640]{2,1,0:T(1,128)S(1)} %collective-permute-done.18.theirs, bf16[4,128,256]{2,1,0:T(8,128)(2,1)S(1)} %get-tuple-element.42.s, ...), custom_call_target="tpu_custom_call" | custom-call | flops 1677721600 | bytes 1703936 | tf_op jit(solution)/shard_map/final/pallas_call | solution.py:309
  (41 shorter events, 5.8 us)
Async XLA Ops:
  1.6 6.0 %collective-permute-start = (bf16[4,128,128]{2,1,0:T(8,128)(2,1)S(1)}, bf16[4,128,128]{2,1,0:T(8,128)(2,1)S(1)}, u32[]{:S(2)}, u32[]{:S(2)}) collective-permute-start(bf16[4,128,128]{2,1,0:T(8,128)(2,1)S(1)} %get-tuple-element.52), channel_id=1, source_target_pairs={{0,1},{1,0},{2,3},{3,2},{4,5},{5,4},{6,7},{7,6},{8,9},{9,8},{10,11... | collective-permute-start | bytes 393224 | tf_op jit(solution)/shard_map/ppermute | solution.py:59
  8.3 12.3 %collective-permute-start.4 = (bf16[2,128,256]{2,1,0:T(8,128)(2,1)S(1)}, bf16[2,128,256]{2,1,0:T(8,128)(2,1)S(1)}, u32[]{:S(2)}, u32[]{:S(2)}) collective-permute-start(bf16[2,128,256]{2,1,0:T(8,128)(2,1)S(1)} %get-tuple-element.31), channel_id=1, source_target_pairs={{0,30},{1,31},{2,4},{3,5},{4,2},{5,3},{6,8},{7,9},{8,6},{9,7},{10,... | collective-permute-start | bytes 393224 | tf_op jit(solution)/shard_map/ppermute | solution.py:50
  12.2 8.4 %collective-permute-start.3 = (bf16[1,128,256]{2,1,0:T(8,128)(2,1)S(1)}, bf16[1,128,256]{2,1,0:T(8,128)(2,1)S(1)}, u32[]{:S(2)}, u32[]{:S(2)}) collective-permute-start(bf16[1,128,256]{2,1,0:T(8,128)(2,1)S(1)} %get-tuple-element.30), channel_id=1, source_target_pairs={{0,2},{1,3},{2,0},{3,1},{4,6},{5,7},{6,4},{7,5},{8,10},{9,11},{10,... | collective-permute-start | bytes 196616 | tf_op jit(solution)/shard_map/ppermute | solution.py:50
  15.1 9.1 %collective-permute-start.1 = (bf16[4,128,256]{2,1,0:T(8,128)(2,1)S(1)}, bf16[4,128,256]{2,1,0:T(8,128)(2,1)S(1)}, u32[]{:S(2)}, u32[]{:S(2)}) collective-permute-start(bf16[4,128,256]{2,1,0:T(8,128)(2,1)S(1)} %get-tuple-element.28.x.rest_0_), channel_id=1, source_target_pairs={{0,32},{1,33},{2,34},{3,35},{4,36},{5,37},{6,38},{7,39},{8,40},{9,... | collective-permute-start | bytes 786440 | tf_op jit(solution)/shard_map/ppermute | solution.py:50
  16.3 10.9 %collective-permute-start.2 = (bf16[4,128,256]{2,1,0:T(8,128)(2,1)S(1)}, bf16[4,128,256]{2,1,0:T(8,128)(2,1)S(1)}, u32[]{:S(2)}, u32[]{:S(2)}) collective-permute-start(bf16[4,128,256]{2,1,0:T(8,128)(2,1)S(1)} %get-tuple-element.28.x.rest_0_), channel_id=1, source_target_pairs={{0,225},{1,224},{2,227},{3,226},{4,229},{5,228},{6,231},{7,230},{8... | collective-permute-start | bytes 786440 | tf_op jit(solution)/shard_map/ppermute | solution.py:50
  20.6 7.6 %collective-permute-start.5 = (bf16[2,128,256]{2,1,0:T(8,128)(2,1)S(1)}, bf16[2,128,256]{2,1,0:T(8,128)(2,1)S(1)}, u32[]{:S(2)}, u32[]{:S(2)}) collective-permute-start(bf16[2,128,256]{2,1,0:T(8,128)(2,1)S(1)} %pad_maximum_fusion.ends), channel_id=1, source_target_pairs={{0,32},{1,33},{2,34},{3,35},{4,36},{5,37},{6,38},{7,39},{8,40},{9,... | collective-permute-start | bytes 393224 | tf_op jit(solution)/shard_map/ppermute | solution.py:50
  20.7 9.3 %collective-permute-start.6 = (bf16[2,128,256]{2,1,0:T(8,128)(2,1)S(1)}, bf16[2,128,256]{2,1,0:T(8,128)(2,1)S(1)}, u32[]{:S(2)}, u32[]{:S(2)}) collective-permute-start(bf16[2,128,256]{2,1,0:T(8,128)(2,1)S(1)} %pad_maximum_fusion.ends), channel_id=1, source_target_pairs={{0,225},{1,224},{2,227},{3,226},{4,229},{5,228},{6,231},{7,230},{8... | collective-permute-start | bytes 393224 | tf_op jit(solution)/shard_map/ppermute | solution.py:50
  21.6 1.7 copy-start
  30.8 5.5 %collective-permute-start.9 = (bf16[2,128,256]{2,1,0:T(8,128)(2,1)S(1)}, bf16[2,128,256]{2,1,0:T(8,128)(2,1)S(1)}, u32[]{:S(2)}, u32[]{:S(2)}) collective-permute-start(bf16[2,128,256]{2,1,0:T(8,128)(2,1)S(1)} %get-tuple-element.38), channel_id=1, source_target_pairs={{0,2},{1,3},{2,0},{3,1},{4,6},{5,7},{6,4},{7,5},{8,10},{9,11},{10,... | collective-permute-start | bytes 393224 | tf_op jit(solution)/shard_map/ppermute | solution.py:50
  32.0 4.7 %collective-permute-start.10 = (bf16[2,128,256]{2,1,0:T(8,128)(2,1)S(1)}, bf16[2,128,256]{2,1,0:T(8,128)(2,1)S(1)}, u32[]{:S(2)}, u32[]{:S(2)}) collective-permute-start(bf16[2,128,256]{2,1,0:T(8,128)(2,1)S(1)} %get-tuple-element.39), channel_id=1, source_target_pairs={{0,30},{1,31},{2,4},{3,5},{4,2},{5,3},{6,8},{7,9},{8,6},{9,7},{10,... | collective-permute-start | bytes 393224 | tf_op jit(solution)/shard_map/ppermute | solution.py:50
  32.0 9.2 %collective-permute-start.7 = (bf16[4,128,256]{2,1,0:T(8,128)(2,1)S(1)}, bf16[4,128,256]{2,1,0:T(8,128)(2,1)S(1)}, u32[]{:S(2)}, u32[]{:S(2)}) collective-permute-start(bf16[4,128,256]{2,1,0:T(8,128)(2,1)S(1)} %get-tuple-element.36.x), channel_id=1, source_target_pairs={{0,32},{1,33},{2,34},{3,35},{4,36},{5,37},{6,38},{7,39},{8,40},{9,... | collective-permute-start | bytes 786440 | tf_op jit(solution)/shard_map/ppermute | solution.py:50
  32.0 9.5 %collective-permute-start.8 = (bf16[4,128,256]{2,1,0:T(8,128)(2,1)S(1)}, bf16[4,128,256]{2,1,0:T(8,128)(2,1)S(1)}, u32[]{:S(2)}, u32[]{:S(2)}) collective-permute-start(bf16[4,128,256]{2,1,0:T(8,128)(2,1)S(1)} %get-tuple-element.36.x), channel_id=1, source_target_pairs={{0,225},{1,224},{2,227},{3,226},{4,229},{5,228},{6,231},{7,230},{8... | collective-permute-start | bytes 786440 | tf_op jit(solution)/shard_map/ppermute | solution.py:50
  36.7 5.8 %collective-permute-start.11 = (bf16[2,128,256]{2,1,0:T(8,128)(2,1)S(1)}, bf16[2,128,256]{2,1,0:T(8,128)(2,1)S(1)}, u32[]{:S(2)}, u32[]{:S(2)}) collective-permute-start(bf16[2,128,256]{2,1,0:T(8,128)(2,1)S(1)} %pad_maximum_fusion.1.ends), channel_id=1, source_target_pairs={{0,32},{1,33},{2,34},{3,35},{4,36},{5,37},{6,38},{7,39},{8,40},{9,... | collective-permute-start | bytes 393224 | tf_op jit(solution)/shard_map/ppermute | solution.py:50
  36.8 8.3 %collective-permute-start.12 = (bf16[2,128,256]{2,1,0:T(8,128)(2,1)S(1)}, bf16[2,128,256]{2,1,0:T(8,128)(2,1)S(1)}, u32[]{:S(2)}, u32[]{:S(2)}) collective-permute-start(bf16[2,128,256]{2,1,0:T(8,128)(2,1)S(1)} %pad_maximum_fusion.1.ends), channel_id=1, source_target_pairs={{0,225},{1,224},{2,227},{3,226},{4,229},{5,228},{6,231},{7,230},{8... | collective-permute-start | bytes 393224 | tf_op jit(solution)/shard_map/ppermute | solution.py:50
  45.9 11.3 %collective-permute-start.15 = (bf16[4,128,256]{2,1,0:T(8,128)(2,1)S(1)}, bf16[4,128,256]{2,1,0:T(8,128)(2,1)S(1)}, u32[]{:S(2)}, u32[]{:S(2)}) collective-permute-start(bf16[4,128,256]{2,1,0:T(8,128)(2,1)S(1)} %get-tuple-element.42.s), channel_id=1, source_target_pairs={{0,225},{1,224},{2,227},{3,226},{4,229},{5,228},{6,231},{7,230},{8... | collective-permute-start | bytes 786440 | tf_op jit(solution)/shard_map/ppermute | solution.py:54
  50.8 2.4 %collective-permute-start.13 = (bf16[1,128,256]{2,1,0:T(8,128)(2,1)S(1)}, bf16[1,128,256]{2,1,0:T(8,128)(2,1)S(1)}, u32[]{:S(2)}, u32[]{:S(2)}) collective-permute-start(bf16[1,128,256]{2,1,0:T(8,128)(2,1)S(1)} %get-tuple-element.43), channel_id=1, source_target_pairs={{0,2},{1,3},{2,0},{3,1},{4,6},{5,7},{6,4},{7,5},{8,10},{9,11},{10,... | collective-permute-start | bytes 196616 | tf_op jit(solution)/shard_map/ppermute | solution.py:50
  52.3 4.0 %collective-permute-start.14 = (bf16[1,128,256]{2,1,0:T(8,128)(2,1)S(1)}, bf16[1,128,256]{2,1,0:T(8,128)(2,1)S(1)}, u32[]{:S(2)}, u32[]{:S(2)}) collective-permute-start(bf16[1,128,256]{2,1,0:T(8,128)(2,1)S(1)} %get-tuple-element.44), channel_id=1, source_target_pairs={{0,30},{1,31},{2,4},{3,5},{4,2},{5,3},{6,8},{7,9},{8,6},{9,7},{10,... | collective-permute-start | bytes 196616 | tf_op jit(solution)/shard_map/ppermute | solution.py:50
  58.6 2.3 %collective-permute-start.16 = (f32[64,1,640]{2,1,0:T(1,128)S(1)}, f32[64,1,640]{2,1,0:T(1,128)S(1)}, u32[]{:S(2)}, u32[]{:S(2)}) collective-permute-start(f32[64,1,640]{2,1,0:T(1,128)S(1)} %get-tuple-element.49), channel_id=1, source_target_pairs={{0,2},{1,3},{2,0},{3,1},{4,6},{5,7},{6,4},{7,5},{8,10},{9,11},{10,... | collective-permute-start | bytes 491528 | tf_op jit(solution)/shard_map/ppermute | solution.py:50
  61.7 22.4 %all-to-all-start = ((f32[64,1,640]{2,1,0:T(1,128)}), f32[64,1,640]{2,1,0:T(1,128)S(1)}, u32[]{:S(2)}, u32[]{:S(2)}) async-start(f32[64,1,640]{2,1,0:T(1,128)} %add.59), calls=%async_computation | async-start | bytes 327680 | tf_op jit(solution)/shard_map/all_to_all | solution.py:74
  72.5 11.8 %collective-permute-start.17 = (bf16[4,128,256]{2,1,0:T(8,128)(2,1)S(1)}, bf16[4,128,256]{2,1,0:T(8,128)(2,1)S(1)}, u32[]{:S(2)}, u32[]{:S(2)}) collective-permute-start(bf16[4,128,256]{2,1,0:T(8,128)(2,1)S(1)} %get-tuple-element.42.s), channel_id=1, source_target_pairs={{0,1},{1,0},{2,3},{3,2},{4,5},{5,4},{6,7},{7,6},{8,9},{9,8},{10,11... | collective-permute-start | bytes 786440 | tf_op jit(solution)/shard_map/ppermute | solution.py:59
  108.6 4.7 %collective-permute-start.18 = (f32[128,1,640]{2,1,0:T(1,128)S(1)}, f32[128,1,640]{2,1,0:T(1,128)S(1)}, u32[]{:S(2)}, u32[]{:S(2)}) collective-permute-start(f32[128,1,640]{2,1,0:T(1,128)S(1)} %all_to_all.10.mine), channel_id=1, source_target_pairs={{0,2},{1,3},{2,0},{3,1},{4,6},{5,7},{6,4},{7,5},{8,10},{9,11},{10,... | collective-permute-start | bytes 983048 | tf_op jit(solution)/shard_map/ppermute | solution.py:50

commit v10 on v9

--- a/solution.py
+++ b/solution.py
@@ -237,7 +237,12 @@
     return corr, jnp.where(rows < cols, both, jnp.where(rows == cols, diagonal, turned))
 
 
-def final_kernel(m, mine, theirs, s, other, ritz, projected, x_ref, a_ref, k_ref):
+def stack_kernel(m, s, other, both):
+    both[pl.ds(m[SPIN], 1)] = s[...][None]
+    both[pl.ds(1 - m[SPIN], 1)] = other[...][None]
+
+
+def final_kernel(m, mine, theirs, both, ritz, projected, x_ref, a_ref, k_ref):
     rows, cols = places()
     unit = (rows == cols).astype(F32)
     scales = []
@@ -289,13 +294,11 @@
             pivots = jnp.sum(jnp.where(rows == cols, a_ref[spin], 0.0), axis=1, keepdims=True)
             x_ref[spin] = x_ref[spin] / jnp.sqrt(pivots)
 
-    mine_first = m[SPIN] == 0
     first_col = m[COL] == 0
     for spin in range(2):
         x = x_ref[spin] * scales[spin]
         part = jnp.where(first_col, x[:T], x[T:])
-        block = jnp.where(mine_first == (spin == 0), s[...], other[...]).reshape(4 * T, 2 * T)
-        ritz[spin, 0] = dot(block, part.astype(BF), ((1,), (1,))).astype(BF).reshape(4, T, T)
+        ritz[spin, 0] = dot(both[spin].reshape(4 * T, 2 * T), part.astype(BF), ((1,), (1,))).astype(BF).reshape(4, T, T)
         projected[spin] = dot3(dot3(x, k_ref[spin]), part, ((1,), (1,)))
 
 
@@ -388,15 +391,16 @@
 
     rows = members * second.shape[0] * second.shape[1]
     partial = mine + swap(sizes, theirs, 0, 1)
-    partner_second = swap_col(sizes, second)
-    total = exchange(sizes, partial, False).sum(axis=0, keepdims=True) / rows
-    total, partner_second = lax.optimization_barrier((total, partner_second))
+    (both,) = call(stack_kernel, m, [second, swap_col(sizes, second)], [shaped((2, *block), BF)], "stack", 200)
+    total = exchange(sizes, partial, False)
+    total, both = lax.optimization_barrier((total, both))
+    total = total.sum(axis=0, keepdims=True) / rows
     mine = exchange(sizes, jnp.broadcast_to(total, (members, 1, 5 * T)), True)
     theirs = swap(sizes, mine, 0, 1)
     squared = pltpu.VMEM((2, *full), F32)
     return tuple(
         call(
-            final_kernel, m, [mine, theirs, second, partner_second],
+            final_kernel, m, [mine, theirs, both],
             [shaped((2, 1, 4, T, T), BF), shaped((2, 2 * T, T), F32)], "final", 200,
             scratch=[squared, squared, squared],
         )

time: 192 us -> 188 us (0.979)
  blocking collectives: 24.1 us -> 20.3 us
  starting transfers between devices: 49.1 us -> 46.5 us
  waiting for transfers between devices: 25.9 us -> 27.9 us
    all_to_all x1, blocking collectives: 24.1 us -> 20.3 us  [exchange(): lax.all_to_all(pieces, AXES, 0, 0, axis_index_groups=groups, tiled=True)]
    ppermute x16, waiting for transfers between devices: 14.2 us -> 16.7 us  [swap(): return lax.ppermute(block, AXES, perm)]
    pallas_call x9 -> x10, Pallas kernels: 85.8 us -> 86.4 us  [call(): pl.pallas_call(kernel, out_shape=outs, grid_spec=pltpu.PrefetchScalarGrid...]
  transfers between devices with their start and end apart: 20 -> 20, of which waited for: 11 -> 11; matrix products, arithmetic and copies ran while one was open for 1% -> 2% of each run, Pallas kernels for 2% -> 2%
where the time goes in v10:
time: 188 us
  Pallas kernels  86.4 us (46%)
  starting transfers between devices  46.5 us (25%)
  waiting for transfers between devices  27.9 us (15%)
  blocking collectives  20.3 us (11%)
  local copies, waits for them, and re-layouts  3.13 us (2%)
  other arithmetic  2.89 us (2%)
    pallas_call x10, Pallas kernels, call(): pl.pallas_call(kernel, out_shape=outs, grid_spec=pltpu.PrefetchScalarGrid...  86.4 us
    ppermute x16, starting transfers between devices, swap(): return lax.ppermute(block, AXES, perm)  28.6 us
    all_to_all x1, blocking collectives, exchange(): lax.all_to_all(pieces, AXES, 0, 0, axis_index_groups=groups, tiled=True)  20.3 us
    ppermute x16, waiting for transfers between devices, swap(): return lax.ppermute(block, AXES, perm)  16.7 us
    all_to_all x1, waiting for transfers between devices, exchange(): lax.all_to_all(pieces, AXES, 0, 0, axis_index_groups=groups, tiled=True)  11 us
    all_to_all x1, starting transfers between devices, exchange(): lax.all_to_all(pieces, AXES, 0, 0, axis_index_groups=groups, tiled=True)  9.9 us
    ppermute x1, starting transfers between devices, shift(): lax.ppermute(block, AXES, pairs(sizes, lambda gx, gy: (gx + dx, gy + dy)))  4.34 us
  transfers between devices with their start and end apart: 20, of which 11 were waited for; matrix products, arithmetic and copies ran while one was open for 2% of the time, Pallas kernels for 2%

profile of v10, /device:TPU:1, one launch (start us, length us, event | category | flops | bytes accessed | tf_op | source)
XLA Modules:
  0.0 187.8 jit_solution(3837766104837669573)
XLA Ops:
  0.6 1.0 dynamic-slice_bitcast_fusion
  1.6 3.7 %collective-permute-start = (bf16[4,128,128]{2,1,0:T(8,128)(2,1)S(1)}, bf16[4,128,128]{2,1,0:T(8,128)(2,1)S(1)}, u32[]{:S(2)}, u32[]{:S(2)}) collective-permute-start(bf16[4,128,128]{2,1,0:T(8,128)(2,1)S(1)} %get-tuple-element.52), channel_id=1, source_target_pairs={{0,1},{1,0},{2,3},{3,2},{4,5},{5,4},{6,7},{7,6},{8,9},{9,8},{10,11... | collective-permute-start | bytes 393224 | tf_op jit(solution)/shard_map/ppermute | solution.py:59
  6.2 1.0 select_reduce_fusion
  8.3 3.9 %collective-permute-start.4 = (bf16[2,128,256]{2,1,0:T(8,128)(2,1)S(1)}, bf16[2,128,256]{2,1,0:T(8,128)(2,1)S(1)}, u32[]{:S(2)}, u32[]{:S(2)}) collective-permute-start(bf16[2,128,256]{2,1,0:T(8,128)(2,1)S(1)} %get-tuple-element.31), channel_id=1, source_target_pairs={{0,30},{1,31},{2,4},{3,5},{4,2},{5,3},{6,8},{7,9},{8,6},{9,7},{10,... | collective-permute-start | bytes 393224 | tf_op jit(solution)/shard_map/ppermute | solution.py:50
  12.2 2.9 %collective-permute-start.3 = (bf16[1,128,256]{2,1,0:T(8,128)(2,1)S(1)}, bf16[1,128,256]{2,1,0:T(8,128)(2,1)S(1)}, u32[]{:S(2)}, u32[]{:S(2)}) collective-permute-start(bf16[1,128,256]{2,1,0:T(8,128)(2,1)S(1)} %get-tuple-element.30), channel_id=1, source_target_pairs={{0,2},{1,3},{2,0},{3,1},{4,6},{5,7},{6,4},{7,5},{8,10},{9,11},{10,... | collective-permute-start | bytes 196616 | tf_op jit(solution)/shard_map/ppermute | solution.py:50
  15.1 1.2 collective-permute-start.1
  16.3 4.3 %collective-permute-start.2 = (bf16[4,128,256]{2,1,0:T(8,128)(2,1)S(1)}, bf16[4,128,256]{2,1,0:T(8,128)(2,1)S(1)}, u32[]{:S(2)}, u32[]{:S(2)}) collective-permute-start(bf16[4,128,256]{2,1,0:T(8,128)(2,1)S(1)} %get-tuple-element.28.x.rest_0_), channel_id=1, source_target_pairs={{0,225},{1,224},{2,227},{3,226},{4,229},{5,228},{6,231},{7,230},{8... | collective-permute-start | bytes 786440 | tf_op jit(solution)/shard_map/ppermute | solution.py:50
  20.7 0.9 collective-permute-start.6
  21.6 1.7 copy-done
  23.3 0.9 order.1
  24.2 3.1 %collective-permute-done.2.b = bf16[4,128,256]{2,1,0:T(8,128)(2,1)S(1)} collective-permute-done((bf16[4,128,256]{2,1,0:T(8,128)(2,1)S(1)}, bf16[4,128,256]{2,1,0:T(8,128)(2,1)S(1)}, u32[]{:S(2)}, u32[]{:S(2)}) %collective-permute-start.2) | collective-permute-done | bytes 262176 | tf_op jit(solution)/shard_map/ppermute | solution.py:50
  27.3 1.0 core.2.acc
  28.3 1.8 collective-permute-done.6.b_ends
  30.9 1.6 collective-permute-start.9
  32.5 4.3 %collective-permute-start.8 = (bf16[4,128,256]{2,1,0:T(8,128)(2,1)S(1)}, bf16[4,128,256]{2,1,0:T(8,128)(2,1)S(1)}, u32[]{:S(2)}, u32[]{:S(2)}) collective-permute-start(bf16[4,128,256]{2,1,0:T(8,128)(2,1)S(1)} %get-tuple-element.36.x), channel_id=1, source_target_pairs={{0,225},{1,224},{2,227},{3,226},{4,229},{5,228},{6,231},{7,230},{8... | collective-permute-start | bytes 786440 | tf_op jit(solution)/shard_map/ppermute | solution.py:50
  36.9 2.9 %collective-permute-start.12 = (bf16[2,128,256]{2,1,0:T(8,128)(2,1)S(1)}, bf16[2,128,256]{2,1,0:T(8,128)(2,1)S(1)}, u32[]{:S(2)}, u32[]{:S(2)}) collective-permute-start(bf16[2,128,256]{2,1,0:T(8,128)(2,1)S(1)} %pad_maximum_fusion.1.ends), channel_id=1, source_target_pairs={{0,225},{1,224},{2,227},{3,226},{4,229},{5,228},{6,231},{7,230},{8... | collective-permute-start | bytes 393224 | tf_op jit(solution)/shard_map/ppermute | solution.py:50
  40.4 3.3 %collective-permute-done.8.b = bf16[4,128,256]{2,1,0:T(8,128)(2,1)S(1)} collective-permute-done((bf16[4,128,256]{2,1,0:T(8,128)(2,1)S(1)}, bf16[4,128,256]{2,1,0:T(8,128)(2,1)S(1)}, u32[]{:S(2)}, u32[]{:S(2)}) %collective-permute-start.8) | collective-permute-done | bytes 262176 | tf_op jit(solution)/shard_map/ppermute | solution.py:50
  43.8 1.0 core.3.acc
  44.8 1.8 collective-permute-done.12.b_ends
  47.4 4.3 %collective-permute-start.15 = (bf16[4,128,256]{2,1,0:T(8,128)(2,1)S(1)}, bf16[4,128,256]{2,1,0:T(8,128)(2,1)S(1)}, u32[]{:S(2)}, u32[]{:S(2)}) collective-permute-start(bf16[4,128,256]{2,1,0:T(8,128)(2,1)S(1)} %get-tuple-element.42.s), channel_id=1, source_target_pairs={{0,225},{1,224},{2,227},{3,226},{4,229},{5,228},{6,231},{7,230},{8... | collective-permute-start | bytes 786440 | tf_op jit(solution)/shard_map/ppermute | solution.py:54
  51.7 1.1 collective-permute-start.13
  53.7 3.1 %collective-permute-done.14.q = bf16[1,128,256]{2,1,0:T(8,128)(2,1)S(1)} collective-permute-done((bf16[1,128,256]{2,1,0:T(8,128)(2,1)S(1)}, bf16[1,128,256]{2,1,0:T(8,128)(2,1)S(1)}, u32[]{:S(2)}, u32[]{:S(2)}) %collective-permute-start.14) | collective-permute-done | bytes 65568 | tf_op jit(solution)/shard_map/ppermute | solution.py:50
  56.8 0.9 corr.1
  57.7 1.3 gram.1
  59.0 1.2 collective-permute-start.16
  60.2 1.0 collective-permute-done.16
  62.1 9.9 %all-to-all-start = ((f32[64,1,640]{2,1,0:T(1,128)}), f32[64,1,640]{2,1,0:T(1,128)S(1)}, u32[]{:S(2)}, u32[]{:S(2)}) async-start(f32[64,1,640]{2,1,0:T(1,128)} %add.59), calls=%async_computation | async-start | bytes 327680 | tf_op jit(solution)/shard_map/all_to_all | solution.py:74
  72.6 11.0 %all-to-all-done = f32[64,1,640]{2,1,0:T(1,128)S(1)} async-done(((f32[64,1,640]{2,1,0:T(1,128)}), f32[64,1,640]{2,1,0:T(1,128)S(1)}, u32[]{:S(2)}, u32[]{:S(2)}) %all-to-all-start) | async-done | bytes 163872 | tf_op jit(solution)/shard_map/all_to_all | solution.py:74
  83.9 20.3 %all_to_all.10.mine = f32[128,1,640]{2,1,0:T(1,128)S(1)} all-to-all(f32[128,1,640]{2,1,0:T(1,128)S(1)} %broadcast_in_dim.20), channel_id=1, replica_groups={{0,4,8,12,16,20,24,28,32,36,40,44,48,52,56,60,65,69,73,77,81,85,89,93,9..., dimensions={0} | all-to-all | bytes 655360 | tf_op jit(solution)/shard_map/all_to_all | solution.py:74
  104.1 3.9 %collective-permute-start.18 = (f32[128,1,640]{2,1,0:T(1,128)S(1)}, f32[128,1,640]{2,1,0:T(1,128)S(1)}, u32[]{:S(2)}, u32[]{:S(2)}) collective-permute-start(f32[128,1,640]{2,1,0:T(1,128)S(1)} %all_to_all.10.mine), channel_id=1, source_target_pairs={{0,2},{1,3},{2,0},{3,1},{4,6},{5,7},{6,4},{7,5},{8,10},{9,11},{10,... | collective-permute-start | bytes 983048 | tf_op jit(solution)/shard_map/ppermute | solution.py:50
  108.1 1.3 collective-permute-done.18.theirs
  109.3 78.5 %final.1 = (bf16[2,1,4,128,128]{4,3,2,1,0:T(8,128)(2,1)}, f32[2,256,128]{2,1,0:T(8,128)}) custom-call(s32[40]{0:T(128)S(1)} %concatenate.13.m, f32[128,1,640]{2,1,0:T(1,128)S(1)} %all_to_all.10.mine, f32[128,1,640]{2,1,0:T(1,128)S(1)} %collective-permute-done.18.theirs, bf16[2,4,128,256]{3,2,1,0:T(8,128)(2,1)S(1)} %stack.29.both), custom_call_target="tpu_custom_call" | custom-call | flops 1677721600 | bytes 1703936 | tf_op jit(solution)/shard_map/final/pallas_call | solution.py:312
  (40 shorter events, 7.1 us)
Async XLA Ops:
  1.6 6.0 %collective-permute-start = (bf16[4,128,128]{2,1,0:T(8,128)(2,1)S(1)}, bf16[4,128,128]{2,1,0:T(8,128)(2,1)S(1)}, u32[]{:S(2)}, u32[]{:S(2)}) collective-permute-start(bf16[4,128,128]{2,1,0:T(8,128)(2,1)S(1)} %get-tuple-element.52), channel_id=1, source_target_pairs={{0,1},{1,0},{2,3},{3,2},{4,5},{5,4},{6,7},{7,6},{8,9},{9,8},{10,11... | collective-permute-start | bytes 393224 | tf_op jit(solution)/shard_map/ppermute | solution.py:59
  8.3 12.3 %collective-permute-start.4 = (bf16[2,128,256]{2,1,0:T(8,128)(2,1)S(1)}, bf16[2,128,256]{2,1,0:T(8,128)(2,1)S(1)}, u32[]{:S(2)}, u32[]{:S(2)}) collective-permute-start(bf16[2,128,256]{2,1,0:T(8,128)(2,1)S(1)} %get-tuple-element.31), channel_id=1, source_target_pairs={{0,30},{1,31},{2,4},{3,5},{4,2},{5,3},{6,8},{7,9},{8,6},{9,7},{10,... | collective-permute-start | bytes 393224 | tf_op jit(solution)/shard_map/ppermute | solution.py:50
  12.2 8.4 %collective-permute-start.3 = (bf16[1,128,256]{2,1,0:T(8,128)(2,1)S(1)}, bf16[1,128,256]{2,1,0:T(8,128)(2,1)S(1)}, u32[]{:S(2)}, u32[]{:S(2)}) collective-permute-start(bf16[1,128,256]{2,1,0:T(8,128)(2,1)S(1)} %get-tuple-element.30), channel_id=1, source_target_pairs={{0,2},{1,3},{2,0},{3,1},{4,6},{5,7},{6,4},{7,5},{8,10},{9,11},{10,... | collective-permute-start | bytes 196616 | tf_op jit(solution)/shard_map/ppermute | solution.py:50
  15.1 9.1 %collective-permute-start.1 = (bf16[4,128,256]{2,1,0:T(8,128)(2,1)S(1)}, bf16[4,128,256]{2,1,0:T(8,128)(2,1)S(1)}, u32[]{:S(2)}, u32[]{:S(2)}) collective-permute-start(bf16[4,128,256]{2,1,0:T(8,128)(2,1)S(1)} %get-tuple-element.28.x.rest_0_), channel_id=1, source_target_pairs={{0,32},{1,33},{2,34},{3,35},{4,36},{5,37},{6,38},{7,39},{8,40},{9,... | collective-permute-start | bytes 786440 | tf_op jit(solution)/shard_map/ppermute | solution.py:50
  16.3 10.9 %collective-permute-start.2 = (bf16[4,128,256]{2,1,0:T(8,128)(2,1)S(1)}, bf16[4,128,256]{2,1,0:T(8,128)(2,1)S(1)}, u32[]{:S(2)}, u32[]{:S(2)}) collective-permute-start(bf16[4,128,256]{2,1,0:T(8,128)(2,1)S(1)} %get-tuple-element.28.x.rest_0_), channel_id=1, source_target_pairs={{0,225},{1,224},{2,227},{3,226},{4,229},{5,228},{6,231},{7,230},{8... | collective-permute-start | bytes 786440 | tf_op jit(solution)/shard_map/ppermute | solution.py:50
  20.6 7.6 %collective-permute-start.5 = (bf16[2,128,256]{2,1,0:T(8,128)(2,1)S(1)}, bf16[2,128,256]{2,1,0:T(8,128)(2,1)S(1)}, u32[]{:S(2)}, u32[]{:S(2)}) collective-permute-start(bf16[2,128,256]{2,1,0:T(8,128)(2,1)S(1)} %pad_maximum_fusion.ends), channel_id=1, source_target_pairs={{0,32},{1,33},{2,34},{3,35},{4,36},{5,37},{6,38},{7,39},{8,40},{9,... | collective-permute-start | bytes 393224 | tf_op jit(solution)/shard_map/ppermute | solution.py:50
  20.7 9.3 %collective-permute-start.6 = (bf16[2,128,256]{2,1,0:T(8,128)(2,1)S(1)}, bf16[2,128,256]{2,1,0:T(8,128)(2,1)S(1)}, u32[]{:S(2)}, u32[]{:S(2)}) collective-permute-start(bf16[2,128,256]{2,1,0:T(8,128)(2,1)S(1)} %pad_maximum_fusion.ends), channel_id=1, source_target_pairs={{0,225},{1,224},{2,227},{3,226},{4,229},{5,228},{6,231},{7,230},{8... | collective-permute-start | bytes 393224 | tf_op jit(solution)/shard_map/ppermute | solution.py:50
  21.6 1.7 copy-start
  30.8 5.9 %collective-permute-start.10 = (bf16[2,128,256]{2,1,0:T(8,128)(2,1)S(1)}, bf16[2,128,256]{2,1,0:T(8,128)(2,1)S(1)}, u32[]{:S(2)}, u32[]{:S(2)}) collective-permute-start(bf16[2,128,256]{2,1,0:T(8,128)(2,1)S(1)} %get-tuple-element.39), channel_id=1, source_target_pairs={{0,30},{1,31},{2,4},{3,5},{4,2},{5,3},{6,8},{7,9},{8,6},{9,7},{10,... | collective-permute-start | bytes 393224 | tf_op jit(solution)/shard_map/ppermute | solution.py:50
  30.9 5.8 %collective-permute-start.9 = (bf16[2,128,256]{2,1,0:T(8,128)(2,1)S(1)}, bf16[2,128,256]{2,1,0:T(8,128)(2,1)S(1)}, u32[]{:S(2)}, u32[]{:S(2)}) collective-permute-start(bf16[2,128,256]{2,1,0:T(8,128)(2,1)S(1)} %get-tuple-element.38), channel_id=1, source_target_pairs={{0,2},{1,3},{2,0},{3,1},{4,6},{5,7},{6,4},{7,5},{8,10},{9,11},{10,... | collective-permute-start | bytes 393224 | tf_op jit(solution)/shard_map/ppermute | solution.py:50
  32.5 7.9 %collective-permute-start.7 = (bf16[4,128,256]{2,1,0:T(8,128)(2,1)S(1)}, bf16[4,128,256]{2,1,0:T(8,128)(2,1)S(1)}, u32[]{:S(2)}, u32[]{:S(2)}) collective-permute-start(bf16[4,128,256]{2,1,0:T(8,128)(2,1)S(1)} %get-tuple-element.36.x), channel_id=1, source_target_pairs={{0,32},{1,33},{2,34},{3,35},{4,36},{5,37},{6,38},{7,39},{8,40},{9,... | collective-permute-start | bytes 786440 | tf_op jit(solution)/shard_map/ppermute | solution.py:50
  32.5 11.3 %collective-permute-start.8 = (bf16[4,128,256]{2,1,0:T(8,128)(2,1)S(1)}, bf16[4,128,256]{2,1,0:T(8,128)(2,1)S(1)}, u32[]{:S(2)}, u32[]{:S(2)}) collective-permute-start(bf16[4,128,256]{2,1,0:T(8,128)(2,1)S(1)} %get-tuple-element.36.x), channel_id=1, source_target_pairs={{0,225},{1,224},{2,227},{3,226},{4,229},{5,228},{6,231},{7,230},{8... | collective-permute-start | bytes 786440 | tf_op jit(solution)/shard_map/ppermute | solution.py:50
  36.8 8.0 %collective-permute-start.11 = (bf16[2,128,256]{2,1,0:T(8,128)(2,1)S(1)}, bf16[2,128,256]{2,1,0:T(8,128)(2,1)S(1)}, u32[]{:S(2)}, u32[]{:S(2)}) collective-permute-start(bf16[2,128,256]{2,1,0:T(8,128)(2,1)S(1)} %pad_maximum_fusion.1.ends), channel_id=1, source_target_pairs={{0,32},{1,33},{2,34},{3,35},{4,36},{5,37},{6,38},{7,39},{8,40},{9,... | collective-permute-start | bytes 393224 | tf_op jit(solution)/shard_map/ppermute | solution.py:50
  36.9 9.6 %collective-permute-start.12 = (bf16[2,128,256]{2,1,0:T(8,128)(2,1)S(1)}, bf16[2,128,256]{2,1,0:T(8,128)(2,1)S(1)}, u32[]{:S(2)}, u32[]{:S(2)}) collective-permute-start(bf16[2,128,256]{2,1,0:T(8,128)(2,1)S(1)} %pad_maximum_fusion.1.ends), channel_id=1, source_target_pairs={{0,225},{1,224},{2,227},{3,226},{4,229},{5,228},{6,231},{7,230},{8... | collective-permute-start | bytes 393224 | tf_op jit(solution)/shard_map/ppermute | solution.py:50
  47.4 10.3 %collective-permute-start.15 = (bf16[4,128,256]{2,1,0:T(8,128)(2,1)S(1)}, bf16[4,128,256]{2,1,0:T(8,128)(2,1)S(1)}, u32[]{:S(2)}, u32[]{:S(2)}) collective-permute-start(bf16[4,128,256]{2,1,0:T(8,128)(2,1)S(1)} %get-tuple-element.42.s), channel_id=1, source_target_pairs={{0,225},{1,224},{2,227},{3,226},{4,229},{5,228},{6,231},{7,230},{8... | collective-permute-start | bytes 786440 | tf_op jit(solution)/shard_map/ppermute | solution.py:54
  51.7 2.0 %collective-permute-start.13 = (bf16[1,128,256]{2,1,0:T(8,128)(2,1)S(1)}, bf16[1,128,256]{2,1,0:T(8,128)(2,1)S(1)}, u32[]{:S(2)}, u32[]{:S(2)}) collective-permute-start(bf16[1,128,256]{2,1,0:T(8,128)(2,1)S(1)} %get-tuple-element.43), channel_id=1, source_target_pairs={{0,2},{1,3},{2,0},{3,1},{4,6},{5,7},{6,4},{7,5},{8,10},{9,11},{10,... | collective-permute-start | bytes 196616 | tf_op jit(solution)/shard_map/ppermute | solution.py:50
  52.8 4.0 %collective-permute-start.14 = (bf16[1,128,256]{2,1,0:T(8,128)(2,1)S(1)}, bf16[1,128,256]{2,1,0:T(8,128)(2,1)S(1)}, u32[]{:S(2)}, u32[]{:S(2)}) collective-permute-start(bf16[1,128,256]{2,1,0:T(8,128)(2,1)S(1)} %get-tuple-element.44), channel_id=1, source_target_pairs={{0,30},{1,31},{2,4},{3,5},{4,2},{5,3},{6,8},{7,9},{8,6},{9,7},{10,... | collective-permute-start | bytes 196616 | tf_op jit(solution)/shard_map/ppermute | solution.py:50
  59.0 2.2 %collective-permute-start.16 = (f32[64,1,640]{2,1,0:T(1,128)S(1)}, f32[64,1,640]{2,1,0:T(1,128)S(1)}, u32[]{:S(2)}, u32[]{:S(2)}) collective-permute-start(f32[64,1,640]{2,1,0:T(1,128)S(1)} %get-tuple-element.49), channel_id=1, source_target_pairs={{0,2},{1,3},{2,0},{3,1},{4,6},{5,7},{6,4},{7,5},{8,10},{9,11},{10,... | collective-permute-start | bytes 491528 | tf_op jit(solution)/shard_map/ppermute | solution.py:50
  60.2 11.8 %collective-permute-start.17 = (bf16[4,128,256]{2,1,0:T(8,128)(2,1)S(1)}, bf16[4,128,256]{2,1,0:T(8,128)(2,1)S(1)}, u32[]{:S(2)}, u32[]{:S(2)}) collective-permute-start(bf16[4,128,256]{2,1,0:T(8,128)(2,1)S(1)} %get-tuple-element.42.s), channel_id=1, source_target_pairs={{0,1},{1,0},{2,3},{3,2},{4,5},{5,4},{6,7},{7,6},{8,9},{9,8},{10,11... | collective-permute-start | bytes 786440 | tf_op jit(solution)/shard_map/ppermute | solution.py:59
  62.1 21.5 %all-to-all-start = ((f32[64,1,640]{2,1,0:T(1,128)}), f32[64,1,640]{2,1,0:T(1,128)S(1)}, u32[]{:S(2)}, u32[]{:S(2)}) async-start(f32[64,1,640]{2,1,0:T(1,128)} %add.59), calls=%async_computation | async-start | bytes 327680 | tf_op jit(solution)/shard_map/all_to_all | solution.py:74
  104.1 5.2 %collective-permute-start.18 = (f32[128,1,640]{2,1,0:T(1,128)S(1)}, f32[128,1,640]{2,1,0:T(1,128)S(1)}, u32[]{:S(2)}, u32[]{:S(2)}) collective-permute-start(f32[128,1,640]{2,1,0:T(1,128)S(1)} %all_to_all.10.mine), channel_id=1, source_target_pairs={{0,2},{1,3},{2,0},{3,1},{4,6},{5,7},{6,4},{7,5},{8,10},{9,11},{10,... | collective-permute-start | bytes 983048 | tf_op jit(solution)/shard_map/ppermute | solution.py:50

commit v11 on v10

--- a/solution.py
+++ b/solution.py
@@ -170,16 +170,15 @@
             to[1, :, T:] = block[...]
 
 
-def corr_kernel(m, o, s, p, q, corr, turned, acc):
+def corr_kernel(m, o, s, corr, turned, acc):
     flat = s[...].reshape(4 * T, 2 * T)
-    turned[:, : 4 * T] = flat.T
-    turned[:, 4 * T : 5 * T] = p[0].T
-    turned[:, 5 * T :] = q[0].T
-    corr[...] = dot(turned[:, : 4 * T], flat)
-    above = jnp.where(m[PAR_Y] == 0, p[0], q[0])
+    turned[...] = flat.T
+    corr[...] = dot(turned[...], flat)
     for tile in range(4):
         total = 0.5 * dot(blocks(o, tile, (0,), (1,)), s[tile])
-        acc[tile] = total + dot(blocks(o, tile, (0,), (2,)), s[tile + 1] if tile < 3 else above)
+        if tile < 3:
+            total += dot(blocks(o, tile, (0,), (2,)), s[tile + 1])
+        acc[tile] = total
 
 
 def places():
@@ -187,17 +186,20 @@
     return lax.broadcasted_iota(jnp.int32, shape, 0), lax.broadcasted_iota(jnp.int32, shape, 1)
 
 
-def gram_kernel(m, o, turned, right, h_p, h_q, acc, corr, mine, theirs):
+def gram_kernel(m, o, turned, p, q, right, h_p, h_q, acc, corr, mine, theirs):
     side = 1 + m[PAR_X]
     parts = []
     for tile in range(4):
         at = [place for place in range(tile, tile + 3) if 1 <= place <= 4]
         parts.append(acc[tile] + product(o, tile, (side,), at, [right[at[0] - 1 : at[-1]]]))
     even = m[PAR_Y] == 0
-    parts.append(dot(h_p[1, :, :T], right[jnp.where(even, 3, 0)]))
-    parts.append(dot(h_q[1, :, :T], right[jnp.where(even, 0, 3)]))
+    above = jnp.where(even, p[...], q[...])
+    parts[3] += product(o, 3, (0,), (5,), [above])
     high, low = split(jnp.concatenate(parts, axis=0))
     half = dot(turned[...], high) + dot(turned[...], low)
+    for tile, block, at in ((p, h_p, jnp.where(even, 3, 0)), (q, h_q, jnp.where(even, 0, 3))):
+        high, low = split(dot(block[1, :, :T], right[at]))
+        half += dot(tile[0], high, ((0,), (0,))) + dot(tile[0], low, ((0,), (0,)))
     coupling = half + half.T
     rows, cols = places()
     both = jnp.where(rows >= cols, corr[...], coupling)
@@ -254,7 +256,13 @@
         scaled = corr * scale_row * scale_col
         scales.append(scale_row)
         a_ref[spin] = scaled
-        x_ref[spin] = unit - lower_part(scaled - unit, rows, cols)
+        e = scaled - unit
+        f = lower_part(e, rows, cols)
+        f_half = f.astype(BF)
+        fe = dot(f_half, e.astype(BF))
+        e = dot((f + fe - e).astype(BF), f_half, ((1,), (1,))) - fe
+        x = unit - f
+        x_ref[spin] = x - dot(lower_part(e, rows, cols).astype(BF), x.astype(BF))
 
     def step(state):
         count, _, _ = state
@@ -262,7 +270,7 @@
         es = [dot3(xs[spin], a_ref[spin]) for spin in range(2)]
         es = [dot3(es[spin], xs[spin], ((1,), (1,))) - unit for spin in range(2)]
         for spin in range(2):
-            x_ref[spin] = xs[spin] - dot3(lower_part(es[spin], rows, cols), xs[spin])
+            x_ref[spin] = xs[spin] - dot(lower_part(es[spin], rows, cols).astype(BF), xs[spin].astype(BF))
         return count + 1, jnp.sum(es[0] * es[0]), jnp.sum(es[1] * es[1])
 
     def more(state):
@@ -381,12 +389,11 @@
     right = shift(sizes, second, -1, 0)
     p, q = swap(sizes, p, 0, 1), swap(sizes, q, 0, 2)
     corr, turned, acc = call(
-        corr_kernel, m, [o, second, p, q],
-        [shaped(full, F32), shaped((2 * T, 6 * T), BF), shaped(block, F32)], "corr", 16,
+        corr_kernel, m, [o, second], [shaped(full, F32), shaped((2 * T, 4 * T), BF), shaped(block, F32)], "corr", 15
     )
     piece = shaped((members // 2, 1, 5 * T), F32)
     mine, theirs = call(
-        gram_kernel, m, [o, turned, right, h_p, h_q, acc, corr], [piece, piece], "gram", 30
+        gram_kernel, m, [o, turned, p, q, right, h_p, h_q, acc, corr], [piece, piece], "gram", 30
     )
 
     rows = members * second.shape[0] * second.shape[1]

time: 188 us -> 189 us (level)
  transfers between devices with their start and end apart: 20 -> 20, of which waited for: 11 -> 10; matrix products, arithmetic and copies ran while one was open for 2% -> 2% of each run, Pallas kernels for 2% -> 2%
where the time goes in v11:
time: 189 us
  Pallas kernels  87.3 us (46%)
  starting transfers between devices  47.4 us (25%)
  waiting for transfers between devices  26.9 us (14%)
  blocking collectives  20.3 us (11%)
  local copies, waits for them, and re-layouts  3.13 us (2%)
  other arithmetic  2.89 us (2%)
    pallas_call x10, Pallas kernels, call(): pl.pallas_call(kernel, out_shape=outs, grid_spec=pltpu.PrefetchScalarGrid...  87.3 us
    ppermute x16, starting transfers between devices, swap(): return lax.ppermute(block, AXES, perm)  29.1 us
    all_to_all x1, blocking collectives, exchange(): lax.all_to_all(pieces, AXES, 0, 0, axis_index_groups=groups, tiled=True)  20.3 us
    ppermute x16, waiting for transfers between devices, swap(): return lax.ppermute(block, AXES, perm)  15.8 us
    all_to_all x1, waiting for transfers between devices, exchange(): lax.all_to_all(pieces, AXES, 0, 0, axis_index_groups=groups, tiled=True)  11 us
    all_to_all x1, starting transfers between devices, exchange(): lax.all_to_all(pieces, AXES, 0, 0, axis_index_groups=groups, tiled=True)  10.3 us
    ppermute x1, starting transfers between devices, shift(): lax.ppermute(block, AXES, pairs(sizes, lambda gx, gy: (gx + dx, gy + dy)))  4.34 us
  transfers between devices with their start and end apart: 20, of which 10 were waited for; matrix products, arithmetic and copies ran while one was open for 2% of the time, Pallas kernels for 2%

profile of v11, /device:TPU:1, one launch (start us, length us, event | category | flops | bytes accessed | tf_op | source)
XLA Modules:
  0.0 188.8 jit_solution(8993370964504935463)
XLA Ops:
  0.6 1.0 dynamic-slice_bitcast_fusion
  1.6 3.7 %collective-permute-start = (bf16[4,128,128]{2,1,0:T(8,128)(2,1)S(1)}, bf16[4,128,128]{2,1,0:T(8,128)(2,1)S(1)}, u32[]{:S(2)}, u32[]{:S(2)}) collective-permute-start(bf16[4,128,128]{2,1,0:T(8,128)(2,1)S(1)} %get-tuple-element.52), channel_id=1, source_target_pairs={{0,1},{1,0},{2,3},{3,2},{4,5},{5,4},{6,7},{7,6},{8,9},{9,8},{10,11... | collective-permute-start | bytes 393224 | tf_op jit(solution)/shard_map/ppermute | solution.py:59
  6.2 1.0 select_reduce_fusion
  8.3 3.9 %collective-permute-start.4 = (bf16[2,128,256]{2,1,0:T(8,128)(2,1)S(1)}, bf16[2,128,256]{2,1,0:T(8,128)(2,1)S(1)}, u32[]{:S(2)}, u32[]{:S(2)}) collective-permute-start(bf16[2,128,256]{2,1,0:T(8,128)(2,1)S(1)} %get-tuple-element.31), channel_id=1, source_target_pairs={{0,30},{1,31},{2,4},{3,5},{4,2},{5,3},{6,8},{7,9},{8,6},{9,7},{10,... | collective-permute-start | bytes 393224 | tf_op jit(solution)/shard_map/ppermute | solution.py:50
  12.2 2.9 %collective-permute-start.3 = (bf16[1,128,256]{2,1,0:T(8,128)(2,1)S(1)}, bf16[1,128,256]{2,1,0:T(8,128)(2,1)S(1)}, u32[]{:S(2)}, u32[]{:S(2)}) collective-permute-start(bf16[1,128,256]{2,1,0:T(8,128)(2,1)S(1)} %get-tuple-element.30), channel_id=1, source_target_pairs={{0,2},{1,3},{2,0},{3,1},{4,6},{5,7},{6,4},{7,5},{8,10},{9,11},{10,... | collective-permute-start | bytes 196616 | tf_op jit(solution)/shard_map/ppermute | solution.py:50
  15.1 1.2 collective-permute-start.1
  16.3 4.3 %collective-permute-start.2 = (bf16[4,128,256]{2,1,0:T(8,128)(2,1)S(1)}, bf16[4,128,256]{2,1,0:T(8,128)(2,1)S(1)}, u32[]{:S(2)}, u32[]{:S(2)}) collective-permute-start(bf16[4,128,256]{2,1,0:T(8,128)(2,1)S(1)} %get-tuple-element.28.x.rest_0_), channel_id=1, source_target_pairs={{0,225},{1,224},{2,227},{3,226},{4,229},{5,228},{6,231},{7,230},{8... | collective-permute-start | bytes 786440 | tf_op jit(solution)/shard_map/ppermute | solution.py:50
  20.7 0.9 collective-permute-start.6
  21.6 1.7 copy-done
  23.3 0.9 order.1
  24.2 3.1 %collective-permute-done.2.b = bf16[4,128,256]{2,1,0:T(8,128)(2,1)S(1)} collective-permute-done((bf16[4,128,256]{2,1,0:T(8,128)(2,1)S(1)}, bf16[4,128,256]{2,1,0:T(8,128)(2,1)S(1)}, u32[]{:S(2)}, u32[]{:S(2)}) %collective-permute-start.2) | collective-permute-done | bytes 262176 | tf_op jit(solution)/shard_map/ppermute | solution.py:50
  27.3 1.0 core.2.acc
  28.3 1.8 collective-permute-done.6.b_ends
  30.9 1.6 collective-permute-start.9
  32.5 4.3 %collective-permute-start.8 = (bf16[4,128,256]{2,1,0:T(8,128)(2,1)S(1)}, bf16[4,128,256]{2,1,0:T(8,128)(2,1)S(1)}, u32[]{:S(2)}, u32[]{:S(2)}) collective-permute-start(bf16[4,128,256]{2,1,0:T(8,128)(2,1)S(1)} %get-tuple-element.36.x), channel_id=1, source_target_pairs={{0,225},{1,224},{2,227},{3,226},{4,229},{5,228},{6,231},{7,230},{8... | collective-permute-start | bytes 786440 | tf_op jit(solution)/shard_map/ppermute | solution.py:50
  36.9 2.9 %collective-permute-start.12 = (bf16[2,128,256]{2,1,0:T(8,128)(2,1)S(1)}, bf16[2,128,256]{2,1,0:T(8,128)(2,1)S(1)}, u32[]{:S(2)}, u32[]{:S(2)}) collective-permute-start(bf16[2,128,256]{2,1,0:T(8,128)(2,1)S(1)} %pad_maximum_fusion.1.ends), channel_id=1, source_target_pairs={{0,225},{1,224},{2,227},{3,226},{4,229},{5,228},{6,231},{7,230},{8... | collective-permute-start | bytes 393224 | tf_op jit(solution)/shard_map/ppermute | solution.py:50
  40.4 3.3 %collective-permute-done.8.b = bf16[4,128,256]{2,1,0:T(8,128)(2,1)S(1)} collective-permute-done((bf16[4,128,256]{2,1,0:T(8,128)(2,1)S(1)}, bf16[4,128,256]{2,1,0:T(8,128)(2,1)S(1)}, u32[]{:S(2)}, u32[]{:S(2)}) %collective-permute-start.8) | collective-permute-done | bytes 262176 | tf_op jit(solution)/shard_map/ppermute | solution.py:50
  43.8 1.0 core.3.acc
  44.8 1.8 collective-permute-done.12.b_ends
  47.4 4.3 %collective-permute-start.15 = (bf16[4,128,256]{2,1,0:T(8,128)(2,1)S(1)}, bf16[4,128,256]{2,1,0:T(8,128)(2,1)S(1)}, u32[]{:S(2)}, u32[]{:S(2)}) collective-permute-start(bf16[4,128,256]{2,1,0:T(8,128)(2,1)S(1)} %get-tuple-element.42.s), channel_id=1, source_target_pairs={{0,225},{1,224},{2,227},{3,226},{4,229},{5,228},{6,231},{7,230},{8... | collective-permute-start | bytes 786440 | tf_op jit(solution)/shard_map/ppermute | solution.py:54
  51.7 1.1 collective-permute-start.13
  53.0 0.9 corr.1
  53.9 2.9 %collective-permute-done.14.q = bf16[1,128,256]{2,1,0:T(8,128)(2,1)S(1)} collective-permute-done((bf16[1,128,256]{2,1,0:T(8,128)(2,1)S(1)}, bf16[1,128,256]{2,1,0:T(8,128)(2,1)S(1)}, u32[]{:S(2)}, u32[]{:S(2)}) %collective-permute-start.14) | collective-permute-done | bytes 65568 | tf_op jit(solution)/shard_map/ppermute | solution.py:50
  56.8 1.7 gram.1
  58.5 1.7 collective-permute-start.16
  60.3 1.0 collective-permute-done.16
  62.1 10.3 %all-to-all-start = ((f32[64,1,640]{2,1,0:T(1,128)}), f32[64,1,640]{2,1,0:T(1,128)S(1)}, u32[]{:S(2)}, u32[]{:S(2)}) async-start(f32[64,1,640]{2,1,0:T(1,128)} %add.59), calls=%async_computation | async-start | bytes 327680 | tf_op jit(solution)/shard_map/all_to_all | solution.py:74
  73.0 11.0 %all-to-all-done = f32[64,1,640]{2,1,0:T(1,128)S(1)} async-done(((f32[64,1,640]{2,1,0:T(1,128)}), f32[64,1,640]{2,1,0:T(1,128)S(1)}, u32[]{:S(2)}, u32[]{:S(2)}) %all-to-all-start) | async-done | bytes 163872 | tf_op jit(solution)/shard_map/all_to_all | solution.py:74
  84.3 20.3 %all_to_all.10.mine = f32[128,1,640]{2,1,0:T(1,128)S(1)} all-to-all(f32[128,1,640]{2,1,0:T(1,128)S(1)} %broadcast_in_dim.20), channel_id=1, replica_groups={{0,4,8,12,16,20,24,28,32,36,40,44,48,52,56,60,65,69,73,77,81,85,89,93,9..., dimensions={0} | all-to-all | bytes 655360 | tf_op jit(solution)/shard_map/all_to_all | solution.py:74
  104.6 3.9 %collective-permute-start.18 = (f32[128,1,640]{2,1,0:T(1,128)S(1)}, f32[128,1,640]{2,1,0:T(1,128)S(1)}, u32[]{:S(2)}, u32[]{:S(2)}) collective-permute-start(f32[128,1,640]{2,1,0:T(1,128)S(1)} %all_to_all.10.mine), channel_id=1, source_target_pairs={{0,2},{1,3},{2,0},{3,1},{4,6},{5,7},{6,4},{7,5},{8,10},{9,11},{10,... | collective-permute-start | bytes 983048 | tf_op jit(solution)/shard_map/ppermute | solution.py:50
  108.5 1.3 collective-permute-done.18.theirs
  109.8 79.0 %final.1 = (bf16[2,1,4,128,128]{4,3,2,1,0:T(8,128)(2,1)}, f32[2,256,128]{2,1,0:T(8,128)}) custom-call(s32[40]{0:T(128)S(1)} %concatenate.13.m, f32[128,1,640]{2,1,0:T(1,128)S(1)} %all_to_all.10.mine, f32[128,1,640]{2,1,0:T(1,128)S(1)} %collective-permute-done.18.theirs, bf16[2,4,128,256]{3,2,1,0:T(8,128)(2,1)S(1)} %stack.29.both), custom_call_target="tpu_custom_call" | custom-call | flops 1677721600 | bytes 1703936 | tf_op jit(solution)/shard_map/final/pallas_call | solution.py:320
  (40 shorter events, 6.4 us)
Async XLA Ops:
  1.6 6.0 %collective-permute-start = (bf16[4,128,128]{2,1,0:T(8,128)(2,1)S(1)}, bf16[4,128,128]{2,1,0:T(8,128)(2,1)S(1)}, u32[]{:S(2)}, u32[]{:S(2)}) collective-permute-start(bf16[4,128,128]{2,1,0:T(8,128)(2,1)S(1)} %get-tuple-element.52), channel_id=1, source_target_pairs={{0,1},{1,0},{2,3},{3,2},{4,5},{5,4},{6,7},{7,6},{8,9},{9,8},{10,11... | collective-permute-start | bytes 393224 | tf_op jit(solution)/shard_map/ppermute | solution.py:59
  8.3 12.3 %collective-permute-start.4 = (bf16[2,128,256]{2,1,0:T(8,128)(2,1)S(1)}, bf16[2,128,256]{2,1,0:T(8,128)(2,1)S(1)}, u32[]{:S(2)}, u32[]{:S(2)}) collective-permute-start(bf16[2,128,256]{2,1,0:T(8,128)(2,1)S(1)} %get-tuple-element.31), channel_id=1, source_target_pairs={{0,30},{1,31},{2,4},{3,5},{4,2},{5,3},{6,8},{7,9},{8,6},{9,7},{10,... | collective-permute-start | bytes 393224 | tf_op jit(solution)/shard_map/ppermute | solution.py:50
  12.2 8.4 %collective-permute-start.3 = (bf16[1,128,256]{2,1,0:T(8,128)(2,1)S(1)}, bf16[1,128,256]{2,1,0:T(8,128)(2,1)S(1)}, u32[]{:S(2)}, u32[]{:S(2)}) collective-permute-start(bf16[1,128,256]{2,1,0:T(8,128)(2,1)S(1)} %get-tuple-element.30), channel_id=1, source_target_pairs={{0,2},{1,3},{2,0},{3,1},{4,6},{5,7},{6,4},{7,5},{8,10},{9,11},{10,... | collective-permute-start | bytes 196616 | tf_op jit(solution)/shard_map/ppermute | solution.py:50
  15.1 9.1 %collective-permute-start.1 = (bf16[4,128,256]{2,1,0:T(8,128)(2,1)S(1)}, bf16[4,128,256]{2,1,0:T(8,128)(2,1)S(1)}, u32[]{:S(2)}, u32[]{:S(2)}) collective-permute-start(bf16[4,128,256]{2,1,0:T(8,128)(2,1)S(1)} %get-tuple-element.28.x.rest_0_), channel_id=1, source_target_pairs={{0,32},{1,33},{2,34},{3,35},{4,36},{5,37},{6,38},{7,39},{8,40},{9,... | collective-permute-start | bytes 786440 | tf_op jit(solution)/shard_map/ppermute | solution.py:50
  16.3 10.9 %collective-permute-start.2 = (bf16[4,128,256]{2,1,0:T(8,128)(2,1)S(1)}, bf16[4,128,256]{2,1,0:T(8,128)(2,1)S(1)}, u32[]{:S(2)}, u32[]{:S(2)}) collective-permute-start(bf16[4,128,256]{2,1,0:T(8,128)(2,1)S(1)} %get-tuple-element.28.x.rest_0_), channel_id=1, source_target_pairs={{0,225},{1,224},{2,227},{3,226},{4,229},{5,228},{6,231},{7,230},{8... | collective-permute-start | bytes 786440 | tf_op jit(solution)/shard_map/ppermute | solution.py:50
  20.6 7.6 %collective-permute-start.5 = (bf16[2,128,256]{2,1,0:T(8,128)(2,1)S(1)}, bf16[2,128,256]{2,1,0:T(8,128)(2,1)S(1)}, u32[]{:S(2)}, u32[]{:S(2)}) collective-permute-start(bf16[2,128,256]{2,1,0:T(8,128)(2,1)S(1)} %pad_maximum_fusion.ends), channel_id=1, source_target_pairs={{0,32},{1,33},{2,34},{3,35},{4,36},{5,37},{6,38},{7,39},{8,40},{9,... | collective-permute-start | bytes 393224 | tf_op jit(solution)/shard_map/ppermute | solution.py:50
  20.7 9.3 %collective-permute-start.6 = (bf16[2,128,256]{2,1,0:T(8,128)(2,1)S(1)}, bf16[2,128,256]{2,1,0:T(8,128)(2,1)S(1)}, u32[]{:S(2)}, u32[]{:S(2)}) collective-permute-start(bf16[2,128,256]{2,1,0:T(8,128)(2,1)S(1)} %pad_maximum_fusion.ends), channel_id=1, source_target_pairs={{0,225},{1,224},{2,227},{3,226},{4,229},{5,228},{6,231},{7,230},{8... | collective-permute-start | bytes 393224 | tf_op jit(solution)/shard_map/ppermute | solution.py:50
  21.6 1.7 copy-start
  30.8 5.9 %collective-permute-start.10 = (bf16[2,128,256]{2,1,0:T(8,128)(2,1)S(1)}, bf16[2,128,256]{2,1,0:T(8,128)(2,1)S(1)}, u32[]{:S(2)}, u32[]{:S(2)}) collective-permute-start(bf16[2,128,256]{2,1,0:T(8,128)(2,1)S(1)} %get-tuple-element.39), channel_id=1, source_target_pairs={{0,30},{1,31},{2,4},{3,5},{4,2},{5,3},{6,8},{7,9},{8,6},{9,7},{10,... | collective-permute-start | bytes 393224 | tf_op jit(solution)/shard_map/ppermute | solution.py:50
  30.9 5.8 %collective-permute-start.9 = (bf16[2,128,256]{2,1,0:T(8,128)(2,1)S(1)}, bf16[2,128,256]{2,1,0:T(8,128)(2,1)S(1)}, u32[]{:S(2)}, u32[]{:S(2)}) collective-permute-start(bf16[2,128,256]{2,1,0:T(8,128)(2,1)S(1)} %get-tuple-element.38), channel_id=1, source_target_pairs={{0,2},{1,3},{2,0},{3,1},{4,6},{5,7},{6,4},{7,5},{8,10},{9,11},{10,... | collective-permute-start | bytes 393224 | tf_op jit(solution)/shard_map/ppermute | solution.py:50
  32.5 7.9 %collective-permute-start.7 = (bf16[4,128,256]{2,1,0:T(8,128)(2,1)S(1)}, bf16[4,128,256]{2,1,0:T(8,128)(2,1)S(1)}, u32[]{:S(2)}, u32[]{:S(2)}) collective-permute-start(bf16[4,128,256]{2,1,0:T(8,128)(2,1)S(1)} %get-tuple-element.36.x), channel_id=1, source_target_pairs={{0,32},{1,33},{2,34},{3,35},{4,36},{5,37},{6,38},{7,39},{8,40},{9,... | collective-permute-start | bytes 786440 | tf_op jit(solution)/shard_map/ppermute | solution.py:50
  32.5 11.3 %collective-permute-start.8 = (bf16[4,128,256]{2,1,0:T(8,128)(2,1)S(1)}, bf16[4,128,256]{2,1,0:T(8,128)(2,1)S(1)}, u32[]{:S(2)}, u32[]{:S(2)}) collective-permute-start(bf16[4,128,256]{2,1,0:T(8,128)(2,1)S(1)} %get-tuple-element.36.x), channel_id=1, source_target_pairs={{0,225},{1,224},{2,227},{3,226},{4,229},{5,228},{6,231},{7,230},{8... | collective-permute-start | bytes 786440 | tf_op jit(solution)/shard_map/ppermute | solution.py:50
  36.8 8.0 %collective-permute-start.11 = (bf16[2,128,256]{2,1,0:T(8,128)(2,1)S(1)}, bf16[2,128,256]{2,1,0:T(8,128)(2,1)S(1)}, u32[]{:S(2)}, u32[]{:S(2)}) collective-permute-start(bf16[2,128,256]{2,1,0:T(8,128)(2,1)S(1)} %pad_maximum_fusion.1.ends), channel_id=1, source_target_pairs={{0,32},{1,33},{2,34},{3,35},{4,36},{5,37},{6,38},{7,39},{8,40},{9,... | collective-permute-start | bytes 393224 | tf_op jit(solution)/shard_map/ppermute | solution.py:50
  36.9 9.6 %collective-permute-start.12 = (bf16[2,128,256]{2,1,0:T(8,128)(2,1)S(1)}, bf16[2,128,256]{2,1,0:T(8,128)(2,1)S(1)}, u32[]{:S(2)}, u32[]{:S(2)}) collective-permute-start(bf16[2,128,256]{2,1,0:T(8,128)(2,1)S(1)} %pad_maximum_fusion.1.ends), channel_id=1, source_target_pairs={{0,225},{1,224},{2,227},{3,226},{4,229},{5,228},{6,231},{7,230},{8... | collective-permute-start | bytes 393224 | tf_op jit(solution)/shard_map/ppermute | solution.py:50
  47.4 9.4 %collective-permute-start.15 = (bf16[4,128,256]{2,1,0:T(8,128)(2,1)S(1)}, bf16[4,128,256]{2,1,0:T(8,128)(2,1)S(1)}, u32[]{:S(2)}, u32[]{:S(2)}) collective-permute-start(bf16[4,128,256]{2,1,0:T(8,128)(2,1)S(1)} %get-tuple-element.42.s), channel_id=1, source_target_pairs={{0,225},{1,224},{2,227},{3,226},{4,229},{5,228},{6,231},{7,230},{8... | collective-permute-start | bytes 786440 | tf_op jit(solution)/shard_map/ppermute | solution.py:54
  51.7 2.1 %collective-permute-start.13 = (bf16[1,128,256]{2,1,0:T(8,128)(2,1)S(1)}, bf16[1,128,256]{2,1,0:T(8,128)(2,1)S(1)}, u32[]{:S(2)}, u32[]{:S(2)}) collective-permute-start(bf16[1,128,256]{2,1,0:T(8,128)(2,1)S(1)} %get-tuple-element.44), channel_id=1, source_target_pairs={{0,2},{1,3},{2,0},{3,1},{4,6},{5,7},{6,4},{7,5},{8,10},{9,11},{10,... | collective-permute-start | bytes 196616 | tf_op jit(solution)/shard_map/ppermute | solution.py:50
  52.8 4.0 %collective-permute-start.14 = (bf16[1,128,256]{2,1,0:T(8,128)(2,1)S(1)}, bf16[1,128,256]{2,1,0:T(8,128)(2,1)S(1)}, u32[]{:S(2)}, u32[]{:S(2)}) collective-permute-start(bf16[1,128,256]{2,1,0:T(8,128)(2,1)S(1)} %get-tuple-element.45), channel_id=1, source_target_pairs={{0,30},{1,31},{2,4},{3,5},{4,2},{5,3},{6,8},{7,9},{8,6},{9,7},{10,... | collective-permute-start | bytes 196616 | tf_op jit(solution)/shard_map/ppermute | solution.py:50
  58.5 2.8 %collective-permute-start.16 = (f32[64,1,640]{2,1,0:T(1,128)S(1)}, f32[64,1,640]{2,1,0:T(1,128)S(1)}, u32[]{:S(2)}, u32[]{:S(2)}) collective-permute-start(f32[64,1,640]{2,1,0:T(1,128)S(1)} %get-tuple-element.49), channel_id=1, source_target_pairs={{0,2},{1,3},{2,0},{3,1},{4,6},{5,7},{6,4},{7,5},{8,10},{9,11},{10,... | collective-permute-start | bytes 491528 | tf_op jit(solution)/shard_map/ppermute | solution.py:50
  60.3 12.1 %collective-permute-start.17 = (bf16[4,128,256]{2,1,0:T(8,128)(2,1)S(1)}, bf16[4,128,256]{2,1,0:T(8,128)(2,1)S(1)}, u32[]{:S(2)}, u32[]{:S(2)}) collective-permute-start(bf16[4,128,256]{2,1,0:T(8,128)(2,1)S(1)} %get-tuple-element.42.s), channel_id=1, source_target_pairs={{0,1},{1,0},{2,3},{3,2},{4,5},{5,4},{6,7},{7,6},{8,9},{9,8},{10,11... | collective-permute-start | bytes 786440 | tf_op jit(solution)/shard_map/ppermute | solution.py:59
  62.1 21.9 %all-to-all-start = ((f32[64,1,640]{2,1,0:T(1,128)}), f32[64,1,640]{2,1,0:T(1,128)S(1)}, u32[]{:S(2)}, u32[]{:S(2)}) async-start(f32[64,1,640]{2,1,0:T(1,128)} %add.59), calls=%async_computation | async-start | bytes 327680 | tf_op jit(solution)/shard_map/all_to_all | solution.py:74
  104.6 5.2 %collective-permute-start.18 = (f32[128,1,640]{2,1,0:T(1,128)S(1)}, f32[128,1,640]{2,1,0:T(1,128)S(1)}, u32[]{:S(2)}, u32[]{:S(2)}) collective-permute-start(f32[128,1,640]{2,1,0:T(1,128)S(1)} %all_to_all.10.mine), channel_id=1, source_target_pairs={{0,2},{1,3},{2,0},{3,1},{4,6},{5,7},{6,4},{7,5},{8,10},{9,11},{10,... | collective-permute-start | bytes 983048 | tf_op jit(solution)/shard_map/ppermute | solution.py:50

commit v12 on v11

--- a/solution.py
+++ b/solution.py
@@ -13,6 +13,8 @@
 BF = jnp.bfloat16
 F32 = jnp.float32
 SPIN, COL, PAR_Y, PAR_X = 36, 37, 38, 39
+HEAD = 16
+PAD = 32
 
 
 def col_of(gx, spin):
@@ -116,21 +118,29 @@
 
 def store_edges(m, ref, p, q):
     even = m[PAR_Y] == 0
-    p[0:1] = ref[pl.ds(jnp.where(even, 3, 0), 1)]
-    q[0:1] = ref[pl.ds(jnp.where(even, 0, 3), 1)]
-
-
-def join_kernel(m, own, other, v, p, q):
+    p[...] = ref[pl.ds(jnp.where(even, 3, 0), 1)].reshape(T, 2 * T)
+    q[...] = ref[pl.ds(jnp.where(even, 0, 3), 1)].reshape(T, 2 * T)
+
+
+def store_bulk(ref, to_b, to_a):
+    flat = ref[...].reshape(4 * T, 2 * T)
+    to_b[...] = flat[HEAD:]
+    to_a[: 4 * T] = flat
+    to_a[4 * T :] = flat[:PAD]
+
+
+def join_kernel(m, own, other, v, p, q, to_b, to_a):
     first_col = m[COL] == 0
     v[:, :, :T] = jnp.where(first_col, own[...], other[...])
     v[:, :, T:] = jnp.where(first_col, other[...], own[...])
     store_edges(m, v, p, q)
-    q[1:2] = v[1:2]
+    store_bulk(v, to_b, to_a)
 
 
 def ends_of(m, ends):
     even = m[PAR_Y] == 0
-    return jnp.where(even, ends[1:2], ends[0:1]), jnp.where(even, ends[0:1], ends[1:2])
+    p, q = ends[:T], ends[ends.shape[0] - T :]
+    return jnp.where(even, q, p), jnp.where(even, p, q)
 
 
 def product(o, tile, sides, at, sources):
@@ -140,34 +150,40 @@
 
 def core_kernel(m, o, x, ends, a, b, acc, ext):
     low, high = ends_of(m, ends)
-    ext[0:1] = low
+    ext[0] = low
     ext[1:5] = x[...]
-    ext[5:6] = high
+    ext[5] = high
     for tile in range(4):
         total = product(o, tile, (0,), range(tile, tile + 3), [ext[tile : tile + 3]])
         at = [place for place in range(tile, tile + 3) if 1 <= place <= 4]
-        sources = [y[at[0] - 1 : at[-1]] for y in (a, b)]
-        acc[tile] = total + product(o, tile, (1, 2), at, sources)
-
-
-def rim_kernel(m, o, a_ends, b_ends, acc, *rest, last):
-    *more, out, p, q = rest
+        total += product(o, tile, (1,), at, [a[(at[0] - 1) * T : at[-1] * T]])
+        at = [place for place in at if place > 1]
+        acc[tile] = total + product(o, tile, (2,), at, [b[(at[0] - 1) * T - HEAD : at[-1] * T - HEAD]])
+
+
+def rim_kernel(m, o, b, a_ends, b_ends, acc, *rest, last):
+    if last:
+        before, out, p, q = rest
+    else:
+        out, p, q, to_b, to_a = rest
     low, high = zip(ends_of(m, a_ends), ends_of(m, b_ends))
+    first = jnp.concatenate([b_ends[T : T + HEAD], b[: T - HEAD]], axis=0)
     for tile in range(4):
         total = acc[tile]
         if tile == 0:
-            total += product(o, tile, (1, 2), (0,), low)
+            total += product(o, tile, (2,), (0, 1), [jnp.concatenate([low[1], first], axis=0)])
+            total += product(o, tile, (1,), (0,), [low[0]])
+        if tile == 1:
+            total += product(o, tile, (2,), (1,), [first])
         if tile == 3:
             total += product(o, tile, (1, 2), (5,), high)
         if last:
-            out[tile] = (total - more[0][tile].astype(F32)).astype(BF)
+            out[tile] = (total - before[tile].astype(F32)).astype(BF)
         else:
             out[tile] = (0.5 * total).astype(BF)
     store_edges(m, out, p, q)
     if not last:
-        for to, block in zip((p, q), more):
-            to[1, :, :T] = block[...]
-            to[1, :, T:] = block[...]
+        store_bulk(out, to_b, to_a)
 
 
 def corr_kernel(m, o, s, corr, turned, acc):
@@ -198,8 +214,8 @@
     high, low = split(jnp.concatenate(parts, axis=0))
     half = dot(turned[...], high) + dot(turned[...], low)
     for tile, block, at in ((p, h_p, jnp.where(even, 3, 0)), (q, h_q, jnp.where(even, 0, 3))):
-        high, low = split(dot(block[1, :, :T], right[at]))
-        half += dot(tile[0], high, ((0,), (0,))) + dot(tile[0], low, ((0,), (0,)))
+        high, low = split(dot(block[...], right[at]))
+        half += dot(tile[...], high, ((0,), (0,))) + dot(tile[...], low, ((0,), (0,)))
     coupling = half + half.T
     rows, cols = places()
     both = jnp.where(rows >= cols, corr[...], coupling)
@@ -366,25 +382,27 @@
     o, h_p, h_q = call(
         order_kernel, m, [hamiltonian], [shaped((4, T, NB * T), BF), corner, corner], "order", specs=[spin_block]
     )
-    tile, two = shaped((1, T, 2 * T), BF), shaped((2, T, 2 * T), BF)
+    h_p, h_q = swap(sizes, h_p, 0, 1), swap(sizes, h_q, 0, 2)
+    tile = shaped((T, 2 * T), BF)
     ext = pltpu.VMEM((6, T, 2 * T), BF)
-    v, p, q = call(join_kernel, m, [own, other], [shaped(block, BF), tile, two], "join")
-
-    def apply_ham(o, x, p, q, more, edges, last):
+    other, o = lax.optimization_barrier((other, o))
+    bulk = [shaped((4 * T - HEAD, 2 * T), BF), shaped((4 * T + PAD, 2 * T), BF)]
+    outs = [shaped(block, BF), tile, tile, *bulk]
+    v, p, q, *rest = call(join_kernel, m, [own, other], outs, "join")
+
+    def apply_ham(x, p, q, rest, more, outs, *kept):
         p, q = swap(sizes, p, 0, 1), swap(sizes, q, 0, 2)
-        ends = jnp.concatenate([p[:1], q[:1]], axis=0)
-        a, b = swap(sizes, x, 1, 0), swap(sizes, x, 2, 0)
-        o, a, b = lax.optimization_barrier((o, a, b))
-        a_ends, b_ends = swap(sizes, ends, 1, 0), swap(sizes, ends, 2, 0)
-        (acc,) = call(core_kernel, m, [o, x, ends, a, b], [shaped(block, F32)], "core", 32, scratch=[ext])
-        out = call(
-            functools.partial(rim_kernel, last=last), m, [o, a_ends, b_ends, acc, *more],
-            [shaped(block, BF), edges, edges], "rim", 4,
-        )
-        return o, p, q, out
-
-    o, _, _, (first, p, q) = apply_ham(o, v, p, q, [h_p, h_q], two, False)
-    o, h_p, h_q, (second, p, q) = apply_ham(o, first, p, q, [v], tile, True)
+        ends = jnp.concatenate([p, q], axis=0)
+        a, b = swap(sizes, rest[1], 1, 0), swap(sizes, rest[0], 2, 0)
+        a_ends = swap(sizes, ends, 1, 0)
+        b_ends = swap(sizes, jnp.concatenate([p, x[0, :HEAD], q], axis=0), 2, 0)
+        (acc,) = call(core_kernel, m, [o, x, ends, a, b], [shaped(block, F32)], "core", 31, scratch=[ext])
+        acc, *kept = lax.optimization_barrier((acc, *kept))
+        kernel = functools.partial(rim_kernel, last=len(more) > 0)
+        return call(kernel, m, [o, b, a_ends, b_ends, acc, *more], outs, "rim", 6), kept
+
+    (first, p, q, *rest), (h_p, h_q) = apply_ham(v, p, q, rest, [], outs, h_p, h_q)
+    (second, p, q), _ = apply_ham(first, p, q, rest, [v], outs[:3])
 
     right = shift(sizes, second, -1, 0)
     p, q = swap(sizes, p, 0, 1), swap(sizes, q, 0, 2)

time: 189 us -> 190 us (level)
  waiting for transfers between devices: 26.9 us -> 28.8 us
    ppermute x16 -> x18, waiting for transfers between devices: 15.8 us -> 17.8 us  [swap(): return lax.ppermute(block, AXES, perm)]
    ppermute x16 -> x18, starting transfers between devices: 29.1 us -> 27.9 us  [swap(): return lax.ppermute(block, AXES, perm)]
  transfers between devices with their start and end apart: 20 -> 22, of which waited for: 10 -> 10; matrix products, arithmetic and copies ran while one was open for 2% -> 2% of each run, Pallas kernels for 2% -> 2%
where the time goes in v12:
time: 190 us
  Pallas kernels  87.4 us (46%)
  starting transfers between devices  46.5 us (24%)
  waiting for transfers between devices  28.8 us (15%)
  blocking collectives  20.3 us (11%)
  local copies, waits for them, and re-layouts  3.14 us (2%)
  other arithmetic  2.88 us (2%)
    pallas_call x10, Pallas kernels, call(): pl.pallas_call(kernel, out_shape=outs, grid_spec=pltpu.PrefetchScalarGrid...  87.4 us
    ppermute x18, starting transfers between devices, swap(): return lax.ppermute(block, AXES, perm)  27.9 us
    all_to_all x1, blocking collectives, exchange(): lax.all_to_all(pieces, AXES, 0, 0, axis_index_groups=groups, tiled=True)  20.3 us
    ppermute x18, waiting for transfers between devices, swap(): return lax.ppermute(block, AXES, perm)  17.8 us
    all_to_all x1, starting transfers between devices, exchange(): lax.all_to_all(pieces, AXES, 0, 0, axis_index_groups=groups, tiled=True)  11.8 us
    all_to_all x1, waiting for transfers between devices, exchange(): lax.all_to_all(pieces, AXES, 0, 0, axis_index_groups=groups, tiled=True)  11 us
  transfers between devices with their start and end apart: 22, of which 10 were waited for; matrix products, arithmetic and copies ran while one was open for 2% of the time, Pallas kernels for 2%

profile of v12, /device:TPU:1, one launch (start us, length us, event | category | flops | bytes accessed | tf_op | source)
XLA Modules:
  0.0 189.8 jit_solution(16044469077929714571)
XLA Ops:
  0.6 1.0 dynamic-slice_bitcast_fusion
  1.6 3.7 %collective-permute-start = (bf16[4,128,128]{2,1,0:T(8,128)(2,1)S(1)}, bf16[4,128,128]{2,1,0:T(8,128)(2,1)S(1)}, u32[]{:S(2)}, u32[]{:S(2)}) collective-permute-start(bf16[4,128,128]{2,1,0:T(8,128)(2,1)S(1)} %get-tuple-element.59), channel_id=1, source_target_pairs={{0,1},{1,0},{2,3},{3,2},{4,5},{5,4},{6,7},{7,6},{8,9},{9,8},{10,11... | collective-permute-start | bytes 393224 | tf_op jit(solution)/shard_map/ppermute | solution.py:61
  6.2 1.0 select_reduce_fusion
  7.5 1.7 copy-done
  10.7 3.4 %collective-permute-start.1 = (bf16[496,256]{1,0:T(8,128)(2,1)S(1)}, bf16[496,256]{1,0:T(8,128)(2,1)S(1)}, u32[]{:S(2)}, u32[]{:S(2)}) collective-permute-start(bf16[496,256]{1,0:T(8,128)(2,1)S(1)} %get-tuple-element.33), channel_id=1, source_target_pairs={{0,225},{1,224},{2,227},{3,226},{4,229},{5,228},{6,231},{7,230},{8... | collective-permute-start | bytes 761864 | tf_op jit(solution)/shard_map/ppermute | solution.py:52
  14.1 1.8 collective-permute-start.2
  15.9 1.5 collective-permute-start.3
  17.5 2.4 %collective-permute-done.3 = bf16[128,256]{1,0:T(8,128)(2,1)S(1)} collective-permute-done((bf16[128,256]{1,0:T(8,128)(2,1)S(1)}, bf16[128,256]{1,0:T(8,128)(2,1)S(1)}, u32[]{:S(2)}, u32[]{:S(2)}) %collective-permute-start.3) | collective-permute-done | bytes 65568 | tf_op jit(solution)/shard_map/ppermute | solution.py:52
  19.9 1.1 collective-permute-start.5
  21.2 4.2 %collective-permute-start.7 = (bf16[128,128]{1,0:T(8,128)(2,1)S(1)}, bf16[128,128]{1,0:T(8,128)(2,1)S(1)}, u32[]{:S(2)}, u32[]{:S(2)}) collective-permute-start(bf16[128,128]{1,0:T(8,128)(2,1)S(1)} %get-tuple-element.38), channel_id=1, source_target_pairs={{0,2},{1,3},{2,0},{3,1},{4,6},{5,7},{6,4},{7,5},{8,10},{9,11},{10,... | collective-permute-start | bytes 98312 | tf_op jit(solution)/shard_map/ppermute | solution.py:52
  25.3 1.0 core.2.acc
  26.4 2.6 %collective-permute-done.8.h_q = bf16[128,128]{1,0:T(8,128)(2,1)S(1)} collective-permute-done((bf16[128,128]{1,0:T(8,128)(2,1)S(1)}, bf16[128,128]{1,0:T(8,128)(2,1)S(1)}, u32[]{:S(2)}, u32[]{:S(2)}) %collective-permute-start.8) | collective-permute-done | bytes 32800 | tf_op jit(solution)/shard_map/ppermute | solution.py:52
  29.8 4.0 %collective-permute-start.9 = (bf16[496,256]{1,0:T(8,128)(2,1)S(1)}, bf16[496,256]{1,0:T(8,128)(2,1)S(1)}, u32[]{:S(2)}, u32[]{:S(2)}) collective-permute-start(bf16[496,256]{1,0:T(8,128)(2,1)S(1)} %get-tuple-element.41), channel_id=1, source_target_pairs={{0,225},{1,224},{2,227},{3,226},{4,229},{5,228},{6,231},{7,230},{8... | collective-permute-start | bytes 761864 | tf_op jit(solution)/shard_map/ppermute | solution.py:52
  33.8 1.5 collective-permute-start.10
  35.3 0.9 collective-permute-done.10
  36.2 3.1 %collective-permute-done.11 = bf16[128,256]{1,0:T(8,128)(2,1)S(1)} collective-permute-done((bf16[128,256]{1,0:T(8,128)(2,1)S(1)}, bf16[128,256]{1,0:T(8,128)(2,1)S(1)}, u32[]{:S(2)}, u32[]{:S(2)}) %collective-permute-start.11) | collective-permute-done | bytes 65568 | tf_op jit(solution)/shard_map/ppermute | solution.py:52
  39.3 3.1 %collective-permute-start.13 = (bf16[272,256]{1,0:T(8,128)(2,1)S(1)}, bf16[272,256]{1,0:T(8,128)(2,1)S(1)}, u32[]{:S(2)}, u32[]{:S(2)}) collective-permute-start(bf16[272,256]{1,0:T(8,128)(2,1)S(1)} %pad_maximum_fusion.1), channel_id=1, source_target_pairs={{0,225},{1,224},{2,227},{3,226},{4,229},{5,228},{6,231},{7,230},{8... | collective-permute-start | bytes 417800 | tf_op jit(solution)/shard_map/ppermute | solution.py:52
  42.5 1.0 core.3.acc
  43.5 2.8 %collective-permute-done.12.a_ends = bf16[256,256]{1,0:T(8,128)(2,1)S(1)} collective-permute-done((bf16[256,256]{1,0:T(8,128)(2,1)S(1)}, bf16[256,256]{1,0:T(8,128)(2,1)S(1)}, u32[]{:S(2)}, u32[]{:S(2)}) %collective-permute-start.12) | collective-permute-done | bytes 131104 | tf_op jit(solution)/shard_map/ppermute | solution.py:52
  47.7 3.1 %collective-permute-start.17 = (bf16[4,128,256]{2,1,0:T(8,128)(2,1)S(1)}, bf16[4,128,256]{2,1,0:T(8,128)(2,1)S(1)}, u32[]{:S(2)}, u32[]{:S(2)}) collective-permute-start(bf16[4,128,256]{2,1,0:T(8,128)(2,1)S(1)} %get-tuple-element.46.s), channel_id=1, source_target_pairs={{0,225},{1,224},{2,227},{3,226},{4,229},{5,228},{6,231},{7,230},{8... | collective-permute-start | bytes 786440 | tf_op jit(solution)/shard_map/ppermute | solution.py:56
  50.8 2.1 %collective-permute-start.15 = (bf16[128,256]{1,0:T(8,128)(2,1)S(1)}, bf16[128,256]{1,0:T(8,128)(2,1)S(1)}, u32[]{:S(2)}, u32[]{:S(2)}) collective-permute-start(bf16[128,256]{1,0:T(8,128)(2,1)S(1)} %get-tuple-element.48), channel_id=1, source_target_pairs={{0,2},{1,3},{2,0},{3,1},{4,6},{5,7},{6,4},{7,5},{8,10},{9,11},{10,... | collective-permute-start | bytes 196616 | tf_op jit(solution)/shard_map/ppermute | solution.py:52
  52.9 0.9 corr.1
  53.9 3.1 %collective-permute-done.16.q = bf16[128,256]{1,0:T(8,128)(2,1)S(1)} collective-permute-done((bf16[128,256]{1,0:T(8,128)(2,1)S(1)}, bf16[128,256]{1,0:T(8,128)(2,1)S(1)}, u32[]{:S(2)}, u32[]{:S(2)}) %collective-permute-start.16) | collective-permute-done | bytes 65568 | tf_op jit(solution)/shard_map/ppermute | solution.py:52
  56.9 1.7 gram.1
  58.7 1.0 collective-permute-start.18
  59.7 1.0 collective-permute-done.18
  61.6 11.8 %all-to-all-start = ((f32[64,1,640]{2,1,0:T(1,128)}), f32[64,1,640]{2,1,0:T(1,128)S(1)}, u32[]{:S(2)}, u32[]{:S(2)}) async-start(f32[64,1,640]{2,1,0:T(1,128)} %add.59), calls=%async_computation | async-start | bytes 327680 | tf_op jit(solution)/shard_map/all_to_all | solution.py:76
  74.0 11.0 %all-to-all-done = f32[64,1,640]{2,1,0:T(1,128)S(1)} async-done(((f32[64,1,640]{2,1,0:T(1,128)}), f32[64,1,640]{2,1,0:T(1,128)S(1)}, u32[]{:S(2)}, u32[]{:S(2)}) %all-to-all-start) | async-done | bytes 163872 | tf_op jit(solution)/shard_map/all_to_all | solution.py:76
  85.3 20.3 %all_to_all.10.mine = f32[128,1,640]{2,1,0:T(1,128)S(1)} all-to-all(f32[128,1,640]{2,1,0:T(1,128)S(1)} %broadcast_in_dim.20), channel_id=1, replica_groups={{0,4,8,12,16,20,24,28,32,36,40,44,48,52,56,60,65,69,73,77,81,85,89,93,9..., dimensions={0} | all-to-all | bytes 655360 | tf_op jit(solution)/shard_map/all_to_all | solution.py:76
  105.6 3.9 %collective-permute-start.20 = (f32[128,1,640]{2,1,0:T(1,128)S(1)}, f32[128,1,640]{2,1,0:T(1,128)S(1)}, u32[]{:S(2)}, u32[]{:S(2)}) collective-permute-start(f32[128,1,640]{2,1,0:T(1,128)S(1)} %all_to_all.10.mine), channel_id=1, source_target_pairs={{0,2},{1,3},{2,0},{3,1},{4,6},{5,7},{6,4},{7,5},{8,10},{9,11},{10,... | collective-permute-start | bytes 983048 | tf_op jit(solution)/shard_map/ppermute | solution.py:52
  109.5 1.3 collective-permute-done.20.theirs
  110.8 79.0 %final.1 = (bf16[2,1,4,128,128]{4,3,2,1,0:T(8,128)(2,1)}, f32[2,256,128]{2,1,0:T(8,128)}) custom-call(s32[40]{0:T(128)S(1)} %concatenate.19.m, f32[128,1,640]{2,1,0:T(1,128)S(1)} %all_to_all.10.mine, f32[128,1,640]{2,1,0:T(1,128)S(1)} %collective-permute-done.20.theirs, bf16[2,4,128,256]{3,2,1,0:T(8,128)(2,1)S(1)} %stack.29.both), custom_call_target="tpu_custom_call" | custom-call | flops 1677721600 | bytes 1703936 | tf_op jit(solution)/shard_map/final/pallas_call | solution.py:336
  (47 shorter events, 6.9 us)
Async XLA Ops:
  1.6 8.4 %collective-permute-start = (bf16[4,128,128]{2,1,0:T(8,128)(2,1)S(1)}, bf16[4,128,128]{2,1,0:T(8,128)(2,1)S(1)}, u32[]{:S(2)}, u32[]{:S(2)}) collective-permute-start(bf16[4,128,128]{2,1,0:T(8,128)(2,1)S(1)} %get-tuple-element.59), channel_id=1, source_target_pairs={{0,1},{1,0},{2,3},{3,2},{4,5},{5,4},{6,7},{7,6},{8,9},{9,8},{10,11... | collective-permute-start | bytes 393224 | tf_op jit(solution)/shard_map/ppermute | solution.py:61
  7.5 1.7 copy-start
  10.7 14.6 %collective-permute-start.1 = (bf16[496,256]{1,0:T(8,128)(2,1)S(1)}, bf16[496,256]{1,0:T(8,128)(2,1)S(1)}, u32[]{:S(2)}, u32[]{:S(2)}) collective-permute-start(bf16[496,256]{1,0:T(8,128)(2,1)S(1)} %get-tuple-element.33), channel_id=1, source_target_pairs={{0,225},{1,224},{2,227},{3,226},{4,229},{5,228},{6,231},{7,230},{8... | collective-permute-start | bytes 761864 | tf_op jit(solution)/shard_map/ppermute | solution.py:52
  14.1 3.4 %collective-permute-start.2 = (bf16[128,256]{1,0:T(8,128)(2,1)S(1)}, bf16[128,256]{1,0:T(8,128)(2,1)S(1)}, u32[]{:S(2)}, u32[]{:S(2)}) collective-permute-start(bf16[128,256]{1,0:T(8,128)(2,1)S(1)} %get-tuple-element.34), channel_id=1, source_target_pairs={{0,2},{1,3},{2,0},{3,1},{4,6},{5,7},{6,4},{7,5},{8,10},{9,11},{10,... | collective-permute-start | bytes 196616 | tf_op jit(solution)/shard_map/ppermute | solution.py:52
  15.9 4.0 %collective-permute-start.3 = (bf16[128,256]{1,0:T(8,128)(2,1)S(1)}, bf16[128,256]{1,0:T(8,128)(2,1)S(1)}, u32[]{:S(2)}, u32[]{:S(2)}) collective-permute-start(bf16[128,256]{1,0:T(8,128)(2,1)S(1)} %get-tuple-element.35), channel_id=1, source_target_pairs={{0,30},{1,31},{2,4},{3,5},{4,2},{5,3},{6,8},{7,9},{8,6},{9,7},{10,... | collective-permute-start | bytes 196616 | tf_op jit(solution)/shard_map/ppermute | solution.py:52
  17.5 7.9 %collective-permute-start.6 = (bf16[544,256]{1,0:T(8,128)(2,1)S(1)}, bf16[544,256]{1,0:T(8,128)(2,1)S(1)}, u32[]{:S(2)}, u32[]{:S(2)}) collective-permute-start(bf16[544,256]{1,0:T(8,128)(2,1)S(1)} %get-tuple-element.37), channel_id=1, source_target_pairs={{0,32},{1,33},{2,34},{3,35},{4,36},{5,37},{6,38},{7,39},{8,40},{9,... | collective-permute-start | bytes 835592 | tf_op jit(solution)/shard_map/ppermute | solution.py:52
  19.9 9.0 %collective-permute-start.5 = (bf16[272,256]{1,0:T(8,128)(2,1)S(1)}, bf16[272,256]{1,0:T(8,128)(2,1)S(1)}, u32[]{:S(2)}, u32[]{:S(2)}) collective-permute-start(bf16[272,256]{1,0:T(8,128)(2,1)S(1)} %pad_maximum_fusion), channel_id=1, source_target_pairs={{0,225},{1,224},{2,227},{3,226},{4,229},{5,228},{6,231},{7,230},{8... | collective-permute-start | bytes 417800 | tf_op jit(solution)/shard_map/ppermute | solution.py:52
  21.1 7.9 %collective-permute-start.4 = (bf16[256,256]{1,0:T(8,128)(2,1)S(1)}, bf16[256,256]{1,0:T(8,128)(2,1)S(1)}, u32[]{:S(2)}, u32[]{:S(2)}) collective-permute-start(bf16[256,256]{1,0:T(8,128)(2,1)S(1)} %constant_dynamic-update-slice_fusion.ends), channel_id=1, source_target_pairs={{0,32},{1,33},{2,34},{3,35},{4,36},{5,37},{6,38},{7,39},{8,40},{9,... | collective-permute-start | bytes 393224 | tf_op jit(solution)/shard_map/ppermute | solution.py:52
  21.2 5.2 %collective-permute-start.7 = (bf16[128,128]{1,0:T(8,128)(2,1)S(1)}, bf16[128,128]{1,0:T(8,128)(2,1)S(1)}, u32[]{:S(2)}, u32[]{:S(2)}) collective-permute-start(bf16[128,128]{1,0:T(8,128)(2,1)S(1)} %get-tuple-element.38), channel_id=1, source_target_pairs={{0,2},{1,3},{2,0},{3,1},{4,6},{5,7},{6,4},{7,5},{8,10},{9,11},{10,... | collective-permute-start | bytes 98312 | tf_op jit(solution)/shard_map/ppermute | solution.py:52
  25.3 3.6 %collective-permute-start.8 = (bf16[128,128]{1,0:T(8,128)(2,1)S(1)}, bf16[128,128]{1,0:T(8,128)(2,1)S(1)}, u32[]{:S(2)}, u32[]{:S(2)}) collective-permute-start(bf16[128,128]{1,0:T(8,128)(2,1)S(1)} %get-tuple-element.39), channel_id=1, source_target_pairs={{0,30},{1,31},{2,4},{3,5},{4,2},{5,3},{6,8},{7,9},{8,6},{9,7},{10,... | collective-permute-start | bytes 98312 | tf_op jit(solution)/shard_map/ppermute | solution.py:52
  29.8 12.7 %collective-permute-start.9 = (bf16[496,256]{1,0:T(8,128)(2,1)S(1)}, bf16[496,256]{1,0:T(8,128)(2,1)S(1)}, u32[]{:S(2)}, u32[]{:S(2)}) collective-permute-start(bf16[496,256]{1,0:T(8,128)(2,1)S(1)} %get-tuple-element.41), channel_id=1, source_target_pairs={{0,225},{1,224},{2,227},{3,226},{4,229},{5,228},{6,231},{7,230},{8... | collective-permute-start | bytes 761864 | tf_op jit(solution)/shard_map/ppermute | solution.py:52
  33.8 2.4 %collective-permute-start.10 = (bf16[128,256]{1,0:T(8,128)(2,1)S(1)}, bf16[128,256]{1,0:T(8,128)(2,1)S(1)}, u32[]{:S(2)}, u32[]{:S(2)}) collective-permute-start(bf16[128,256]{1,0:T(8,128)(2,1)S(1)} %get-tuple-element.42), channel_id=1, source_target_pairs={{0,2},{1,3},{2,0},{3,1},{4,6},{5,7},{6,4},{7,5},{8,10},{9,11},{10,... | collective-permute-start | bytes 196616 | tf_op jit(solution)/shard_map/ppermute | solution.py:52
  35.3 4.0 %collective-permute-start.11 = (bf16[128,256]{1,0:T(8,128)(2,1)S(1)}, bf16[128,256]{1,0:T(8,128)(2,1)S(1)}, u32[]{:S(2)}, u32[]{:S(2)}) collective-permute-start(bf16[128,256]{1,0:T(8,128)(2,1)S(1)} %get-tuple-element.43), channel_id=1, source_target_pairs={{0,30},{1,31},{2,4},{3,5},{4,2},{5,3},{6,8},{7,9},{8,6},{9,7},{10,... | collective-permute-start | bytes 196616 | tf_op jit(solution)/shard_map/ppermute | solution.py:52
  35.3 7.2 %collective-permute-start.14 = (bf16[544,256]{1,0:T(8,128)(2,1)S(1)}, bf16[544,256]{1,0:T(8,128)(2,1)S(1)}, u32[]{:S(2)}, u32[]{:S(2)}) collective-permute-start(bf16[544,256]{1,0:T(8,128)(2,1)S(1)} %get-tuple-element.45), channel_id=1, source_target_pairs={{0,32},{1,33},{2,34},{3,35},{4,36},{5,37},{6,38},{7,39},{8,40},{9,... | collective-permute-start | bytes 835592 | tf_op jit(solution)/shard_map/ppermute | solution.py:52
  39.3 7.7 %collective-permute-start.13 = (bf16[272,256]{1,0:T(8,128)(2,1)S(1)}, bf16[272,256]{1,0:T(8,128)(2,1)S(1)}, u32[]{:S(2)}, u32[]{:S(2)}) collective-permute-start(bf16[272,256]{1,0:T(8,128)(2,1)S(1)} %pad_maximum_fusion.1), channel_id=1, source_target_pairs={{0,225},{1,224},{2,227},{3,226},{4,229},{5,228},{6,231},{7,230},{8... | collective-permute-start | bytes 417800 | tf_op jit(solution)/shard_map/ppermute | solution.py:52
  42.4 3.9 %collective-permute-start.12 = (bf16[256,256]{1,0:T(8,128)(2,1)S(1)}, bf16[256,256]{1,0:T(8,128)(2,1)S(1)}, u32[]{:S(2)}, u32[]{:S(2)}) collective-permute-start(bf16[256,256]{1,0:T(8,128)(2,1)S(1)} %constant_dynamic-update-slice_fusion.2.ends), channel_id=1, source_target_pairs={{0,32},{1,33},{2,34},{3,35},{4,36},{5,37},{6,38},{7,39},{8,40},{9,... | collective-permute-start | bytes 393224 | tf_op jit(solution)/shard_map/ppermute | solution.py:52
  47.7 9.2 %collective-permute-start.17 = (bf16[4,128,256]{2,1,0:T(8,128)(2,1)S(1)}, bf16[4,128,256]{2,1,0:T(8,128)(2,1)S(1)}, u32[]{:S(2)}, u32[]{:S(2)}) collective-permute-start(bf16[4,128,256]{2,1,0:T(8,128)(2,1)S(1)} %get-tuple-element.46.s), channel_id=1, source_target_pairs={{0,225},{1,224},{2,227},{3,226},{4,229},{5,228},{6,231},{7,230},{8... | collective-permute-start | bytes 786440 | tf_op jit(solution)/shard_map/ppermute | solution.py:56
  50.8 3.0 %collective-permute-start.15 = (bf16[128,256]{1,0:T(8,128)(2,1)S(1)}, bf16[128,256]{1,0:T(8,128)(2,1)S(1)}, u32[]{:S(2)}, u32[]{:S(2)}) collective-permute-start(bf16[128,256]{1,0:T(8,128)(2,1)S(1)} %get-tuple-element.48), channel_id=1, source_target_pairs={{0,2},{1,3},{2,0},{3,1},{4,6},{5,7},{6,4},{7,5},{8,10},{9,11},{10,... | collective-permute-start | bytes 196616 | tf_op jit(solution)/shard_map/ppermute | solution.py:52
  52.9 4.0 %collective-permute-start.16 = (bf16[128,256]{1,0:T(8,128)(2,1)S(1)}, bf16[128,256]{1,0:T(8,128)(2,1)S(1)}, u32[]{:S(2)}, u32[]{:S(2)}) collective-permute-start(bf16[128,256]{1,0:T(8,128)(2,1)S(1)} %get-tuple-element.49), channel_id=1, source_target_pairs={{0,30},{1,31},{2,4},{3,5},{4,2},{5,3},{6,8},{7,9},{8,6},{9,7},{10,... | collective-permute-start | bytes 196616 | tf_op jit(solution)/shard_map/ppermute | solution.py:52
  58.7 2.0 %collective-permute-start.18 = (f32[64,1,640]{2,1,0:T(1,128)S(1)}, f32[64,1,640]{2,1,0:T(1,128)S(1)}, u32[]{:S(2)}, u32[]{:S(2)}) collective-permute-start(f32[64,1,640]{2,1,0:T(1,128)S(1)} %get-tuple-element.55), channel_id=1, source_target_pairs={{0,2},{1,3},{2,0},{3,1},{4,6},{5,7},{6,4},{7,5},{8,10},{9,11},{10,... | collective-permute-start | bytes 491528 | tf_op jit(solution)/shard_map/ppermute | solution.py:52
  59.7 13.7 %collective-permute-start.19 = (bf16[4,128,256]{2,1,0:T(8,128)(2,1)S(1)}, bf16[4,128,256]{2,1,0:T(8,128)(2,1)S(1)}, u32[]{:S(2)}, u32[]{:S(2)}) collective-permute-start(bf16[4,128,256]{2,1,0:T(8,128)(2,1)S(1)} %get-tuple-element.46.s), channel_id=1, source_target_pairs={{0,1},{1,0},{2,3},{3,2},{4,5},{5,4},{6,7},{7,6},{8,9},{9,8},{10,11... | collective-permute-start | bytes 786440 | tf_op jit(solution)/shard_map/ppermute | solution.py:61
  61.6 23.5 %all-to-all-start = ((f32[64,1,640]{2,1,0:T(1,128)}), f32[64,1,640]{2,1,0:T(1,128)S(1)}, u32[]{:S(2)}, u32[]{:S(2)}) async-start(f32[64,1,640]{2,1,0:T(1,128)} %add.59), calls=%async_computation | async-start | bytes 327680 | tf_op jit(solution)/shard_map/all_to_all | solution.py:76
  105.6 5.2 %collective-permute-start.20 = (f32[128,1,640]{2,1,0:T(1,128)S(1)}, f32[128,1,640]{2,1,0:T(1,128)S(1)}, u32[]{:S(2)}, u32[]{:S(2)}) collective-permute-start(f32[128,1,640]{2,1,0:T(1,128)S(1)} %all_to_all.10.mine), channel_id=1, source_target_pairs={{0,2},{1,3},{2,0},{3,1},{4,6},{5,7},{6,4},{7,5},{8,10},{9,11},{10,... | collective-permute-start | bytes 983048 | tf_op jit(solution)/shard_map/ppermute | solution.py:52

commit v13 on v12

--- a/solution.py
+++ b/solution.py
@@ -118,8 +118,8 @@
 
 def store_edges(m, ref, p, q):
     even = m[PAR_Y] == 0
-    p[...] = ref[pl.ds(jnp.where(even, 3, 0), 1)].reshape(T, 2 * T)
-    q[...] = ref[pl.ds(jnp.where(even, 0, 3), 1)].reshape(T, 2 * T)
+    p[:T] = ref[pl.ds(jnp.where(even, 3, 0), 1)].reshape(T, 2 * T)
+    q[:T] = ref[pl.ds(jnp.where(even, 0, 3), 1)].reshape(T, 2 * T)
 
 
 def store_bulk(ref, to_b, to_a):
@@ -163,7 +163,7 @@
 
 def rim_kernel(m, o, b, a_ends, b_ends, acc, *rest, last):
     if last:
-        before, out, p, q = rest
+        before, h_p, h_q, out, p, q = rest
     else:
         out, p, q, to_b, to_a = rest
     low, high = zip(ends_of(m, a_ends), ends_of(m, b_ends))
@@ -182,7 +182,11 @@
         else:
             out[tile] = (0.5 * total).astype(BF)
     store_edges(m, out, p, q)
-    if not last:
+    if last:
+        for to, block in ((p, h_p), (q, h_q)):
+            to[T:, :T] = block[: T // 2]
+            to[T:, T:] = block[T // 2 :]
+    else:
         store_bulk(out, to_b, to_a)
 
 
@@ -202,20 +206,21 @@
     return lax.broadcasted_iota(jnp.int32, shape, 0), lax.broadcasted_iota(jnp.int32, shape, 1)
 
 
-def gram_kernel(m, o, turned, p, q, right, h_p, h_q, acc, corr, mine, theirs):
+def gram_kernel(m, o, turned, p, q, right, acc, corr, mine, theirs):
     side = 1 + m[PAR_X]
     parts = []
     for tile in range(4):
         at = [place for place in range(tile, tile + 3) if 1 <= place <= 4]
         parts.append(acc[tile] + product(o, tile, (side,), at, [right[at[0] - 1 : at[-1]]]))
     even = m[PAR_Y] == 0
-    above = jnp.where(even, p[...], q[...])
+    above = jnp.where(even, p[:T], q[:T])
     parts[3] += product(o, 3, (0,), (5,), [above])
     high, low = split(jnp.concatenate(parts, axis=0))
     half = dot(turned[...], high) + dot(turned[...], low)
-    for tile, block, at in ((p, h_p, jnp.where(even, 3, 0)), (q, h_q, jnp.where(even, 0, 3))):
-        high, low = split(dot(block[...], right[at]))
-        half += dot(tile[...], high, ((0,), (0,))) + dot(tile[...], low, ((0,), (0,)))
+    for got, at in ((p, jnp.where(even, 3, 0)), (q, jnp.where(even, 0, 3))):
+        block = jnp.concatenate([got[T:, :T], got[T:, T:]], axis=0)
+        high, low = split(dot(block, right[at]))
+        half += dot(got[:T], high, ((0,), (0,))) + dot(got[:T], low, ((0,), (0,)))
     coupling = half + half.T
     rows, cols = places()
     both = jnp.where(rows >= cols, corr[...], coupling)
@@ -382,7 +387,6 @@
     o, h_p, h_q = call(
         order_kernel, m, [hamiltonian], [shaped((4, T, NB * T), BF), corner, corner], "order", specs=[spin_block]
     )
-    h_p, h_q = swap(sizes, h_p, 0, 1), swap(sizes, h_q, 0, 2)
     tile = shaped((T, 2 * T), BF)
     ext = pltpu.VMEM((6, T, 2 * T), BF)
     other, o = lax.optimization_barrier((other, o))
@@ -390,19 +394,19 @@
     outs = [shaped(block, BF), tile, tile, *bulk]
     v, p, q, *rest = call(join_kernel, m, [own, other], outs, "join")
 
-    def apply_ham(x, p, q, rest, more, outs, *kept):
+    def apply_ham(x, p, q, rest, more, outs):
         p, q = swap(sizes, p, 0, 1), swap(sizes, q, 0, 2)
         ends = jnp.concatenate([p, q], axis=0)
         a, b = swap(sizes, rest[1], 1, 0), swap(sizes, rest[0], 2, 0)
         a_ends = swap(sizes, ends, 1, 0)
         b_ends = swap(sizes, jnp.concatenate([p, x[0, :HEAD], q], axis=0), 2, 0)
         (acc,) = call(core_kernel, m, [o, x, ends, a, b], [shaped(block, F32)], "core", 31, scratch=[ext])
-        acc, *kept = lax.optimization_barrier((acc, *kept))
         kernel = functools.partial(rim_kernel, last=len(more) > 0)
-        return call(kernel, m, [o, b, a_ends, b_ends, acc, *more], outs, "rim", 6), kept
-
-    (first, p, q, *rest), (h_p, h_q) = apply_ham(v, p, q, rest, [], outs, h_p, h_q)
-    (second, p, q), _ = apply_ham(first, p, q, rest, [v], outs[:3])
+        return call(kernel, m, [o, b, a_ends, b_ends, acc, *more], outs, "rim", 6)
+
+    first, p, q, *rest = apply_ham(v, p, q, rest, [], outs)
+    longer = shaped((3 * T // 2, 2 * T), BF)
+    second, p, q = apply_ham(first, p, q, rest, [v, h_p, h_q], [shaped(block, BF), longer, longer])
 
     right = shift(sizes, second, -1, 0)
     p, q = swap(sizes, p, 0, 1), swap(sizes, q, 0, 2)
@@ -411,7 +415,7 @@
     )
     piece = shaped((members // 2, 1, 5 * T), F32)
     mine, theirs = call(
-        gram_kernel, m, [o, turned, p, q, right, h_p, h_q, acc, corr], [piece, piece], "gram", 30
+        gram_kernel, m, [o, turned, p, q, right, acc, corr], [piece, piece], "gram", 30
     )
 
     rows = members * second.shape[0] * second.shape[1]

time: 190 us -> 190 us (level)
  waiting for transfers between devices: 28.8 us -> 31.6 us
  starting transfers between devices: 46.5 us -> 43.7 us
    ppermute x18 -> x16, waiting for transfers between devices: 17.8 us -> 20.6 us  [swap(): return lax.ppermute(block, AXES, perm)]
    ppermute x18 -> x16, starting transfers between devices: 27.9 us -> 25.4 us  [swap(): return lax.ppermute(block, AXES, perm)]
  transfers between devices with their start and end apart: 22 -> 20, of which waited for: 10 -> 12; matrix products, arithmetic and copies ran while one was open for 2% -> 2% of each run, Pallas kernels for 2% -> 2%
where the time goes in v13:
time: 190 us
  Pallas kernels  87.4 us (46%)
  starting transfers between devices  43.7 us (23%)
  waiting for transfers between devices  31.6 us (17%)
  blocking collectives  20.3 us (11%)
  local copies, waits for them, and re-layouts  3.14 us (2%)
  other arithmetic  2.88 us (2%)
    pallas_call x10, Pallas kernels, call(): pl.pallas_call(kernel, out_shape=outs, grid_spec=pltpu.PrefetchScalarGrid...  87.4 us
    ppermute x16, starting transfers between devices, swap(): return lax.ppermute(block, AXES, perm)  25.4 us
    ppermute x16, waiting for transfers between devices, swap(): return lax.ppermute(block, AXES, perm)  20.6 us
    all_to_all x1, blocking collectives, exchange(): lax.all_to_all(pieces, AXES, 0, 0, axis_index_groups=groups, tiled=True)  20.3 us
    all_to_all x1, starting transfers between devices, exchange(): lax.all_to_all(pieces, AXES, 0, 0, axis_index_groups=groups, tiled=True)  11.5 us
    all_to_all x1, waiting for transfers between devices, exchange(): lax.all_to_all(pieces, AXES, 0, 0, axis_index_groups=groups, tiled=True)  11 us
  transfers between devices with their start and end apart: 20, of which 12 were waited for; matrix products, arithmetic and copies ran while one was open for 2% of the time, Pallas kernels for 2%

profile of v13, /device:TPU:1, one launch (start us, length us, event | category | flops | bytes accessed | tf_op | source)
XLA Modules:
  0.0 189.8 jit_solution(6471897610136065534)
XLA Ops:
  0.6 1.0 dynamic-slice_bitcast_fusion
  1.6 3.7 %collective-permute-start = (bf16[4,128,128]{2,1,0:T(8,128)(2,1)S(1)}, bf16[4,128,128]{2,1,0:T(8,128)(2,1)S(1)}, u32[]{:S(2)}, u32[]{:S(2)}) collective-permute-start(bf16[4,128,128]{2,1,0:T(8,128)(2,1)S(1)} %get-tuple-element.53), channel_id=1, source_target_pairs={{0,1},{1,0},{2,3},{3,2},{4,5},{5,4},{6,7},{7,6},{8,9},{9,8},{10,11... | collective-permute-start | bytes 393224 | tf_op jit(solution)/shard_map/ppermute | solution.py:61
  6.2 1.0 select_reduce_fusion
  7.5 1.7 copy-done
  10.7 3.4 %collective-permute-start.1 = (bf16[496,256]{1,0:T(8,128)(2,1)S(1)}, bf16[496,256]{1,0:T(8,128)(2,1)S(1)}, u32[]{:S(2)}, u32[]{:S(2)}) collective-permute-start(bf16[496,256]{1,0:T(8,128)(2,1)S(1)} %get-tuple-element.30), channel_id=1, source_target_pairs={{0,225},{1,224},{2,227},{3,226},{4,229},{5,228},{6,231},{7,230},{8... | collective-permute-start | bytes 761864 | tf_op jit(solution)/shard_map/ppermute | solution.py:52
  14.1 1.8 collective-permute-start.2
  15.9 1.5 collective-permute-start.3
  17.5 2.4 %collective-permute-done.3 = bf16[128,256]{1,0:T(8,128)(2,1)S(1)} collective-permute-done((bf16[128,256]{1,0:T(8,128)(2,1)S(1)}, bf16[128,256]{1,0:T(8,128)(2,1)S(1)}, u32[]{:S(2)}, u32[]{:S(2)}) %collective-permute-start.3) | collective-permute-done | bytes 65568 | tf_op jit(solution)/shard_map/ppermute | solution.py:52
  19.9 1.1 collective-permute-start.5
  21.2 2.0 %collective-permute-done.6.a = bf16[544,256]{1,0:T(8,128)(2,1)S(1)} collective-permute-done((bf16[544,256]{1,0:T(8,128)(2,1)S(1)}, bf16[544,256]{1,0:T(8,128)(2,1)S(1)}, u32[]{:S(2)}, u32[]{:S(2)}) %collective-permute-start.6) | collective-permute-done | bytes 278560 | tf_op jit(solution)/shard_map/ppermute | solution.py:52
  23.1 1.0 core.2.acc
  24.2 1.2 collective-permute-done.4.a_ends
  25.4 1.8 collective-permute-done.5.b_ends
  28.0 3.0 %collective-permute-start.7 = (bf16[496,256]{1,0:T(8,128)(2,1)S(1)}, bf16[496,256]{1,0:T(8,128)(2,1)S(1)}, u32[]{:S(2)}, u32[]{:S(2)}) collective-permute-start(bf16[496,256]{1,0:T(8,128)(2,1)S(1)} %get-tuple-element.35), channel_id=1, source_target_pairs={{0,225},{1,224},{2,227},{3,226},{4,229},{5,228},{6,231},{7,230},{8... | collective-permute-start | bytes 761864 | tf_op jit(solution)/shard_map/ppermute | solution.py:52
  31.1 4.2 %collective-permute-start.8 = (bf16[128,256]{1,0:T(8,128)(2,1)S(1)}, bf16[128,256]{1,0:T(8,128)(2,1)S(1)}, u32[]{:S(2)}, u32[]{:S(2)}) collective-permute-start(bf16[128,256]{1,0:T(8,128)(2,1)S(1)} %get-tuple-element.36), channel_id=1, source_target_pairs={{0,2},{1,3},{2,0},{3,1},{4,6},{5,7},{6,4},{7,5},{8,10},{9,11},{10,... | collective-permute-start | bytes 196616 | tf_op jit(solution)/shard_map/ppermute | solution.py:52
  36.2 3.1 %collective-permute-done.9 = bf16[128,256]{1,0:T(8,128)(2,1)S(1)} collective-permute-done((bf16[128,256]{1,0:T(8,128)(2,1)S(1)}, bf16[128,256]{1,0:T(8,128)(2,1)S(1)}, u32[]{:S(2)}, u32[]{:S(2)}) %collective-permute-start.9) | collective-permute-done | bytes 65568 | tf_op jit(solution)/shard_map/ppermute | solution.py:52
  39.3 3.1 %collective-permute-start.11 = (bf16[272,256]{1,0:T(8,128)(2,1)S(1)}, bf16[272,256]{1,0:T(8,128)(2,1)S(1)}, u32[]{:S(2)}, u32[]{:S(2)}) collective-permute-start(bf16[272,256]{1,0:T(8,128)(2,1)S(1)} %pad_maximum_fusion.1), channel_id=1, source_target_pairs={{0,225},{1,224},{2,227},{3,226},{4,229},{5,228},{6,231},{7,230},{8... | collective-permute-start | bytes 417800 | tf_op jit(solution)/shard_map/ppermute | solution.py:52
  42.5 1.0 core.3.acc
  43.5 2.7 %collective-permute-done.10.a_ends = bf16[256,256]{1,0:T(8,128)(2,1)S(1)} collective-permute-done((bf16[256,256]{1,0:T(8,128)(2,1)S(1)}, bf16[256,256]{1,0:T(8,128)(2,1)S(1)}, u32[]{:S(2)}, u32[]{:S(2)}) %collective-permute-start.10) | collective-permute-done | bytes 131104 | tf_op jit(solution)/shard_map/ppermute | solution.py:52
  47.7 3.1 %collective-permute-start.15 = (bf16[4,128,256]{2,1,0:T(8,128)(2,1)S(1)}, bf16[4,128,256]{2,1,0:T(8,128)(2,1)S(1)}, u32[]{:S(2)}, u32[]{:S(2)}) collective-permute-start(bf16[4,128,256]{2,1,0:T(8,128)(2,1)S(1)} %get-tuple-element.42.s), channel_id=1, source_target_pairs={{0,225},{1,224},{2,227},{3,226},{4,229},{5,228},{6,231},{7,230},{8... | collective-permute-start | bytes 786440 | tf_op jit(solution)/shard_map/ppermute | solution.py:56
  50.8 2.1 %collective-permute-start.13 = (bf16[192,256]{1,0:T(8,128)(2,1)S(1)}, bf16[192,256]{1,0:T(8,128)(2,1)S(1)}, u32[]{:S(2)}, u32[]{:S(2)}) collective-permute-start(bf16[192,256]{1,0:T(8,128)(2,1)S(1)} %get-tuple-element.44), channel_id=1, source_target_pairs={{0,2},{1,3},{2,0},{3,1},{4,6},{5,7},{6,4},{7,5},{8,10},{9,11},{10,... | collective-permute-start | bytes 294920 | tf_op jit(solution)/shard_map/ppermute | solution.py:52
  52.9 0.9 corr.1
  53.9 3.4 %collective-permute-done.14.q = bf16[192,256]{1,0:T(8,128)(2,1)S(1)} collective-permute-done((bf16[192,256]{1,0:T(8,128)(2,1)S(1)}, bf16[192,256]{1,0:T(8,128)(2,1)S(1)}, u32[]{:S(2)}, u32[]{:S(2)}) %collective-permute-start.14) | collective-permute-done | bytes 98336 | tf_op jit(solution)/shard_map/ppermute | solution.py:52
  57.3 1.7 gram.1
  59.0 1.0 collective-permute-start.16
  60.0 1.0 collective-permute-done.16
  61.9 11.5 %all-to-all-start = ((f32[64,1,640]{2,1,0:T(1,128)}), f32[64,1,640]{2,1,0:T(1,128)S(1)}, u32[]{:S(2)}, u32[]{:S(2)}) async-start(f32[64,1,640]{2,1,0:T(1,128)} %add.59), calls=%async_computation | async-start | bytes 327680 | tf_op jit(solution)/shard_map/all_to_all | solution.py:76
  74.0 11.0 %all-to-all-done = f32[64,1,640]{2,1,0:T(1,128)S(1)} async-done(((f32[64,1,640]{2,1,0:T(1,128)}), f32[64,1,640]{2,1,0:T(1,128)S(1)}, u32[]{:S(2)}, u32[]{:S(2)}) %all-to-all-start) | async-done | bytes 163872 | tf_op jit(solution)/shard_map/all_to_all | solution.py:76
  85.3 20.3 %all_to_all.10.mine = f32[128,1,640]{2,1,0:T(1,128)S(1)} all-to-all(f32[128,1,640]{2,1,0:T(1,128)S(1)} %broadcast_in_dim.20), channel_id=1, replica_groups={{0,4,8,12,16,20,24,28,32,36,40,44,48,52,56,60,65,69,73,77,81,85,89,93,9..., dimensions={0} | all-to-all | bytes 655360 | tf_op jit(solution)/shard_map/all_to_all | solution.py:76
  105.6 3.9 %collective-permute-start.18 = (f32[128,1,640]{2,1,0:T(1,128)S(1)}, f32[128,1,640]{2,1,0:T(1,128)S(1)}, u32[]{:S(2)}, u32[]{:S(2)}) collective-permute-start(f32[128,1,640]{2,1,0:T(1,128)S(1)} %all_to_all.10.mine), channel_id=1, source_target_pairs={{0,2},{1,3},{2,0},{3,1},{4,6},{5,7},{6,4},{7,5},{8,10},{9,11},{10,... | collective-permute-start | bytes 983048 | tf_op jit(solution)/shard_map/ppermute | solution.py:52
  109.5 1.3 collective-permute-done.18.theirs
  110.8 79.0 %final.1 = (bf16[2,1,4,128,128]{4,3,2,1,0:T(8,128)(2,1)}, f32[2,256,128]{2,1,0:T(8,128)}) custom-call(s32[40]{0:T(128)S(1)} %concatenate.19.m, f32[128,1,640]{2,1,0:T(1,128)S(1)} %all_to_all.10.mine, f32[128,1,640]{2,1,0:T(1,128)S(1)} %collective-permute-done.18.theirs, bf16[2,4,128,256]{3,2,1,0:T(8,128)(2,1)S(1)} %stack.29.both), custom_call_target="tpu_custom_call" | custom-call | flops 1677721600 | bytes 1703936 | tf_op jit(solution)/shard_map/final/pallas_call | solution.py:341
  (43 shorter events, 7.8 us)
Async XLA Ops:
  1.6 8.4 %collective-permute-start = (bf16[4,128,128]{2,1,0:T(8,128)(2,1)S(1)}, bf16[4,128,128]{2,1,0:T(8,128)(2,1)S(1)}, u32[]{:S(2)}, u32[]{:S(2)}) collective-permute-start(bf16[4,128,128]{2,1,0:T(8,128)(2,1)S(1)} %get-tuple-element.53), channel_id=1, source_target_pairs={{0,1},{1,0},{2,3},{3,2},{4,5},{5,4},{6,7},{7,6},{8,9},{9,8},{10,11... | collective-permute-start | bytes 393224 | tf_op jit(solution)/shard_map/ppermute | solution.py:61
  7.5 1.7 copy-start
  10.7 10.5 %collective-permute-start.1 = (bf16[496,256]{1,0:T(8,128)(2,1)S(1)}, bf16[496,256]{1,0:T(8,128)(2,1)S(1)}, u32[]{:S(2)}, u32[]{:S(2)}) collective-permute-start(bf16[496,256]{1,0:T(8,128)(2,1)S(1)} %get-tuple-element.30), channel_id=1, source_target_pairs={{0,225},{1,224},{2,227},{3,226},{4,229},{5,228},{6,231},{7,230},{8... | collective-permute-start | bytes 761864 | tf_op jit(solution)/shard_map/ppermute | solution.py:52
  14.1 3.4 %collective-permute-start.2 = (bf16[128,256]{1,0:T(8,128)(2,1)S(1)}, bf16[128,256]{1,0:T(8,128)(2,1)S(1)}, u32[]{:S(2)}, u32[]{:S(2)}) collective-permute-start(bf16[128,256]{1,0:T(8,128)(2,1)S(1)} %get-tuple-element.31), channel_id=1, source_target_pairs={{0,2},{1,3},{2,0},{3,1},{4,6},{5,7},{6,4},{7,5},{8,10},{9,11},{10,... | collective-permute-start | bytes 196616 | tf_op jit(solution)/shard_map/ppermute | solution.py:52
  15.9 4.0 %collective-permute-start.3 = (bf16[128,256]{1,0:T(8,128)(2,1)S(1)}, bf16[128,256]{1,0:T(8,128)(2,1)S(1)}, u32[]{:S(2)}, u32[]{:S(2)}) collective-permute-start(bf16[128,256]{1,0:T(8,128)(2,1)S(1)} %get-tuple-element.32), channel_id=1, source_target_pairs={{0,30},{1,31},{2,4},{3,5},{4,2},{5,3},{6,8},{7,9},{8,6},{9,7},{10,... | collective-permute-start | bytes 196616 | tf_op jit(solution)/shard_map/ppermute | solution.py:52
  17.5 5.7 %collective-permute-start.6 = (bf16[544,256]{1,0:T(8,128)(2,1)S(1)}, bf16[544,256]{1,0:T(8,128)(2,1)S(1)}, u32[]{:S(2)}, u32[]{:S(2)}) collective-permute-start(bf16[544,256]{1,0:T(8,128)(2,1)S(1)} %get-tuple-element.34), channel_id=1, source_target_pairs={{0,32},{1,33},{2,34},{3,35},{4,36},{5,37},{6,38},{7,39},{8,40},{9,... | collective-permute-start | bytes 835592 | tf_op jit(solution)/shard_map/ppermute | solution.py:52
  19.9 7.3 %collective-permute-start.5 = (bf16[272,256]{1,0:T(8,128)(2,1)S(1)}, bf16[272,256]{1,0:T(8,128)(2,1)S(1)}, u32[]{:S(2)}, u32[]{:S(2)}) collective-permute-start(bf16[272,256]{1,0:T(8,128)(2,1)S(1)} %pad_maximum_fusion), channel_id=1, source_target_pairs={{0,225},{1,224},{2,227},{3,226},{4,229},{5,228},{6,231},{7,230},{8... | collective-permute-start | bytes 417800 | tf_op jit(solution)/shard_map/ppermute | solution.py:52
  21.1 4.4 %collective-permute-start.4 = (bf16[256,256]{1,0:T(8,128)(2,1)S(1)}, bf16[256,256]{1,0:T(8,128)(2,1)S(1)}, u32[]{:S(2)}, u32[]{:S(2)}) collective-permute-start(bf16[256,256]{1,0:T(8,128)(2,1)S(1)} %constant_dynamic-update-slice_fusion.ends), channel_id=1, source_target_pairs={{0,32},{1,33},{2,34},{3,35},{4,36},{5,37},{6,38},{7,39},{8,40},{9,... | collective-permute-start | bytes 393224 | tf_op jit(solution)/shard_map/ppermute | solution.py:52
  28.0 14.4 %collective-permute-start.7 = (bf16[496,256]{1,0:T(8,128)(2,1)S(1)}, bf16[496,256]{1,0:T(8,128)(2,1)S(1)}, u32[]{:S(2)}, u32[]{:S(2)}) collective-permute-start(bf16[496,256]{1,0:T(8,128)(2,1)S(1)} %get-tuple-element.35), channel_id=1, source_target_pairs={{0,225},{1,224},{2,227},{3,226},{4,229},{5,228},{6,231},{7,230},{8... | collective-permute-start | bytes 761864 | tf_op jit(solution)/shard_map/ppermute | solution.py:52
  31.1 5.1 %collective-permute-start.8 = (bf16[128,256]{1,0:T(8,128)(2,1)S(1)}, bf16[128,256]{1,0:T(8,128)(2,1)S(1)}, u32[]{:S(2)}, u32[]{:S(2)}) collective-permute-start(bf16[128,256]{1,0:T(8,128)(2,1)S(1)} %get-tuple-element.36), channel_id=1, source_target_pairs={{0,2},{1,3},{2,0},{3,1},{4,6},{5,7},{6,4},{7,5},{8,10},{9,11},{10,... | collective-permute-start | bytes 196616 | tf_op jit(solution)/shard_map/ppermute | solution.py:52
  35.3 4.0 %collective-permute-start.9 = (bf16[128,256]{1,0:T(8,128)(2,1)S(1)}, bf16[128,256]{1,0:T(8,128)(2,1)S(1)}, u32[]{:S(2)}, u32[]{:S(2)}) collective-permute-start(bf16[128,256]{1,0:T(8,128)(2,1)S(1)} %get-tuple-element.37), channel_id=1, source_target_pairs={{0,30},{1,31},{2,4},{3,5},{4,2},{5,3},{6,8},{7,9},{8,6},{9,7},{10,... | collective-permute-start | bytes 196616 | tf_op jit(solution)/shard_map/ppermute | solution.py:52
  35.3 7.2 %collective-permute-start.12 = (bf16[544,256]{1,0:T(8,128)(2,1)S(1)}, bf16[544,256]{1,0:T(8,128)(2,1)S(1)}, u32[]{:S(2)}, u32[]{:S(2)}) collective-permute-start(bf16[544,256]{1,0:T(8,128)(2,1)S(1)} %get-tuple-element.39), channel_id=1, source_target_pairs={{0,32},{1,33},{2,34},{3,35},{4,36},{5,37},{6,38},{7,39},{8,40},{9,... | collective-permute-start | bytes 835592 | tf_op jit(solution)/shard_map/ppermute | solution.py:52
  39.3 7.7 %collective-permute-start.11 = (bf16[272,256]{1,0:T(8,128)(2,1)S(1)}, bf16[272,256]{1,0:T(8,128)(2,1)S(1)}, u32[]{:S(2)}, u32[]{:S(2)}) collective-permute-start(bf16[272,256]{1,0:T(8,128)(2,1)S(1)} %pad_maximum_fusion.1), channel_id=1, source_target_pairs={{0,225},{1,224},{2,227},{3,226},{4,229},{5,228},{6,231},{7,230},{8... | collective-permute-start | bytes 417800 | tf_op jit(solution)/shard_map/ppermute | solution.py:52
  42.4 3.9 %collective-permute-start.10 = (bf16[256,256]{1,0:T(8,128)(2,1)S(1)}, bf16[256,256]{1,0:T(8,128)(2,1)S(1)}, u32[]{:S(2)}, u32[]{:S(2)}) collective-permute-start(bf16[256,256]{1,0:T(8,128)(2,1)S(1)} %constant_dynamic-update-slice_fusion.2.ends), channel_id=1, source_target_pairs={{0,32},{1,33},{2,34},{3,35},{4,36},{5,37},{6,38},{7,39},{8,40},{9,... | collective-permute-start | bytes 393224 | tf_op jit(solution)/shard_map/ppermute | solution.py:52
  47.7 9.5 %collective-permute-start.15 = (bf16[4,128,256]{2,1,0:T(8,128)(2,1)S(1)}, bf16[4,128,256]{2,1,0:T(8,128)(2,1)S(1)}, u32[]{:S(2)}, u32[]{:S(2)}) collective-permute-start(bf16[4,128,256]{2,1,0:T(8,128)(2,1)S(1)} %get-tuple-element.42.s), channel_id=1, source_target_pairs={{0,225},{1,224},{2,227},{3,226},{4,229},{5,228},{6,231},{7,230},{8... | collective-permute-start | bytes 786440 | tf_op jit(solution)/shard_map/ppermute | solution.py:56
  50.8 3.1 %collective-permute-start.13 = (bf16[192,256]{1,0:T(8,128)(2,1)S(1)}, bf16[192,256]{1,0:T(8,128)(2,1)S(1)}, u32[]{:S(2)}, u32[]{:S(2)}) collective-permute-start(bf16[192,256]{1,0:T(8,128)(2,1)S(1)} %get-tuple-element.44), channel_id=1, source_target_pairs={{0,2},{1,3},{2,0},{3,1},{4,6},{5,7},{6,4},{7,5},{8,10},{9,11},{10,... | collective-permute-start | bytes 294920 | tf_op jit(solution)/shard_map/ppermute | solution.py:52
  52.9 4.3 %collective-permute-start.14 = (bf16[192,256]{1,0:T(8,128)(2,1)S(1)}, bf16[192,256]{1,0:T(8,128)(2,1)S(1)}, u32[]{:S(2)}, u32[]{:S(2)}) collective-permute-start(bf16[192,256]{1,0:T(8,128)(2,1)S(1)} %get-tuple-element.45), channel_id=1, source_target_pairs={{0,30},{1,31},{2,4},{3,5},{4,2},{5,3},{6,8},{7,9},{8,6},{9,7},{10,... | collective-permute-start | bytes 294920 | tf_op jit(solution)/shard_map/ppermute | solution.py:52
  59.0 2.0 %collective-permute-start.16 = (f32[64,1,640]{2,1,0:T(1,128)S(1)}, f32[64,1,640]{2,1,0:T(1,128)S(1)}, u32[]{:S(2)}, u32[]{:S(2)}) collective-permute-start(f32[64,1,640]{2,1,0:T(1,128)S(1)} %get-tuple-element.49), channel_id=1, source_target_pairs={{0,2},{1,3},{2,0},{3,1},{4,6},{5,7},{6,4},{7,5},{8,10},{9,11},{10,... | collective-permute-start | bytes 491528 | tf_op jit(solution)/shard_map/ppermute | solution.py:52
  60.0 13.4 %collective-permute-start.17 = (bf16[4,128,256]{2,1,0:T(8,128)(2,1)S(1)}, bf16[4,128,256]{2,1,0:T(8,128)(2,1)S(1)}, u32[]{:S(2)}, u32[]{:S(2)}) collective-permute-start(bf16[4,128,256]{2,1,0:T(8,128)(2,1)S(1)} %get-tuple-element.42.s), channel_id=1, source_target_pairs={{0,1},{1,0},{2,3},{3,2},{4,5},{5,4},{6,7},{7,6},{8,9},{9,8},{10,11... | collective-permute-start | bytes 786440 | tf_op jit(solution)/shard_map/ppermute | solution.py:61
  61.9 23.1 %all-to-all-start = ((f32[64,1,640]{2,1,0:T(1,128)}), f32[64,1,640]{2,1,0:T(1,128)S(1)}, u32[]{:S(2)}, u32[]{:S(2)}) async-start(f32[64,1,640]{2,1,0:T(1,128)} %add.59), calls=%async_computation | async-start | bytes 327680 | tf_op jit(solution)/shard_map/all_to_all | solution.py:76
  105.6 5.2 %collective-permute-start.18 = (f32[128,1,640]{2,1,0:T(1,128)S(1)}, f32[128,1,640]{2,1,0:T(1,128)S(1)}, u32[]{:S(2)}, u32[]{:S(2)}) collective-permute-start(f32[128,1,640]{2,1,0:T(1,128)S(1)} %all_to_all.10.mine), channel_id=1, source_target_pairs={{0,2},{1,3},{2,0},{3,1},{4,6},{5,7},{6,4},{7,5},{8,10},{9,11},{10,... | collective-permute-start | bytes 983048 | tf_op jit(solution)/shard_map/ppermute | solution.py:52

commit v14 on v13

--- a/solution.py
+++ b/solution.py
@@ -13,8 +13,6 @@
 BF = jnp.bfloat16
 F32 = jnp.float32
 SPIN, COL, PAR_Y, PAR_X = 36, 37, 38, 39
-HEAD = 16
-PAD = 32
 
 
 def col_of(gx, spin):
@@ -122,24 +120,21 @@
     q[:T] = ref[pl.ds(jnp.where(even, 0, 3), 1)].reshape(T, 2 * T)
 
 
-def store_bulk(ref, to_b, to_a):
-    flat = ref[...].reshape(4 * T, 2 * T)
-    to_b[...] = flat[HEAD:]
-    to_a[: 4 * T] = flat
-    to_a[4 * T :] = flat[:PAD]
-
-
-def join_kernel(m, own, other, v, p, q, to_b, to_a):
+def join_kernel(m, own, other, v, p, q):
     first_col = m[COL] == 0
     v[:, :, :T] = jnp.where(first_col, own[...], other[...])
     v[:, :, T:] = jnp.where(first_col, other[...], own[...])
     store_edges(m, v, p, q)
-    store_bulk(v, to_b, to_a)
-
-
-def ends_of(m, ends):
-    even = m[PAR_Y] == 0
-    p, q = ends[:T], ends[ends.shape[0] - T :]
+
+
+def edge_kernel(m, a, b, out):
+    at = pl.ds(jnp.where(m[PAR_Y] == 0, 3, 0), 1)
+    out[0:1] = a[at]
+    out[1:2] = b[at]
+
+
+def low_high(m, p, q):
+    even = m[PAR_Y] == 0
     return jnp.where(even, q, p), jnp.where(even, p, q)
 
 
@@ -148,35 +143,37 @@
     return dot(row, jnp.concatenate([x.reshape(len(at) * T, 2 * T) for x in sources], axis=0))
 
 
-def core_kernel(m, o, x, ends, a, b, acc, ext):
-    low, high = ends_of(m, ends)
-    ext[0] = low
+def outer_product(m, o, at_p, tiles):
+    high = m[PAR_Y] == 0 if at_p else m[PAR_Y] != 0
+    top = blocks(o, 3, (1, 2), (2,))
+    bottom = blocks(o, 0, (1, 2), (0,))
+    return dot(jnp.where(high, top, bottom), jnp.concatenate(tiles, axis=0)), high
+
+
+def core_kernel(m, o, x, p, q, a, b, a_corner, b_corner, acc, ext):
+    ext[0], ext[5] = low_high(m, p[...], q[...])
     ext[1:5] = x[...]
-    ext[5] = high
     for tile in range(4):
         total = product(o, tile, (0,), range(tile, tile + 3), [ext[tile : tile + 3]])
         at = [place for place in range(tile, tile + 3) if 1 <= place <= 4]
-        total += product(o, tile, (1,), at, [a[(at[0] - 1) * T : at[-1] * T]])
-        at = [place for place in at if place > 1]
-        acc[tile] = total + product(o, tile, (2,), at, [b[(at[0] - 1) * T - HEAD : at[-1] * T - HEAD]])
-
-
-def rim_kernel(m, o, b, a_ends, b_ends, acc, *rest, last):
+        acc[tile] = total + product(o, tile, (1, 2), at, [y[at[0] - 1 : at[-1]] for y in (a, b)])
+    part, high = outer_product(m, o, False, [a_corner[...], b_corner[...]])
+    acc[pl.ds(jnp.where(high, 3, 0), 1)] += part[None]
+
+
+def rim_kernel(m, o, edge, acc, *rest, last):
     if last:
         before, h_p, h_q, out, p, q = rest
     else:
-        out, p, q, to_b, to_a = rest
-    low, high = zip(ends_of(m, a_ends), ends_of(m, b_ends))
-    first = jnp.concatenate([b_ends[T : T + HEAD], b[: T - HEAD]], axis=0)
+        out, p, q = rest
+    part, high = outer_product(m, o, True, [edge[0], edge[1]])
+    nothing = jnp.zeros_like(part)
     for tile in range(4):
         total = acc[tile]
         if tile == 0:
-            total += product(o, tile, (2,), (0, 1), [jnp.concatenate([low[1], first], axis=0)])
-            total += product(o, tile, (1,), (0,), [low[0]])
-        if tile == 1:
-            total += product(o, tile, (2,), (1,), [first])
+            total += jnp.where(high, nothing, part)
         if tile == 3:
-            total += product(o, tile, (1, 2), (5,), high)
+            total += jnp.where(high, part, nothing)
         if last:
             out[tile] = (total - before[tile].astype(F32)).astype(BF)
         else:
@@ -186,8 +183,6 @@
         for to, block in ((p, h_p), (q, h_q)):
             to[T:, :T] = block[: T // 2]
             to[T:, T:] = block[T // 2 :]
-    else:
-        store_bulk(out, to_b, to_a)
 
 
 def corr_kernel(m, o, s, corr, turned, acc):
@@ -390,23 +385,24 @@
     tile = shaped((T, 2 * T), BF)
     ext = pltpu.VMEM((6, T, 2 * T), BF)
     other, o = lax.optimization_barrier((other, o))
-    bulk = [shaped((4 * T - HEAD, 2 * T), BF), shaped((4 * T + PAD, 2 * T), BF)]
-    outs = [shaped(block, BF), tile, tile, *bulk]
-    v, p, q, *rest = call(join_kernel, m, [own, other], outs, "join")
-
-    def apply_ham(x, p, q, rest, more, outs):
+    outs = [shaped(block, BF), tile, tile]
+    v, p, q = call(join_kernel, m, [own, other], outs, "join")
+
+    def apply_ham(x, p, q, more, outs):
         p, q = swap(sizes, p, 0, 1), swap(sizes, q, 0, 2)
-        ends = jnp.concatenate([p, q], axis=0)
-        a, b = swap(sizes, rest[1], 1, 0), swap(sizes, rest[0], 2, 0)
-        a_ends = swap(sizes, ends, 1, 0)
-        b_ends = swap(sizes, jnp.concatenate([p, x[0, :HEAD], q], axis=0), 2, 0)
-        (acc,) = call(core_kernel, m, [o, x, ends, a, b], [shaped(block, F32)], "core", 31, scratch=[ext])
+        a, b = swap(sizes, x, 1, 0), swap(sizes, x, 2, 0)
+        a_corner, b_corner = swap(sizes, q, 1, 0), swap(sizes, q, 2, 0)
+        (edge,) = call(edge_kernel, m, [a, b], [shaped((2, T, 2 * T), BF)], "edge")
+        edge = swap(sizes, edge, 0, 1)
+        (acc,) = call(
+            core_kernel, m, [o, x, p, q, a, b, a_corner, b_corner], [shaped(block, F32)], "core", 150, scratch=[ext]
+        )
         kernel = functools.partial(rim_kernel, last=len(more) > 0)
-        return call(kernel, m, [o, b, a_ends, b_ends, acc, *more], outs, "rim", 6)
-
-    first, p, q, *rest = apply_ham(v, p, q, rest, [], outs)
+        return call(kernel, m, [o, edge, acc, *more], outs, "rim", 2)
+
+    first, p, q = apply_ham(v, p, q, [], outs)
     longer = shaped((3 * T // 2, 2 * T), BF)
-    second, p, q = apply_ham(first, p, q, rest, [v, h_p, h_q], [shaped(block, BF), longer, longer])
+    second, p, q = apply_ham(first, p, q, [v, h_p, h_q], [shaped(block, BF), longer, longer])
 
     right = shift(sizes, second, -1, 0)
     p, q = swap(sizes, p, 0, 1), swap(sizes, q, 0, 2)

time: 190 us -> 190 us (level)
  waiting for transfers between devices: 31.6 us -> 17.6 us
  starting transfers between devices: 43.7 us -> 56.3 us
    ppermute x16 -> x18, waiting for transfers between devices: 20.6 us -> 6.56 us  [swap(): return lax.ppermute(block, AXES, perm)]
    ppermute x16 -> x18, starting transfers between devices: 25.4 us -> 37.7 us  [swap(): return lax.ppermute(block, AXES, perm)]
    pallas_call x10 -> x12, Pallas kernels: 87.4 us -> 88.5 us  [call(): pl.pallas_call(kernel, out_shape=outs, grid_spec=pltpu.PrefetchScalarGrid...]
  transfers between devices with their start and end apart: 20 -> 22, of which waited for: 12 -> 5; matrix products, arithmetic and copies ran while one was open for 2% -> 2% of each run, Pallas kernels for 2% -> 3%
where the time goes in v14:
time: 190 us; the launch traced here: 189 us
  Pallas kernels  88.5 us (47%)
  starting transfers between devices  56.3 us (30%)
  blocking collectives  20.3 us (11%)
  waiting for transfers between devices  17.6 us (9%)
  local copies, waits for them, and re-layouts  3.12 us (2%)
  other arithmetic  2.86 us (2%)
    pallas_call x12, Pallas kernels, call(): pl.pallas_call(kernel, out_shape=outs, grid_spec=pltpu.PrefetchScalarGrid...  88.5 us
    ppermute x18, starting transfers between devices, swap(): return lax.ppermute(block, AXES, perm)  37.7 us
    all_to_all x1, blocking collectives, exchange(): lax.all_to_all(pieces, AXES, 0, 0, axis_index_groups=groups, tiled=True)  20.3 us
    all_to_all x1, starting transfers between devices, exchange(): lax.all_to_all(pieces, AXES, 0, 0, axis_index_groups=groups, tiled=True)  12.2 us
    all_to_all x1, waiting for transfers between devices, exchange(): lax.all_to_all(pieces, AXES, 0, 0, axis_index_groups=groups, tiled=True)  11 us
    ppermute x18, waiting for transfers between devices, swap(): return lax.ppermute(block, AXES, perm)  6.56 us
    ppermute x2, starting transfers between devices, swap_col(): return lax.ppermute(block, AXES, perm)  3.81 us
  transfers between devices with their start and end apart: 22, of which 5 were waited for; matrix products, arithmetic and copies ran while one was open for 2% of the time, Pallas kernels for 3%

profile of v14, /device:TPU:1, one launch (start us, length us, event | category | flops | bytes accessed | tf_op | source)
XLA Modules:
  0.0 189.4 jit_solution(5774645604804422015)
XLA Ops:
  0.6 1.0 dynamic-slice_bitcast_fusion
  1.6 3.7 %collective-permute-start = (bf16[4,128,128]{2,1,0:T(8,128)(2,1)S(1)}, bf16[4,128,128]{2,1,0:T(8,128)(2,1)S(1)}, u32[]{:S(2)}, u32[]{:S(2)}) collective-permute-start(bf16[4,128,128]{2,1,0:T(8,128)(2,1)S(1)} %get-tuple-element.45), channel_id=1, source_target_pairs={{0,1},{1,0},{2,3},{3,2},{4,5},{5,4},{6,7},{7,6},{8,9},{9,8},{10,11... | collective-permute-start | bytes 393224 | tf_op jit(solution)/shard_map/ppermute | solution.py:59
  6.2 1.0 select_reduce_fusion
  7.5 1.7 copy-done
  9.2 0.9 order.1
  11.1 3.5 %collective-permute-start.2 = (bf16[4,128,256]{2,1,0:T(8,128)(2,1)S(1)}, bf16[4,128,256]{2,1,0:T(8,128)(2,1)S(1)}, u32[]{:S(2)}, u32[]{:S(2)}) collective-permute-start(bf16[4,128,256]{2,1,0:T(8,128)(2,1)S(1)} %get-tuple-element.26.x.rest_0_), channel_id=1, source_target_pairs={{0,225},{1,224},{2,227},{3,226},{4,229},{5,228},{6,231},{7,230},{8... | collective-permute-start | bytes 786440 | tf_op jit(solution)/shard_map/ppermute | solution.py:50
  14.6 3.6 %collective-permute-start.5 = (bf16[128,256]{1,0:T(8,128)(2,1)S(1)}, bf16[128,256]{1,0:T(8,128)(2,1)S(1)}, u32[]{:S(2)}, u32[]{:S(2)}) collective-permute-start(bf16[128,256]{1,0:T(8,128)(2,1)S(1)} %get-tuple-element.28), channel_id=1, source_target_pairs={{0,30},{1,31},{2,4},{3,5},{4,2},{5,3},{6,8},{7,9},{8,6},{9,7},{10,... | collective-permute-start | bytes 196616 | tf_op jit(solution)/shard_map/ppermute | solution.py:50
  18.2 2.3 %collective-permute-start.4 = (bf16[128,256]{1,0:T(8,128)(2,1)S(1)}, bf16[128,256]{1,0:T(8,128)(2,1)S(1)}, u32[]{:S(2)}, u32[]{:S(2)}) collective-permute-start(bf16[128,256]{1,0:T(8,128)(2,1)S(1)} %get-tuple-element.27), channel_id=1, source_target_pairs={{0,2},{1,3},{2,0},{3,1},{4,6},{5,7},{6,4},{7,5},{8,10},{9,11},{10,... | collective-permute-start | bytes 196616 | tf_op jit(solution)/shard_map/ppermute | solution.py:50
  20.6 2.3 %collective-permute-start.7 = (bf16[128,256]{1,0:T(8,128)(2,1)S(1)}, bf16[128,256]{1,0:T(8,128)(2,1)S(1)}, u32[]{:S(2)}, u32[]{:S(2)}) collective-permute-start(bf16[128,256]{1,0:T(8,128)(2,1)S(1)} %collective-permute-done.5.q), channel_id=1, source_target_pairs={{0,225},{1,224},{2,227},{3,226},{4,229},{5,228},{6,231},{7,230},{8... | collective-permute-start | bytes 196616 | tf_op jit(solution)/shard_map/ppermute | solution.py:50
  23.5 2.6 %collective-permute-start.3 = (bf16[2,128,256]{2,1,0:T(8,128)(2,1)S(1)}, bf16[2,128,256]{2,1,0:T(8,128)(2,1)S(1)}, u32[]{:S(2)}, u32[]{:S(2)}) collective-permute-start(bf16[2,128,256]{2,1,0:T(8,128)(2,1)S(1)} %edge.2), channel_id=1, source_target_pairs={{0,2},{1,3},{2,0},{3,1},{4,6},{5,7},{6,4},{7,5},{8,10},{9,11},{10,... | collective-permute-start | bytes 393224 | tf_op jit(solution)/shard_map/ppermute | solution.py:50
  26.1 1.0 collective-permute-done.7.b_corner
  27.0 1.1 core.2.acc
  29.0 2.4 %collective-permute-start.9 = (bf16[4,128,256]{2,1,0:T(8,128)(2,1)S(1)}, bf16[4,128,256]{2,1,0:T(8,128)(2,1)S(1)}, u32[]{:S(2)}, u32[]{:S(2)}) collective-permute-start(bf16[4,128,256]{2,1,0:T(8,128)(2,1)S(1)} %get-tuple-element.29.x), channel_id=1, source_target_pairs={{0,225},{1,224},{2,227},{3,226},{4,229},{5,228},{6,231},{7,230},{8... | collective-permute-start | bytes 786440 | tf_op jit(solution)/shard_map/ppermute | solution.py:50
  31.4 2.5 %collective-permute-start.12 = (bf16[128,256]{1,0:T(8,128)(2,1)S(1)}, bf16[128,256]{1,0:T(8,128)(2,1)S(1)}, u32[]{:S(2)}, u32[]{:S(2)}) collective-permute-start(bf16[128,256]{1,0:T(8,128)(2,1)S(1)} %get-tuple-element.31), channel_id=1, source_target_pairs={{0,30},{1,31},{2,4},{3,5},{4,2},{5,3},{6,8},{7,9},{8,6},{9,7},{10,... | collective-permute-start | bytes 196616 | tf_op jit(solution)/shard_map/ppermute | solution.py:50
  33.8 2.5 %collective-permute-start.11 = (bf16[128,256]{1,0:T(8,128)(2,1)S(1)}, bf16[128,256]{1,0:T(8,128)(2,1)S(1)}, u32[]{:S(2)}, u32[]{:S(2)}) collective-permute-start(bf16[128,256]{1,0:T(8,128)(2,1)S(1)} %get-tuple-element.30), channel_id=1, source_target_pairs={{0,2},{1,3},{2,0},{3,1},{4,6},{5,7},{6,4},{7,5},{8,10},{9,11},{10,... | collective-permute-start | bytes 196616 | tf_op jit(solution)/shard_map/ppermute | solution.py:50
  36.4 2.8 %collective-permute-start.14 = (bf16[128,256]{1,0:T(8,128)(2,1)S(1)}, bf16[128,256]{1,0:T(8,128)(2,1)S(1)}, u32[]{:S(2)}, u32[]{:S(2)}) collective-permute-start(bf16[128,256]{1,0:T(8,128)(2,1)S(1)} %collective-permute-done.12.q), channel_id=1, source_target_pairs={{0,225},{1,224},{2,227},{3,226},{4,229},{5,228},{6,231},{7,230},{8... | collective-permute-start | bytes 196616 | tf_op jit(solution)/shard_map/ppermute | solution.py:50
  39.7 3.3 %collective-permute-start.10 = (bf16[2,128,256]{2,1,0:T(8,128)(2,1)S(1)}, bf16[2,128,256]{2,1,0:T(8,128)(2,1)S(1)}, u32[]{:S(2)}, u32[]{:S(2)}) collective-permute-start(bf16[2,128,256]{2,1,0:T(8,128)(2,1)S(1)} %edge.3), channel_id=1, source_target_pairs={{0,2},{1,3},{2,0},{3,1},{4,6},{5,7},{6,4},{7,5},{8,10},{9,11},{10,... | collective-permute-start | bytes 393224 | tf_op jit(solution)/shard_map/ppermute | solution.py:50
  43.1 1.1 core.3.acc
  44.9 2.7 %collective-permute-start.17 = (bf16[4,128,256]{2,1,0:T(8,128)(2,1)S(1)}, bf16[4,128,256]{2,1,0:T(8,128)(2,1)S(1)}, u32[]{:S(2)}, u32[]{:S(2)}) collective-permute-start(bf16[4,128,256]{2,1,0:T(8,128)(2,1)S(1)} %get-tuple-element.34.s), channel_id=1, source_target_pairs={{0,225},{1,224},{2,227},{3,226},{4,229},{5,228},{6,231},{7,230},{8... | collective-permute-start | bytes 786440 | tf_op jit(solution)/shard_map/ppermute | solution.py:54
  47.6 4.3 %collective-permute-start.15 = (bf16[192,256]{1,0:T(8,128)(2,1)S(1)}, bf16[192,256]{1,0:T(8,128)(2,1)S(1)}, u32[]{:S(2)}, u32[]{:S(2)}) collective-permute-start(bf16[192,256]{1,0:T(8,128)(2,1)S(1)} %get-tuple-element.36), channel_id=1, source_target_pairs={{0,2},{1,3},{2,0},{3,1},{4,6},{5,7},{6,4},{7,5},{8,10},{9,11},{10,... | collective-permute-start | bytes 294920 | tf_op jit(solution)/shard_map/ppermute | solution.py:50
  51.9 0.9 corr.1
  52.8 3.4 %collective-permute-done.16.q = bf16[192,256]{1,0:T(8,128)(2,1)S(1)} collective-permute-done((bf16[192,256]{1,0:T(8,128)(2,1)S(1)}, bf16[192,256]{1,0:T(8,128)(2,1)S(1)}, u32[]{:S(2)}, u32[]{:S(2)}) %collective-permute-start.16) | collective-permute-done | bytes 98336 | tf_op jit(solution)/shard_map/ppermute | solution.py:50
  56.2 1.7 gram.1
  58.0 1.0 collective-permute-start.18
  59.1 0.9 collective-permute-done.18
  60.0 0.8 add.59
  60.8 12.2 %all-to-all-start = ((f32[64,1,640]{2,1,0:T(1,128)}), f32[64,1,640]{2,1,0:T(1,128)S(1)}, u32[]{:S(2)}, u32[]{:S(2)}) async-start(f32[64,1,640]{2,1,0:T(1,128)} %add.59), calls=%async_computation | async-start | bytes 327680 | tf_op jit(solution)/shard_map/all_to_all | solution.py:74
  73.6 11.0 %all-to-all-done = f32[64,1,640]{2,1,0:T(1,128)S(1)} async-done(((f32[64,1,640]{2,1,0:T(1,128)}), f32[64,1,640]{2,1,0:T(1,128)S(1)}, u32[]{:S(2)}, u32[]{:S(2)}) %all-to-all-start) | async-done | bytes 163872 | tf_op jit(solution)/shard_map/all_to_all | solution.py:74
  84.9 20.3 %all_to_all.10.mine = f32[128,1,640]{2,1,0:T(1,128)S(1)} all-to-all(f32[128,1,640]{2,1,0:T(1,128)S(1)} %broadcast_in_dim.20), channel_id=1, replica_groups={{0,4,8,12,16,20,24,28,32,36,40,44,48,52,56,60,65,69,73,77,81,85,89,93,9..., dimensions={0} | all-to-all | bytes 655360 | tf_op jit(solution)/shard_map/all_to_all | solution.py:74
  105.2 3.9 %collective-permute-start.20 = (f32[128,1,640]{2,1,0:T(1,128)S(1)}, f32[128,1,640]{2,1,0:T(1,128)S(1)}, u32[]{:S(2)}, u32[]{:S(2)}) collective-permute-start(f32[128,1,640]{2,1,0:T(1,128)S(1)} %all_to_all.10.mine), channel_id=1, source_target_pairs={{0,2},{1,3},{2,0},{3,1},{4,6},{5,7},{6,4},{7,5},{8,10},{9,11},{10,... | collective-permute-start | bytes 983048 | tf_op jit(solution)/shard_map/ppermute | solution.py:50
  109.1 1.3 collective-permute-done.20.theirs
  110.4 79.0 %final.1 = (bf16[2,1,4,128,128]{4,3,2,1,0:T(8,128)(2,1)}, f32[2,256,128]{2,1,0:T(8,128)}) custom-call(s32[40]{0:T(128)S(1)} %concatenate.7.m, f32[128,1,640]{2,1,0:T(1,128)S(1)} %all_to_all.10.mine, f32[128,1,640]{2,1,0:T(1,128)S(1)} %collective-permute-done.20.theirs, bf16[2,4,128,256]{3,2,1,0:T(8,128)(2,1)S(1)} %stack.29.both), custom_call_target="tpu_custom_call" | custom-call | flops 1677721600 | bytes 1703936 | tf_op jit(solution)/shard_map/final/pallas_call | solution.py:336
  (41 shorter events, 6.1 us)
Async XLA Ops:
  1.6 8.4 %collective-permute-start = (bf16[4,128,128]{2,1,0:T(8,128)(2,1)S(1)}, bf16[4,128,128]{2,1,0:T(8,128)(2,1)S(1)}, u32[]{:S(2)}, u32[]{:S(2)}) collective-permute-start(bf16[4,128,128]{2,1,0:T(8,128)(2,1)S(1)} %get-tuple-element.45), channel_id=1, source_target_pairs={{0,1},{1,0},{2,3},{3,2},{4,5},{5,4},{6,7},{7,6},{8,9},{9,8},{10,11... | collective-permute-start | bytes 393224 | tf_op jit(solution)/shard_map/ppermute | solution.py:59
  7.5 1.7 copy-start
  10.7 12.2 %collective-permute-start.1 = (bf16[4,128,256]{2,1,0:T(8,128)(2,1)S(1)}, bf16[4,128,256]{2,1,0:T(8,128)(2,1)S(1)}, u32[]{:S(2)}, u32[]{:S(2)}) collective-permute-start(bf16[4,128,256]{2,1,0:T(8,128)(2,1)S(1)} %get-tuple-element.26.x.rest_0_), channel_id=1, source_target_pairs={{0,32},{1,33},{2,34},{3,35},{4,36},{5,37},{6,38},{7,39},{8,40},{9,... | collective-permute-start | bytes 786440 | tf_op jit(solution)/shard_map/ppermute | solution.py:50
  11.1 11.8 %collective-permute-start.2 = (bf16[4,128,256]{2,1,0:T(8,128)(2,1)S(1)}, bf16[4,128,256]{2,1,0:T(8,128)(2,1)S(1)}, u32[]{:S(2)}, u32[]{:S(2)}) collective-permute-start(bf16[4,128,256]{2,1,0:T(8,128)(2,1)S(1)} %get-tuple-element.26.x.rest_0_), channel_id=1, source_target_pairs={{0,225},{1,224},{2,227},{3,226},{4,229},{5,228},{6,231},{7,230},{8... | collective-permute-start | bytes 786440 | tf_op jit(solution)/shard_map/ppermute | solution.py:50
  14.6 6.0 %collective-permute-start.5 = (bf16[128,256]{1,0:T(8,128)(2,1)S(1)}, bf16[128,256]{1,0:T(8,128)(2,1)S(1)}, u32[]{:S(2)}, u32[]{:S(2)}) collective-permute-start(bf16[128,256]{1,0:T(8,128)(2,1)S(1)} %get-tuple-element.28), channel_id=1, source_target_pairs={{0,30},{1,31},{2,4},{3,5},{4,2},{5,3},{6,8},{7,9},{8,6},{9,7},{10,... | collective-permute-start | bytes 196616 | tf_op jit(solution)/shard_map/ppermute | solution.py:50
  18.2 7.8 %collective-permute-start.4 = (bf16[128,256]{1,0:T(8,128)(2,1)S(1)}, bf16[128,256]{1,0:T(8,128)(2,1)S(1)}, u32[]{:S(2)}, u32[]{:S(2)}) collective-permute-start(bf16[128,256]{1,0:T(8,128)(2,1)S(1)} %get-tuple-element.27), channel_id=1, source_target_pairs={{0,2},{1,3},{2,0},{3,1},{4,6},{5,7},{6,4},{7,5},{8,10},{9,11},{10,... | collective-permute-start | bytes 196616 | tf_op jit(solution)/shard_map/ppermute | solution.py:50
  20.6 5.5 %collective-permute-start.6 = (bf16[128,256]{1,0:T(8,128)(2,1)S(1)}, bf16[128,256]{1,0:T(8,128)(2,1)S(1)}, u32[]{:S(2)}, u32[]{:S(2)}) collective-permute-start(bf16[128,256]{1,0:T(8,128)(2,1)S(1)} %collective-permute-done.5.q), channel_id=1, source_target_pairs={{0,32},{1,33},{2,34},{3,35},{4,36},{5,37},{6,38},{7,39},{8,40},{9,... | collective-permute-start | bytes 196616 | tf_op jit(solution)/shard_map/ppermute | solution.py:50
  20.6 6.4 %collective-permute-start.7 = (bf16[128,256]{1,0:T(8,128)(2,1)S(1)}, bf16[128,256]{1,0:T(8,128)(2,1)S(1)}, u32[]{:S(2)}, u32[]{:S(2)}) collective-permute-start(bf16[128,256]{1,0:T(8,128)(2,1)S(1)} %collective-permute-done.5.q), channel_id=1, source_target_pairs={{0,225},{1,224},{2,227},{3,226},{4,229},{5,228},{6,231},{7,230},{8... | collective-permute-start | bytes 196616 | tf_op jit(solution)/shard_map/ppermute | solution.py:50
  23.5 4.6 %collective-permute-start.3 = (bf16[2,128,256]{2,1,0:T(8,128)(2,1)S(1)}, bf16[2,128,256]{2,1,0:T(8,128)(2,1)S(1)}, u32[]{:S(2)}, u32[]{:S(2)}) collective-permute-start(bf16[2,128,256]{2,1,0:T(8,128)(2,1)S(1)} %edge.2), channel_id=1, source_target_pairs={{0,2},{1,3},{2,0},{3,1},{4,6},{5,7},{6,4},{7,5},{8,10},{9,11},{10,... | collective-permute-start | bytes 393224 | tf_op jit(solution)/shard_map/ppermute | solution.py:50
  28.9 10.3 %collective-permute-start.8 = (bf16[4,128,256]{2,1,0:T(8,128)(2,1)S(1)}, bf16[4,128,256]{2,1,0:T(8,128)(2,1)S(1)}, u32[]{:S(2)}, u32[]{:S(2)}) collective-permute-start(bf16[4,128,256]{2,1,0:T(8,128)(2,1)S(1)} %get-tuple-element.29.x), channel_id=1, source_target_pairs={{0,32},{1,33},{2,34},{3,35},{4,36},{5,37},{6,38},{7,39},{8,40},{9,... | collective-permute-start | bytes 786440 | tf_op jit(solution)/shard_map/ppermute | solution.py:50
  29.0 10.2 %collective-permute-start.9 = (bf16[4,128,256]{2,1,0:T(8,128)(2,1)S(1)}, bf16[4,128,256]{2,1,0:T(8,128)(2,1)S(1)}, u32[]{:S(2)}, u32[]{:S(2)}) collective-permute-start(bf16[4,128,256]{2,1,0:T(8,128)(2,1)S(1)} %get-tuple-element.29.x), channel_id=1, source_target_pairs={{0,225},{1,224},{2,227},{3,226},{4,229},{5,228},{6,231},{7,230},{8... | collective-permute-start | bytes 786440 | tf_op jit(solution)/shard_map/ppermute | solution.py:50
  31.4 5.0 %collective-permute-start.12 = (bf16[128,256]{1,0:T(8,128)(2,1)S(1)}, bf16[128,256]{1,0:T(8,128)(2,1)S(1)}, u32[]{:S(2)}, u32[]{:S(2)}) collective-permute-start(bf16[128,256]{1,0:T(8,128)(2,1)S(1)} %get-tuple-element.31), channel_id=1, source_target_pairs={{0,30},{1,31},{2,4},{3,5},{4,2},{5,3},{6,8},{7,9},{8,6},{9,7},{10,... | collective-permute-start | bytes 196616 | tf_op jit(solution)/shard_map/ppermute | solution.py:50
  33.8 9.2 %collective-permute-start.11 = (bf16[128,256]{1,0:T(8,128)(2,1)S(1)}, bf16[128,256]{1,0:T(8,128)(2,1)S(1)}, u32[]{:S(2)}, u32[]{:S(2)}) collective-permute-start(bf16[128,256]{1,0:T(8,128)(2,1)S(1)} %get-tuple-element.30), channel_id=1, source_target_pairs={{0,2},{1,3},{2,0},{3,1},{4,6},{5,7},{6,4},{7,5},{8,10},{9,11},{10,... | collective-permute-start | bytes 196616 | tf_op jit(solution)/shard_map/ppermute | solution.py:50
  36.4 6.7 %collective-permute-start.13 = (bf16[128,256]{1,0:T(8,128)(2,1)S(1)}, bf16[128,256]{1,0:T(8,128)(2,1)S(1)}, u32[]{:S(2)}, u32[]{:S(2)}) collective-permute-start(bf16[128,256]{1,0:T(8,128)(2,1)S(1)} %collective-permute-done.12.q), channel_id=1, source_target_pairs={{0,32},{1,33},{2,34},{3,35},{4,36},{5,37},{6,38},{7,39},{8,40},{9,... | collective-permute-start | bytes 196616 | tf_op jit(solution)/shard_map/ppermute | solution.py:50
  36.4 6.7 %collective-permute-start.14 = (bf16[128,256]{1,0:T(8,128)(2,1)S(1)}, bf16[128,256]{1,0:T(8,128)(2,1)S(1)}, u32[]{:S(2)}, u32[]{:S(2)}) collective-permute-start(bf16[128,256]{1,0:T(8,128)(2,1)S(1)} %collective-permute-done.12.q), channel_id=1, source_target_pairs={{0,225},{1,224},{2,227},{3,226},{4,229},{5,228},{6,231},{7,230},{8... | collective-permute-start | bytes 196616 | tf_op jit(solution)/shard_map/ppermute | solution.py:50
  39.7 4.4 %collective-permute-start.10 = (bf16[2,128,256]{2,1,0:T(8,128)(2,1)S(1)}, bf16[2,128,256]{2,1,0:T(8,128)(2,1)S(1)}, u32[]{:S(2)}, u32[]{:S(2)}) collective-permute-start(bf16[2,128,256]{2,1,0:T(8,128)(2,1)S(1)} %edge.3), channel_id=1, source_target_pairs={{0,2},{1,3},{2,0},{3,1},{4,6},{5,7},{6,4},{7,5},{8,10},{9,11},{10,... | collective-permute-start | bytes 393224 | tf_op jit(solution)/shard_map/ppermute | solution.py:50
  44.9 11.3 %collective-permute-start.17 = (bf16[4,128,256]{2,1,0:T(8,128)(2,1)S(1)}, bf16[4,128,256]{2,1,0:T(8,128)(2,1)S(1)}, u32[]{:S(2)}, u32[]{:S(2)}) collective-permute-start(bf16[4,128,256]{2,1,0:T(8,128)(2,1)S(1)} %get-tuple-element.34.s), channel_id=1, source_target_pairs={{0,225},{1,224},{2,227},{3,226},{4,229},{5,228},{6,231},{7,230},{8... | collective-permute-start | bytes 786440 | tf_op jit(solution)/shard_map/ppermute | solution.py:54
  47.6 5.3 %collective-permute-start.15 = (bf16[192,256]{1,0:T(8,128)(2,1)S(1)}, bf16[192,256]{1,0:T(8,128)(2,1)S(1)}, u32[]{:S(2)}, u32[]{:S(2)}) collective-permute-start(bf16[192,256]{1,0:T(8,128)(2,1)S(1)} %get-tuple-element.36), channel_id=1, source_target_pairs={{0,2},{1,3},{2,0},{3,1},{4,6},{5,7},{6,4},{7,5},{8,10},{9,11},{10,... | collective-permute-start | bytes 294920 | tf_op jit(solution)/shard_map/ppermute | solution.py:50
  51.9 4.3 %collective-permute-start.16 = (bf16[192,256]{1,0:T(8,128)(2,1)S(1)}, bf16[192,256]{1,0:T(8,128)(2,1)S(1)}, u32[]{:S(2)}, u32[]{:S(2)}) collective-permute-start(bf16[192,256]{1,0:T(8,128)(2,1)S(1)} %get-tuple-element.37), channel_id=1, source_target_pairs={{0,30},{1,31},{2,4},{3,5},{4,2},{5,3},{6,8},{7,9},{8,6},{9,7},{10,... | collective-permute-start | bytes 294920 | tf_op jit(solution)/shard_map/ppermute | solution.py:50
  58.0 2.0 %collective-permute-start.18 = (f32[64,1,640]{2,1,0:T(1,128)S(1)}, f32[64,1,640]{2,1,0:T(1,128)S(1)}, u32[]{:S(2)}, u32[]{:S(2)}) collective-permute-start(f32[64,1,640]{2,1,0:T(1,128)S(1)} %get-tuple-element.41), channel_id=1, source_target_pairs={{0,2},{1,3},{2,0},{3,1},{4,6},{5,7},{6,4},{7,5},{8,10},{9,11},{10,... | collective-permute-start | bytes 491528 | tf_op jit(solution)/shard_map/ppermute | solution.py:50
  59.0 14.0 %collective-permute-start.19 = (bf16[4,128,256]{2,1,0:T(8,128)(2,1)S(1)}, bf16[4,128,256]{2,1,0:T(8,128)(2,1)S(1)}, u32[]{:S(2)}, u32[]{:S(2)}) collective-permute-start(bf16[4,128,256]{2,1,0:T(8,128)(2,1)S(1)} %get-tuple-element.34.s), channel_id=1, source_target_pairs={{0,1},{1,0},{2,3},{3,2},{4,5},{5,4},{6,7},{7,6},{8,9},{9,8},{10,11... | collective-permute-start | bytes 786440 | tf_op jit(solution)/shard_map/ppermute | solution.py:59
  60.8 23.8 %all-to-all-start = ((f32[64,1,640]{2,1,0:T(1,128)}), f32[64,1,640]{2,1,0:T(1,128)S(1)}, u32[]{:S(2)}, u32[]{:S(2)}) async-start(f32[64,1,640]{2,1,0:T(1,128)} %add.59), calls=%async_computation | async-start | bytes 327680 | tf_op jit(solution)/shard_map/all_to_all | solution.py:74
  105.2 5.2 %collective-permute-start.20 = (f32[128,1,640]{2,1,0:T(1,128)S(1)}, f32[128,1,640]{2,1,0:T(1,128)S(1)}, u32[]{:S(2)}, u32[]{:S(2)}) collective-permute-start(f32[128,1,640]{2,1,0:T(1,128)S(1)} %all_to_all.10.mine), channel_id=1, source_target_pairs={{0,2},{1,3},{2,0},{3,1},{4,6},{5,7},{6,4},{7,5},{8,10},{9,11},{10,... | collective-permute-start | bytes 983048 | tf_op jit(solution)/shard_map/ppermute | solution.py:50

commit v15 on v14

--- a/solution.py
+++ b/solution.py
@@ -416,7 +416,7 @@
 
     rows = members * second.shape[0] * second.shape[1]
     partial = mine + swap(sizes, theirs, 0, 1)
-    (both,) = call(stack_kernel, m, [second, swap_col(sizes, second)], [shaped((2, *block), BF)], "stack", 200)
+    (both,) = call(stack_kernel, m, [second, swap_col(sizes, second)], [shaped((2, *block), BF)], "stack", 300)
     total = exchange(sizes, partial, False)
     total, both = lax.optimization_barrier((total, both))
     total = total.sum(axis=0, keepdims=True) / rows

time: 190 us -> 194 us (1.021)
  starting transfers between devices: 56.3 us -> 60.3 us
    ppermute x18, starting transfers between devices: 37.7 us -> 40.7 us  [swap(): return lax.ppermute(block, AXES, perm)]
  transfers between devices with their start and end apart: 22 -> 22, of which waited for: 5 -> 5; matrix products, arithmetic and copies ran while one was open for 2% -> 2% of each run, Pallas kernels for 3% -> 4%
where the time goes in v15:
time: 194 us
  Pallas kernels  88.5 us (46%)
  starting transfers between devices  60.3 us (31%)
  blocking collectives  20.4 us (11%)
  waiting for transfers between devices  17.6 us (9%)
  local copies, waits for them, and re-layouts  3.12 us (2%)
  other arithmetic  2.86 us (1%)
    pallas_call x12, Pallas kernels, call(): pl.pallas_call(kernel, out_shape=outs, grid_spec=pltpu.PrefetchScalarGrid...  88.5 us
    ppermute x18, starting transfers between devices, swap(): return lax.ppermute(block, AXES, perm)  40.7 us
    all_to_all x1, blocking collectives, exchange(): lax.all_to_all(pieces, AXES, 0, 0, axis_index_groups=groups, tiled=True)  20.4 us
    all_to_all x1, starting transfers between devices, exchange(): lax.all_to_all(pieces, AXES, 0, 0, axis_index_groups=groups, tiled=True)  13.2 us
    all_to_all x1, waiting for transfers between devices, exchange(): lax.all_to_all(pieces, AXES, 0, 0, axis_index_groups=groups, tiled=True)  11 us
    ppermute x18, waiting for transfers between devices, swap(): return lax.ppermute(block, AXES, perm)  6.57 us
  transfers between devices with their start and end apart: 22, of which 5 were waited for; matrix products, arithmetic and copies ran while one was open for 2% of the time, Pallas kernels for 4%

profile of v15, /device:TPU:1, one launch (start us, length us, event | category | flops | bytes accessed | tf_op | source)
XLA Modules:
  0.0 193.6 jit_solution(2139393944887790774)
XLA Ops:
  0.6 1.0 dynamic-slice_bitcast_fusion
  1.6 3.7 %collective-permute-start = (bf16[4,128,128]{2,1,0:T(8,128)(2,1)S(1)}, bf16[4,128,128]{2,1,0:T(8,128)(2,1)S(1)}, u32[]{:S(2)}, u32[]{:S(2)}) collective-permute-start(bf16[4,128,128]{2,1,0:T(8,128)(2,1)S(1)} %get-tuple-element.45), channel_id=1, source_target_pairs={{0,1},{1,0},{2,3},{3,2},{4,5},{5,4},{6,7},{7,6},{8,9},{9,8},{10,11... | collective-permute-start | bytes 393224 | tf_op jit(solution)/shard_map/ppermute | solution.py:59
  6.2 1.0 select_reduce_fusion
  7.5 1.7 copy-done
  9.2 0.9 order.1
  11.1 3.5 %collective-permute-start.2 = (bf16[4,128,256]{2,1,0:T(8,128)(2,1)S(1)}, bf16[4,128,256]{2,1,0:T(8,128)(2,1)S(1)}, u32[]{:S(2)}, u32[]{:S(2)}) collective-permute-start(bf16[4,128,256]{2,1,0:T(8,128)(2,1)S(1)} %get-tuple-element.26.x.rest_0_), channel_id=1, source_target_pairs={{0,225},{1,224},{2,227},{3,226},{4,229},{5,228},{6,231},{7,230},{8... | collective-permute-start | bytes 786440 | tf_op jit(solution)/shard_map/ppermute | solution.py:50
  14.6 3.6 %collective-permute-start.5 = (bf16[128,256]{1,0:T(8,128)(2,1)S(1)}, bf16[128,256]{1,0:T(8,128)(2,1)S(1)}, u32[]{:S(2)}, u32[]{:S(2)}) collective-permute-start(bf16[128,256]{1,0:T(8,128)(2,1)S(1)} %get-tuple-element.28), channel_id=1, source_target_pairs={{0,30},{1,31},{2,4},{3,5},{4,2},{5,3},{6,8},{7,9},{8,6},{9,7},{10,... | collective-permute-start | bytes 196616 | tf_op jit(solution)/shard_map/ppermute | solution.py:50
  18.2 2.3 %collective-permute-start.4 = (bf16[128,256]{1,0:T(8,128)(2,1)S(1)}, bf16[128,256]{1,0:T(8,128)(2,1)S(1)}, u32[]{:S(2)}, u32[]{:S(2)}) collective-permute-start(bf16[128,256]{1,0:T(8,128)(2,1)S(1)} %get-tuple-element.27), channel_id=1, source_target_pairs={{0,2},{1,3},{2,0},{3,1},{4,6},{5,7},{6,4},{7,5},{8,10},{9,11},{10,... | collective-permute-start | bytes 196616 | tf_op jit(solution)/shard_map/ppermute | solution.py:50
  20.6 2.3 %collective-permute-start.7 = (bf16[128,256]{1,0:T(8,128)(2,1)S(1)}, bf16[128,256]{1,0:T(8,128)(2,1)S(1)}, u32[]{:S(2)}, u32[]{:S(2)}) collective-permute-start(bf16[128,256]{1,0:T(8,128)(2,1)S(1)} %collective-permute-done.5.q), channel_id=1, source_target_pairs={{0,225},{1,224},{2,227},{3,226},{4,229},{5,228},{6,231},{7,230},{8... | collective-permute-start | bytes 196616 | tf_op jit(solution)/shard_map/ppermute | solution.py:50
  23.5 2.6 %collective-permute-start.3 = (bf16[2,128,256]{2,1,0:T(8,128)(2,1)S(1)}, bf16[2,128,256]{2,1,0:T(8,128)(2,1)S(1)}, u32[]{:S(2)}, u32[]{:S(2)}) collective-permute-start(bf16[2,128,256]{2,1,0:T(8,128)(2,1)S(1)} %edge.2), channel_id=1, source_target_pairs={{0,2},{1,3},{2,0},{3,1},{4,6},{5,7},{6,4},{7,5},{8,10},{9,11},{10,... | collective-permute-start | bytes 393224 | tf_op jit(solution)/shard_map/ppermute | solution.py:50
  26.1 1.0 collective-permute-done.7.b_corner
  27.0 1.1 core.2.acc
  29.0 2.4 %collective-permute-start.9 = (bf16[4,128,256]{2,1,0:T(8,128)(2,1)S(1)}, bf16[4,128,256]{2,1,0:T(8,128)(2,1)S(1)}, u32[]{:S(2)}, u32[]{:S(2)}) collective-permute-start(bf16[4,128,256]{2,1,0:T(8,128)(2,1)S(1)} %get-tuple-element.29.x), channel_id=1, source_target_pairs={{0,225},{1,224},{2,227},{3,226},{4,229},{5,228},{6,231},{7,230},{8... | collective-permute-start | bytes 786440 | tf_op jit(solution)/shard_map/ppermute | solution.py:50
  31.4 2.5 %collective-permute-start.12 = (bf16[128,256]{1,0:T(8,128)(2,1)S(1)}, bf16[128,256]{1,0:T(8,128)(2,1)S(1)}, u32[]{:S(2)}, u32[]{:S(2)}) collective-permute-start(bf16[128,256]{1,0:T(8,128)(2,1)S(1)} %get-tuple-element.31), channel_id=1, source_target_pairs={{0,30},{1,31},{2,4},{3,5},{4,2},{5,3},{6,8},{7,9},{8,6},{9,7},{10,... | collective-permute-start | bytes 196616 | tf_op jit(solution)/shard_map/ppermute | solution.py:50
  33.8 2.5 %collective-permute-start.11 = (bf16[128,256]{1,0:T(8,128)(2,1)S(1)}, bf16[128,256]{1,0:T(8,128)(2,1)S(1)}, u32[]{:S(2)}, u32[]{:S(2)}) collective-permute-start(bf16[128,256]{1,0:T(8,128)(2,1)S(1)} %get-tuple-element.30), channel_id=1, source_target_pairs={{0,2},{1,3},{2,0},{3,1},{4,6},{5,7},{6,4},{7,5},{8,10},{9,11},{10,... | collective-permute-start | bytes 196616 | tf_op jit(solution)/shard_map/ppermute | solution.py:50
  36.4 2.8 %collective-permute-start.14 = (bf16[128,256]{1,0:T(8,128)(2,1)S(1)}, bf16[128,256]{1,0:T(8,128)(2,1)S(1)}, u32[]{:S(2)}, u32[]{:S(2)}) collective-permute-start(bf16[128,256]{1,0:T(8,128)(2,1)S(1)} %collective-permute-done.12.q), channel_id=1, source_target_pairs={{0,225},{1,224},{2,227},{3,226},{4,229},{5,228},{6,231},{7,230},{8... | collective-permute-start | bytes 196616 | tf_op jit(solution)/shard_map/ppermute | solution.py:50
  39.7 3.3 %collective-permute-start.10 = (bf16[2,128,256]{2,1,0:T(8,128)(2,1)S(1)}, bf16[2,128,256]{2,1,0:T(8,128)(2,1)S(1)}, u32[]{:S(2)}, u32[]{:S(2)}) collective-permute-start(bf16[2,128,256]{2,1,0:T(8,128)(2,1)S(1)} %edge.3), channel_id=1, source_target_pairs={{0,2},{1,3},{2,0},{3,1},{4,6},{5,7},{6,4},{7,5},{8,10},{9,11},{10,... | collective-permute-start | bytes 393224 | tf_op jit(solution)/shard_map/ppermute | solution.py:50
  43.1 1.1 core.3.acc
  44.9 2.7 %collective-permute-start.17 = (bf16[4,128,256]{2,1,0:T(8,128)(2,1)S(1)}, bf16[4,128,256]{2,1,0:T(8,128)(2,1)S(1)}, u32[]{:S(2)}, u32[]{:S(2)}) collective-permute-start(bf16[4,128,256]{2,1,0:T(8,128)(2,1)S(1)} %get-tuple-element.34.s), channel_id=1, source_target_pairs={{0,225},{1,224},{2,227},{3,226},{4,229},{5,228},{6,231},{7,230},{8... | collective-permute-start | bytes 786440 | tf_op jit(solution)/shard_map/ppermute | solution.py:54
  47.6 4.3 %collective-permute-start.15 = (bf16[192,256]{1,0:T(8,128)(2,1)S(1)}, bf16[192,256]{1,0:T(8,128)(2,1)S(1)}, u32[]{:S(2)}, u32[]{:S(2)}) collective-permute-start(bf16[192,256]{1,0:T(8,128)(2,1)S(1)} %get-tuple-element.36), channel_id=1, source_target_pairs={{0,2},{1,3},{2,0},{3,1},{4,6},{5,7},{6,4},{7,5},{8,10},{9,11},{10,... | collective-permute-start | bytes 294920 | tf_op jit(solution)/shard_map/ppermute | solution.py:50
  52.0 0.9 corr.1
  52.9 3.3 %collective-permute-done.16.q = bf16[192,256]{1,0:T(8,128)(2,1)S(1)} collective-permute-done((bf16[192,256]{1,0:T(8,128)(2,1)S(1)}, bf16[192,256]{1,0:T(8,128)(2,1)S(1)}, u32[]{:S(2)}, u32[]{:S(2)}) %collective-permute-start.16) | collective-permute-done | bytes 98336 | tf_op jit(solution)/shard_map/ppermute | solution.py:50
  56.2 1.7 gram.1
  58.0 4.6 %collective-permute-start.18 = (f32[64,1,640]{2,1,0:T(1,128)S(1)}, f32[64,1,640]{2,1,0:T(1,128)S(1)}, u32[]{:S(2)}, u32[]{:S(2)}) collective-permute-start(f32[64,1,640]{2,1,0:T(1,128)S(1)} %get-tuple-element.41), channel_id=1, source_target_pairs={{0,2},{1,3},{2,0},{3,1},{4,6},{5,7},{6,4},{7,5},{8,10},{9,11},{10,... | collective-permute-start | bytes 491528 | tf_op jit(solution)/shard_map/ppermute | solution.py:50
  62.6 1.0 collective-permute-done.18
  63.6 0.8 add.59
  64.4 13.2 %all-to-all-start = ((f32[64,1,640]{2,1,0:T(1,128)}), f32[64,1,640]{2,1,0:T(1,128)S(1)}, u32[]{:S(2)}, u32[]{:S(2)}) async-start(f32[64,1,640]{2,1,0:T(1,128)} %add.59), calls=%async_computation | async-start | bytes 327680 | tf_op jit(solution)/shard_map/all_to_all | solution.py:74
  78.2 11.0 %all-to-all-done = f32[64,1,640]{2,1,0:T(1,128)S(1)} async-done(((f32[64,1,640]{2,1,0:T(1,128)}), f32[64,1,640]{2,1,0:T(1,128)S(1)}, u32[]{:S(2)}, u32[]{:S(2)}) %all-to-all-start) | async-done | bytes 163872 | tf_op jit(solution)/shard_map/all_to_all | solution.py:74
  89.6 20.4 %all_to_all.10.mine = f32[128,1,640]{2,1,0:T(1,128)S(1)} all-to-all(f32[128,1,640]{2,1,0:T(1,128)S(1)} %broadcast_in_dim.20), channel_id=1, replica_groups={{0,4,8,12,16,20,24,28,32,36,40,44,48,52,56,60,65,69,73,77,81,85,89,93,9..., dimensions={0} | all-to-all | bytes 655360 | tf_op jit(solution)/shard_map/all_to_all | solution.py:74
  110.0 3.3 %collective-permute-start.20 = (f32[128,1,640]{2,1,0:T(1,128)S(1)}, f32[128,1,640]{2,1,0:T(1,128)S(1)}, u32[]{:S(2)}, u32[]{:S(2)}) collective-permute-start(f32[128,1,640]{2,1,0:T(1,128)S(1)} %all_to_all.10.mine), channel_id=1, source_target_pairs={{0,2},{1,3},{2,0},{3,1},{4,6},{5,7},{6,4},{7,5},{8,10},{9,11},{10,... | collective-permute-start | bytes 983048 | tf_op jit(solution)/shard_map/ppermute | solution.py:50
  113.4 1.3 collective-permute-done.20.theirs
  114.6 79.0 %final.1 = (bf16[2,1,4,128,128]{4,3,2,1,0:T(8,128)(2,1)}, f32[2,256,128]{2,1,0:T(8,128)}) custom-call(s32[40]{0:T(128)S(1)} %concatenate.7.m, f32[128,1,640]{2,1,0:T(1,128)S(1)} %all_to_all.10.mine, f32[128,1,640]{2,1,0:T(1,128)S(1)} %collective-permute-done.20.theirs, bf16[2,4,128,256]{3,2,1,0:T(8,128)(2,1)S(1)} %stack.29.both), custom_call_target="tpu_custom_call" | custom-call | flops 1677721600 | bytes 1703936 | tf_op jit(solution)/shard_map/final/pallas_call | solution.py:336
  (41 shorter events, 6.0 us)
Async XLA Ops:
  1.6 8.4 %collective-permute-start = (bf16[4,128,128]{2,1,0:T(8,128)(2,1)S(1)}, bf16[4,128,128]{2,1,0:T(8,128)(2,1)S(1)}, u32[]{:S(2)}, u32[]{:S(2)}) collective-permute-start(bf16[4,128,128]{2,1,0:T(8,128)(2,1)S(1)} %get-tuple-element.45), channel_id=1, source_target_pairs={{0,1},{1,0},{2,3},{3,2},{4,5},{5,4},{6,7},{7,6},{8,9},{9,8},{10,11... | collective-permute-start | bytes 393224 | tf_op jit(solution)/shard_map/ppermute | solution.py:59
  7.5 1.7 copy-start
  10.7 12.2 %collective-permute-start.1 = (bf16[4,128,256]{2,1,0:T(8,128)(2,1)S(1)}, bf16[4,128,256]{2,1,0:T(8,128)(2,1)S(1)}, u32[]{:S(2)}, u32[]{:S(2)}) collective-permute-start(bf16[4,128,256]{2,1,0:T(8,128)(2,1)S(1)} %get-tuple-element.26.x.rest_0_), channel_id=1, source_target_pairs={{0,32},{1,33},{2,34},{3,35},{4,36},{5,37},{6,38},{7,39},{8,40},{9,... | collective-permute-start | bytes 786440 | tf_op jit(solution)/shard_map/ppermute | solution.py:50
  11.1 11.8 %collective-permute-start.2 = (bf16[4,128,256]{2,1,0:T(8,128)(2,1)S(1)}, bf16[4,128,256]{2,1,0:T(8,128)(2,1)S(1)}, u32[]{:S(2)}, u32[]{:S(2)}) collective-permute-start(bf16[4,128,256]{2,1,0:T(8,128)(2,1)S(1)} %get-tuple-element.26.x.rest_0_), channel_id=1, source_target_pairs={{0,225},{1,224},{2,227},{3,226},{4,229},{5,228},{6,231},{7,230},{8... | collective-permute-start | bytes 786440 | tf_op jit(solution)/shard_map/ppermute | solution.py:50
  14.6 6.0 %collective-permute-start.5 = (bf16[128,256]{1,0:T(8,128)(2,1)S(1)}, bf16[128,256]{1,0:T(8,128)(2,1)S(1)}, u32[]{:S(2)}, u32[]{:S(2)}) collective-permute-start(bf16[128,256]{1,0:T(8,128)(2,1)S(1)} %get-tuple-element.28), channel_id=1, source_target_pairs={{0,30},{1,31},{2,4},{3,5},{4,2},{5,3},{6,8},{7,9},{8,6},{9,7},{10,... | collective-permute-start | bytes 196616 | tf_op jit(solution)/shard_map/ppermute | solution.py:50
  18.2 7.8 %collective-permute-start.4 = (bf16[128,256]{1,0:T(8,128)(2,1)S(1)}, bf16[128,256]{1,0:T(8,128)(2,1)S(1)}, u32[]{:S(2)}, u32[]{:S(2)}) collective-permute-start(bf16[128,256]{1,0:T(8,128)(2,1)S(1)} %get-tuple-element.27), channel_id=1, source_target_pairs={{0,2},{1,3},{2,0},{3,1},{4,6},{5,7},{6,4},{7,5},{8,10},{9,11},{10,... | collective-permute-start | bytes 196616 | tf_op jit(solution)/shard_map/ppermute | solution.py:50
  20.6 5.5 %collective-permute-start.6 = (bf16[128,256]{1,0:T(8,128)(2,1)S(1)}, bf16[128,256]{1,0:T(8,128)(2,1)S(1)}, u32[]{:S(2)}, u32[]{:S(2)}) collective-permute-start(bf16[128,256]{1,0:T(8,128)(2,1)S(1)} %collective-permute-done.5.q), channel_id=1, source_target_pairs={{0,32},{1,33},{2,34},{3,35},{4,36},{5,37},{6,38},{7,39},{8,40},{9,... | collective-permute-start | bytes 196616 | tf_op jit(solution)/shard_map/ppermute | solution.py:50
  20.6 6.4 %collective-permute-start.7 = (bf16[128,256]{1,0:T(8,128)(2,1)S(1)}, bf16[128,256]{1,0:T(8,128)(2,1)S(1)}, u32[]{:S(2)}, u32[]{:S(2)}) collective-permute-start(bf16[128,256]{1,0:T(8,128)(2,1)S(1)} %collective-permute-done.5.q), channel_id=1, source_target_pairs={{0,225},{1,224},{2,227},{3,226},{4,229},{5,228},{6,231},{7,230},{8... | collective-permute-start | bytes 196616 | tf_op jit(solution)/shard_map/ppermute | solution.py:50
  23.5 4.6 %collective-permute-start.3 = (bf16[2,128,256]{2,1,0:T(8,128)(2,1)S(1)}, bf16[2,128,256]{2,1,0:T(8,128)(2,1)S(1)}, u32[]{:S(2)}, u32[]{:S(2)}) collective-permute-start(bf16[2,128,256]{2,1,0:T(8,128)(2,1)S(1)} %edge.2), channel_id=1, source_target_pairs={{0,2},{1,3},{2,0},{3,1},{4,6},{5,7},{6,4},{7,5},{8,10},{9,11},{10,... | collective-permute-start | bytes 393224 | tf_op jit(solution)/shard_map/ppermute | solution.py:50
  28.9 10.3 %collective-permute-start.8 = (bf16[4,128,256]{2,1,0:T(8,128)(2,1)S(1)}, bf16[4,128,256]{2,1,0:T(8,128)(2,1)S(1)}, u32[]{:S(2)}, u32[]{:S(2)}) collective-permute-start(bf16[4,128,256]{2,1,0:T(8,128)(2,1)S(1)} %get-tuple-element.29.x), channel_id=1, source_target_pairs={{0,32},{1,33},{2,34},{3,35},{4,36},{5,37},{6,38},{7,39},{8,40},{9,... | collective-permute-start | bytes 786440 | tf_op jit(solution)/shard_map/ppermute | solution.py:50
  29.0 10.2 %collective-permute-start.9 = (bf16[4,128,256]{2,1,0:T(8,128)(2,1)S(1)}, bf16[4,128,256]{2,1,0:T(8,128)(2,1)S(1)}, u32[]{:S(2)}, u32[]{:S(2)}) collective-permute-start(bf16[4,128,256]{2,1,0:T(8,128)(2,1)S(1)} %get-tuple-element.29.x), channel_id=1, source_target_pairs={{0,225},{1,224},{2,227},{3,226},{4,229},{5,228},{6,231},{7,230},{8... | collective-permute-start | bytes 786440 | tf_op jit(solution)/shard_map/ppermute | solution.py:50
  31.4 5.0 %collective-permute-start.12 = (bf16[128,256]{1,0:T(8,128)(2,1)S(1)}, bf16[128,256]{1,0:T(8,128)(2,1)S(1)}, u32[]{:S(2)}, u32[]{:S(2)}) collective-permute-start(bf16[128,256]{1,0:T(8,128)(2,1)S(1)} %get-tuple-element.31), channel_id=1, source_target_pairs={{0,30},{1,31},{2,4},{3,5},{4,2},{5,3},{6,8},{7,9},{8,6},{9,7},{10,... | collective-permute-start | bytes 196616 | tf_op jit(solution)/shard_map/ppermute | solution.py:50
  33.8 9.2 %collective-permute-start.11 = (bf16[128,256]{1,0:T(8,128)(2,1)S(1)}, bf16[128,256]{1,0:T(8,128)(2,1)S(1)}, u32[]{:S(2)}, u32[]{:S(2)}) collective-permute-start(bf16[128,256]{1,0:T(8,128)(2,1)S(1)} %get-tuple-element.30), channel_id=1, source_target_pairs={{0,2},{1,3},{2,0},{3,1},{4,6},{5,7},{6,4},{7,5},{8,10},{9,11},{10,... | collective-permute-start | bytes 196616 | tf_op jit(solution)/shard_map/ppermute | solution.py:50
  36.4 6.7 %collective-permute-start.13 = (bf16[128,256]{1,0:T(8,128)(2,1)S(1)}, bf16[128,256]{1,0:T(8,128)(2,1)S(1)}, u32[]{:S(2)}, u32[]{:S(2)}) collective-permute-start(bf16[128,256]{1,0:T(8,128)(2,1)S(1)} %collective-permute-done.12.q), channel_id=1, source_target_pairs={{0,32},{1,33},{2,34},{3,35},{4,36},{5,37},{6,38},{7,39},{8,40},{9,... | collective-permute-start | bytes 196616 | tf_op jit(solution)/shard_map/ppermute | solution.py:50
  36.4 6.7 %collective-permute-start.14 = (bf16[128,256]{1,0:T(8,128)(2,1)S(1)}, bf16[128,256]{1,0:T(8,128)(2,1)S(1)}, u32[]{:S(2)}, u32[]{:S(2)}) collective-permute-start(bf16[128,256]{1,0:T(8,128)(2,1)S(1)} %collective-permute-done.12.q), channel_id=1, source_target_pairs={{0,225},{1,224},{2,227},{3,226},{4,229},{5,228},{6,231},{7,230},{8... | collective-permute-start | bytes 196616 | tf_op jit(solution)/shard_map/ppermute | solution.py:50
  39.7 4.4 %collective-permute-start.10 = (bf16[2,128,256]{2,1,0:T(8,128)(2,1)S(1)}, bf16[2,128,256]{2,1,0:T(8,128)(2,1)S(1)}, u32[]{:S(2)}, u32[]{:S(2)}) collective-permute-start(bf16[2,128,256]{2,1,0:T(8,128)(2,1)S(1)} %edge.3), channel_id=1, source_target_pairs={{0,2},{1,3},{2,0},{3,1},{4,6},{5,7},{6,4},{7,5},{8,10},{9,11},{10,... | collective-permute-start | bytes 393224 | tf_op jit(solution)/shard_map/ppermute | solution.py:50
  44.9 11.3 %collective-permute-start.17 = (bf16[4,128,256]{2,1,0:T(8,128)(2,1)S(1)}, bf16[4,128,256]{2,1,0:T(8,128)(2,1)S(1)}, u32[]{:S(2)}, u32[]{:S(2)}) collective-permute-start(bf16[4,128,256]{2,1,0:T(8,128)(2,1)S(1)} %get-tuple-element.34.s), channel_id=1, source_target_pairs={{0,225},{1,224},{2,227},{3,226},{4,229},{5,228},{6,231},{7,230},{8... | collective-permute-start | bytes 786440 | tf_op jit(solution)/shard_map/ppermute | solution.py:54
  47.6 5.4 %collective-permute-start.15 = (bf16[192,256]{1,0:T(8,128)(2,1)S(1)}, bf16[192,256]{1,0:T(8,128)(2,1)S(1)}, u32[]{:S(2)}, u32[]{:S(2)}) collective-permute-start(bf16[192,256]{1,0:T(8,128)(2,1)S(1)} %get-tuple-element.36), channel_id=1, source_target_pairs={{0,2},{1,3},{2,0},{3,1},{4,6},{5,7},{6,4},{7,5},{8,10},{9,11},{10,... | collective-permute-start | bytes 294920 | tf_op jit(solution)/shard_map/ppermute | solution.py:50
  51.9 4.3 %collective-permute-start.16 = (bf16[192,256]{1,0:T(8,128)(2,1)S(1)}, bf16[192,256]{1,0:T(8,128)(2,1)S(1)}, u32[]{:S(2)}, u32[]{:S(2)}) collective-permute-start(bf16[192,256]{1,0:T(8,128)(2,1)S(1)} %get-tuple-element.37), channel_id=1, source_target_pairs={{0,30},{1,31},{2,4},{3,5},{4,2},{5,3},{6,8},{7,9},{8,6},{9,7},{10,... | collective-permute-start | bytes 294920 | tf_op jit(solution)/shard_map/ppermute | solution.py:50
  51.9 25.8 %collective-permute-start.19 = (bf16[4,128,256]{2,1,0:T(8,128)(2,1)S(1)}, bf16[4,128,256]{2,1,0:T(8,128)(2,1)S(1)}, u32[]{:S(2)}, u32[]{:S(2)}) collective-permute-start(bf16[4,128,256]{2,1,0:T(8,128)(2,1)S(1)} %get-tuple-element.34.s), channel_id=1, source_target_pairs={{0,1},{1,0},{2,3},{3,2},{4,5},{5,4},{6,7},{7,6},{8,9},{9,8},{10,11... | collective-permute-start | bytes 786440 | tf_op jit(solution)/shard_map/ppermute | solution.py:59
  58.0 5.6 %collective-permute-start.18 = (f32[64,1,640]{2,1,0:T(1,128)S(1)}, f32[64,1,640]{2,1,0:T(1,128)S(1)}, u32[]{:S(2)}, u32[]{:S(2)}) collective-permute-start(f32[64,1,640]{2,1,0:T(1,128)S(1)} %get-tuple-element.41), channel_id=1, source_target_pairs={{0,2},{1,3},{2,0},{3,1},{4,6},{5,7},{6,4},{7,5},{8,10},{9,11},{10,... | collective-permute-start | bytes 491528 | tf_op jit(solution)/shard_map/ppermute | solution.py:50
  64.4 24.8 %all-to-all-start = ((f32[64,1,640]{2,1,0:T(1,128)}), f32[64,1,640]{2,1,0:T(1,128)S(1)}, u32[]{:S(2)}, u32[]{:S(2)}) async-start(f32[64,1,640]{2,1,0:T(1,128)} %add.59), calls=%async_computation | async-start | bytes 327680 | tf_op jit(solution)/shard_map/all_to_all | solution.py:74
  110.0 4.6 %collective-permute-start.20 = (f32[128,1,640]{2,1,0:T(1,128)S(1)}, f32[128,1,640]{2,1,0:T(1,128)S(1)}, u32[]{:S(2)}, u32[]{:S(2)}) collective-permute-start(f32[128,1,640]{2,1,0:T(1,128)S(1)} %all_to_all.10.mine), channel_id=1, source_target_pairs={{0,2},{1,3},{2,0},{3,1},{4,6},{5,7},{6,4},{7,5},{8,10},{9,11},{10,... | collective-permute-start | bytes 983048 | tf_op jit(solution)/shard_map/ppermute | solution.py:50

commit v16 on v14

--- a/solution.py
+++ b/solution.py
@@ -125,12 +125,13 @@
     v[:, :, :T] = jnp.where(first_col, own[...], other[...])
     v[:, :, T:] = jnp.where(first_col, other[...], own[...])
     store_edges(m, v, p, q)
-
-
-def edge_kernel(m, a, b, out):
-    at = pl.ds(jnp.where(m[PAR_Y] == 0, 3, 0), 1)
-    out[0:1] = a[at]
-    out[1:2] = b[at]
+    q[T:] = v[0, : q.shape[0] - T]
+
+
+def edge_kernel(m, a, b, a_out, b_out):
+    at = jnp.where(m[PAR_Y] == 0, 3, 0)
+    a_out[...] = a[at]
+    b_out[...] = b[at]
 
 
 def low_high(m, p, q):
@@ -150,30 +151,28 @@
     return dot(jnp.where(high, top, bottom), jnp.concatenate(tiles, axis=0)), high
 
 
-def core_kernel(m, o, x, p, q, a, b, a_corner, b_corner, acc, ext):
-    ext[0], ext[5] = low_high(m, p[...], q[...])
+def core_kernel(m, o, x, p, q, a, b, acc, ext):
+    ext[0], ext[5] = low_high(m, p[...], q[:T])
     ext[1:5] = x[...]
     for tile in range(4):
         total = product(o, tile, (0,), range(tile, tile + 3), [ext[tile : tile + 3]])
         at = [place for place in range(tile, tile + 3) if 1 <= place <= 4]
         acc[tile] = total + product(o, tile, (1, 2), at, [y[at[0] - 1 : at[-1]] for y in (a, b)])
-    part, high = outer_product(m, o, False, [a_corner[...], b_corner[...]])
-    acc[pl.ds(jnp.where(high, 3, 0), 1)] += part[None]
-
-
-def rim_kernel(m, o, edge, acc, *rest, last):
+
+
+def rim_kernel(m, o, a_edge, b_edge, a_corner, b_corner, acc, *rest, last):
     if last:
         before, h_p, h_q, out, p, q = rest
     else:
         out, p, q = rest
-    part, high = outer_product(m, o, True, [edge[0], edge[1]])
-    nothing = jnp.zeros_like(part)
+    at_p, high = outer_product(m, o, True, [a_edge[...], b_edge[...]])
+    at_q, _ = outer_product(m, o, False, [a_corner[:T], b_corner[:T]])
     for tile in range(4):
         total = acc[tile]
         if tile == 0:
-            total += jnp.where(high, nothing, part)
+            total += jnp.where(high, at_q, at_p)
         if tile == 3:
-            total += jnp.where(high, part, nothing)
+            total += jnp.where(high, at_p, at_q)
         if last:
             out[tile] = (total - before[tile].astype(F32)).astype(BF)
         else:
@@ -183,6 +182,8 @@
         for to, block in ((p, h_p), (q, h_q)):
             to[T:, :T] = block[: T // 2]
             to[T:, T:] = block[T // 2 :]
+    else:
+        q[T:] = out[0, : q.shape[0] - T]
 
 
 def corr_kernel(m, o, s, corr, turned, acc):
@@ -330,9 +331,9 @@
     return pl.BlockSpec(shape, lambda i, m, n=len(shape): (0,) * n)
 
 
-def call(kernel, m, arrays, outs, name, flops=0, specs=None, scratch=()):
+def call(kernel, m, arrays, outs, name, flops=0, specs=None, scratch=(), free=False):
     arrays = list(arrays)
-    moved = sum(a.size * a.dtype.itemsize for a in [*arrays, *outs])
+    moved = 0 if free else sum(a.size * a.dtype.itemsize for a in [*arrays, *outs])
     return pl.pallas_call(
         kernel,
         out_shape=outs,
@@ -385,20 +386,20 @@
     tile = shaped((T, 2 * T), BF)
     ext = pltpu.VMEM((6, T, 2 * T), BF)
     other, o = lax.optimization_barrier((other, o))
-    outs = [shaped(block, BF), tile, tile]
+    outs = [shaped(block, BF), tile, shaped((T + 16, 2 * T), BF)]
     v, p, q = call(join_kernel, m, [own, other], outs, "join")
 
     def apply_ham(x, p, q, more, outs):
         p, q = swap(sizes, p, 0, 1), swap(sizes, q, 0, 2)
         a, b = swap(sizes, x, 1, 0), swap(sizes, x, 2, 0)
         a_corner, b_corner = swap(sizes, q, 1, 0), swap(sizes, q, 2, 0)
-        (edge,) = call(edge_kernel, m, [a, b], [shaped((2, T, 2 * T), BF)], "edge")
-        edge = swap(sizes, edge, 0, 1)
+        a_edge, b_edge = call(edge_kernel, m, [a, b], [tile, tile], "edge", free=True)
+        a_edge, b_edge = swap(sizes, a_edge, 0, 1), swap(sizes, b_edge, 0, 1)
         (acc,) = call(
-            core_kernel, m, [o, x, p, q, a, b, a_corner, b_corner], [shaped(block, F32)], "core", 150, scratch=[ext]
+            core_kernel, m, [o, x, p, q, a, b], [shaped(block, F32)], "core", free=True, scratch=[ext]
         )
         kernel = functools.partial(rim_kernel, last=len(more) > 0)
-        return call(kernel, m, [o, edge, acc, *more], outs, "rim", 2)
+        return call(kernel, m, [o, a_edge, b_edge, a_corner, b_corner, acc, *more], outs, "rim", 2)
 
     first, p, q = apply_ham(v, p, q, [], outs)
     longer = shaped((3 * T // 2, 2 * T), BF)

time: 190 us -> 188 us (0.989)
  starting transfers between devices: 56.3 us -> 50.9 us
  waiting for transfers between devices: 17.6 us -> 21.3 us
    ppermute x18 -> x20, starting transfers between devices: 37.7 us -> 32.2 us  [swap(): return lax.ppermute(block, AXES, perm)]
    ppermute x18 -> x20, waiting for transfers between devices: 6.56 us -> 10.3 us  [swap(): return lax.ppermute(block, AXES, perm)]
  transfers between devices with their start and end apart: 22 -> 24, of which waited for: 5 -> 6; matrix products, arithmetic and copies ran while one was open for 2% -> 2% of each run, Pallas kernels for 3% -> 3%
where the time goes in v16:
time: 188 us
  Pallas kernels  88.4 us (47%)
  starting transfers between devices  50.9 us (27%)
  waiting for transfers between devices  21.3 us (11%)
  blocking collectives  20.3 us (11%)
  local copies, waits for them, and re-layouts  3.12 us (2%)
  other arithmetic  2.86 us (2%)
    pallas_call x12, Pallas kernels, call(): pl.pallas_call(kernel, out_shape=outs, grid_spec=pltpu.PrefetchScalarGrid...  88.4 us
    ppermute x20, starting transfers between devices, swap(): return lax.ppermute(block, AXES, perm)  32.2 us
    all_to_all x1, blocking collectives, exchange(): lax.all_to_all(pieces, AXES, 0, 0, axis_index_groups=groups, tiled=True)  20.3 us
    all_to_all x1, starting transfers between devices, exchange(): lax.all_to_all(pieces, AXES, 0, 0, axis_index_groups=groups, tiled=True)  12.2 us
    all_to_all x1, waiting for transfers between devices, exchange(): lax.all_to_all(pieces, AXES, 0, 0, axis_index_groups=groups, tiled=True)  11 us
    ppermute x20, waiting for transfers between devices, swap(): return lax.ppermute(block, AXES, perm)  10.3 us
    ppermute x2, starting transfers between devices, swap_col(): return lax.ppermute(block, AXES, perm)  3.82 us
  transfers between devices with their start and end apart: 24, of which 6 were waited for; matrix products, arithmetic and copies ran while one was open for 2% of the time, Pallas kernels for 3%

profile of v16, /device:TPU:1, one launch (start us, length us, event | category | flops | bytes accessed | tf_op | source)
XLA Modules:
  0.0 187.6 jit_solution(12405328630458263921)
XLA Ops:
  0.6 1.0 dynamic-slice_bitcast_fusion
  1.6 3.7 %collective-permute-start = (bf16[4,128,128]{2,1,0:T(8,128)(2,1)S(1)}, bf16[4,128,128]{2,1,0:T(8,128)(2,1)S(1)}, u32[]{:S(2)}, u32[]{:S(2)}) collective-permute-start(bf16[4,128,128]{2,1,0:T(8,128)(2,1)S(1)} %get-tuple-element.53), channel_id=1, source_target_pairs={{0,1},{1,0},{2,3},{3,2},{4,5},{5,4},{6,7},{7,6},{8,9},{9,8},{10,11... | collective-permute-start | bytes 393224 | tf_op jit(solution)/shard_map/ppermute | solution.py:59
  6.2 1.0 select_reduce_fusion
  7.5 1.7 copy-done
  9.2 0.9 order.1
  11.1 3.5 %collective-permute-start.2 = (bf16[4,128,256]{2,1,0:T(8,128)(2,1)S(1)}, bf16[4,128,256]{2,1,0:T(8,128)(2,1)S(1)}, u32[]{:S(2)}, u32[]{:S(2)}) collective-permute-start(bf16[4,128,256]{2,1,0:T(8,128)(2,1)S(1)} %get-tuple-element.30.x.rest_0_), channel_id=1, source_target_pairs={{0,225},{1,224},{2,227},{3,226},{4,229},{5,228},{6,231},{7,230},{8... | collective-permute-start | bytes 786440 | tf_op jit(solution)/shard_map/ppermute | solution.py:50
  14.6 3.6 %collective-permute-start.5 = (bf16[144,256]{1,0:T(8,128)(2,1)S(1)}, bf16[144,256]{1,0:T(8,128)(2,1)S(1)}, u32[]{:S(2)}, u32[]{:S(2)}) collective-permute-start(bf16[144,256]{1,0:T(8,128)(2,1)S(1)} %get-tuple-element.33), channel_id=1, source_target_pairs={{0,30},{1,31},{2,4},{3,5},{4,2},{5,3},{6,8},{7,9},{8,6},{9,7},{10,... | collective-permute-start | bytes 221192 | tf_op jit(solution)/shard_map/ppermute | solution.py:50
  18.2 2.3 %collective-permute-done.5.q = bf16[144,256]{1,0:T(8,128)(2,1)S(1)} collective-permute-done((bf16[144,256]{1,0:T(8,128)(2,1)S(1)}, bf16[144,256]{1,0:T(8,128)(2,1)S(1)}, u32[]{:S(2)}, u32[]{:S(2)}) %collective-permute-start.5) | collective-permute-done | bytes 73760 | tf_op jit(solution)/shard_map/ppermute | solution.py:50
  20.6 1.7 collective-permute-start.7
  22.3 3.2 %collective-permute-start.8 = (bf16[128,256]{1,0:T(8,128)(2,1)S(1)}, bf16[128,256]{1,0:T(8,128)(2,1)S(1)}, u32[]{:S(2)}, u32[]{:S(2)}) collective-permute-start(bf16[128,256]{1,0:T(8,128)(2,1)S(1)} %get-tuple-element.34), channel_id=1, source_target_pairs={{0,2},{1,3},{2,0},{3,1},{4,6},{5,7},{6,4},{7,5},{8,10},{9,11},{10,... | collective-permute-start | bytes 196616 | tf_op jit(solution)/shard_map/ppermute | solution.py:50
  26.7 1.0 core.2.acc
  28.6 2.3 %collective-permute-start.10 = (bf16[4,128,256]{2,1,0:T(8,128)(2,1)S(1)}, bf16[4,128,256]{2,1,0:T(8,128)(2,1)S(1)}, u32[]{:S(2)}, u32[]{:S(2)}) collective-permute-start(bf16[4,128,256]{2,1,0:T(8,128)(2,1)S(1)} %get-tuple-element.35.x), channel_id=1, source_target_pairs={{0,225},{1,224},{2,227},{3,226},{4,229},{5,228},{6,231},{7,230},{8... | collective-permute-start | bytes 786440 | tf_op jit(solution)/shard_map/ppermute | solution.py:50
  30.9 2.2 %collective-permute-start.13 = (bf16[144,256]{1,0:T(8,128)(2,1)S(1)}, bf16[144,256]{1,0:T(8,128)(2,1)S(1)}, u32[]{:S(2)}, u32[]{:S(2)}) collective-permute-start(bf16[144,256]{1,0:T(8,128)(2,1)S(1)} %get-tuple-element.38), channel_id=1, source_target_pairs={{0,30},{1,31},{2,4},{3,5},{4,2},{5,3},{6,8},{7,9},{8,6},{9,7},{10,... | collective-permute-start | bytes 221192 | tf_op jit(solution)/shard_map/ppermute | solution.py:50
  33.1 2.3 %collective-permute-done.13.q = bf16[144,256]{1,0:T(8,128)(2,1)S(1)} collective-permute-done((bf16[144,256]{1,0:T(8,128)(2,1)S(1)}, bf16[144,256]{1,0:T(8,128)(2,1)S(1)}, u32[]{:S(2)}, u32[]{:S(2)}) %collective-permute-start.13) | collective-permute-done | bytes 73760 | tf_op jit(solution)/shard_map/ppermute | solution.py:50
  35.4 3.1 %collective-permute-start.15 = (bf16[144,256]{1,0:T(8,128)(2,1)S(1)}, bf16[144,256]{1,0:T(8,128)(2,1)S(1)}, u32[]{:S(2)}, u32[]{:S(2)}) collective-permute-start(bf16[144,256]{1,0:T(8,128)(2,1)S(1)} %collective-permute-done.13.q), channel_id=1, source_target_pairs={{0,225},{1,224},{2,227},{3,226},{4,229},{5,228},{6,231},{7,230},{8... | collective-permute-start | bytes 221192 | tf_op jit(solution)/shard_map/ppermute | solution.py:50
  38.5 3.1 %collective-permute-start.16 = (bf16[128,256]{1,0:T(8,128)(2,1)S(1)}, bf16[128,256]{1,0:T(8,128)(2,1)S(1)}, u32[]{:S(2)}, u32[]{:S(2)}) collective-permute-start(bf16[128,256]{1,0:T(8,128)(2,1)S(1)} %get-tuple-element.39), channel_id=1, source_target_pairs={{0,2},{1,3},{2,0},{3,1},{4,6},{5,7},{6,4},{7,5},{8,10},{9,11},{10,... | collective-permute-start | bytes 196616 | tf_op jit(solution)/shard_map/ppermute | solution.py:50
  42.8 1.0 core.3.acc
  43.8 0.8 rim.3
  44.6 2.7 %collective-permute-start.19 = (bf16[4,128,256]{2,1,0:T(8,128)(2,1)S(1)}, bf16[4,128,256]{2,1,0:T(8,128)(2,1)S(1)}, u32[]{:S(2)}, u32[]{:S(2)}) collective-permute-start(bf16[4,128,256]{2,1,0:T(8,128)(2,1)S(1)} %get-tuple-element.42.s), channel_id=1, source_target_pairs={{0,225},{1,224},{2,227},{3,226},{4,229},{5,228},{6,231},{7,230},{8... | collective-permute-start | bytes 786440 | tf_op jit(solution)/shard_map/ppermute | solution.py:54
  47.3 2.9 %collective-permute-start.17 = (bf16[192,256]{1,0:T(8,128)(2,1)S(1)}, bf16[192,256]{1,0:T(8,128)(2,1)S(1)}, u32[]{:S(2)}, u32[]{:S(2)}) collective-permute-start(bf16[192,256]{1,0:T(8,128)(2,1)S(1)} %get-tuple-element.44), channel_id=1, source_target_pairs={{0,2},{1,3},{2,0},{3,1},{4,6},{5,7},{6,4},{7,5},{8,10},{9,11},{10,... | collective-permute-start | bytes 294920 | tf_op jit(solution)/shard_map/ppermute | solution.py:50
  50.1 0.9 corr.1
  51.1 3.4 %collective-permute-done.18.q = bf16[192,256]{1,0:T(8,128)(2,1)S(1)} collective-permute-done((bf16[192,256]{1,0:T(8,128)(2,1)S(1)}, bf16[192,256]{1,0:T(8,128)(2,1)S(1)}, u32[]{:S(2)}, u32[]{:S(2)}) %collective-permute-start.18) | collective-permute-done | bytes 98336 | tf_op jit(solution)/shard_map/ppermute | solution.py:50
  54.5 1.7 gram.1
  56.2 1.0 collective-permute-start.20
  57.4 0.9 collective-permute-done.20
  58.3 0.8 add.59
  59.1 12.2 %all-to-all-start = ((f32[64,1,640]{2,1,0:T(1,128)}), f32[64,1,640]{2,1,0:T(1,128)S(1)}, u32[]{:S(2)}, u32[]{:S(2)}) async-start(f32[64,1,640]{2,1,0:T(1,128)} %add.59), calls=%async_computation | async-start | bytes 327680 | tf_op jit(solution)/shard_map/all_to_all | solution.py:74
  71.9 11.0 %all-to-all-done = f32[64,1,640]{2,1,0:T(1,128)S(1)} async-done(((f32[64,1,640]{2,1,0:T(1,128)}), f32[64,1,640]{2,1,0:T(1,128)S(1)}, u32[]{:S(2)}, u32[]{:S(2)}) %all-to-all-start) | async-done | bytes 163872 | tf_op jit(solution)/shard_map/all_to_all | solution.py:74
  83.2 20.3 %all_to_all.10.mine = f32[128,1,640]{2,1,0:T(1,128)S(1)} all-to-all(f32[128,1,640]{2,1,0:T(1,128)S(1)} %broadcast_in_dim.20), channel_id=1, replica_groups={{0,4,8,12,16,20,24,28,32,36,40,44,48,52,56,60,65,69,73,77,81,85,89,93,9..., dimensions={0} | all-to-all | bytes 655360 | tf_op jit(solution)/shard_map/all_to_all | solution.py:74
  103.4 3.9 %collective-permute-start.22 = (f32[128,1,640]{2,1,0:T(1,128)S(1)}, f32[128,1,640]{2,1,0:T(1,128)S(1)}, u32[]{:S(2)}, u32[]{:S(2)}) collective-permute-start(f32[128,1,640]{2,1,0:T(1,128)S(1)} %all_to_all.10.mine), channel_id=1, source_target_pairs={{0,2},{1,3},{2,0},{3,1},{4,6},{5,7},{6,4},{7,5},{8,10},{9,11},{10,... | collective-permute-start | bytes 983048 | tf_op jit(solution)/shard_map/ppermute | solution.py:50
  107.4 1.3 collective-permute-done.22.theirs
  108.6 79.0 %final.1 = (bf16[2,1,4,128,128]{4,3,2,1,0:T(8,128)(2,1)}, f32[2,256,128]{2,1,0:T(8,128)}) custom-call(s32[40]{0:T(128)S(1)} %concatenate.7.m, f32[128,1,640]{2,1,0:T(1,128)S(1)} %all_to_all.10.mine, f32[128,1,640]{2,1,0:T(1,128)S(1)} %collective-permute-done.22.theirs, bf16[2,4,128,256]{3,2,1,0:T(8,128)(2,1)S(1)} %stack.29.both), custom_call_target="tpu_custom_call" | custom-call | flops 1677721600 | bytes 1703936 | tf_op jit(solution)/shard_map/final/pallas_call | solution.py:337
  (45 shorter events, 6.5 us)
Async XLA Ops:
  1.6 8.4 %collective-permute-start = (bf16[4,128,128]{2,1,0:T(8,128)(2,1)S(1)}, bf16[4,128,128]{2,1,0:T(8,128)(2,1)S(1)}, u32[]{:S(2)}, u32[]{:S(2)}) collective-permute-start(bf16[4,128,128]{2,1,0:T(8,128)(2,1)S(1)} %get-tuple-element.53), channel_id=1, source_target_pairs={{0,1},{1,0},{2,3},{3,2},{4,5},{5,4},{6,7},{7,6},{8,9},{9,8},{10,11... | collective-permute-start | bytes 393224 | tf_op jit(solution)/shard_map/ppermute | solution.py:59
  7.5 1.7 copy-start
  10.7 14.8 %collective-permute-start.1 = (bf16[4,128,256]{2,1,0:T(8,128)(2,1)S(1)}, bf16[4,128,256]{2,1,0:T(8,128)(2,1)S(1)}, u32[]{:S(2)}, u32[]{:S(2)}) collective-permute-start(bf16[4,128,256]{2,1,0:T(8,128)(2,1)S(1)} %get-tuple-element.30.x.rest_0_), channel_id=1, source_target_pairs={{0,32},{1,33},{2,34},{3,35},{4,36},{5,37},{6,38},{7,39},{8,40},{9,... | collective-permute-start | bytes 786440 | tf_op jit(solution)/shard_map/ppermute | solution.py:50
  11.1 14.4 %collective-permute-start.2 = (bf16[4,128,256]{2,1,0:T(8,128)(2,1)S(1)}, bf16[4,128,256]{2,1,0:T(8,128)(2,1)S(1)}, u32[]{:S(2)}, u32[]{:S(2)}) collective-permute-start(bf16[4,128,256]{2,1,0:T(8,128)(2,1)S(1)} %get-tuple-element.30.x.rest_0_), channel_id=1, source_target_pairs={{0,225},{1,224},{2,227},{3,226},{4,229},{5,228},{6,231},{7,230},{8... | collective-permute-start | bytes 786440 | tf_op jit(solution)/shard_map/ppermute | solution.py:50
  14.6 6.0 %collective-permute-start.5 = (bf16[144,256]{1,0:T(8,128)(2,1)S(1)}, bf16[144,256]{1,0:T(8,128)(2,1)S(1)}, u32[]{:S(2)}, u32[]{:S(2)}) collective-permute-start(bf16[144,256]{1,0:T(8,128)(2,1)S(1)} %get-tuple-element.33), channel_id=1, source_target_pairs={{0,30},{1,31},{2,4},{3,5},{4,2},{5,3},{6,8},{7,9},{8,6},{9,7},{10,... | collective-permute-start | bytes 221192 | tf_op jit(solution)/shard_map/ppermute | solution.py:50
  20.6 7.1 %collective-permute-start.6 = (bf16[144,256]{1,0:T(8,128)(2,1)S(1)}, bf16[144,256]{1,0:T(8,128)(2,1)S(1)}, u32[]{:S(2)}, u32[]{:S(2)}) collective-permute-start(bf16[144,256]{1,0:T(8,128)(2,1)S(1)} %collective-permute-done.5.q), channel_id=1, source_target_pairs={{0,32},{1,33},{2,34},{3,35},{4,36},{5,37},{6,38},{7,39},{8,40},{9,... | collective-permute-start | bytes 221192 | tf_op jit(solution)/shard_map/ppermute | solution.py:50
  20.6 7.1 %collective-permute-start.7 = (bf16[144,256]{1,0:T(8,128)(2,1)S(1)}, bf16[144,256]{1,0:T(8,128)(2,1)S(1)}, u32[]{:S(2)}, u32[]{:S(2)}) collective-permute-start(bf16[144,256]{1,0:T(8,128)(2,1)S(1)} %collective-permute-done.5.q), channel_id=1, source_target_pairs={{0,225},{1,224},{2,227},{3,226},{4,229},{5,228},{6,231},{7,230},{8... | collective-permute-start | bytes 221192 | tf_op jit(solution)/shard_map/ppermute | solution.py:50
  22.3 4.4 %collective-permute-start.8 = (bf16[128,256]{1,0:T(8,128)(2,1)S(1)}, bf16[128,256]{1,0:T(8,128)(2,1)S(1)}, u32[]{:S(2)}, u32[]{:S(2)}) collective-permute-start(bf16[128,256]{1,0:T(8,128)(2,1)S(1)} %get-tuple-element.34), channel_id=1, source_target_pairs={{0,2},{1,3},{2,0},{3,1},{4,6},{5,7},{6,4},{7,5},{8,10},{9,11},{10,... | collective-permute-start | bytes 196616 | tf_op jit(solution)/shard_map/ppermute | solution.py:50
  26.1 1.6 collective-permute-start.3
  26.2 1.6 collective-permute-start.4
  28.5 13.1 %collective-permute-start.9 = (bf16[4,128,256]{2,1,0:T(8,128)(2,1)S(1)}, bf16[4,128,256]{2,1,0:T(8,128)(2,1)S(1)}, u32[]{:S(2)}, u32[]{:S(2)}) collective-permute-start(bf16[4,128,256]{2,1,0:T(8,128)(2,1)S(1)} %get-tuple-element.35.x), channel_id=1, source_target_pairs={{0,32},{1,33},{2,34},{3,35},{4,36},{5,37},{6,38},{7,39},{8,40},{9,... | collective-permute-start | bytes 786440 | tf_op jit(solution)/shard_map/ppermute | solution.py:50
  28.6 13.0 %collective-permute-start.10 = (bf16[4,128,256]{2,1,0:T(8,128)(2,1)S(1)}, bf16[4,128,256]{2,1,0:T(8,128)(2,1)S(1)}, u32[]{:S(2)}, u32[]{:S(2)}) collective-permute-start(bf16[4,128,256]{2,1,0:T(8,128)(2,1)S(1)} %get-tuple-element.35.x), channel_id=1, source_target_pairs={{0,225},{1,224},{2,227},{3,226},{4,229},{5,228},{6,231},{7,230},{8... | collective-permute-start | bytes 786440 | tf_op jit(solution)/shard_map/ppermute | solution.py:50
  30.9 4.5 %collective-permute-start.13 = (bf16[144,256]{1,0:T(8,128)(2,1)S(1)}, bf16[144,256]{1,0:T(8,128)(2,1)S(1)}, u32[]{:S(2)}, u32[]{:S(2)}) collective-permute-start(bf16[144,256]{1,0:T(8,128)(2,1)S(1)} %get-tuple-element.38), channel_id=1, source_target_pairs={{0,30},{1,31},{2,4},{3,5},{4,2},{5,3},{6,8},{7,9},{8,6},{9,7},{10,... | collective-permute-start | bytes 221192 | tf_op jit(solution)/shard_map/ppermute | solution.py:50
  35.4 8.4 %collective-permute-start.14 = (bf16[144,256]{1,0:T(8,128)(2,1)S(1)}, bf16[144,256]{1,0:T(8,128)(2,1)S(1)}, u32[]{:S(2)}, u32[]{:S(2)}) collective-permute-start(bf16[144,256]{1,0:T(8,128)(2,1)S(1)} %collective-permute-done.13.q), channel_id=1, source_target_pairs={{0,32},{1,33},{2,34},{3,35},{4,36},{5,37},{6,38},{7,39},{8,40},{9,... | collective-permute-start | bytes 221192 | tf_op jit(solution)/shard_map/ppermute | solution.py:50
  35.4 8.4 %collective-permute-start.15 = (bf16[144,256]{1,0:T(8,128)(2,1)S(1)}, bf16[144,256]{1,0:T(8,128)(2,1)S(1)}, u32[]{:S(2)}, u32[]{:S(2)}) collective-permute-start(bf16[144,256]{1,0:T(8,128)(2,1)S(1)} %collective-permute-done.13.q), channel_id=1, source_target_pairs={{0,225},{1,224},{2,227},{3,226},{4,229},{5,228},{6,231},{7,230},{8... | collective-permute-start | bytes 221192 | tf_op jit(solution)/shard_map/ppermute | solution.py:50
  38.5 4.3 %collective-permute-start.16 = (bf16[128,256]{1,0:T(8,128)(2,1)S(1)}, bf16[128,256]{1,0:T(8,128)(2,1)S(1)}, u32[]{:S(2)}, u32[]{:S(2)}) collective-permute-start(bf16[128,256]{1,0:T(8,128)(2,1)S(1)} %get-tuple-element.39), channel_id=1, source_target_pairs={{0,2},{1,3},{2,0},{3,1},{4,6},{5,7},{6,4},{7,5},{8,10},{9,11},{10,... | collective-permute-start | bytes 196616 | tf_op jit(solution)/shard_map/ppermute | solution.py:50
  42.2 1.7 collective-permute-start.11
  42.3 1.6 collective-permute-start.12
  44.6 9.9 %collective-permute-start.19 = (bf16[4,128,256]{2,1,0:T(8,128)(2,1)S(1)}, bf16[4,128,256]{2,1,0:T(8,128)(2,1)S(1)}, u32[]{:S(2)}, u32[]{:S(2)}) collective-permute-start(bf16[4,128,256]{2,1,0:T(8,128)(2,1)S(1)} %get-tuple-element.42.s), channel_id=1, source_target_pairs={{0,225},{1,224},{2,227},{3,226},{4,229},{5,228},{6,231},{7,230},{8... | collective-permute-start | bytes 786440 | tf_op jit(solution)/shard_map/ppermute | solution.py:54
  47.3 3.8 %collective-permute-start.17 = (bf16[192,256]{1,0:T(8,128)(2,1)S(1)}, bf16[192,256]{1,0:T(8,128)(2,1)S(1)}, u32[]{:S(2)}, u32[]{:S(2)}) collective-permute-start(bf16[192,256]{1,0:T(8,128)(2,1)S(1)} %get-tuple-element.44), channel_id=1, source_target_pairs={{0,2},{1,3},{2,0},{3,1},{4,6},{5,7},{6,4},{7,5},{8,10},{9,11},{10,... | collective-permute-start | bytes 294920 | tf_op jit(solution)/shard_map/ppermute | solution.py:50
  50.1 4.3 %collective-permute-start.18 = (bf16[192,256]{1,0:T(8,128)(2,1)S(1)}, bf16[192,256]{1,0:T(8,128)(2,1)S(1)}, u32[]{:S(2)}, u32[]{:S(2)}) collective-permute-start(bf16[192,256]{1,0:T(8,128)(2,1)S(1)} %get-tuple-element.45), channel_id=1, source_target_pairs={{0,30},{1,31},{2,4},{3,5},{4,2},{5,3},{6,8},{7,9},{8,6},{9,7},{10,... | collective-permute-start | bytes 294920 | tf_op jit(solution)/shard_map/ppermute | solution.py:50
  56.2 2.0 %collective-permute-start.20 = (f32[64,1,640]{2,1,0:T(1,128)S(1)}, f32[64,1,640]{2,1,0:T(1,128)S(1)}, u32[]{:S(2)}, u32[]{:S(2)}) collective-permute-start(f32[64,1,640]{2,1,0:T(1,128)S(1)} %get-tuple-element.49), channel_id=1, source_target_pairs={{0,2},{1,3},{2,0},{3,1},{4,6},{5,7},{6,4},{7,5},{8,10},{9,11},{10,... | collective-permute-start | bytes 491528 | tf_op jit(solution)/shard_map/ppermute | solution.py:50
  57.2 14.0 %collective-permute-start.21 = (bf16[4,128,256]{2,1,0:T(8,128)(2,1)S(1)}, bf16[4,128,256]{2,1,0:T(8,128)(2,1)S(1)}, u32[]{:S(2)}, u32[]{:S(2)}) collective-permute-start(bf16[4,128,256]{2,1,0:T(8,128)(2,1)S(1)} %get-tuple-element.42.s), channel_id=1, source_target_pairs={{0,1},{1,0},{2,3},{3,2},{4,5},{5,4},{6,7},{7,6},{8,9},{9,8},{10,11... | collective-permute-start | bytes 786440 | tf_op jit(solution)/shard_map/ppermute | solution.py:59
  59.1 23.8 %all-to-all-start = ((f32[64,1,640]{2,1,0:T(1,128)}), f32[64,1,640]{2,1,0:T(1,128)S(1)}, u32[]{:S(2)}, u32[]{:S(2)}) async-start(f32[64,1,640]{2,1,0:T(1,128)} %add.59), calls=%async_computation | async-start | bytes 327680 | tf_op jit(solution)/shard_map/all_to_all | solution.py:74
  103.4 5.2 %collective-permute-start.22 = (f32[128,1,640]{2,1,0:T(1,128)S(1)}, f32[128,1,640]{2,1,0:T(1,128)S(1)}, u32[]{:S(2)}, u32[]{:S(2)}) collective-permute-start(f32[128,1,640]{2,1,0:T(1,128)S(1)} %all_to_all.10.mine), channel_id=1, source_target_pairs={{0,2},{1,3},{2,0},{3,1},{4,6},{5,7},{6,4},{7,5},{8,10},{9,11},{10,... | collective-permute-start | bytes 983048 | tf_op jit(solution)/shard_map/ppermute | solution.py:50

commit v17 on v16

--- a/solution.py
+++ b/solution.py
@@ -125,7 +125,11 @@
     v[:, :, :T] = jnp.where(first_col, own[...], other[...])
     v[:, :, T:] = jnp.where(first_col, other[...], own[...])
     store_edges(m, v, p, q)
-    q[T:] = v[0, : q.shape[0] - T]
+
+
+def corner_kernel(m, q, out):
+    out[:T] = q[...]
+    out[T:] = q[: out.shape[0] - T]
 
 
 def edge_kernel(m, a, b, a_out, b_out):
@@ -152,7 +156,7 @@
 
 
 def core_kernel(m, o, x, p, q, a, b, acc, ext):
-    ext[0], ext[5] = low_high(m, p[...], q[:T])
+    ext[0], ext[5] = low_high(m, p[...], q[...])
     ext[1:5] = x[...]
     for tile in range(4):
         total = product(o, tile, (0,), range(tile, tile + 3), [ext[tile : tile + 3]])
@@ -182,8 +186,6 @@
         for to, block in ((p, h_p), (q, h_q)):
             to[T:, :T] = block[: T // 2]
             to[T:, T:] = block[T // 2 :]
-    else:
-        q[T:] = out[0, : q.shape[0] - T]
 
 
 def corr_kernel(m, o, s, corr, turned, acc):
@@ -386,13 +388,14 @@
     tile = shaped((T, 2 * T), BF)
     ext = pltpu.VMEM((6, T, 2 * T), BF)
     other, o = lax.optimization_barrier((other, o))
-    outs = [shaped(block, BF), tile, shaped((T + 16, 2 * T), BF)]
+    outs = [shaped(block, BF), tile, tile]
     v, p, q = call(join_kernel, m, [own, other], outs, "join")
 
     def apply_ham(x, p, q, more, outs):
         p, q = swap(sizes, p, 0, 1), swap(sizes, q, 0, 2)
         a, b = swap(sizes, x, 1, 0), swap(sizes, x, 2, 0)
-        a_corner, b_corner = swap(sizes, q, 1, 0), swap(sizes, q, 2, 0)
+        (corner,) = call(corner_kernel, m, [q], [shaped((T + 16, 2 * T), BF)], "corner", 300)
+        a_corner, b_corner = swap(sizes, corner, 1, 0), swap(sizes, corner, 2, 0)
         a_edge, b_edge = call(edge_kernel, m, [a, b], [tile, tile], "edge", free=True)
         a_edge, b_edge = swap(sizes, a_edge, 0, 1), swap(sizes, b_edge, 0, 1)
         (acc,) = call(

time: 188 us -> 189 us (level)
  waiting for transfers between devices: 21.3 us -> 18 us
  starting transfers between devices: 50.9 us -> 54.1 us
    ppermute x20, waiting for transfers between devices: 10.3 us -> 6.56 us  [swap(): return lax.ppermute(block, AXES, perm)]
    ppermute x20, starting transfers between devices: 32.2 us -> 34.6 us  [swap(): return lax.ppermute(block, AXES, perm)]
    pallas_call x12 -> x14, Pallas kernels: 88.4 us -> 89.5 us  [call(): pl.pallas_call(kernel, out_shape=outs, grid_spec=pltpu.PrefetchScalarGrid...]
  transfers between devices with their start and end apart: 24 -> 24, of which waited for: 6 -> 9; matrix products, arithmetic and copies ran while one was open for 2% -> 2% of each run, Pallas kernels for 3% -> 3%
where the time goes in v17:
time: 189 us
  Pallas kernels  89.5 us (47%)
  starting transfers between devices  54.1 us (29%)
  blocking collectives  20.3 us (11%)
  waiting for transfers between devices  18 us (10%)
  local copies, waits for them, and re-layouts  3.12 us (2%)
  other arithmetic  2.86 us (2%)
    pallas_call x14, Pallas kernels, call(): pl.pallas_call(kernel, out_shape=outs, grid_spec=pltpu.PrefetchScalarGrid...  89.5 us
    ppermute x20, starting transfers between devices, swap(): return lax.ppermute(block, AXES, perm)  34.6 us
    all_to_all x1, blocking collectives, exchange(): lax.all_to_all(pieces, AXES, 0, 0, axis_index_groups=groups, tiled=True)  20.3 us
    all_to_all x1, starting transfers between devices, exchange(): lax.all_to_all(pieces, AXES, 0, 0, axis_index_groups=groups, tiled=True)  12.5 us
    all_to_all x1, waiting for transfers between devices, exchange(): lax.all_to_all(pieces, AXES, 0, 0, axis_index_groups=groups, tiled=True)  11 us
    ppermute x20, waiting for transfers between devices, swap(): return lax.ppermute(block, AXES, perm)  6.56 us
  transfers between devices with their start and end apart: 24, of which 9 were waited for; matrix products, arithmetic and copies ran while one was open for 2% of the time, Pallas kernels for 3%

profile of v17, /device:TPU:1, one launch (start us, length us, event | category | flops | bytes accessed | tf_op | source)
XLA Modules:
  0.0 188.7 jit_solution(13671831584112568660)
XLA Ops:
  0.6 1.0 dynamic-slice_bitcast_fusion
  1.6 3.7 %collective-permute-start = (bf16[4,128,128]{2,1,0:T(8,128)(2,1)S(1)}, bf16[4,128,128]{2,1,0:T(8,128)(2,1)S(1)}, u32[]{:S(2)}, u32[]{:S(2)}) collective-permute-start(bf16[4,128,128]{2,1,0:T(8,128)(2,1)S(1)} %get-tuple-element.53), channel_id=1, source_target_pairs={{0,1},{1,0},{2,3},{3,2},{4,5},{5,4},{6,7},{7,6},{8,9},{9,8},{10,11... | collective-permute-start | bytes 393224 | tf_op jit(solution)/shard_map/ppermute | solution.py:59
  6.2 1.0 select_reduce_fusion
  7.5 1.7 copy-done
  9.2 0.9 order.1
  10.7 2.6 %collective-permute-start.5 = (bf16[128,256]{1,0:T(8,128)(2,1)S(1)}, bf16[128,256]{1,0:T(8,128)(2,1)S(1)}, u32[]{:S(2)}, u32[]{:S(2)}) collective-permute-start(bf16[128,256]{1,0:T(8,128)(2,1)S(1)} %get-tuple-element.33), channel_id=1, source_target_pairs={{0,30},{1,31},{2,4},{3,5},{4,2},{5,3},{6,8},{7,9},{8,6},{9,7},{10,... | collective-permute-start | bytes 196616 | tf_op jit(solution)/shard_map/ppermute | solution.py:50
  13.5 4.1 %collective-permute-start.2 = (bf16[4,128,256]{2,1,0:T(8,128)(2,1)S(1)}, bf16[4,128,256]{2,1,0:T(8,128)(2,1)S(1)}, u32[]{:S(2)}, u32[]{:S(2)}) collective-permute-start(bf16[4,128,256]{2,1,0:T(8,128)(2,1)S(1)} %get-tuple-element.30.x.rest_0_), channel_id=1, source_target_pairs={{0,225},{1,224},{2,227},{3,226},{4,229},{5,228},{6,231},{7,230},{8... | collective-permute-start | bytes 786440 | tf_op jit(solution)/shard_map/ppermute | solution.py:50
  18.3 1.9 %collective-permute-start.7 = (bf16[144,256]{1,0:T(8,128)(2,1)S(1)}, bf16[144,256]{1,0:T(8,128)(2,1)S(1)}, u32[]{:S(2)}, u32[]{:S(2)}) collective-permute-start(bf16[144,256]{1,0:T(8,128)(2,1)S(1)} %corner.2), channel_id=1, source_target_pairs={{0,225},{1,224},{2,227},{3,226},{4,229},{5,228},{6,231},{7,230},{8... | collective-permute-start | bytes 221192 | tf_op jit(solution)/shard_map/ppermute | solution.py:50
  20.3 4.4 %collective-permute-start.8 = (bf16[128,256]{1,0:T(8,128)(2,1)S(1)}, bf16[128,256]{1,0:T(8,128)(2,1)S(1)}, u32[]{:S(2)}, u32[]{:S(2)}) collective-permute-start(bf16[128,256]{1,0:T(8,128)(2,1)S(1)} %get-tuple-element.34), channel_id=1, source_target_pairs={{0,2},{1,3},{2,0},{3,1},{4,6},{5,7},{6,4},{7,5},{8,10},{9,11},{10,... | collective-permute-start | bytes 196616 | tf_op jit(solution)/shard_map/ppermute | solution.py:50
  25.2 3.2 %collective-permute-start.3 = (bf16[128,256]{1,0:T(8,128)(2,1)S(1)}, bf16[128,256]{1,0:T(8,128)(2,1)S(1)}, u32[]{:S(2)}, u32[]{:S(2)}) collective-permute-start(bf16[128,256]{1,0:T(8,128)(2,1)S(1)} %get-tuple-element.31), channel_id=1, source_target_pairs={{0,2},{1,3},{2,0},{3,1},{4,6},{5,7},{6,4},{7,5},{8,10},{9,11},{10,... | collective-permute-start | bytes 196616 | tf_op jit(solution)/shard_map/ppermute | solution.py:50
  28.5 1.0 core.2.acc
  29.7 0.8 rim.2
  30.7 3.4 %collective-permute-start.10 = (bf16[4,128,256]{2,1,0:T(8,128)(2,1)S(1)}, bf16[4,128,256]{2,1,0:T(8,128)(2,1)S(1)}, u32[]{:S(2)}, u32[]{:S(2)}) collective-permute-start(bf16[4,128,256]{2,1,0:T(8,128)(2,1)S(1)} %get-tuple-element.35.x), channel_id=1, source_target_pairs={{0,225},{1,224},{2,227},{3,226},{4,229},{5,228},{6,231},{7,230},{8... | collective-permute-start | bytes 786440 | tf_op jit(solution)/shard_map/ppermute | solution.py:50
  34.9 2.8 %collective-permute-start.15 = (bf16[144,256]{1,0:T(8,128)(2,1)S(1)}, bf16[144,256]{1,0:T(8,128)(2,1)S(1)}, u32[]{:S(2)}, u32[]{:S(2)}) collective-permute-start(bf16[144,256]{1,0:T(8,128)(2,1)S(1)} %corner.3), channel_id=1, source_target_pairs={{0,225},{1,224},{2,227},{3,226},{4,229},{5,228},{6,231},{7,230},{8... | collective-permute-start | bytes 221192 | tf_op jit(solution)/shard_map/ppermute | solution.py:50
  37.7 1.8 collective-permute-start.16
  39.6 1.0 collective-permute-done.10.b
  41.2 3.1 %collective-permute-start.11 = (bf16[128,256]{1,0:T(8,128)(2,1)S(1)}, bf16[128,256]{1,0:T(8,128)(2,1)S(1)}, u32[]{:S(2)}, u32[]{:S(2)}) collective-permute-start(bf16[128,256]{1,0:T(8,128)(2,1)S(1)} %get-tuple-element.36), channel_id=1, source_target_pairs={{0,2},{1,3},{2,0},{3,1},{4,6},{5,7},{6,4},{7,5},{8,10},{9,11},{10,... | collective-permute-start | bytes 196616 | tf_op jit(solution)/shard_map/ppermute | solution.py:50
  44.3 1.0 core.3.acc
  45.5 0.8 rim.3
  46.3 3.4 %collective-permute-start.19 = (bf16[4,128,256]{2,1,0:T(8,128)(2,1)S(1)}, bf16[4,128,256]{2,1,0:T(8,128)(2,1)S(1)}, u32[]{:S(2)}, u32[]{:S(2)}) collective-permute-start(bf16[4,128,256]{2,1,0:T(8,128)(2,1)S(1)} %get-tuple-element.42.s), channel_id=1, source_target_pairs={{0,225},{1,224},{2,227},{3,226},{4,229},{5,228},{6,231},{7,230},{8... | collective-permute-start | bytes 786440 | tf_op jit(solution)/shard_map/ppermute | solution.py:54
  50.8 0.9 corr.1
  51.8 2.8 %collective-permute-done.18.q = bf16[192,256]{1,0:T(8,128)(2,1)S(1)} collective-permute-done((bf16[192,256]{1,0:T(8,128)(2,1)S(1)}, bf16[192,256]{1,0:T(8,128)(2,1)S(1)}, u32[]{:S(2)}, u32[]{:S(2)}) %collective-permute-start.18) | collective-permute-done | bytes 98336 | tf_op jit(solution)/shard_map/ppermute | solution.py:50
  55.0 1.7 gram.1
  56.8 1.2 collective-permute-start.20
  58.0 1.0 collective-permute-done.20
  59.0 0.8 add.59
  59.9 12.5 %all-to-all-start = ((f32[64,1,640]{2,1,0:T(1,128)}), f32[64,1,640]{2,1,0:T(1,128)S(1)}, u32[]{:S(2)}, u32[]{:S(2)}) async-start(f32[64,1,640]{2,1,0:T(1,128)} %add.59), calls=%async_computation | async-start | bytes 327680 | tf_op jit(solution)/shard_map/all_to_all | solution.py:74
  73.0 11.0 %all-to-all-done = f32[64,1,640]{2,1,0:T(1,128)S(1)} async-done(((f32[64,1,640]{2,1,0:T(1,128)}), f32[64,1,640]{2,1,0:T(1,128)S(1)}, u32[]{:S(2)}, u32[]{:S(2)}) %all-to-all-start) | async-done | bytes 163872 | tf_op jit(solution)/shard_map/all_to_all | solution.py:74
  84.3 20.3 %all_to_all.10.mine = f32[128,1,640]{2,1,0:T(1,128)S(1)} all-to-all(f32[128,1,640]{2,1,0:T(1,128)S(1)} %broadcast_in_dim.20), channel_id=1, replica_groups={{0,4,8,12,16,20,24,28,32,36,40,44,48,52,56,60,65,69,73,77,81,85,89,93,9..., dimensions={0} | all-to-all | bytes 655360 | tf_op jit(solution)/shard_map/all_to_all | solution.py:74
  104.5 3.9 %collective-permute-start.22 = (f32[128,1,640]{2,1,0:T(1,128)S(1)}, f32[128,1,640]{2,1,0:T(1,128)S(1)}, u32[]{:S(2)}, u32[]{:S(2)}) collective-permute-start(f32[128,1,640]{2,1,0:T(1,128)S(1)} %all_to_all.10.mine), channel_id=1, source_target_pairs={{0,2},{1,3},{2,0},{3,1},{4,6},{5,7},{6,4},{7,5},{8,10},{9,11},{10,... | collective-permute-start | bytes 983048 | tf_op jit(solution)/shard_map/ppermute | solution.py:50
  108.5 1.3 collective-permute-done.22.theirs
  109.7 79.0 %final.1 = (bf16[2,1,4,128,128]{4,3,2,1,0:T(8,128)(2,1)}, f32[2,256,128]{2,1,0:T(8,128)}) custom-call(s32[40]{0:T(128)S(1)} %concatenate.7.m, f32[128,1,640]{2,1,0:T(1,128)S(1)} %all_to_all.10.mine, f32[128,1,640]{2,1,0:T(1,128)S(1)} %collective-permute-done.22.theirs, bf16[2,4,128,256]{3,2,1,0:T(8,128)(2,1)S(1)} %stack.29.both), custom_call_target="tpu_custom_call" | custom-call | flops 1677721600 | bytes 1703936 | tf_op jit(solution)/shard_map/final/pallas_call | solution.py:339
  (47 shorter events, 7.8 us)
Async XLA Ops:
  1.6 8.4 %collective-permute-start = (bf16[4,128,128]{2,1,0:T(8,128)(2,1)S(1)}, bf16[4,128,128]{2,1,0:T(8,128)(2,1)S(1)}, u32[]{:S(2)}, u32[]{:S(2)}) collective-permute-start(bf16[4,128,128]{2,1,0:T(8,128)(2,1)S(1)} %get-tuple-element.53), channel_id=1, source_target_pairs={{0,1},{1,0},{2,3},{3,2},{4,5},{5,4},{6,7},{7,6},{8,9},{9,8},{10,11... | collective-permute-start | bytes 393224 | tf_op jit(solution)/shard_map/ppermute | solution.py:59
  7.5 1.7 copy-start
  10.7 7.0 %collective-permute-start.5 = (bf16[128,256]{1,0:T(8,128)(2,1)S(1)}, bf16[128,256]{1,0:T(8,128)(2,1)S(1)}, u32[]{:S(2)}, u32[]{:S(2)}) collective-permute-start(bf16[128,256]{1,0:T(8,128)(2,1)S(1)} %get-tuple-element.33), channel_id=1, source_target_pairs={{0,30},{1,31},{2,4},{3,5},{4,2},{5,3},{6,8},{7,9},{8,6},{9,7},{10,... | collective-permute-start | bytes 196616 | tf_op jit(solution)/shard_map/ppermute | solution.py:50
  13.2 11.4 %collective-permute-start.1 = (bf16[4,128,256]{2,1,0:T(8,128)(2,1)S(1)}, bf16[4,128,256]{2,1,0:T(8,128)(2,1)S(1)}, u32[]{:S(2)}, u32[]{:S(2)}) collective-permute-start(bf16[4,128,256]{2,1,0:T(8,128)(2,1)S(1)} %get-tuple-element.30.x.rest_0_), channel_id=1, source_target_pairs={{0,32},{1,33},{2,34},{3,35},{4,36},{5,37},{6,38},{7,39},{8,40},{9,... | collective-permute-start | bytes 786440 | tf_op jit(solution)/shard_map/ppermute | solution.py:50
  13.5 11.1 %collective-permute-start.2 = (bf16[4,128,256]{2,1,0:T(8,128)(2,1)S(1)}, bf16[4,128,256]{2,1,0:T(8,128)(2,1)S(1)}, u32[]{:S(2)}, u32[]{:S(2)}) collective-permute-start(bf16[4,128,256]{2,1,0:T(8,128)(2,1)S(1)} %get-tuple-element.30.x.rest_0_), channel_id=1, source_target_pairs={{0,225},{1,224},{2,227},{3,226},{4,229},{5,228},{6,231},{7,230},{8... | collective-permute-start | bytes 786440 | tf_op jit(solution)/shard_map/ppermute | solution.py:50
  18.2 11.3 %collective-permute-start.6 = (bf16[144,256]{1,0:T(8,128)(2,1)S(1)}, bf16[144,256]{1,0:T(8,128)(2,1)S(1)}, u32[]{:S(2)}, u32[]{:S(2)}) collective-permute-start(bf16[144,256]{1,0:T(8,128)(2,1)S(1)} %corner.2), channel_id=1, source_target_pairs={{0,32},{1,33},{2,34},{3,35},{4,36},{5,37},{6,38},{7,39},{8,40},{9,... | collective-permute-start | bytes 221192 | tf_op jit(solution)/shard_map/ppermute | solution.py:50
  18.3 11.2 %collective-permute-start.7 = (bf16[144,256]{1,0:T(8,128)(2,1)S(1)}, bf16[144,256]{1,0:T(8,128)(2,1)S(1)}, u32[]{:S(2)}, u32[]{:S(2)}) collective-permute-start(bf16[144,256]{1,0:T(8,128)(2,1)S(1)} %corner.2), channel_id=1, source_target_pairs={{0,225},{1,224},{2,227},{3,226},{4,229},{5,228},{6,231},{7,230},{8... | collective-permute-start | bytes 221192 | tf_op jit(solution)/shard_map/ppermute | solution.py:50
  20.3 8.3 %collective-permute-start.8 = (bf16[128,256]{1,0:T(8,128)(2,1)S(1)}, bf16[128,256]{1,0:T(8,128)(2,1)S(1)}, u32[]{:S(2)}, u32[]{:S(2)}) collective-permute-start(bf16[128,256]{1,0:T(8,128)(2,1)S(1)} %get-tuple-element.34), channel_id=1, source_target_pairs={{0,2},{1,3},{2,0},{3,1},{4,6},{5,7},{6,4},{7,5},{8,10},{9,11},{10,... | collective-permute-start | bytes 196616 | tf_op jit(solution)/shard_map/ppermute | solution.py:50
  25.2 4.4 %collective-permute-start.3 = (bf16[128,256]{1,0:T(8,128)(2,1)S(1)}, bf16[128,256]{1,0:T(8,128)(2,1)S(1)}, u32[]{:S(2)}, u32[]{:S(2)}) collective-permute-start(bf16[128,256]{1,0:T(8,128)(2,1)S(1)} %get-tuple-element.31), channel_id=1, source_target_pairs={{0,2},{1,3},{2,0},{3,1},{4,6},{5,7},{6,4},{7,5},{8,10},{9,11},{10,... | collective-permute-start | bytes 196616 | tf_op jit(solution)/shard_map/ppermute | solution.py:50
  28.4 1.3 collective-permute-start.4
  30.5 3.8 %collective-permute-start.13 = (bf16[128,256]{1,0:T(8,128)(2,1)S(1)}, bf16[128,256]{1,0:T(8,128)(2,1)S(1)}, u32[]{:S(2)}, u32[]{:S(2)}) collective-permute-start(bf16[128,256]{1,0:T(8,128)(2,1)S(1)} %get-tuple-element.38), channel_id=1, source_target_pairs={{0,30},{1,31},{2,4},{3,5},{4,2},{5,3},{6,8},{7,9},{8,6},{9,7},{10,... | collective-permute-start | bytes 196616 | tf_op jit(solution)/shard_map/ppermute | solution.py:50
  30.6 9.0 %collective-permute-start.9 = (bf16[4,128,256]{2,1,0:T(8,128)(2,1)S(1)}, bf16[4,128,256]{2,1,0:T(8,128)(2,1)S(1)}, u32[]{:S(2)}, u32[]{:S(2)}) collective-permute-start(bf16[4,128,256]{2,1,0:T(8,128)(2,1)S(1)} %get-tuple-element.35.x), channel_id=1, source_target_pairs={{0,32},{1,33},{2,34},{3,35},{4,36},{5,37},{6,38},{7,39},{8,40},{9,... | collective-permute-start | bytes 786440 | tf_op jit(solution)/shard_map/ppermute | solution.py:50
  30.7 9.9 %collective-permute-start.10 = (bf16[4,128,256]{2,1,0:T(8,128)(2,1)S(1)}, bf16[4,128,256]{2,1,0:T(8,128)(2,1)S(1)}, u32[]{:S(2)}, u32[]{:S(2)}) collective-permute-start(bf16[4,128,256]{2,1,0:T(8,128)(2,1)S(1)} %get-tuple-element.35.x), channel_id=1, source_target_pairs={{0,225},{1,224},{2,227},{3,226},{4,229},{5,228},{6,231},{7,230},{8... | collective-permute-start | bytes 786440 | tf_op jit(solution)/shard_map/ppermute | solution.py:50
  34.8 10.6 %collective-permute-start.14 = (bf16[144,256]{1,0:T(8,128)(2,1)S(1)}, bf16[144,256]{1,0:T(8,128)(2,1)S(1)}, u32[]{:S(2)}, u32[]{:S(2)}) collective-permute-start(bf16[144,256]{1,0:T(8,128)(2,1)S(1)} %corner.3), channel_id=1, source_target_pairs={{0,32},{1,33},{2,34},{3,35},{4,36},{5,37},{6,38},{7,39},{8,40},{9,... | collective-permute-start | bytes 221192 | tf_op jit(solution)/shard_map/ppermute | solution.py:50
  34.9 10.5 %collective-permute-start.15 = (bf16[144,256]{1,0:T(8,128)(2,1)S(1)}, bf16[144,256]{1,0:T(8,128)(2,1)S(1)}, u32[]{:S(2)}, u32[]{:S(2)}) collective-permute-start(bf16[144,256]{1,0:T(8,128)(2,1)S(1)} %corner.3), channel_id=1, source_target_pairs={{0,225},{1,224},{2,227},{3,226},{4,229},{5,228},{6,231},{7,230},{8... | collective-permute-start | bytes 221192 | tf_op jit(solution)/shard_map/ppermute | solution.py:50
  37.7 6.6 %collective-permute-start.16 = (bf16[128,256]{1,0:T(8,128)(2,1)S(1)}, bf16[128,256]{1,0:T(8,128)(2,1)S(1)}, u32[]{:S(2)}, u32[]{:S(2)}) collective-permute-start(bf16[128,256]{1,0:T(8,128)(2,1)S(1)} %get-tuple-element.39), channel_id=1, source_target_pairs={{0,2},{1,3},{2,0},{3,1},{4,6},{5,7},{6,4},{7,5},{8,10},{9,11},{10,... | collective-permute-start | bytes 196616 | tf_op jit(solution)/shard_map/ppermute | solution.py:50
  41.2 4.2 %collective-permute-start.11 = (bf16[128,256]{1,0:T(8,128)(2,1)S(1)}, bf16[128,256]{1,0:T(8,128)(2,1)S(1)}, u32[]{:S(2)}, u32[]{:S(2)}) collective-permute-start(bf16[128,256]{1,0:T(8,128)(2,1)S(1)} %get-tuple-element.36), channel_id=1, source_target_pairs={{0,2},{1,3},{2,0},{3,1},{4,6},{5,7},{6,4},{7,5},{8,10},{9,11},{10,... | collective-permute-start | bytes 196616 | tf_op jit(solution)/shard_map/ppermute | solution.py:50
  44.2 1.3 collective-permute-start.12
  46.3 8.8 %collective-permute-start.19 = (bf16[4,128,256]{2,1,0:T(8,128)(2,1)S(1)}, bf16[4,128,256]{2,1,0:T(8,128)(2,1)S(1)}, u32[]{:S(2)}, u32[]{:S(2)}) collective-permute-start(bf16[4,128,256]{2,1,0:T(8,128)(2,1)S(1)} %get-tuple-element.42.s), channel_id=1, source_target_pairs={{0,225},{1,224},{2,227},{3,226},{4,229},{5,228},{6,231},{7,230},{8... | collective-permute-start | bytes 786440 | tf_op jit(solution)/shard_map/ppermute | solution.py:54
  49.7 2.1 %collective-permute-start.17 = (bf16[192,256]{1,0:T(8,128)(2,1)S(1)}, bf16[192,256]{1,0:T(8,128)(2,1)S(1)}, u32[]{:S(2)}, u32[]{:S(2)}) collective-permute-start(bf16[192,256]{1,0:T(8,128)(2,1)S(1)} %get-tuple-element.44), channel_id=1, source_target_pairs={{0,2},{1,3},{2,0},{3,1},{4,6},{5,7},{6,4},{7,5},{8,10},{9,11},{10,... | collective-permute-start | bytes 294920 | tf_op jit(solution)/shard_map/ppermute | solution.py:50
  50.3 4.3 %collective-permute-start.18 = (bf16[192,256]{1,0:T(8,128)(2,1)S(1)}, bf16[192,256]{1,0:T(8,128)(2,1)S(1)}, u32[]{:S(2)}, u32[]{:S(2)}) collective-permute-start(bf16[192,256]{1,0:T(8,128)(2,1)S(1)} %get-tuple-element.45), channel_id=1, source_target_pairs={{0,30},{1,31},{2,4},{3,5},{4,2},{5,3},{6,8},{7,9},{8,6},{9,7},{10,... | collective-permute-start | bytes 294920 | tf_op jit(solution)/shard_map/ppermute | solution.py:50
  56.8 2.3 %collective-permute-start.20 = (f32[64,1,640]{2,1,0:T(1,128)S(1)}, f32[64,1,640]{2,1,0:T(1,128)S(1)}, u32[]{:S(2)}, u32[]{:S(2)}) collective-permute-start(f32[64,1,640]{2,1,0:T(1,128)S(1)} %get-tuple-element.49), channel_id=1, source_target_pairs={{0,2},{1,3},{2,0},{3,1},{4,6},{5,7},{6,4},{7,5},{8,10},{9,11},{10,... | collective-permute-start | bytes 491528 | tf_op jit(solution)/shard_map/ppermute | solution.py:50
  58.0 14.3 %collective-permute-start.21 = (bf16[4,128,256]{2,1,0:T(8,128)(2,1)S(1)}, bf16[4,128,256]{2,1,0:T(8,128)(2,1)S(1)}, u32[]{:S(2)}, u32[]{:S(2)}) collective-permute-start(bf16[4,128,256]{2,1,0:T(8,128)(2,1)S(1)} %get-tuple-element.42.s), channel_id=1, source_target_pairs={{0,1},{1,0},{2,3},{3,2},{4,5},{5,4},{6,7},{7,6},{8,9},{9,8},{10,11... | collective-permute-start | bytes 786440 | tf_op jit(solution)/shard_map/ppermute | solution.py:59
  59.9 24.1 %all-to-all-start = ((f32[64,1,640]{2,1,0:T(1,128)}), f32[64,1,640]{2,1,0:T(1,128)S(1)}, u32[]{:S(2)}, u32[]{:S(2)}) async-start(f32[64,1,640]{2,1,0:T(1,128)} %add.59), calls=%async_computation | async-start | bytes 327680 | tf_op jit(solution)/shard_map/all_to_all | solution.py:74
  104.5 5.2 %collective-permute-start.22 = (f32[128,1,640]{2,1,0:T(1,128)S(1)}, f32[128,1,640]{2,1,0:T(1,128)S(1)}, u32[]{:S(2)}, u32[]{:S(2)}) collective-permute-start(f32[128,1,640]{2,1,0:T(1,128)S(1)} %all_to_all.10.mine), channel_id=1, source_target_pairs={{0,2},{1,3},{2,0},{3,1},{4,6},{5,7},{6,4},{7,5},{8,10},{9,11},{10,... | collective-permute-start | bytes 983048 | tf_op jit(solution)/shard_map/ppermute | solution.py:50

commit v18 on v16

--- a/solution.py
+++ b/solution.py
@@ -128,7 +128,7 @@
     q[T:] = v[0, : q.shape[0] - T]
 
 
-def edge_kernel(m, a, b, a_out, b_out):
+def edge_kernel(m, b, a, a_out, b_out):
     at = jnp.where(m[PAR_Y] == 0, 3, 0)
     a_out[...] = a[at]
     b_out[...] = b[at]
@@ -151,7 +151,7 @@
     return dot(jnp.where(high, top, bottom), jnp.concatenate(tiles, axis=0)), high
 
 
-def core_kernel(m, o, x, p, q, a, b, acc, ext):
+def core_kernel(m, o, x, p, q, b, a, acc, ext):
     ext[0], ext[5] = low_high(m, p[...], q[:T])
     ext[1:5] = x[...]
     for tile in range(4):
@@ -160,7 +160,7 @@
         acc[tile] = total + product(o, tile, (1, 2), at, [y[at[0] - 1 : at[-1]] for y in (a, b)])
 
 
-def rim_kernel(m, o, a_edge, b_edge, a_corner, b_corner, acc, *rest, last):
+def rim_kernel(m, o, a_edge, b_edge, b_corner, a_corner, acc, *rest, last):
     if last:
         before, h_p, h_q, out, p, q = rest
     else:
@@ -391,15 +391,15 @@
 
     def apply_ham(x, p, q, more, outs):
         p, q = swap(sizes, p, 0, 1), swap(sizes, q, 0, 2)
-        a, b = swap(sizes, x, 1, 0), swap(sizes, x, 2, 0)
-        a_corner, b_corner = swap(sizes, q, 1, 0), swap(sizes, q, 2, 0)
-        a_edge, b_edge = call(edge_kernel, m, [a, b], [tile, tile], "edge", free=True)
+        b, a = swap(sizes, x, 2, 0), swap(sizes, x, 1, 0)
+        b_corner, a_corner = swap(sizes, q, 2, 0), swap(sizes, q, 1, 0)
+        a_edge, b_edge = call(edge_kernel, m, [b, a], [tile, tile], "edge", free=True)
         a_edge, b_edge = swap(sizes, a_edge, 0, 1), swap(sizes, b_edge, 0, 1)
         (acc,) = call(
-            core_kernel, m, [o, x, p, q, a, b], [shaped(block, F32)], "core", free=True, scratch=[ext]
+            core_kernel, m, [o, x, p, q, b, a], [shaped(block, F32)], "core", free=True, scratch=[ext]
         )
         kernel = functools.partial(rim_kernel, last=len(more) > 0)
-        return call(kernel, m, [o, a_edge, b_edge, a_corner, b_corner, acc, *more], outs, "rim", 2)
+        return call(kernel, m, [o, a_edge, b_edge, b_corner, a_corner, acc, *more], outs, "rim", 2)
 
     first, p, q = apply_ham(v, p, q, [], outs)
     longer = shaped((3 * T // 2, 2 * T), BF)

time: 188 us -> 187 us (level)
  no operation moved by 1% of the time
where the time goes in v18:
time: 187 us
  Pallas kernels  88.4 us (47%)
  starting transfers between devices  50 us (27%)
  waiting for transfers between devices  21.2 us (11%)
  blocking collectives  20.3 us (11%)
  local copies, waits for them, and re-layouts  3.12 us (2%)
  other arithmetic  2.86 us (2%)
    pallas_call x12, Pallas kernels, call(): pl.pallas_call(kernel, out_shape=outs, grid_spec=pltpu.PrefetchScalarGrid...  88.4 us
    ppermute x20, starting transfers between devices, swap(): return lax.ppermute(block, AXES, perm)  32.7 us
    all_to_all x1, blocking collectives, exchange(): lax.all_to_all(pieces, AXES, 0, 0, axis_index_groups=groups, tiled=True)  20.3 us
    all_to_all x1, starting transfers between devices, exchange(): lax.all_to_all(pieces, AXES, 0, 0, axis_index_groups=groups, tiled=True)  11.9 us
    all_to_all x1, waiting for transfers between devices, exchange(): lax.all_to_all(pieces, AXES, 0, 0, axis_index_groups=groups, tiled=True)  11 us
    ppermute x20, waiting for transfers between devices, swap(): return lax.ppermute(block, AXES, perm)  10.2 us
  transfers between devices with their start and end apart: 24, of which 6 were waited for; matrix products, arithmetic and copies ran while one was open for 2% of the time, Pallas kernels for 3%

profile of v18, /device:TPU:1, one launch (start us, length us, event | category | flops | bytes accessed | tf_op | source)
XLA Modules:
  0.0 186.7 jit_solution(10044443509712825702)
XLA Ops:
  0.6 1.0 dynamic-slice_bitcast_fusion
  1.6 3.7 %collective-permute-start = (bf16[4,128,128]{2,1,0:T(8,128)(2,1)S(1)}, bf16[4,128,128]{2,1,0:T(8,128)(2,1)S(1)}, u32[]{:S(2)}, u32[]{:S(2)}) collective-permute-start(bf16[4,128,128]{2,1,0:T(8,128)(2,1)S(1)} %get-tuple-element.53), channel_id=1, source_target_pairs={{0,1},{1,0},{2,3},{3,2},{4,5},{5,4},{6,7},{7,6},{8,9},{9,8},{10,11... | collective-permute-start | bytes 393224 | tf_op jit(solution)/shard_map/ppermute | solution.py:59
  6.2 1.0 select_reduce_fusion
  7.5 1.7 copy-done
  9.2 0.9 order.1
  10.7 3.4 %collective-permute-start.1 = (bf16[4,128,256]{2,1,0:T(8,128)(2,1)S(1)}, bf16[4,128,256]{2,1,0:T(8,128)(2,1)S(1)}, u32[]{:S(2)}, u32[]{:S(2)}) collective-permute-start(bf16[4,128,256]{2,1,0:T(8,128)(2,1)S(1)} %get-tuple-element.30.x.rest_0_), channel_id=1, source_target_pairs={{0,225},{1,224},{2,227},{3,226},{4,229},{5,228},{6,231},{7,230},{8... | collective-permute-start | bytes 786440 | tf_op jit(solution)/shard_map/ppermute | solution.py:50
  14.1 3.4 %collective-permute-start.5 = (bf16[144,256]{1,0:T(8,128)(2,1)S(1)}, bf16[144,256]{1,0:T(8,128)(2,1)S(1)}, u32[]{:S(2)}, u32[]{:S(2)}) collective-permute-start(bf16[144,256]{1,0:T(8,128)(2,1)S(1)} %get-tuple-element.33), channel_id=1, source_target_pairs={{0,30},{1,31},{2,4},{3,5},{4,2},{5,3},{6,8},{7,9},{8,6},{9,7},{10,... | collective-permute-start | bytes 221192 | tf_op jit(solution)/shard_map/ppermute | solution.py:50
  17.4 2.3 %collective-permute-done.5.q = bf16[144,256]{1,0:T(8,128)(2,1)S(1)} collective-permute-done((bf16[144,256]{1,0:T(8,128)(2,1)S(1)}, bf16[144,256]{1,0:T(8,128)(2,1)S(1)}, u32[]{:S(2)}, u32[]{:S(2)}) %collective-permute-start.5) | collective-permute-done | bytes 73760 | tf_op jit(solution)/shard_map/ppermute | solution.py:50
  19.7 1.4 collective-permute-start.6
  21.7 3.2 %collective-permute-start.8 = (bf16[128,256]{1,0:T(8,128)(2,1)S(1)}, bf16[128,256]{1,0:T(8,128)(2,1)S(1)}, u32[]{:S(2)}, u32[]{:S(2)}) collective-permute-start(bf16[128,256]{1,0:T(8,128)(2,1)S(1)} %get-tuple-element.34), channel_id=1, source_target_pairs={{0,2},{1,3},{2,0},{3,1},{4,6},{5,7},{6,4},{7,5},{8,10},{9,11},{10,... | collective-permute-start | bytes 196616 | tf_op jit(solution)/shard_map/ppermute | solution.py:50
  26.1 1.0 core.2.acc
  27.1 0.8 rim.2
  27.9 2.3 %collective-permute-start.9 = (bf16[4,128,256]{2,1,0:T(8,128)(2,1)S(1)}, bf16[4,128,256]{2,1,0:T(8,128)(2,1)S(1)}, u32[]{:S(2)}, u32[]{:S(2)}) collective-permute-start(bf16[4,128,256]{2,1,0:T(8,128)(2,1)S(1)} %get-tuple-element.35.x), channel_id=1, source_target_pairs={{0,225},{1,224},{2,227},{3,226},{4,229},{5,228},{6,231},{7,230},{8... | collective-permute-start | bytes 786440 | tf_op jit(solution)/shard_map/ppermute | solution.py:50
  30.2 1.6 collective-permute-start.13
  31.9 2.1 %collective-permute-done.13.q = bf16[144,256]{1,0:T(8,128)(2,1)S(1)} collective-permute-done((bf16[144,256]{1,0:T(8,128)(2,1)S(1)}, bf16[144,256]{1,0:T(8,128)(2,1)S(1)}, u32[]{:S(2)}, u32[]{:S(2)}) %collective-permute-start.13) | collective-permute-done | bytes 73760 | tf_op jit(solution)/shard_map/ppermute | solution.py:50
  34.0 3.2 %collective-permute-start.14 = (bf16[144,256]{1,0:T(8,128)(2,1)S(1)}, bf16[144,256]{1,0:T(8,128)(2,1)S(1)}, u32[]{:S(2)}, u32[]{:S(2)}) collective-permute-start(bf16[144,256]{1,0:T(8,128)(2,1)S(1)} %collective-permute-done.13.q), channel_id=1, source_target_pairs={{0,225},{1,224},{2,227},{3,226},{4,229},{5,228},{6,231},{7,230},{8... | collective-permute-start | bytes 221192 | tf_op jit(solution)/shard_map/ppermute | solution.py:50
  37.3 3.7 %collective-permute-start.16 = (bf16[128,256]{1,0:T(8,128)(2,1)S(1)}, bf16[128,256]{1,0:T(8,128)(2,1)S(1)}, u32[]{:S(2)}, u32[]{:S(2)}) collective-permute-start(bf16[128,256]{1,0:T(8,128)(2,1)S(1)} %get-tuple-element.39), channel_id=1, source_target_pairs={{0,2},{1,3},{2,0},{3,1},{4,6},{5,7},{6,4},{7,5},{8,10},{9,11},{10,... | collective-permute-start | bytes 196616 | tf_op jit(solution)/shard_map/ppermute | solution.py:50
  42.1 1.0 core.3.acc
  44.0 1.8 collective-permute-start.19
  45.8 3.7 %collective-permute-start.17 = (bf16[192,256]{1,0:T(8,128)(2,1)S(1)}, bf16[192,256]{1,0:T(8,128)(2,1)S(1)}, u32[]{:S(2)}, u32[]{:S(2)}) collective-permute-start(bf16[192,256]{1,0:T(8,128)(2,1)S(1)} %get-tuple-element.44), channel_id=1, source_target_pairs={{0,2},{1,3},{2,0},{3,1},{4,6},{5,7},{6,4},{7,5},{8,10},{9,11},{10,... | collective-permute-start | bytes 294920 | tf_op jit(solution)/shard_map/ppermute | solution.py:50
  49.5 0.9 corr.1
  50.4 3.4 %collective-permute-done.18.q = bf16[192,256]{1,0:T(8,128)(2,1)S(1)} collective-permute-done((bf16[192,256]{1,0:T(8,128)(2,1)S(1)}, bf16[192,256]{1,0:T(8,128)(2,1)S(1)}, u32[]{:S(2)}, u32[]{:S(2)}) %collective-permute-start.18) | collective-permute-done | bytes 98336 | tf_op jit(solution)/shard_map/ppermute | solution.py:50
  53.8 1.7 gram.1
  55.6 1.0 collective-permute-start.20
  56.6 1.0 collective-permute-done.20
  57.6 0.8 add.59
  58.5 11.9 %all-to-all-start = ((f32[64,1,640]{2,1,0:T(1,128)}), f32[64,1,640]{2,1,0:T(1,128)S(1)}, u32[]{:S(2)}, u32[]{:S(2)}) async-start(f32[64,1,640]{2,1,0:T(1,128)} %add.59), calls=%async_computation | async-start | bytes 327680 | tf_op jit(solution)/shard_map/all_to_all | solution.py:74
  70.9 11.0 %all-to-all-done = f32[64,1,640]{2,1,0:T(1,128)S(1)} async-done(((f32[64,1,640]{2,1,0:T(1,128)}), f32[64,1,640]{2,1,0:T(1,128)S(1)}, u32[]{:S(2)}, u32[]{:S(2)}) %all-to-all-start) | async-done | bytes 163872 | tf_op jit(solution)/shard_map/all_to_all | solution.py:74
  82.3 20.3 %all_to_all.10.mine = f32[128,1,640]{2,1,0:T(1,128)S(1)} all-to-all(f32[128,1,640]{2,1,0:T(1,128)S(1)} %broadcast_in_dim.20), channel_id=1, replica_groups={{0,4,8,12,16,20,24,28,32,36,40,44,48,52,56,60,65,69,73,77,81,85,89,93,9..., dimensions={0} | all-to-all | bytes 655360 | tf_op jit(solution)/shard_map/all_to_all | solution.py:74
  102.5 3.9 %collective-permute-start.22 = (f32[128,1,640]{2,1,0:T(1,128)S(1)}, f32[128,1,640]{2,1,0:T(1,128)S(1)}, u32[]{:S(2)}, u32[]{:S(2)}) collective-permute-start(f32[128,1,640]{2,1,0:T(1,128)S(1)} %all_to_all.10.mine), channel_id=1, source_target_pairs={{0,2},{1,3},{2,0},{3,1},{4,6},{5,7},{6,4},{7,5},{8,10},{9,11},{10,... | collective-permute-start | bytes 983048 | tf_op jit(solution)/shard_map/ppermute | solution.py:50
  106.5 1.3 collective-permute-done.22.theirs
  107.7 79.0 %final.1 = (bf16[2,1,4,128,128]{4,3,2,1,0:T(8,128)(2,1)}, f32[2,256,128]{2,1,0:T(8,128)}) custom-call(s32[40]{0:T(128)S(1)} %concatenate.7.m, f32[128,1,640]{2,1,0:T(1,128)S(1)} %all_to_all.10.mine, f32[128,1,640]{2,1,0:T(1,128)S(1)} %collective-permute-done.22.theirs, bf16[2,4,128,256]{3,2,1,0:T(8,128)(2,1)S(1)} %stack.29.both), custom_call_target="tpu_custom_call" | custom-call | flops 1677721600 | bytes 1703936 | tf_op jit(solution)/shard_map/final/pallas_call | solution.py:337
  (45 shorter events, 6.4 us)
Async XLA Ops:
  1.6 8.4 %collective-permute-start = (bf16[4,128,128]{2,1,0:T(8,128)(2,1)S(1)}, bf16[4,128,128]{2,1,0:T(8,128)(2,1)S(1)}, u32[]{:S(2)}, u32[]{:S(2)}) collective-permute-start(bf16[4,128,128]{2,1,0:T(8,128)(2,1)S(1)} %get-tuple-element.53), channel_id=1, source_target_pairs={{0,1},{1,0},{2,3},{3,2},{4,5},{5,4},{6,7},{7,6},{8,9},{9,8},{10,11... | collective-permute-start | bytes 393224 | tf_op jit(solution)/shard_map/ppermute | solution.py:59
  7.5 1.7 copy-start
  10.7 14.2 %collective-permute-start.1 = (bf16[4,128,256]{2,1,0:T(8,128)(2,1)S(1)}, bf16[4,128,256]{2,1,0:T(8,128)(2,1)S(1)}, u32[]{:S(2)}, u32[]{:S(2)}) collective-permute-start(bf16[4,128,256]{2,1,0:T(8,128)(2,1)S(1)} %get-tuple-element.30.x.rest_0_), channel_id=1, source_target_pairs={{0,225},{1,224},{2,227},{3,226},{4,229},{5,228},{6,231},{7,230},{8... | collective-permute-start | bytes 786440 | tf_op jit(solution)/shard_map/ppermute | solution.py:50
  14.1 10.8 %collective-permute-start.2 = (bf16[4,128,256]{2,1,0:T(8,128)(2,1)S(1)}, bf16[4,128,256]{2,1,0:T(8,128)(2,1)S(1)}, u32[]{:S(2)}, u32[]{:S(2)}) collective-permute-start(bf16[4,128,256]{2,1,0:T(8,128)(2,1)S(1)} %get-tuple-element.30.x.rest_0_), channel_id=1, source_target_pairs={{0,32},{1,33},{2,34},{3,35},{4,36},{5,37},{6,38},{7,39},{8,40},{9,... | collective-permute-start | bytes 786440 | tf_op jit(solution)/shard_map/ppermute | solution.py:50
  14.1 5.7 %collective-permute-start.5 = (bf16[144,256]{1,0:T(8,128)(2,1)S(1)}, bf16[144,256]{1,0:T(8,128)(2,1)S(1)}, u32[]{:S(2)}, u32[]{:S(2)}) collective-permute-start(bf16[144,256]{1,0:T(8,128)(2,1)S(1)} %get-tuple-element.33), channel_id=1, source_target_pairs={{0,30},{1,31},{2,4},{3,5},{4,2},{5,3},{6,8},{7,9},{8,6},{9,7},{10,... | collective-permute-start | bytes 221192 | tf_op jit(solution)/shard_map/ppermute | solution.py:50
  19.7 7.3 %collective-permute-start.6 = (bf16[144,256]{1,0:T(8,128)(2,1)S(1)}, bf16[144,256]{1,0:T(8,128)(2,1)S(1)}, u32[]{:S(2)}, u32[]{:S(2)}) collective-permute-start(bf16[144,256]{1,0:T(8,128)(2,1)S(1)} %collective-permute-done.5.q), channel_id=1, source_target_pairs={{0,225},{1,224},{2,227},{3,226},{4,229},{5,228},{6,231},{7,230},{8... | collective-permute-start | bytes 221192 | tf_op jit(solution)/shard_map/ppermute | solution.py:50
  21.1 6.0 %collective-permute-start.7 = (bf16[144,256]{1,0:T(8,128)(2,1)S(1)}, bf16[144,256]{1,0:T(8,128)(2,1)S(1)}, u32[]{:S(2)}, u32[]{:S(2)}) collective-permute-start(bf16[144,256]{1,0:T(8,128)(2,1)S(1)} %collective-permute-done.5.q), channel_id=1, source_target_pairs={{0,32},{1,33},{2,34},{3,35},{4,36},{5,37},{6,38},{7,39},{8,40},{9,... | collective-permute-start | bytes 221192 | tf_op jit(solution)/shard_map/ppermute | solution.py:50
  21.7 4.4 %collective-permute-start.8 = (bf16[128,256]{1,0:T(8,128)(2,1)S(1)}, bf16[128,256]{1,0:T(8,128)(2,1)S(1)}, u32[]{:S(2)}, u32[]{:S(2)}) collective-permute-start(bf16[128,256]{1,0:T(8,128)(2,1)S(1)} %get-tuple-element.34), channel_id=1, source_target_pairs={{0,2},{1,3},{2,0},{3,1},{4,6},{5,7},{6,4},{7,5},{8,10},{9,11},{10,... | collective-permute-start | bytes 196616 | tf_op jit(solution)/shard_map/ppermute | solution.py:50
  25.5 1.6 collective-permute-start.3
  25.6 1.6 collective-permute-start.4
  27.9 13.1 %collective-permute-start.9 = (bf16[4,128,256]{2,1,0:T(8,128)(2,1)S(1)}, bf16[4,128,256]{2,1,0:T(8,128)(2,1)S(1)}, u32[]{:S(2)}, u32[]{:S(2)}) collective-permute-start(bf16[4,128,256]{2,1,0:T(8,128)(2,1)S(1)} %get-tuple-element.35.x), channel_id=1, source_target_pairs={{0,225},{1,224},{2,227},{3,226},{4,229},{5,228},{6,231},{7,230},{8... | collective-permute-start | bytes 786440 | tf_op jit(solution)/shard_map/ppermute | solution.py:50
  30.2 10.7 %collective-permute-start.10 = (bf16[4,128,256]{2,1,0:T(8,128)(2,1)S(1)}, bf16[4,128,256]{2,1,0:T(8,128)(2,1)S(1)}, u32[]{:S(2)}, u32[]{:S(2)}) collective-permute-start(bf16[4,128,256]{2,1,0:T(8,128)(2,1)S(1)} %get-tuple-element.35.x), channel_id=1, source_target_pairs={{0,32},{1,33},{2,34},{3,35},{4,36},{5,37},{6,38},{7,39},{8,40},{9,... | collective-permute-start | bytes 786440 | tf_op jit(solution)/shard_map/ppermute | solution.py:50
  30.2 3.8 %collective-permute-start.13 = (bf16[144,256]{1,0:T(8,128)(2,1)S(1)}, bf16[144,256]{1,0:T(8,128)(2,1)S(1)}, u32[]{:S(2)}, u32[]{:S(2)}) collective-permute-start(bf16[144,256]{1,0:T(8,128)(2,1)S(1)} %get-tuple-element.38), channel_id=1, source_target_pairs={{0,30},{1,31},{2,4},{3,5},{4,2},{5,3},{6,8},{7,9},{8,6},{9,7},{10,... | collective-permute-start | bytes 221192 | tf_op jit(solution)/shard_map/ppermute | solution.py:50
  34.0 9.1 %collective-permute-start.14 = (bf16[144,256]{1,0:T(8,128)(2,1)S(1)}, bf16[144,256]{1,0:T(8,128)(2,1)S(1)}, u32[]{:S(2)}, u32[]{:S(2)}) collective-permute-start(bf16[144,256]{1,0:T(8,128)(2,1)S(1)} %collective-permute-done.13.q), channel_id=1, source_target_pairs={{0,225},{1,224},{2,227},{3,226},{4,229},{5,228},{6,231},{7,230},{8... | collective-permute-start | bytes 221192 | tf_op jit(solution)/shard_map/ppermute | solution.py:50
  37.3 5.9 %collective-permute-start.15 = (bf16[144,256]{1,0:T(8,128)(2,1)S(1)}, bf16[144,256]{1,0:T(8,128)(2,1)S(1)}, u32[]{:S(2)}, u32[]{:S(2)}) collective-permute-start(bf16[144,256]{1,0:T(8,128)(2,1)S(1)} %collective-permute-done.13.q), channel_id=1, source_target_pairs={{0,32},{1,33},{2,34},{3,35},{4,36},{5,37},{6,38},{7,39},{8,40},{9,... | collective-permute-start | bytes 221192 | tf_op jit(solution)/shard_map/ppermute | solution.py:50
  37.3 4.9 %collective-permute-start.16 = (bf16[128,256]{1,0:T(8,128)(2,1)S(1)}, bf16[128,256]{1,0:T(8,128)(2,1)S(1)}, u32[]{:S(2)}, u32[]{:S(2)}) collective-permute-start(bf16[128,256]{1,0:T(8,128)(2,1)S(1)} %get-tuple-element.39), channel_id=1, source_target_pairs={{0,2},{1,3},{2,0},{3,1},{4,6},{5,7},{6,4},{7,5},{8,10},{9,11},{10,... | collective-permute-start | bytes 196616 | tf_op jit(solution)/shard_map/ppermute | solution.py:50
  41.5 1.7 collective-permute-start.11
  41.6 1.6 collective-permute-start.12
  44.0 9.9 %collective-permute-start.19 = (bf16[4,128,256]{2,1,0:T(8,128)(2,1)S(1)}, bf16[4,128,256]{2,1,0:T(8,128)(2,1)S(1)}, u32[]{:S(2)}, u32[]{:S(2)}) collective-permute-start(bf16[4,128,256]{2,1,0:T(8,128)(2,1)S(1)} %get-tuple-element.42.s), channel_id=1, source_target_pairs={{0,225},{1,224},{2,227},{3,226},{4,229},{5,228},{6,231},{7,230},{8... | collective-permute-start | bytes 786440 | tf_op jit(solution)/shard_map/ppermute | solution.py:54
  45.8 4.6 %collective-permute-start.17 = (bf16[192,256]{1,0:T(8,128)(2,1)S(1)}, bf16[192,256]{1,0:T(8,128)(2,1)S(1)}, u32[]{:S(2)}, u32[]{:S(2)}) collective-permute-start(bf16[192,256]{1,0:T(8,128)(2,1)S(1)} %get-tuple-element.44), channel_id=1, source_target_pairs={{0,2},{1,3},{2,0},{3,1},{4,6},{5,7},{6,4},{7,5},{8,10},{9,11},{10,... | collective-permute-start | bytes 294920 | tf_op jit(solution)/shard_map/ppermute | solution.py:50
  49.5 4.3 %collective-permute-start.18 = (bf16[192,256]{1,0:T(8,128)(2,1)S(1)}, bf16[192,256]{1,0:T(8,128)(2,1)S(1)}, u32[]{:S(2)}, u32[]{:S(2)}) collective-permute-start(bf16[192,256]{1,0:T(8,128)(2,1)S(1)} %get-tuple-element.45), channel_id=1, source_target_pairs={{0,30},{1,31},{2,4},{3,5},{4,2},{5,3},{6,8},{7,9},{8,6},{9,7},{10,... | collective-permute-start | bytes 294920 | tf_op jit(solution)/shard_map/ppermute | solution.py:50
  55.6 2.0 %collective-permute-start.20 = (f32[64,1,640]{2,1,0:T(1,128)S(1)}, f32[64,1,640]{2,1,0:T(1,128)S(1)}, u32[]{:S(2)}, u32[]{:S(2)}) collective-permute-start(f32[64,1,640]{2,1,0:T(1,128)S(1)} %get-tuple-element.49), channel_id=1, source_target_pairs={{0,2},{1,3},{2,0},{3,1},{4,6},{5,7},{6,4},{7,5},{8,10},{9,11},{10,... | collective-permute-start | bytes 491528 | tf_op jit(solution)/shard_map/ppermute | solution.py:50
  56.6 13.8 %collective-permute-start.21 = (bf16[4,128,256]{2,1,0:T(8,128)(2,1)S(1)}, bf16[4,128,256]{2,1,0:T(8,128)(2,1)S(1)}, u32[]{:S(2)}, u32[]{:S(2)}) collective-permute-start(bf16[4,128,256]{2,1,0:T(8,128)(2,1)S(1)} %get-tuple-element.42.s), channel_id=1, source_target_pairs={{0,1},{1,0},{2,3},{3,2},{4,5},{5,4},{6,7},{7,6},{8,9},{9,8},{10,11... | collective-permute-start | bytes 786440 | tf_op jit(solution)/shard_map/ppermute | solution.py:59
  58.5 23.5 %all-to-all-start = ((f32[64,1,640]{2,1,0:T(1,128)}), f32[64,1,640]{2,1,0:T(1,128)S(1)}, u32[]{:S(2)}, u32[]{:S(2)}) async-start(f32[64,1,640]{2,1,0:T(1,128)} %add.59), calls=%async_computation | async-start | bytes 327680 | tf_op jit(solution)/shard_map/all_to_all | solution.py:74
  102.5 5.2 %collective-permute-start.22 = (f32[128,1,640]{2,1,0:T(1,128)S(1)}, f32[128,1,640]{2,1,0:T(1,128)S(1)}, u32[]{:S(2)}, u32[]{:S(2)}) collective-permute-start(f32[128,1,640]{2,1,0:T(1,128)S(1)} %all_to_all.10.mine), channel_id=1, source_target_pairs={{0,2},{1,3},{2,0},{3,1},{4,6},{5,7},{6,4},{7,5},{8,10},{9,11},{10,... | collective-permute-start | bytes 983048 | tf_op jit(solution)/shard_map/ppermute | solution.py:50

commit v19 on v18

--- a/solution.py
+++ b/solution.py
@@ -202,7 +202,7 @@
     return lax.broadcasted_iota(jnp.int32, shape, 0), lax.broadcasted_iota(jnp.int32, shape, 1)
 
 
-def gram_kernel(m, o, turned, p, q, right, acc, corr, mine, theirs):
+def gram_kernel(m, o, turned, q, p, right, acc, corr, mine, theirs):
     side = 1 + m[PAR_X]
     parts = []
     for tile in range(4):
@@ -406,13 +406,13 @@
     second, p, q = apply_ham(first, p, q, [v, h_p, h_q], [shaped(block, BF), longer, longer])
 
     right = shift(sizes, second, -1, 0)
-    p, q = swap(sizes, p, 0, 1), swap(sizes, q, 0, 2)
+    q, p = swap(sizes, q, 0, 2), swap(sizes, p, 0, 1)
     corr, turned, acc = call(
         corr_kernel, m, [o, second], [shaped(full, F32), shaped((2 * T, 4 * T), BF), shaped(block, F32)], "corr", 15
     )
     piece = shaped((members // 2, 1, 5 * T), F32)
     mine, theirs = call(
-        gram_kernel, m, [o, turned, p, q, right, acc, corr], [piece, piece], "gram", 30
+        gram_kernel, m, [o, turned, q, p, right, acc, corr], [piece, piece], "gram", 30
     )
 
     rows = members * second.shape[0] * second.shape[1]

time: 187 us -> 187 us (level)
  starting transfers between devices: 50 us -> 53.4 us
  waiting for transfers between devices: 21.2 us -> 17.8 us
    ppermute x20, waiting for transfers between devices: 10.2 us -> 6.81 us  [swap(): return lax.ppermute(block, AXES, perm)]
    ppermute x20, starting transfers between devices: 32.7 us -> 36.1 us  [swap(): return lax.ppermute(block, AXES, perm)]
  transfers between devices with their start and end apart: 24 -> 24, of which waited for: 6 -> 5; matrix products, arithmetic and copies ran while one was open for 2% -> 2% of each run, Pallas kernels for 3% -> 3%
where the time goes in v19:
time: 187 us
  Pallas kernels  88.4 us (47%)
  starting transfers between devices  53.4 us (29%)
  blocking collectives  20.3 us (11%)
  waiting for transfers between devices  17.8 us (10%)
  local copies, waits for them, and re-layouts  3.12 us (2%)
  other arithmetic  2.86 us (2%)
    pallas_call x12, Pallas kernels, call(): pl.pallas_call(kernel, out_shape=outs, grid_spec=pltpu.PrefetchScalarGrid...  88.4 us
    ppermute x20, starting transfers between devices, swap(): return lax.ppermute(block, AXES, perm)  36.1 us
    all_to_all x1, blocking collectives, exchange(): lax.all_to_all(pieces, AXES, 0, 0, axis_index_groups=groups, tiled=True)  20.3 us
    all_to_all x1, starting transfers between devices, exchange(): lax.all_to_all(pieces, AXES, 0, 0, axis_index_groups=groups, tiled=True)  11.9 us
    all_to_all x1, waiting for transfers between devices, exchange(): lax.all_to_all(pieces, AXES, 0, 0, axis_index_groups=groups, tiled=True)  11 us
    ppermute x20, waiting for transfers between devices, swap(): return lax.ppermute(block, AXES, perm)  6.81 us
  transfers between devices with their start and end apart: 24, of which 5 were waited for; matrix products, arithmetic and copies ran while one was open for 2% of the time, Pallas kernels for 3%

profile of v19, /device:TPU:1, one launch (start us, length us, event | category | flops | bytes accessed | tf_op | source)
XLA Modules:
  0.0 186.7 jit_solution(11861616753596763610)
XLA Ops:
  0.6 1.0 dynamic-slice_bitcast_fusion
  1.6 3.7 %collective-permute-start = (bf16[4,128,128]{2,1,0:T(8,128)(2,1)S(1)}, bf16[4,128,128]{2,1,0:T(8,128)(2,1)S(1)}, u32[]{:S(2)}, u32[]{:S(2)}) collective-permute-start(bf16[4,128,128]{2,1,0:T(8,128)(2,1)S(1)} %get-tuple-element.53), channel_id=1, source_target_pairs={{0,1},{1,0},{2,3},{3,2},{4,5},{5,4},{6,7},{7,6},{8,9},{9,8},{10,11... | collective-permute-start | bytes 393224 | tf_op jit(solution)/shard_map/ppermute | solution.py:59
  6.2 1.0 select_reduce_fusion
  7.5 1.7 copy-done
  9.2 0.9 order.1
  10.7 3.4 %collective-permute-start.1 = (bf16[4,128,256]{2,1,0:T(8,128)(2,1)S(1)}, bf16[4,128,256]{2,1,0:T(8,128)(2,1)S(1)}, u32[]{:S(2)}, u32[]{:S(2)}) collective-permute-start(bf16[4,128,256]{2,1,0:T(8,128)(2,1)S(1)} %get-tuple-element.30.x.rest_0_), channel_id=1, source_target_pairs={{0,225},{1,224},{2,227},{3,226},{4,229},{5,228},{6,231},{7,230},{8... | collective-permute-start | bytes 786440 | tf_op jit(solution)/shard_map/ppermute | solution.py:50
  14.1 3.4 %collective-permute-start.5 = (bf16[144,256]{1,0:T(8,128)(2,1)S(1)}, bf16[144,256]{1,0:T(8,128)(2,1)S(1)}, u32[]{:S(2)}, u32[]{:S(2)}) collective-permute-start(bf16[144,256]{1,0:T(8,128)(2,1)S(1)} %get-tuple-element.33), channel_id=1, source_target_pairs={{0,30},{1,31},{2,4},{3,5},{4,2},{5,3},{6,8},{7,9},{8,6},{9,7},{10,... | collective-permute-start | bytes 221192 | tf_op jit(solution)/shard_map/ppermute | solution.py:50
  17.4 2.3 %collective-permute-done.5.q = bf16[144,256]{1,0:T(8,128)(2,1)S(1)} collective-permute-done((bf16[144,256]{1,0:T(8,128)(2,1)S(1)}, bf16[144,256]{1,0:T(8,128)(2,1)S(1)}, u32[]{:S(2)}, u32[]{:S(2)}) %collective-permute-start.5) | collective-permute-done | bytes 73760 | tf_op jit(solution)/shard_map/ppermute | solution.py:50
  19.7 1.4 collective-permute-start.6
  21.7 3.2 %collective-permute-start.8 = (bf16[128,256]{1,0:T(8,128)(2,1)S(1)}, bf16[128,256]{1,0:T(8,128)(2,1)S(1)}, u32[]{:S(2)}, u32[]{:S(2)}) collective-permute-start(bf16[128,256]{1,0:T(8,128)(2,1)S(1)} %get-tuple-element.34), channel_id=1, source_target_pairs={{0,2},{1,3},{2,0},{3,1},{4,6},{5,7},{6,4},{7,5},{8,10},{9,11},{10,... | collective-permute-start | bytes 196616 | tf_op jit(solution)/shard_map/ppermute | solution.py:50
  26.1 1.0 core.2.acc
  27.1 0.8 rim.2
  27.9 2.3 %collective-permute-start.9 = (bf16[4,128,256]{2,1,0:T(8,128)(2,1)S(1)}, bf16[4,128,256]{2,1,0:T(8,128)(2,1)S(1)}, u32[]{:S(2)}, u32[]{:S(2)}) collective-permute-start(bf16[4,128,256]{2,1,0:T(8,128)(2,1)S(1)} %get-tuple-element.35.x), channel_id=1, source_target_pairs={{0,225},{1,224},{2,227},{3,226},{4,229},{5,228},{6,231},{7,230},{8... | collective-permute-start | bytes 786440 | tf_op jit(solution)/shard_map/ppermute | solution.py:50
  30.2 1.6 collective-permute-start.13
  31.9 2.1 %collective-permute-done.13.q = bf16[144,256]{1,0:T(8,128)(2,1)S(1)} collective-permute-done((bf16[144,256]{1,0:T(8,128)(2,1)S(1)}, bf16[144,256]{1,0:T(8,128)(2,1)S(1)}, u32[]{:S(2)}, u32[]{:S(2)}) %collective-permute-start.13) | collective-permute-done | bytes 73760 | tf_op jit(solution)/shard_map/ppermute | solution.py:50
  34.0 3.2 %collective-permute-start.14 = (bf16[144,256]{1,0:T(8,128)(2,1)S(1)}, bf16[144,256]{1,0:T(8,128)(2,1)S(1)}, u32[]{:S(2)}, u32[]{:S(2)}) collective-permute-start(bf16[144,256]{1,0:T(8,128)(2,1)S(1)} %collective-permute-done.13.q), channel_id=1, source_target_pairs={{0,225},{1,224},{2,227},{3,226},{4,229},{5,228},{6,231},{7,230},{8... | collective-permute-start | bytes 221192 | tf_op jit(solution)/shard_map/ppermute | solution.py:50
  37.3 3.7 %collective-permute-start.16 = (bf16[128,256]{1,0:T(8,128)(2,1)S(1)}, bf16[128,256]{1,0:T(8,128)(2,1)S(1)}, u32[]{:S(2)}, u32[]{:S(2)}) collective-permute-start(bf16[128,256]{1,0:T(8,128)(2,1)S(1)} %get-tuple-element.39), channel_id=1, source_target_pairs={{0,2},{1,3},{2,0},{3,1},{4,6},{5,7},{6,4},{7,5},{8,10},{9,11},{10,... | collective-permute-start | bytes 196616 | tf_op jit(solution)/shard_map/ppermute | solution.py:50
  42.1 1.0 core.3.acc
  44.0 1.8 collective-permute-start.19
  45.8 2.4 %collective-permute-start.17 = (bf16[192,256]{1,0:T(8,128)(2,1)S(1)}, bf16[192,256]{1,0:T(8,128)(2,1)S(1)}, u32[]{:S(2)}, u32[]{:S(2)}) collective-permute-start(bf16[192,256]{1,0:T(8,128)(2,1)S(1)} %get-tuple-element.44), channel_id=1, source_target_pairs={{0,30},{1,31},{2,4},{3,5},{4,2},{5,3},{6,8},{7,9},{8,6},{9,7},{10,... | collective-permute-start | bytes 294920 | tf_op jit(solution)/shard_map/ppermute | solution.py:50
  48.2 3.1 %collective-permute-start.18 = (bf16[192,256]{1,0:T(8,128)(2,1)S(1)}, bf16[192,256]{1,0:T(8,128)(2,1)S(1)}, u32[]{:S(2)}, u32[]{:S(2)}) collective-permute-start(bf16[192,256]{1,0:T(8,128)(2,1)S(1)} %get-tuple-element.45), channel_id=1, source_target_pairs={{0,2},{1,3},{2,0},{3,1},{4,6},{5,7},{6,4},{7,5},{8,10},{9,11},{10,... | collective-permute-start | bytes 294920 | tf_op jit(solution)/shard_map/ppermute | solution.py:50
  51.3 0.9 corr.1
  52.3 1.7 gram.1
  54.0 2.6 %collective-permute-start.20 = (f32[64,1,640]{2,1,0:T(1,128)S(1)}, f32[64,1,640]{2,1,0:T(1,128)S(1)}, u32[]{:S(2)}, u32[]{:S(2)}) collective-permute-start(f32[64,1,640]{2,1,0:T(1,128)S(1)} %get-tuple-element.49), channel_id=1, source_target_pairs={{0,2},{1,3},{2,0},{3,1},{4,6},{5,7},{6,4},{7,5},{8,10},{9,11},{10,... | collective-permute-start | bytes 491528 | tf_op jit(solution)/shard_map/ppermute | solution.py:50
  56.6 1.0 collective-permute-done.20
  57.6 0.8 add.59
  58.5 11.9 %all-to-all-start = ((f32[64,1,640]{2,1,0:T(1,128)}), f32[64,1,640]{2,1,0:T(1,128)S(1)}, u32[]{:S(2)}, u32[]{:S(2)}) async-start(f32[64,1,640]{2,1,0:T(1,128)} %add.59), calls=%async_computation | async-start | bytes 327680 | tf_op jit(solution)/shard_map/all_to_all | solution.py:74
  70.9 11.0 %all-to-all-done = f32[64,1,640]{2,1,0:T(1,128)S(1)} async-done(((f32[64,1,640]{2,1,0:T(1,128)}), f32[64,1,640]{2,1,0:T(1,128)S(1)}, u32[]{:S(2)}, u32[]{:S(2)}) %all-to-all-start) | async-done | bytes 163872 | tf_op jit(solution)/shard_map/all_to_all | solution.py:74
  82.3 20.3 %all_to_all.10.mine = f32[128,1,640]{2,1,0:T(1,128)S(1)} all-to-all(f32[128,1,640]{2,1,0:T(1,128)S(1)} %broadcast_in_dim.20), channel_id=1, replica_groups={{0,4,8,12,16,20,24,28,32,36,40,44,48,52,56,60,65,69,73,77,81,85,89,93,9..., dimensions={0} | all-to-all | bytes 655360 | tf_op jit(solution)/shard_map/all_to_all | solution.py:74
  102.5 3.9 %collective-permute-start.22 = (f32[128,1,640]{2,1,0:T(1,128)S(1)}, f32[128,1,640]{2,1,0:T(1,128)S(1)}, u32[]{:S(2)}, u32[]{:S(2)}) collective-permute-start(f32[128,1,640]{2,1,0:T(1,128)S(1)} %all_to_all.10.mine), channel_id=1, source_target_pairs={{0,2},{1,3},{2,0},{3,1},{4,6},{5,7},{6,4},{7,5},{8,10},{9,11},{10,... | collective-permute-start | bytes 983048 | tf_op jit(solution)/shard_map/ppermute | solution.py:50
  106.5 1.3 collective-permute-done.22.theirs
  107.7 79.0 %final.1 = (bf16[2,1,4,128,128]{4,3,2,1,0:T(8,128)(2,1)}, f32[2,256,128]{2,1,0:T(8,128)}) custom-call(s32[40]{0:T(128)S(1)} %concatenate.7.m, f32[128,1,640]{2,1,0:T(1,128)S(1)} %all_to_all.10.mine, f32[128,1,640]{2,1,0:T(1,128)S(1)} %collective-permute-done.22.theirs, bf16[2,4,128,256]{3,2,1,0:T(8,128)(2,1)S(1)} %stack.29.both), custom_call_target="tpu_custom_call" | custom-call | flops 1677721600 | bytes 1703936 | tf_op jit(solution)/shard_map/final/pallas_call | solution.py:337
  (45 shorter events, 6.4 us)
Async XLA Ops:
  1.6 8.4 %collective-permute-start = (bf16[4,128,128]{2,1,0:T(8,128)(2,1)S(1)}, bf16[4,128,128]{2,1,0:T(8,128)(2,1)S(1)}, u32[]{:S(2)}, u32[]{:S(2)}) collective-permute-start(bf16[4,128,128]{2,1,0:T(8,128)(2,1)S(1)} %get-tuple-element.53), channel_id=1, source_target_pairs={{0,1},{1,0},{2,3},{3,2},{4,5},{5,4},{6,7},{7,6},{8,9},{9,8},{10,11... | collective-permute-start | bytes 393224 | tf_op jit(solution)/shard_map/ppermute | solution.py:59
  7.5 1.7 copy-start
  10.7 14.2 %collective-permute-start.1 = (bf16[4,128,256]{2,1,0:T(8,128)(2,1)S(1)}, bf16[4,128,256]{2,1,0:T(8,128)(2,1)S(1)}, u32[]{:S(2)}, u32[]{:S(2)}) collective-permute-start(bf16[4,128,256]{2,1,0:T(8,128)(2,1)S(1)} %get-tuple-element.30.x.rest_0_), channel_id=1, source_target_pairs={{0,225},{1,224},{2,227},{3,226},{4,229},{5,228},{6,231},{7,230},{8... | collective-permute-start | bytes 786440 | tf_op jit(solution)/shard_map/ppermute | solution.py:50
  14.1 10.8 %collective-permute-start.2 = (bf16[4,128,256]{2,1,0:T(8,128)(2,1)S(1)}, bf16[4,128,256]{2,1,0:T(8,128)(2,1)S(1)}, u32[]{:S(2)}, u32[]{:S(2)}) collective-permute-start(bf16[4,128,256]{2,1,0:T(8,128)(2,1)S(1)} %get-tuple-element.30.x.rest_0_), channel_id=1, source_target_pairs={{0,32},{1,33},{2,34},{3,35},{4,36},{5,37},{6,38},{7,39},{8,40},{9,... | collective-permute-start | bytes 786440 | tf_op jit(solution)/shard_map/ppermute | solution.py:50
  14.1 5.7 %collective-permute-start.5 = (bf16[144,256]{1,0:T(8,128)(2,1)S(1)}, bf16[144,256]{1,0:T(8,128)(2,1)S(1)}, u32[]{:S(2)}, u32[]{:S(2)}) collective-permute-start(bf16[144,256]{1,0:T(8,128)(2,1)S(1)} %get-tuple-element.33), channel_id=1, source_target_pairs={{0,30},{1,31},{2,4},{3,5},{4,2},{5,3},{6,8},{7,9},{8,6},{9,7},{10,... | collective-permute-start | bytes 221192 | tf_op jit(solution)/shard_map/ppermute | solution.py:50
  19.7 7.3 %collective-permute-start.6 = (bf16[144,256]{1,0:T(8,128)(2,1)S(1)}, bf16[144,256]{1,0:T(8,128)(2,1)S(1)}, u32[]{:S(2)}, u32[]{:S(2)}) collective-permute-start(bf16[144,256]{1,0:T(8,128)(2,1)S(1)} %collective-permute-done.5.q), channel_id=1, source_target_pairs={{0,225},{1,224},{2,227},{3,226},{4,229},{5,228},{6,231},{7,230},{8... | collective-permute-start | bytes 221192 | tf_op jit(solution)/shard_map/ppermute | solution.py:50
  21.1 6.0 %collective-permute-start.7 = (bf16[144,256]{1,0:T(8,128)(2,1)S(1)}, bf16[144,256]{1,0:T(8,128)(2,1)S(1)}, u32[]{:S(2)}, u32[]{:S(2)}) collective-permute-start(bf16[144,256]{1,0:T(8,128)(2,1)S(1)} %collective-permute-done.5.q), channel_id=1, source_target_pairs={{0,32},{1,33},{2,34},{3,35},{4,36},{5,37},{6,38},{7,39},{8,40},{9,... | collective-permute-start | bytes 221192 | tf_op jit(solution)/shard_map/ppermute | solution.py:50
  21.7 4.4 %collective-permute-start.8 = (bf16[128,256]{1,0:T(8,128)(2,1)S(1)}, bf16[128,256]{1,0:T(8,128)(2,1)S(1)}, u32[]{:S(2)}, u32[]{:S(2)}) collective-permute-start(bf16[128,256]{1,0:T(8,128)(2,1)S(1)} %get-tuple-element.34), channel_id=1, source_target_pairs={{0,2},{1,3},{2,0},{3,1},{4,6},{5,7},{6,4},{7,5},{8,10},{9,11},{10,... | collective-permute-start | bytes 196616 | tf_op jit(solution)/shard_map/ppermute | solution.py:50
  25.5 1.6 collective-permute-start.3
  25.6 1.6 collective-permute-start.4
  27.9 13.1 %collective-permute-start.9 = (bf16[4,128,256]{2,1,0:T(8,128)(2,1)S(1)}, bf16[4,128,256]{2,1,0:T(8,128)(2,1)S(1)}, u32[]{:S(2)}, u32[]{:S(2)}) collective-permute-start(bf16[4,128,256]{2,1,0:T(8,128)(2,1)S(1)} %get-tuple-element.35.x), channel_id=1, source_target_pairs={{0,225},{1,224},{2,227},{3,226},{4,229},{5,228},{6,231},{7,230},{8... | collective-permute-start | bytes 786440 | tf_op jit(solution)/shard_map/ppermute | solution.py:50
  30.2 10.7 %collective-permute-start.10 = (bf16[4,128,256]{2,1,0:T(8,128)(2,1)S(1)}, bf16[4,128,256]{2,1,0:T(8,128)(2,1)S(1)}, u32[]{:S(2)}, u32[]{:S(2)}) collective-permute-start(bf16[4,128,256]{2,1,0:T(8,128)(2,1)S(1)} %get-tuple-element.35.x), channel_id=1, source_target_pairs={{0,32},{1,33},{2,34},{3,35},{4,36},{5,37},{6,38},{7,39},{8,40},{9,... | collective-permute-start | bytes 786440 | tf_op jit(solution)/shard_map/ppermute | solution.py:50
  30.2 3.8 %collective-permute-start.13 = (bf16[144,256]{1,0:T(8,128)(2,1)S(1)}, bf16[144,256]{1,0:T(8,128)(2,1)S(1)}, u32[]{:S(2)}, u32[]{:S(2)}) collective-permute-start(bf16[144,256]{1,0:T(8,128)(2,1)S(1)} %get-tuple-element.38), channel_id=1, source_target_pairs={{0,30},{1,31},{2,4},{3,5},{4,2},{5,3},{6,8},{7,9},{8,6},{9,7},{10,... | collective-permute-start | bytes 221192 | tf_op jit(solution)/shard_map/ppermute | solution.py:50
  34.0 9.1 %collective-permute-start.14 = (bf16[144,256]{1,0:T(8,128)(2,1)S(1)}, bf16[144,256]{1,0:T(8,128)(2,1)S(1)}, u32[]{:S(2)}, u32[]{:S(2)}) collective-permute-start(bf16[144,256]{1,0:T(8,128)(2,1)S(1)} %collective-permute-done.13.q), channel_id=1, source_target_pairs={{0,225},{1,224},{2,227},{3,226},{4,229},{5,228},{6,231},{7,230},{8... | collective-permute-start | bytes 221192 | tf_op jit(solution)/shard_map/ppermute | solution.py:50
  37.3 5.9 %collective-permute-start.15 = (bf16[144,256]{1,0:T(8,128)(2,1)S(1)}, bf16[144,256]{1,0:T(8,128)(2,1)S(1)}, u32[]{:S(2)}, u32[]{:S(2)}) collective-permute-start(bf16[144,256]{1,0:T(8,128)(2,1)S(1)} %collective-permute-done.13.q), channel_id=1, source_target_pairs={{0,32},{1,33},{2,34},{3,35},{4,36},{5,37},{6,38},{7,39},{8,40},{9,... | collective-permute-start | bytes 221192 | tf_op jit(solution)/shard_map/ppermute | solution.py:50
  37.3 4.9 %collective-permute-start.16 = (bf16[128,256]{1,0:T(8,128)(2,1)S(1)}, bf16[128,256]{1,0:T(8,128)(2,1)S(1)}, u32[]{:S(2)}, u32[]{:S(2)}) collective-permute-start(bf16[128,256]{1,0:T(8,128)(2,1)S(1)} %get-tuple-element.39), channel_id=1, source_target_pairs={{0,2},{1,3},{2,0},{3,1},{4,6},{5,7},{6,4},{7,5},{8,10},{9,11},{10,... | collective-permute-start | bytes 196616 | tf_op jit(solution)/shard_map/ppermute | solution.py:50
  41.5 1.7 collective-permute-start.11
  41.6 1.6 collective-permute-start.12
  44.0 8.3 %collective-permute-start.19 = (bf16[4,128,256]{2,1,0:T(8,128)(2,1)S(1)}, bf16[4,128,256]{2,1,0:T(8,128)(2,1)S(1)}, u32[]{:S(2)}, u32[]{:S(2)}) collective-permute-start(bf16[4,128,256]{2,1,0:T(8,128)(2,1)S(1)} %get-tuple-element.42.s), channel_id=1, source_target_pairs={{0,225},{1,224},{2,227},{3,226},{4,229},{5,228},{6,231},{7,230},{8... | collective-permute-start | bytes 786440 | tf_op jit(solution)/shard_map/ppermute | solution.py:54
  45.8 6.4 %collective-permute-start.17 = (bf16[192,256]{1,0:T(8,128)(2,1)S(1)}, bf16[192,256]{1,0:T(8,128)(2,1)S(1)}, u32[]{:S(2)}, u32[]{:S(2)}) collective-permute-start(bf16[192,256]{1,0:T(8,128)(2,1)S(1)} %get-tuple-element.44), channel_id=1, source_target_pairs={{0,30},{1,31},{2,4},{3,5},{4,2},{5,3},{6,8},{7,9},{8,6},{9,7},{10,... | collective-permute-start | bytes 294920 | tf_op jit(solution)/shard_map/ppermute | solution.py:50
  48.2 4.0 %collective-permute-start.18 = (bf16[192,256]{1,0:T(8,128)(2,1)S(1)}, bf16[192,256]{1,0:T(8,128)(2,1)S(1)}, u32[]{:S(2)}, u32[]{:S(2)}) collective-permute-start(bf16[192,256]{1,0:T(8,128)(2,1)S(1)} %get-tuple-element.45), channel_id=1, source_target_pairs={{0,2},{1,3},{2,0},{3,1},{4,6},{5,7},{6,4},{7,5},{8,10},{9,11},{10,... | collective-permute-start | bytes 294920 | tf_op jit(solution)/shard_map/ppermute | solution.py:50
  54.0 3.6 %collective-permute-start.20 = (f32[64,1,640]{2,1,0:T(1,128)S(1)}, f32[64,1,640]{2,1,0:T(1,128)S(1)}, u32[]{:S(2)}, u32[]{:S(2)}) collective-permute-start(f32[64,1,640]{2,1,0:T(1,128)S(1)} %get-tuple-element.49), channel_id=1, source_target_pairs={{0,2},{1,3},{2,0},{3,1},{4,6},{5,7},{6,4},{7,5},{8,10},{9,11},{10,... | collective-permute-start | bytes 491528 | tf_op jit(solution)/shard_map/ppermute | solution.py:50
  56.6 13.8 %collective-permute-start.21 = (bf16[4,128,256]{2,1,0:T(8,128)(2,1)S(1)}, bf16[4,128,256]{2,1,0:T(8,128)(2,1)S(1)}, u32[]{:S(2)}, u32[]{:S(2)}) collective-permute-start(bf16[4,128,256]{2,1,0:T(8,128)(2,1)S(1)} %get-tuple-element.42.s), channel_id=1, source_target_pairs={{0,1},{1,0},{2,3},{3,2},{4,5},{5,4},{6,7},{7,6},{8,9},{9,8},{10,11... | collective-permute-start | bytes 786440 | tf_op jit(solution)/shard_map/ppermute | solution.py:59
  58.5 23.5 %all-to-all-start = ((f32[64,1,640]{2,1,0:T(1,128)}), f32[64,1,640]{2,1,0:T(1,128)S(1)}, u32[]{:S(2)}, u32[]{:S(2)}) async-start(f32[64,1,640]{2,1,0:T(1,128)} %add.59), calls=%async_computation | async-start | bytes 327680 | tf_op jit(solution)/shard_map/all_to_all | solution.py:74
  102.5 5.2 %collective-permute-start.22 = (f32[128,1,640]{2,1,0:T(1,128)S(1)}, f32[128,1,640]{2,1,0:T(1,128)S(1)}, u32[]{:S(2)}, u32[]{:S(2)}) collective-permute-start(f32[128,1,640]{2,1,0:T(1,128)S(1)} %all_to_all.10.mine), channel_id=1, source_target_pairs={{0,2},{1,3},{2,0},{3,1},{4,6},{5,7},{6,4},{7,5},{8,10},{9,11},{10,... | collective-permute-start | bytes 983048 | tf_op jit(solution)/shard_map/ppermute | solution.py:50

commit v20 on v18

--- a/solution.py
+++ b/solution.py
@@ -125,7 +125,11 @@
     v[:, :, :T] = jnp.where(first_col, own[...], other[...])
     v[:, :, T:] = jnp.where(first_col, other[...], own[...])
     store_edges(m, v, p, q)
-    q[T:] = v[0, : q.shape[0] - T]
+
+
+def corner_kernel(m, q, out):
+    out[:T] = q[...]
+    out[T:] = q[: out.shape[0] - T]
 
 
 def edge_kernel(m, b, a, a_out, b_out):
@@ -152,7 +156,7 @@
 
 
 def core_kernel(m, o, x, p, q, b, a, acc, ext):
-    ext[0], ext[5] = low_high(m, p[...], q[:T])
+    ext[0], ext[5] = low_high(m, p[...], q[...])
     ext[1:5] = x[...]
     for tile in range(4):
         total = product(o, tile, (0,), range(tile, tile + 3), [ext[tile : tile + 3]])
@@ -182,8 +186,6 @@
         for to, block in ((p, h_p), (q, h_q)):
             to[T:, :T] = block[: T // 2]
             to[T:, T:] = block[T // 2 :]
-    else:
-        q[T:] = out[0, : q.shape[0] - T]
 
 
 def corr_kernel(m, o, s, corr, turned, acc):
@@ -386,13 +388,14 @@
     tile = shaped((T, 2 * T), BF)
     ext = pltpu.VMEM((6, T, 2 * T), BF)
     other, o = lax.optimization_barrier((other, o))
-    outs = [shaped(block, BF), tile, shaped((T + 16, 2 * T), BF)]
+    outs = [shaped(block, BF), tile, tile]
     v, p, q = call(join_kernel, m, [own, other], outs, "join")
 
     def apply_ham(x, p, q, more, outs):
         p, q = swap(sizes, p, 0, 1), swap(sizes, q, 0, 2)
         b, a = swap(sizes, x, 2, 0), swap(sizes, x, 1, 0)
-        b_corner, a_corner = swap(sizes, q, 2, 0), swap(sizes, q, 1, 0)
+        (corner,) = call(corner_kernel, m, [q], [shaped((T + 16, 2 * T), BF)], "corner", 300)
+        b_corner, a_corner = swap(sizes, corner, 2, 0), swap(sizes, corner, 1, 0)
         a_edge, b_edge = call(edge_kernel, m, [b, a], [tile, tile], "edge", free=True)
         a_edge, b_edge = swap(sizes, a_edge, 0, 1), swap(sizes, b_edge, 0, 1)
         (acc,) = call(

time: 187 us -> 188 us (level)
  starting transfers between devices: 50 us -> 53.6 us
  waiting for transfers between devices: 21.2 us -> 17.8 us
    ppermute x20, waiting for transfers between devices: 10.2 us -> 6.36 us  [swap(): return lax.ppermute(block, AXES, perm)]
    pallas_call x12 -> x14, Pallas kernels: 88.4 us -> 89.4 us  [call(): pl.pallas_call(kernel, out_shape=outs, grid_spec=pltpu.PrefetchScalarGrid...]
  transfers between devices with their start and end apart: 24 -> 24, of which waited for: 6 -> 9; matrix products, arithmetic and copies ran while one was open for 2% -> 2% of each run, Pallas kernels for 3% -> 3%
where the time goes in v20:
time: 188 us
  Pallas kernels  89.4 us (48%)
  starting transfers between devices  53.6 us (29%)
  blocking collectives  20.3 us (11%)
  waiting for transfers between devices  17.8 us (9%)
  local copies, waits for them, and re-layouts  3.12 us (2%)
  other arithmetic  2.86 us (2%)
    pallas_call x14, Pallas kernels, call(): pl.pallas_call(kernel, out_shape=outs, grid_spec=pltpu.PrefetchScalarGrid...  89.4 us
    ppermute x20, starting transfers between devices, swap(): return lax.ppermute(block, AXES, perm)  34.3 us
    all_to_all x1, blocking collectives, exchange(): lax.all_to_all(pieces, AXES, 0, 0, axis_index_groups=groups, tiled=True)  20.3 us
    all_to_all x1, starting transfers between devices, exchange(): lax.all_to_all(pieces, AXES, 0, 0, axis_index_groups=groups, tiled=True)  12.5 us
    all_to_all x1, waiting for transfers between devices, exchange(): lax.all_to_all(pieces, AXES, 0, 0, axis_index_groups=groups, tiled=True)  11 us
    ppermute x20, waiting for transfers between devices, swap(): return lax.ppermute(block, AXES, perm)  6.36 us
  transfers between devices with their start and end apart: 24, of which 9 were waited for; matrix products, arithmetic and copies ran while one was open for 2% of the time, Pallas kernels for 3%

profile of v20, /device:TPU:1, one launch (start us, length us, event | category | flops | bytes accessed | tf_op | source)
XLA Modules:
  0.0 187.9 jit_solution(4218129209885848835)
XLA Ops:
  0.6 1.0 dynamic-slice_bitcast_fusion
  1.6 3.7 %collective-permute-start = (bf16[4,128,128]{2,1,0:T(8,128)(2,1)S(1)}, bf16[4,128,128]{2,1,0:T(8,128)(2,1)S(1)}, u32[]{:S(2)}, u32[]{:S(2)}) collective-permute-start(bf16[4,128,128]{2,1,0:T(8,128)(2,1)S(1)} %get-tuple-element.53), channel_id=1, source_target_pairs={{0,1},{1,0},{2,3},{3,2},{4,5},{5,4},{6,7},{7,6},{8,9},{9,8},{10,11... | collective-permute-start | bytes 393224 | tf_op jit(solution)/shard_map/ppermute | solution.py:59
  6.2 1.0 select_reduce_fusion
  7.5 1.7 copy-done
  9.2 0.9 order.1
  10.7 2.6 %collective-permute-start.5 = (bf16[128,256]{1,0:T(8,128)(2,1)S(1)}, bf16[128,256]{1,0:T(8,128)(2,1)S(1)}, u32[]{:S(2)}, u32[]{:S(2)}) collective-permute-start(bf16[128,256]{1,0:T(8,128)(2,1)S(1)} %get-tuple-element.33), channel_id=1, source_target_pairs={{0,30},{1,31},{2,4},{3,5},{4,2},{5,3},{6,8},{7,9},{8,6},{9,7},{10,... | collective-permute-start | bytes 196616 | tf_op jit(solution)/shard_map/ppermute | solution.py:50
  13.2 3.9 %collective-permute-start.1 = (bf16[4,128,256]{2,1,0:T(8,128)(2,1)S(1)}, bf16[4,128,256]{2,1,0:T(8,128)(2,1)S(1)}, u32[]{:S(2)}, u32[]{:S(2)}) collective-permute-start(bf16[4,128,256]{2,1,0:T(8,128)(2,1)S(1)} %get-tuple-element.30.x.rest_0_), channel_id=1, source_target_pairs={{0,225},{1,224},{2,227},{3,226},{4,229},{5,228},{6,231},{7,230},{8... | collective-permute-start | bytes 786440 | tf_op jit(solution)/shard_map/ppermute | solution.py:50
  17.7 2.0 %collective-permute-start.6 = (bf16[144,256]{1,0:T(8,128)(2,1)S(1)}, bf16[144,256]{1,0:T(8,128)(2,1)S(1)}, u32[]{:S(2)}, u32[]{:S(2)}) collective-permute-start(bf16[144,256]{1,0:T(8,128)(2,1)S(1)} %corner.2), channel_id=1, source_target_pairs={{0,225},{1,224},{2,227},{3,226},{4,229},{5,228},{6,231},{7,230},{8... | collective-permute-start | bytes 221192 | tf_op jit(solution)/shard_map/ppermute | solution.py:50
  19.7 4.3 %collective-permute-start.8 = (bf16[128,256]{1,0:T(8,128)(2,1)S(1)}, bf16[128,256]{1,0:T(8,128)(2,1)S(1)}, u32[]{:S(2)}, u32[]{:S(2)}) collective-permute-start(bf16[128,256]{1,0:T(8,128)(2,1)S(1)} %get-tuple-element.34), channel_id=1, source_target_pairs={{0,2},{1,3},{2,0},{3,1},{4,6},{5,7},{6,4},{7,5},{8,10},{9,11},{10,... | collective-permute-start | bytes 196616 | tf_op jit(solution)/shard_map/ppermute | solution.py:50
  24.6 3.2 %collective-permute-start.3 = (bf16[128,256]{1,0:T(8,128)(2,1)S(1)}, bf16[128,256]{1,0:T(8,128)(2,1)S(1)}, u32[]{:S(2)}, u32[]{:S(2)}) collective-permute-start(bf16[128,256]{1,0:T(8,128)(2,1)S(1)} %get-tuple-element.31), channel_id=1, source_target_pairs={{0,2},{1,3},{2,0},{3,1},{4,6},{5,7},{6,4},{7,5},{8,10},{9,11},{10,... | collective-permute-start | bytes 196616 | tf_op jit(solution)/shard_map/ppermute | solution.py:50
  28.0 1.0 core.2.acc
  30.2 3.0 %collective-permute-start.9 = (bf16[4,128,256]{2,1,0:T(8,128)(2,1)S(1)}, bf16[4,128,256]{2,1,0:T(8,128)(2,1)S(1)}, u32[]{:S(2)}, u32[]{:S(2)}) collective-permute-start(bf16[4,128,256]{2,1,0:T(8,128)(2,1)S(1)} %get-tuple-element.35.x), channel_id=1, source_target_pairs={{0,225},{1,224},{2,227},{3,226},{4,229},{5,228},{6,231},{7,230},{8... | collective-permute-start | bytes 786440 | tf_op jit(solution)/shard_map/ppermute | solution.py:50
  34.2 2.8 %collective-permute-start.14 = (bf16[144,256]{1,0:T(8,128)(2,1)S(1)}, bf16[144,256]{1,0:T(8,128)(2,1)S(1)}, u32[]{:S(2)}, u32[]{:S(2)}) collective-permute-start(bf16[144,256]{1,0:T(8,128)(2,1)S(1)} %corner.3), channel_id=1, source_target_pairs={{0,225},{1,224},{2,227},{3,226},{4,229},{5,228},{6,231},{7,230},{8... | collective-permute-start | bytes 221192 | tf_op jit(solution)/shard_map/ppermute | solution.py:50
  37.1 1.8 collective-permute-start.16
  38.9 0.9 collective-permute-done.9.b
  40.4 3.3 %collective-permute-start.11 = (bf16[128,256]{1,0:T(8,128)(2,1)S(1)}, bf16[128,256]{1,0:T(8,128)(2,1)S(1)}, u32[]{:S(2)}, u32[]{:S(2)}) collective-permute-start(bf16[128,256]{1,0:T(8,128)(2,1)S(1)} %get-tuple-element.36), channel_id=1, source_target_pairs={{0,2},{1,3},{2,0},{3,1},{4,6},{5,7},{6,4},{7,5},{8,10},{9,11},{10,... | collective-permute-start | bytes 196616 | tf_op jit(solution)/shard_map/ppermute | solution.py:50
  43.8 1.0 core.3.acc
  44.9 0.8 rim.3
  45.7 3.1 %collective-permute-start.19 = (bf16[4,128,256]{2,1,0:T(8,128)(2,1)S(1)}, bf16[4,128,256]{2,1,0:T(8,128)(2,1)S(1)}, u32[]{:S(2)}, u32[]{:S(2)}) collective-permute-start(bf16[4,128,256]{2,1,0:T(8,128)(2,1)S(1)} %get-tuple-element.42.s), channel_id=1, source_target_pairs={{0,225},{1,224},{2,227},{3,226},{4,229},{5,228},{6,231},{7,230},{8... | collective-permute-start | bytes 786440 | tf_op jit(solution)/shard_map/ppermute | solution.py:54
  49.4 0.9 collective-permute-start.18
  50.3 0.9 corr.1
  51.3 2.5 %collective-permute-done.18.q = bf16[192,256]{1,0:T(8,128)(2,1)S(1)} collective-permute-done((bf16[192,256]{1,0:T(8,128)(2,1)S(1)}, bf16[192,256]{1,0:T(8,128)(2,1)S(1)}, u32[]{:S(2)}, u32[]{:S(2)}) %collective-permute-start.18) | collective-permute-done | bytes 98336 | tf_op jit(solution)/shard_map/ppermute | solution.py:50
  54.2 1.7 gram.1
  56.0 1.2 collective-permute-start.20
  57.2 1.0 collective-permute-done.20
  58.2 0.8 add.59
  59.0 12.5 %all-to-all-start = ((f32[64,1,640]{2,1,0:T(1,128)}), f32[64,1,640]{2,1,0:T(1,128)S(1)}, u32[]{:S(2)}, u32[]{:S(2)}) async-start(f32[64,1,640]{2,1,0:T(1,128)} %add.59), calls=%async_computation | async-start | bytes 327680 | tf_op jit(solution)/shard_map/all_to_all | solution.py:74
  72.1 11.0 %all-to-all-done = f32[64,1,640]{2,1,0:T(1,128)S(1)} async-done(((f32[64,1,640]{2,1,0:T(1,128)}), f32[64,1,640]{2,1,0:T(1,128)S(1)}, u32[]{:S(2)}, u32[]{:S(2)}) %all-to-all-start) | async-done | bytes 163872 | tf_op jit(solution)/shard_map/all_to_all | solution.py:74
  83.4 20.3 %all_to_all.10.mine = f32[128,1,640]{2,1,0:T(1,128)S(1)} all-to-all(f32[128,1,640]{2,1,0:T(1,128)S(1)} %broadcast_in_dim.20), channel_id=1, replica_groups={{0,4,8,12,16,20,24,28,32,36,40,44,48,52,56,60,65,69,73,77,81,85,89,93,9..., dimensions={0} | all-to-all | bytes 655360 | tf_op jit(solution)/shard_map/all_to_all | solution.py:74
  103.7 3.9 %collective-permute-start.22 = (f32[128,1,640]{2,1,0:T(1,128)S(1)}, f32[128,1,640]{2,1,0:T(1,128)S(1)}, u32[]{:S(2)}, u32[]{:S(2)}) collective-permute-start(f32[128,1,640]{2,1,0:T(1,128)S(1)} %all_to_all.10.mine), channel_id=1, source_target_pairs={{0,2},{1,3},{2,0},{3,1},{4,6},{5,7},{6,4},{7,5},{8,10},{9,11},{10,... | collective-permute-start | bytes 983048 | tf_op jit(solution)/shard_map/ppermute | solution.py:50
  107.6 1.3 collective-permute-done.22.theirs
  108.9 79.0 %final.1 = (bf16[2,1,4,128,128]{4,3,2,1,0:T(8,128)(2,1)}, f32[2,256,128]{2,1,0:T(8,128)}) custom-call(s32[40]{0:T(128)S(1)} %concatenate.7.m, f32[128,1,640]{2,1,0:T(1,128)S(1)} %all_to_all.10.mine, f32[128,1,640]{2,1,0:T(1,128)S(1)} %collective-permute-done.22.theirs, bf16[2,4,128,256]{3,2,1,0:T(8,128)(2,1)S(1)} %stack.29.both), custom_call_target="tpu_custom_call" | custom-call | flops 1677721600 | bytes 1703936 | tf_op jit(solution)/shard_map/final/pallas_call | solution.py:339
  (47 shorter events, 7.9 us)
Async XLA Ops:
  1.6 8.4 %collective-permute-start = (bf16[4,128,128]{2,1,0:T(8,128)(2,1)S(1)}, bf16[4,128,128]{2,1,0:T(8,128)(2,1)S(1)}, u32[]{:S(2)}, u32[]{:S(2)}) collective-permute-start(bf16[4,128,128]{2,1,0:T(8,128)(2,1)S(1)} %get-tuple-element.53), channel_id=1, source_target_pairs={{0,1},{1,0},{2,3},{3,2},{4,5},{5,4},{6,7},{7,6},{8,9},{9,8},{10,11... | collective-permute-start | bytes 393224 | tf_op jit(solution)/shard_map/ppermute | solution.py:59
  7.5 1.7 copy-start
  10.7 6.5 %collective-permute-start.5 = (bf16[128,256]{1,0:T(8,128)(2,1)S(1)}, bf16[128,256]{1,0:T(8,128)(2,1)S(1)}, u32[]{:S(2)}, u32[]{:S(2)}) collective-permute-start(bf16[128,256]{1,0:T(8,128)(2,1)S(1)} %get-tuple-element.33), channel_id=1, source_target_pairs={{0,30},{1,31},{2,4},{3,5},{4,2},{5,3},{6,8},{7,9},{8,6},{9,7},{10,... | collective-permute-start | bytes 196616 | tf_op jit(solution)/shard_map/ppermute | solution.py:50
  13.2 10.8 %collective-permute-start.1 = (bf16[4,128,256]{2,1,0:T(8,128)(2,1)S(1)}, bf16[4,128,256]{2,1,0:T(8,128)(2,1)S(1)}, u32[]{:S(2)}, u32[]{:S(2)}) collective-permute-start(bf16[4,128,256]{2,1,0:T(8,128)(2,1)S(1)} %get-tuple-element.30.x.rest_0_), channel_id=1, source_target_pairs={{0,225},{1,224},{2,227},{3,226},{4,229},{5,228},{6,231},{7,230},{8... | collective-permute-start | bytes 786440 | tf_op jit(solution)/shard_map/ppermute | solution.py:50
  17.1 6.9 %collective-permute-start.2 = (bf16[4,128,256]{2,1,0:T(8,128)(2,1)S(1)}, bf16[4,128,256]{2,1,0:T(8,128)(2,1)S(1)}, u32[]{:S(2)}, u32[]{:S(2)}) collective-permute-start(bf16[4,128,256]{2,1,0:T(8,128)(2,1)S(1)} %get-tuple-element.30.x.rest_0_), channel_id=1, source_target_pairs={{0,32},{1,33},{2,34},{3,35},{4,36},{5,37},{6,38},{7,39},{8,40},{9,... | collective-permute-start | bytes 786440 | tf_op jit(solution)/shard_map/ppermute | solution.py:50
  17.7 11.3 %collective-permute-start.6 = (bf16[144,256]{1,0:T(8,128)(2,1)S(1)}, bf16[144,256]{1,0:T(8,128)(2,1)S(1)}, u32[]{:S(2)}, u32[]{:S(2)}) collective-permute-start(bf16[144,256]{1,0:T(8,128)(2,1)S(1)} %corner.2), channel_id=1, source_target_pairs={{0,225},{1,224},{2,227},{3,226},{4,229},{5,228},{6,231},{7,230},{8... | collective-permute-start | bytes 221192 | tf_op jit(solution)/shard_map/ppermute | solution.py:50
  19.7 9.3 %collective-permute-start.7 = (bf16[144,256]{1,0:T(8,128)(2,1)S(1)}, bf16[144,256]{1,0:T(8,128)(2,1)S(1)}, u32[]{:S(2)}, u32[]{:S(2)}) collective-permute-start(bf16[144,256]{1,0:T(8,128)(2,1)S(1)} %corner.2), channel_id=1, source_target_pairs={{0,32},{1,33},{2,34},{3,35},{4,36},{5,37},{6,38},{7,39},{8,40},{9,... | collective-permute-start | bytes 221192 | tf_op jit(solution)/shard_map/ppermute | solution.py:50
  19.7 8.2 %collective-permute-start.8 = (bf16[128,256]{1,0:T(8,128)(2,1)S(1)}, bf16[128,256]{1,0:T(8,128)(2,1)S(1)}, u32[]{:S(2)}, u32[]{:S(2)}) collective-permute-start(bf16[128,256]{1,0:T(8,128)(2,1)S(1)} %get-tuple-element.34), channel_id=1, source_target_pairs={{0,2},{1,3},{2,0},{3,1},{4,6},{5,7},{6,4},{7,5},{8,10},{9,11},{10,... | collective-permute-start | bytes 196616 | tf_op jit(solution)/shard_map/ppermute | solution.py:50
  24.6 4.4 %collective-permute-start.3 = (bf16[128,256]{1,0:T(8,128)(2,1)S(1)}, bf16[128,256]{1,0:T(8,128)(2,1)S(1)}, u32[]{:S(2)}, u32[]{:S(2)}) collective-permute-start(bf16[128,256]{1,0:T(8,128)(2,1)S(1)} %get-tuple-element.31), channel_id=1, source_target_pairs={{0,2},{1,3},{2,0},{3,1},{4,6},{5,7},{6,4},{7,5},{8,10},{9,11},{10,... | collective-permute-start | bytes 196616 | tf_op jit(solution)/shard_map/ppermute | solution.py:50
  27.9 1.3 collective-permute-start.4
  29.9 3.8 %collective-permute-start.13 = (bf16[128,256]{1,0:T(8,128)(2,1)S(1)}, bf16[128,256]{1,0:T(8,128)(2,1)S(1)}, u32[]{:S(2)}, u32[]{:S(2)}) collective-permute-start(bf16[128,256]{1,0:T(8,128)(2,1)S(1)} %get-tuple-element.38), channel_id=1, source_target_pairs={{0,30},{1,31},{2,4},{3,5},{4,2},{5,3},{6,8},{7,9},{8,6},{9,7},{10,... | collective-permute-start | bytes 196616 | tf_op jit(solution)/shard_map/ppermute | solution.py:50
  30.2 9.6 %collective-permute-start.9 = (bf16[4,128,256]{2,1,0:T(8,128)(2,1)S(1)}, bf16[4,128,256]{2,1,0:T(8,128)(2,1)S(1)}, u32[]{:S(2)}, u32[]{:S(2)}) collective-permute-start(bf16[4,128,256]{2,1,0:T(8,128)(2,1)S(1)} %get-tuple-element.35.x), channel_id=1, source_target_pairs={{0,225},{1,224},{2,227},{3,226},{4,229},{5,228},{6,231},{7,230},{8... | collective-permute-start | bytes 786440 | tf_op jit(solution)/shard_map/ppermute | solution.py:50
  33.2 6.6 %collective-permute-start.10 = (bf16[4,128,256]{2,1,0:T(8,128)(2,1)S(1)}, bf16[4,128,256]{2,1,0:T(8,128)(2,1)S(1)}, u32[]{:S(2)}, u32[]{:S(2)}) collective-permute-start(bf16[4,128,256]{2,1,0:T(8,128)(2,1)S(1)} %get-tuple-element.35.x), channel_id=1, source_target_pairs={{0,32},{1,33},{2,34},{3,35},{4,36},{5,37},{6,38},{7,39},{8,40},{9,... | collective-permute-start | bytes 786440 | tf_op jit(solution)/shard_map/ppermute | solution.py:50
  34.2 10.6 %collective-permute-start.14 = (bf16[144,256]{1,0:T(8,128)(2,1)S(1)}, bf16[144,256]{1,0:T(8,128)(2,1)S(1)}, u32[]{:S(2)}, u32[]{:S(2)}) collective-permute-start(bf16[144,256]{1,0:T(8,128)(2,1)S(1)} %corner.3), channel_id=1, source_target_pairs={{0,225},{1,224},{2,227},{3,226},{4,229},{5,228},{6,231},{7,230},{8... | collective-permute-start | bytes 221192 | tf_op jit(solution)/shard_map/ppermute | solution.py:50
  37.1 7.8 %collective-permute-start.15 = (bf16[144,256]{1,0:T(8,128)(2,1)S(1)}, bf16[144,256]{1,0:T(8,128)(2,1)S(1)}, u32[]{:S(2)}, u32[]{:S(2)}) collective-permute-start(bf16[144,256]{1,0:T(8,128)(2,1)S(1)} %corner.3), channel_id=1, source_target_pairs={{0,32},{1,33},{2,34},{3,35},{4,36},{5,37},{6,38},{7,39},{8,40},{9,... | collective-permute-start | bytes 221192 | tf_op jit(solution)/shard_map/ppermute | solution.py:50
  37.1 6.7 %collective-permute-start.16 = (bf16[128,256]{1,0:T(8,128)(2,1)S(1)}, bf16[128,256]{1,0:T(8,128)(2,1)S(1)}, u32[]{:S(2)}, u32[]{:S(2)}) collective-permute-start(bf16[128,256]{1,0:T(8,128)(2,1)S(1)} %get-tuple-element.39), channel_id=1, source_target_pairs={{0,2},{1,3},{2,0},{3,1},{4,6},{5,7},{6,4},{7,5},{8,10},{9,11},{10,... | collective-permute-start | bytes 196616 | tf_op jit(solution)/shard_map/ppermute | solution.py:50
  40.4 4.5 %collective-permute-start.11 = (bf16[128,256]{1,0:T(8,128)(2,1)S(1)}, bf16[128,256]{1,0:T(8,128)(2,1)S(1)}, u32[]{:S(2)}, u32[]{:S(2)}) collective-permute-start(bf16[128,256]{1,0:T(8,128)(2,1)S(1)} %get-tuple-element.36), channel_id=1, source_target_pairs={{0,2},{1,3},{2,0},{3,1},{4,6},{5,7},{6,4},{7,5},{8,10},{9,11},{10,... | collective-permute-start | bytes 196616 | tf_op jit(solution)/shard_map/ppermute | solution.py:50
  43.7 1.3 collective-permute-start.12
  45.7 8.5 %collective-permute-start.19 = (bf16[4,128,256]{2,1,0:T(8,128)(2,1)S(1)}, bf16[4,128,256]{2,1,0:T(8,128)(2,1)S(1)}, u32[]{:S(2)}, u32[]{:S(2)}) collective-permute-start(bf16[4,128,256]{2,1,0:T(8,128)(2,1)S(1)} %get-tuple-element.42.s), channel_id=1, source_target_pairs={{0,225},{1,224},{2,227},{3,226},{4,229},{5,228},{6,231},{7,230},{8... | collective-permute-start | bytes 786440 | tf_op jit(solution)/shard_map/ppermute | solution.py:54
  48.8 2.4 %collective-permute-start.17 = (bf16[192,256]{1,0:T(8,128)(2,1)S(1)}, bf16[192,256]{1,0:T(8,128)(2,1)S(1)}, u32[]{:S(2)}, u32[]{:S(2)}) collective-permute-start(bf16[192,256]{1,0:T(8,128)(2,1)S(1)} %get-tuple-element.44), channel_id=1, source_target_pairs={{0,2},{1,3},{2,0},{3,1},{4,6},{5,7},{6,4},{7,5},{8,10},{9,11},{10,... | collective-permute-start | bytes 294920 | tf_op jit(solution)/shard_map/ppermute | solution.py:50
  49.4 4.3 %collective-permute-start.18 = (bf16[192,256]{1,0:T(8,128)(2,1)S(1)}, bf16[192,256]{1,0:T(8,128)(2,1)S(1)}, u32[]{:S(2)}, u32[]{:S(2)}) collective-permute-start(bf16[192,256]{1,0:T(8,128)(2,1)S(1)} %get-tuple-element.45), channel_id=1, source_target_pairs={{0,30},{1,31},{2,4},{3,5},{4,2},{5,3},{6,8},{7,9},{8,6},{9,7},{10,... | collective-permute-start | bytes 294920 | tf_op jit(solution)/shard_map/ppermute | solution.py:50
  56.0 2.3 %collective-permute-start.20 = (f32[64,1,640]{2,1,0:T(1,128)S(1)}, f32[64,1,640]{2,1,0:T(1,128)S(1)}, u32[]{:S(2)}, u32[]{:S(2)}) collective-permute-start(f32[64,1,640]{2,1,0:T(1,128)S(1)} %get-tuple-element.49), channel_id=1, source_target_pairs={{0,2},{1,3},{2,0},{3,1},{4,6},{5,7},{6,4},{7,5},{8,10},{9,11},{10,... | collective-permute-start | bytes 491528 | tf_op jit(solution)/shard_map/ppermute | solution.py:50
  57.2 14.4 %collective-permute-start.21 = (bf16[4,128,256]{2,1,0:T(8,128)(2,1)S(1)}, bf16[4,128,256]{2,1,0:T(8,128)(2,1)S(1)}, u32[]{:S(2)}, u32[]{:S(2)}) collective-permute-start(bf16[4,128,256]{2,1,0:T(8,128)(2,1)S(1)} %get-tuple-element.42.s), channel_id=1, source_target_pairs={{0,1},{1,0},{2,3},{3,2},{4,5},{5,4},{6,7},{7,6},{8,9},{9,8},{10,11... | collective-permute-start | bytes 786440 | tf_op jit(solution)/shard_map/ppermute | solution.py:59
  59.0 24.1 %all-to-all-start = ((f32[64,1,640]{2,1,0:T(1,128)}), f32[64,1,640]{2,1,0:T(1,128)S(1)}, u32[]{:S(2)}, u32[]{:S(2)}) async-start(f32[64,1,640]{2,1,0:T(1,128)} %add.59), calls=%async_computation | async-start | bytes 327680 | tf_op jit(solution)/shard_map/all_to_all | solution.py:74
  103.7 5.2 %collective-permute-start.22 = (f32[128,1,640]{2,1,0:T(1,128)S(1)}, f32[128,1,640]{2,1,0:T(1,128)S(1)}, u32[]{:S(2)}, u32[]{:S(2)}) collective-permute-start(f32[128,1,640]{2,1,0:T(1,128)S(1)} %all_to_all.10.mine), channel_id=1, source_target_pairs={{0,2},{1,3},{2,0},{3,1},{4,6},{5,7},{6,4},{7,5},{8,10},{9,11},{10,... | collective-permute-start | bytes 983048 | tf_op jit(solution)/shard_map/ppermute | solution.py:50
